TPU v7x, 32 devices: a whole 2x2x4 slice. The times are simulated.
32 devices in a mesh: seq: 16 (over z, y, x), ch: 2 (over core).
Axes of the slice: x: 2, y: 2, z: 4, core: 2. Of those that a mesh axis runs over, the one named last changes fastest.
Arguments:
- inputs: bfloat16 [4096, 2560], P('seq'), may hold values from -30 to 30
- norm_gain: float32 [2560], replicated, may hold values from 0.5 to 1.5
- branch_weight: bfloat16 [2560, 2560], P('seq', 'ch'), may hold values from -0.125 to 0.125
- input_weight: bfloat16 [2560, 2560], P('seq', 'ch'), may hold values from -0.125 to 0.125
- channel_params: float32 [8, 2560], P(None, 'ch'), may hold values from -16 to 4, as said below
- gate_x_blocks: bfloat16 [10, 256, 256], P('ch', 'seq'), may hold values from -0.375 to 0.375
- gate_a_blocks: bfloat16 [10, 256, 256], P('ch', 'seq'), may hold values from -0.375 to 0.375
- out_weight: bfloat16 [2560, 2560], P('ch', 'seq'), may hold values from -0.125 to 0.125
- ffn_gain: float32 [2560], replicated, may hold values from 0.5 to 1.5
- ffn_gate: bfloat16 [2560, 7680], P('seq', 'ch'), may hold values from -0.125 to 0.125
- ffn_up: bfloat16 [2560, 7680], P('seq', 'ch'), may hold values from -0.125 to 0.125
- ffn_down: bfloat16 [7680, 2560], P('ch', 'seq'), may hold values from -0.0625 to 0.0625
- cotangent: bfloat16 [4096, 2560], P('seq'), may hold values from -6 to 6
Outputs:
- block_out: bfloat16 [4096, 2560], P('seq')
- d_inputs: float32 [4096, 2560], P('seq')
- d_norm_gain: float32 [2560], replicated
- d_branch: float32 [2560, 2560], P('seq', 'ch')
- d_input_w: float32 [2560, 2560], P('seq', 'ch')
- d_channel: float32 [8, 2560], P(None, 'ch')
- d_gate_x: float32 [10, 256, 256], P('ch', 'seq')
- d_gate_a: float32 [10, 256, 256], P('ch', 'seq')
- d_out_weight: float32 [2560, 2560], P('ch', 'seq')
- d_ffn_gain: float32 [2560], replicated
- d_ffn_gate: float32 [2560, 7680], P('seq', 'ch')
- d_ffn_up: float32 [2560, 7680], P('seq', 'ch')
- d_ffn_down: float32 [7680, 2560], P('ch', 'seq')
Inputs may be any that keep to these rules, and one draw needn't show every extreme that they name: Rows 0 to 3 of channel_params are the conv taps, row 4 the conv bias, rows 5 and 6 the gate biases, row 7 the decay parameter of each channel.
All inputs are finite; a program needn't handle non-finite values.
Results may differ from a plain program's by a relative error of at most 0.012.
Values may be sent and summed in bfloat16 or wider, within the bound.
A program may use at most 384 MiB of HBM per device.

v0:
```python
import jax
import jax.numpy as jnp
from jax import lax
from jax.sharding import PartitionSpec as P


def shifted(value, axis, by):
    length = lax.axis_size(axis)
    pairs = [(i, i + by) for i in range(length) if 0 <= i + by < length]
    return lax.ppermute(value, axis, pairs)


def prefix(part, axis, combine, identity, reverse):
    count = lax.axis_size(axis)
    place = lax.axis_index(axis)
    ahead = count - 1 - place if reverse else place
    gathered = jax.tree.map(lambda a: lax.all_gather(a, axis), part)
    state = jax.tree.map(lambda a, e: jnp.zeros_like(a) + jnp.asarray(e, a.dtype), part, identity)

    def one(turn, state):
        source = count - 1 - turn if reverse else turn
        return combine(
            state, jax.tree.map(lambda a: lax.dynamic_index_in_dim(a, source, 0, False), gathered)
        )

    return lax.fori_loop(0, ahead, one, state)


def scaled_norm(values, gain):
    return values * lax.rsqrt(jnp.mean(values * values, axis=-1, keepdims=True) + 1e-06) * gain


def gelu_tanh(values):
    return jax.nn.gelu(values, approximate=True)


def decay_gates(conv_out, pre_x, pre_a, bias_x, bias_a, decay_param, first):
    gate_x = jax.nn.sigmoid(pre_x + bias_x)
    gate_a = jax.nn.sigmoid(pre_a + bias_a)
    log_a = -8.0 * gate_a * jax.nn.softplus(decay_param)
    decay = jnp.exp(log_a)
    mult = jnp.sqrt(jnp.maximum(1.0 - decay * decay, 0.001))
    mult = jnp.where(first, jnp.ones_like(mult), mult)
    return (conv_out * gate_x * mult, decay)


def combine(earlier, later):
    return (earlier[0] * later[0], later[0] * earlier[1] + later[1])


def fetch_mixer(branch_weight, input_weight, gate_x_blocks, gate_a_blocks, out_weight):
    return (
        lax.all_gather(branch_weight, "seq", axis=0, tiled=True),
        lax.all_gather(input_weight, "seq", axis=0, tiled=True),
        lax.all_gather(gate_x_blocks, "seq", axis=1, tiled=True),
        lax.all_gather(gate_a_blocks, "seq", axis=1, tiled=True),
        lax.all_gather(out_weight, "seq", axis=1, tiled=True),
    )


def fetch_ffn(ffn_gate, ffn_up, ffn_down):
    return (
        lax.all_gather(ffn_gate, "seq", axis=0, tiled=True),
        lax.all_gather(ffn_up, "seq", axis=0, tiled=True),
        lax.all_gather(ffn_down, "seq", axis=1, tiled=True),
    )


def shards(
    inputs,
    norm_gain,
    branch_weight,
    input_weight,
    channel_params,
    gate_x_blocks,
    gate_a_blocks,
    out_weight,
    ffn_gain,
    ffn_gate,
    ffn_up,
    ffn_down,
    cotangent,
):
    f32 = jnp.float32
    bf16 = jnp.bfloat16
    tok_rows = inputs.shape[0]
    heads_here = gate_x_blocks.shape[0]
    block_size = gate_x_blocks.shape[2]
    width_here = heads_here * block_size
    first = jnp.logical_and(
        lax.axis_index("seq") == 0, lax.broadcasted_iota(jnp.int32, (tok_rows, 1), 0) == 0
    )
    x_float = inputs.astype(f32)
    n_one_f, norm_back_one = jax.vjp(scaled_norm, x_float, norm_gain)
    n_one = n_one_f.astype(bf16)
    mixer_set = fetch_mixer(branch_weight, input_weight, gate_x_blocks, gate_a_blocks, out_weight)
    full_branch, full_input, full_gx, full_ga, full_out = mixer_set
    y_pre = jnp.dot(n_one, full_branch, preferred_element_type=f32)
    gelu_y, gelu_back_y = jax.vjp(gelu_tanh, y_pre)
    x_branch = jnp.dot(n_one, full_input, preferred_element_type=f32).astype(bf16)
    previous = shifted(x_branch[tok_rows - 3 :], "seq", 1)
    extended = jnp.concatenate([previous, x_branch], axis=0).astype(f32)
    conv_sum = channel_params[4][None, :]
    for offset in range(4):
        conv_sum = (
            conv_sum
            + channel_params[offset][None, :] * extended[3 - offset : 3 - offset + tok_rows]
        )
    conv_out = conv_sum.astype(bf16)
    conv_blocks = conv_out.reshape(tok_rows, heads_here, block_size)
    pre_x = jnp.einsum("thi,hij->thj", conv_blocks, full_gx, preferred_element_type=f32).reshape(
        tok_rows, width_here
    )
    pre_a = jnp.einsum("thi,hij->thj", conv_blocks, full_ga, preferred_element_type=f32).reshape(
        tok_rows, width_here
    )

    def gate_piece(conv_in, px_in, pa_in, bias_x, bias_a, decay_param):
        return decay_gates(conv_in, px_in, pa_in, bias_x, bias_a, decay_param, first)

    (driven, decay), gate_back = jax.vjp(
        gate_piece,
        conv_out.astype(f32),
        pre_x,
        pre_a,
        channel_params[5],
        channel_params[6],
        channel_params[7],
    )
    cum_decay, local_state = lax.associative_scan(combine, (decay, driven))
    identity = (jnp.ones((width_here,), f32), jnp.zeros((width_here,), f32))
    carry_decay, carry_state = prefix(
        (cum_decay[-1], local_state[-1]), "seq", combine, identity, False
    )
    states = local_state + cum_decay * carry_state[None, :]
    branch_out = (states * gelu_y).astype(bf16)
    mixed = lax.psum(jnp.dot(branch_out, full_out, preferred_element_type=f32), "ch")
    resid = x_float + mixed
    n_two_f, norm_back_two = jax.vjp(scaled_norm, resid, ffn_gain)
    n_two = n_two_f.astype(bf16)
    ffn_set = fetch_ffn(ffn_gate, ffn_up, ffn_down)
    full_gate, full_up, full_down = ffn_set
    gate_pre = jnp.dot(n_two, full_gate, preferred_element_type=f32)
    up_pre = jnp.dot(n_two, full_up, preferred_element_type=f32)
    gate_act, gelu_back_gate = jax.vjp(gelu_tanh, gate_pre)
    hidden = (gate_act * up_pre).astype(bf16)
    ffn_out = lax.psum(
        jnp.dot(hidden, full_down, preferred_element_type=f32).astype(jnp.bfloat16), "ch"
    ).astype(jnp.float32)
    block_out = (resid + ffn_out).astype(bf16)
    back_gate, back_up, back_down = fetch_ffn(ffn_gate, ffn_up, ffn_down)
    d_hidden = jnp.einsum("td,fd->tf", cotangent, back_down, preferred_element_type=f32)
    d_down_term = jnp.einsum("tf,td->fd", hidden, cotangent, preferred_element_type=f32)
    d_gate = gelu_back_gate(d_hidden * up_pre)[0].astype(bf16)
    d_up = (d_hidden * gate_act).astype(bf16)
    d_n_two = lax.psum(
        (
            jnp.einsum("tf,df->td", d_gate, back_gate, preferred_element_type=f32)
            + jnp.einsum("tf,df->td", d_up, back_up, preferred_element_type=f32)
        ).astype(jnp.bfloat16),
        "ch",
    ).astype(jnp.float32)
    d_gate_term = jnp.einsum("td,tf->df", n_two, d_gate, preferred_element_type=f32)
    d_up_term = jnp.einsum("td,tf->df", n_two, d_up, preferred_element_type=f32)
    ffn_grads = (
        lax.psum_scatter(d_gate_term, "seq", scatter_dimension=0, tiled=True),
        lax.psum_scatter(d_up_term, "seq", scatter_dimension=0, tiled=True),
        lax.psum_scatter(d_down_term, "seq", scatter_dimension=1, tiled=True),
    )
    d_resid_norm, d_ffn_gain_term = norm_back_two(d_n_two)
    d_resid = cotangent.astype(f32) + d_resid_norm
    d_mixed = d_resid.astype(bf16)
    back_branch, back_input, back_gx, back_ga, back_out = fetch_mixer(
        branch_weight, input_weight, gate_x_blocks, gate_a_blocks, out_weight
    )
    d_branch_out = jnp.einsum("td,wd->tw", d_mixed, back_out, preferred_element_type=f32)
    d_out_term = jnp.einsum("tw,td->wd", branch_out, d_mixed, preferred_element_type=f32)
    d_y = gelu_back_y(d_branch_out * states)[0].astype(bf16)
    direct_grad = d_branch_out * gelu_y
    shifted_decay = jnp.concatenate([decay[1:], jnp.ones((1, width_here), f32)], axis=0)
    cum_later, local_adj = lax.associative_scan(combine, (shifted_decay, direct_grad), reverse=True)
    _, carry_adj = prefix(
        (decay[0] * cum_later[0], decay[0] * local_adj[0]), "seq", combine, identity, True
    )
    adjoint = local_adj + cum_later * carry_adj[None, :]
    states_before = jnp.concatenate([carry_state[None, :], states[:-1]], axis=0)
    d_decay = adjoint * states_before
    d_conv_direct, d_pre_x, d_pre_a, d_bias_x, d_bias_a, d_decay_param = gate_back(
        (adjoint, d_decay)
    )
    d_px_low = d_pre_x.astype(bf16).reshape(tok_rows, heads_here, block_size)
    d_pa_low = d_pre_a.astype(bf16).reshape(tok_rows, heads_here, block_size)
    d_conv = d_conv_direct + (
        jnp.einsum("thj,hij->thi", d_px_low, back_gx, preferred_element_type=f32)
        + jnp.einsum("thj,hij->thi", d_pa_low, back_ga, preferred_element_type=f32)
    ).reshape(tok_rows, width_here)
    d_gx_term = jnp.einsum("thi,thj->hij", conv_blocks, d_px_low, preferred_element_type=f32)
    d_ga_term = jnp.einsum("thi,thj->hij", conv_blocks, d_pa_low, preferred_element_type=f32)
    following = shifted(d_conv[:3], "seq", -1)
    d_extended = jnp.concatenate([d_conv, following], axis=0)
    d_xb_sum = jnp.zeros((tok_rows, width_here), f32)
    tap_grads = []
    for offset in range(4):
        d_xb_sum = (
            d_xb_sum + channel_params[offset][None, :] * d_extended[offset : offset + tok_rows]
        )
        tap_grads.append(jnp.sum(d_conv * extended[3 - offset : 3 - offset + tok_rows], axis=0))
    d_xb = d_xb_sum.astype(bf16)
    d_channel_term = jnp.stack(
        tap_grads + [jnp.sum(d_conv, axis=0), d_bias_x, d_bias_a, d_decay_param], axis=0
    )
    d_n_one = lax.psum(
        (
            jnp.einsum("tw,dw->td", d_y, back_branch, preferred_element_type=f32)
            + jnp.einsum("tw,dw->td", d_xb, back_input, preferred_element_type=f32)
        ).astype(jnp.bfloat16),
        "ch",
    ).astype(jnp.float32)
    d_branch_term = jnp.einsum("td,tw->dw", n_one, d_y, preferred_element_type=f32)
    d_input_term = jnp.einsum("td,tw->dw", n_one, d_xb, preferred_element_type=f32)
    mixer_grads = (
        lax.psum_scatter(d_branch_term, "seq", scatter_dimension=0, tiled=True),
        lax.psum_scatter(d_input_term, "seq", scatter_dimension=0, tiled=True),
        lax.psum_scatter(d_gx_term, "seq", scatter_dimension=1, tiled=True),
        lax.psum_scatter(d_ga_term, "seq", scatter_dimension=1, tiled=True),
        lax.psum_scatter(d_out_term, "seq", scatter_dimension=1, tiled=True),
    )
    d_x_norm, d_norm_gain_term = norm_back_one(d_n_one)
    d_inputs = d_resid + d_x_norm
    d_norm_gain, d_ffn_gain, d_channel = lax.psum(
        (d_norm_gain_term, d_ffn_gain_term, d_channel_term), "seq"
    )
    return (
        block_out,
        d_inputs,
        d_norm_gain,
        mixer_grads[0],
        mixer_grads[1],
        d_channel,
        mixer_grads[2],
        mixer_grads[3],
        mixer_grads[4],
        d_ffn_gain,
        ffn_grads[0],
        ffn_grads[1],
        ffn_grads[2],
    )


def solution(mesh):
    placed = (
        P("seq", None),
        P(),
        P("seq", "ch"),
        P("seq", "ch"),
        P(None, "ch"),
        P("ch", "seq", None),
        P("ch", "seq", None),
        P("ch", "seq"),
        P(),
        P("seq", "ch"),
        P("seq", "ch"),
        P("ch", "seq"),
        P("seq", None),
    )
    return jax.shard_map(
        shards,
        mesh=mesh,
        in_specs=placed,
        out_specs=(
            P("seq", None),
            P("seq", None),
            P(),
            P("seq", "ch"),
            P("seq", "ch"),
            P(None, "ch"),
            P("ch", "seq", None),
            P("ch", "seq", None),
            P("ch", "seq"),
            P(),
            P("seq", "ch"),
            P("seq", "ch"),
            P("ch", "seq"),
        ),
        check_vma=False,
    )
```

profile of v0, /device:TPU:25, one launch (start us, length us, event | category | flops | bytes accessed | tf_op | source)
XLA Modules:
  0.0 4124.8 jit_solution(14448737786410291529)
XLA Ops:
  12.0 35.5 all_gather.47
  47.6 45.0 %all_gather.48 = bf16[5,256,256]{2,1,0:T(8,128)(2,1)} all-gather(bf16[5,16,256]{2,1,0:T(8,128)(2,1)S(1)} %copy-done.87), channel_id=1, replica_groups=mesh['seq'=16,'ch'=2] {'seq'}, dimensions={1}, use_global_device_ids=true | all-gather | bytes 696320 | tf_op jit(solution)/shard_map/all_gather | solution.py:56
  92.6 26.2 all-gather.11.cloned.1.call-done
  288.0 25.1 all-gather
  324.5 29.3 all-gather.1
  386.6 25.6 all-reduce.72.cloned.1.call-done
  416.3 216.6 %all-gather.17.cloned.1.call-done = bf16[2560,3840]{1,0:T(8,128)(2,1)} async-done(((bf16[160,3840]{1,0:T(8,128)(2,1)}), bf16[2560,3840]{1,0:T(8,128)(2,1)}) %all-gather.17.cloned.1.call-update) | async-done | bytes 19660816 | tf_op jit(solution)/shard_map/all_gather | solution.py:63
  646.5 206.6 %all-gather.19.cloned.1.call-done = bf16[2560,3840]{1,0:T(8,128)(2,1)} async-done(((bf16[160,3840]{1,0:T(8,128)(2,1)}), bf16[2560,3840]{1,0:T(8,128)(2,1)}) %all-gather.19.cloned.1.call-update) | async-done | bytes 19660816 | tf_op jit(solution)/shard_map/all_gather | solution.py:64
  853.1 13.6 fusion.101
  866.7 206.7 %all-gather.21.cloned.1.call-done = bf16[3840,2560]{0,1:T(8,128)(2,1)} async-done(((bf16[3840,160]{0,1:T(8,128)(2,1)}), bf16[3840,2560]{0,1:T(8,128)(2,1)}) %all-gather.21.cloned.1.call-update) | async-done | bytes 19660816 | tf_op jit(solution)/shard_map/all_gather | solution.py:65
  1073.4 14.8 multiply_convert_fusion
  1263.6 26.0 all-gather.2
  1289.7 30.6 all-gather.3
  1387.2 16.5 fusion.106
  1405.2 15.5 fusion.107
  1422.6 15.3 fusion.108
  1442.9 60.7 %all-reduce.66 = (f32[2560]{0:T(1024)}, f32[8,1280]{1,0:T(8,128)}, f32[2560]{0:T(1024)}) all-reduce(f32[2560]{0:T(1024)S(1)} %get-tuple-element.151, f32[8,1280]{1,0:T(8,128)S(1)} %stack.26, f32[2560]{0:T(1024)S(1)} %copy-done.81), channel_id=1, replica_groups=mesh['seq'=16,'ch'=2] {'seq'}, use_global_device_ids=true, to_apply=%region_13.14 | all-reduce | flops 15360 | bytes 122880 | tf_op jit(solution)/shard_map/psum | solution.py:230
  1509.3 31.2 reduce-scatter.15.cloned.1.call-done
  1540.5 289.6 %reduce-scatter.9.cloned.1.call-done = f32[160,1280]{1,0:T(8,128)} async-done(((f32[2560,1280]{1,0:T(8,128)}), f32[160,1280]{1,0:T(8,128)}) %reduce-scatter.9.cloned.1.call-update) | async-done | bytes 819216 | tf_op jit(solution)/shard_map/reduce_scatter | solution.py:222
  1830.1 280.5 %reduce-scatter.17.cloned.1.call-done = f32[1280,160]{0,1:T(8,128)} async-done(((f32[1280,2560]{0,1:T(8,128)}), f32[1280,160]{0,1:T(8,128)}) %reduce-scatter.17.cloned.1.call-update) | async-done | bytes 819216 | tf_op jit(solution)/shard_map/reduce_scatter | solution.py:226
  2110.6 280.4 %reduce-scatter.11.cloned.1.call-done = f32[160,1280]{1,0:T(8,128)} async-done(((f32[2560,1280]{1,0:T(8,128)}), f32[160,1280]{1,0:T(8,128)}) %reduce-scatter.11.cloned.1.call-update) | async-done | bytes 819216 | tf_op jit(solution)/shard_map/reduce_scatter | solution.py:223
  2391.0 579.2 %reduce-scatter.19.cloned.1.call-done = f32[160,3840]{1,0:T(8,128)} async-done(((f32[2560,3840]{1,0:T(8,128)}), f32[160,3840]{1,0:T(8,128)}) %reduce-scatter.19.cloned.1.call-update) | async-done | bytes 2457616 | tf_op jit(solution)/shard_map/reduce_scatter | solution.py:166
  2970.2 573.9 %reduce-scatter.21.cloned.1.call-done = f32[160,3840]{1,0:T(8,128)} async-done(((f32[2560,3840]{1,0:T(8,128)}), f32[160,3840]{1,0:T(8,128)}) %reduce-scatter.21.cloned.1.call-update) | async-done | bytes 2457616 | tf_op jit(solution)/shard_map/reduce_scatter | solution.py:167
  3544.1 574.0 %reduce-scatter.23.cloned.1.call-done = f32[3840,160]{0,1:T(8,128)} async-done(((f32[3840,2560]{0,1:T(8,128)}), f32[3840,160]{0,1:T(8,128)}) %reduce-scatter.23.cloned.1.call-update) | async-done | bytes 2457616 | tf_op jit(solution)/shard_map/reduce_scatter | solution.py:168
  (629 shorter events, 490.9 us)
Async XLA Ops:
  7.2 111.6 %all-gather.11.cloned.1.call-start = ((), (), s32[]{:S(2)}) async-start(), calls=%async_computation.8 | async-start | bytes 6963200 | tf_op jit(solution)/shard_map/all_gather | solution.py:54
  7.9 347.3 %all-gather.13.cloned.1.call-start = ((), (), s32[]{:S(2)}) async-start(), calls=%async_computation.9 | async-start | bytes 6963200 | tf_op jit(solution)/shard_map/all_gather | solution.py:53
  8.7 354.5 %all-gather.15.cloned.1.call-start = ((), (), s32[]{:S(2)}) async-start(), calls=%async_computation.10 | async-start | bytes 6963200 | tf_op jit(solution)/shard_map/all_gather | solution.py:57
  9.4 402.8 %all-reduce.72.cloned.1.call-start = ((), (), s32[]{:S(2)}) async-start(), calls=%async_computation.11 | async-start | bytes 5242880 | tf_op jit(solution)/shard_map/psum | solution.py:137
  12.0 131.7 %copy-start.51 = (f32[1280]{0:T(1024)}, f32[1280]{0:T(1024)S(1)}, u32[]{:S(2)}) copy-start(f32[1280]{0:T(1024)S(1)} %get-tuple-element.253) | copy-start | bytes 15364
  12.0 131.7 %copy-start.53 = (f32[1280]{0:T(1024)}, f32[1280]{0:T(1024)S(1)}, u32[]{:S(2)}) copy-start(f32[1280]{0:T(1024)S(1)} %get-tuple-element.254) | copy-start | bytes 15364
  12.0 131.7 %copy-start.55 = (f32[1280]{0:T(1024)}, f32[1280]{0:T(1024)S(1)}, u32[]{:S(2)}) copy-start(f32[1280]{0:T(1024)S(1)} %get-tuple-element.255) | copy-start | bytes 15364
  12.0 131.7 %copy-start.57 = (f32[1280]{0:T(1024)}, f32[1280]{0:T(1024)S(1)}, u32[]{:S(2)}) copy-start(f32[1280]{0:T(1024)S(1)} %get-tuple-element.256) | copy-start | bytes 15364
  123.6 6.2 collective-permute-start
  369.7 263.2 %all-gather.17.cloned.1.call-start = ((), (), s32[]{:S(2)}) async-start(), calls=%async_computation.12 | async-start | bytes 20889600 | tf_op jit(solution)/shard_map/all_gather | solution.py:63
  370.3 482.8 %all-gather.19.cloned.1.call-start = ((), (), s32[]{:S(2)}) async-start(), calls=%async_computation.13 | async-start | bytes 20889600 | tf_op jit(solution)/shard_map/all_gather | solution.py:64
  370.9 702.5 %all-gather.21.cloned.1.call-start = ((), (), s32[]{:S(2)}) async-start(), calls=%async_computation.14 | async-start | bytes 20889600 | tf_op jit(solution)/shard_map/all_gather | solution.py:65
  371.6 759.5 %all-reduce.74.cloned.1.call-start = ((), (), s32[]{:S(2)}) async-start(), calls=%async_computation.15 | async-start | bytes 2621440 | tf_op jit(solution)/shard_map/psum | solution.py:156
  414.7 719.4 %copy-start.2 = (f32[256,2560]{1,0:T(8,128)}, f32[256,2560]{1,0:T(8,128)S(1)}, u32[]{:S(2)}) copy-start(f32[256,2560]{1,0:T(8,128)S(1)} %get-tuple-element.191) | copy-start | bytes 7864324
  1110.3 329.2 %all-reduce.76.cloned.1.call-start = ((), (), s32[]{:S(2)}) async-start(), calls=%async_computation.24 | async-start | bytes 5242880 | tf_op jit(solution)/shard_map/psum | solution.py:147
  1344.3 6.9 collective-permute-start.1
  1354.8 154.5 %reduce-scatter.13.cloned.1.call-start = ((), (), s32[]{:S(2)}) async-start(), calls=%async_computation.18 | async-start | bytes 1392640 | tf_op jit(solution)/shard_map/reduce_scatter | solution.py:224
  1357.5 183.0 %reduce-scatter.15.cloned.1.call-start = ((), (), s32[]{:S(2)}) async-start(), calls=%async_computation.19 | async-start | bytes 1392640 | tf_op jit(solution)/shard_map/reduce_scatter | solution.py:225
  1360.0 470.1 %reduce-scatter.9.cloned.1.call-start = ((), (), s32[]{:S(2)}) async-start(), calls=%async_computation.16 | async-start | bytes 13926400 | tf_op jit(solution)/shard_map/reduce_scatter | solution.py:222
  1368.1 742.5 %reduce-scatter.17.cloned.1.call-start = ((), (), s32[]{:S(2)}) async-start(), calls=%async_computation.20 | async-start | bytes 13926400 | tf_op jit(solution)/shard_map/reduce_scatter | solution.py:226
  1377.5 1013.6 %reduce-scatter.11.cloned.1.call-start = ((), (), s32[]{:S(2)}) async-start(), calls=%async_computation.17 | async-start | bytes 13926400 | tf_op jit(solution)/shard_map/reduce_scatter | solution.py:223
  1385.2 1585.0 %reduce-scatter.19.cloned.1.call-start = ((), (), s32[]{:S(2)}) async-start(), calls=%async_computation.21 | async-start | bytes 41779200 | tf_op jit(solution)/shard_map/reduce_scatter | solution.py:166
  1403.7 2140.4 %reduce-scatter.21.cloned.1.call-start = ((), (), s32[]{:S(2)}) async-start(), calls=%async_computation.22 | async-start | bytes 41779200 | tf_op jit(solution)/shard_map/reduce_scatter | solution.py:167
  1420.7 2697.3 %reduce-scatter.23.cloned.1.call-start = ((), (), s32[]{:S(2)}) async-start(), calls=%async_computation.23 | async-start | bytes 41779200 | tf_op jit(solution)/shard_map/reduce_scatter | solution.py:168
  (109 other events, 2333.7 us)
Sparse Core Ops, SparseCore 0:
  10.7 107.9 all-gather.10
  121.4 96.1 all-gather.12
  220.3 95.8 all-gather.14
  369.8 42.3 all-reduce.71
  415.2 217.6 all-gather.16
  635.9 217.0 all-gather.18
  856.3 217.0 all-gather.20
  1110.5 20.6 all-reduce.73
  1354.9 43.0 all-reduce.75
  1400.8 62.3 reduce-scatter.12
  1466.1 74.3 reduce-scatter.14
  1543.4 286.7 reduce-scatter.8
  1833.1 277.4 reduce-scatter.16
  2113.5 277.4 reduce-scatter.10
  2398.6 571.5 reduce-scatter.18
  2977.7 566.2 reduce-scatter.20
  3551.6 566.4 reduce-scatter.22
where the time goes:
time: 4140 us; the launch traced here: 4120 us
  waiting for transfers between devices  3310 us (80%)
  local copies, waits for them, and re-layouts  255 us (6%)
  blocking collectives  252 us (6%)
  matrix products  192 us (5%)
  other arithmetic  94.8 us (2%)
    reduce_scatter x1, waiting for transfers between devices, shards(): lax.psum_scatter(d_gate_term, 'seq', scatter_dimension=0, tiled=True)  579 us
    reduce_scatter x1, waiting for transfers between devices, shards(): lax.psum_scatter(d_down_term, 'seq', scatter_dimension=1, tiled=True)  574 us
    reduce_scatter x1, waiting for transfers between devices, shards(): lax.psum_scatter(d_up_term, 'seq', scatter_dimension=0, tiled=True)  574 us
    reduce_scatter x1, waiting for transfers between devices, shards(): lax.psum_scatter(d_branch_term, 'seq', scatter_dimension=0, tiled=True)  290 us
    reduce_scatter x1, waiting for transfers between devices, shards(): lax.psum_scatter(d_out_term, 'seq', scatter_dimension=1, tiled=True)  280 us
    reduce_scatter x1, waiting for transfers between devices, shards(): lax.psum_scatter(d_input_term, 'seq', scatter_dimension=0, tiled=True)  280 us
    all_gather x1, waiting for transfers between devices, fetch_ffn(): lax.all_gather(ffn_gate, 'seq', axis=0, tiled=True)  217 us
    all_gather x1, waiting for transfers between devices, fetch_ffn(): lax.all_gather(ffn_down, 'seq', axis=1, tiled=True)  207 us
  transfers between devices with their start and end apart: 19, of which 14 were waited for; matrix products, arithmetic and copies ran while one was open for 8% of the time, Pallas kernels for 0%

commit v1 on v0

--- a/solution.py
+++ b/solution.py
@@ -3,11 +3,27 @@
 from jax import lax
 from jax.sharding import PartitionSpec as P
 
+F32 = jnp.float32
+BF16 = jnp.bfloat16
+INNER = 4
+
 
 def shifted(value, axis, by):
     length = lax.axis_size(axis)
     pairs = [(i, i + by) for i in range(length) if 0 <= i + by < length]
     return lax.ppermute(value, axis, pairs)
+
+
+def swap(value, axis, mask):
+    return lax.ppermute(value, axis, [(i, i ^ mask) for i in range(lax.axis_size(axis))])
+
+
+def pick(array, index, axis=0):
+    return lax.dynamic_index_in_dim(array, index, axis, False)
+
+
+def put(array, block, index, axis=0):
+    return lax.dynamic_update_index_in_dim(array, block, index, axis)
 
 
 def prefix(part, axis, combine, identity, reverse):
@@ -48,22 +64,106 @@
     return (earlier[0] * later[0], later[0] * earlier[1] + later[1])
 
 
-def fetch_mixer(branch_weight, input_weight, gate_x_blocks, gate_a_blocks, out_weight):
-    return (
-        lax.all_gather(branch_weight, "seq", axis=0, tiled=True),
-        lax.all_gather(input_weight, "seq", axis=0, tiled=True),
-        lax.all_gather(gate_x_blocks, "seq", axis=1, tiled=True),
-        lax.all_gather(gate_a_blocks, "seq", axis=1, tiled=True),
-        lax.all_gather(out_weight, "seq", axis=1, tiled=True),
-    )
-
-
-def fetch_ffn(ffn_gate, ffn_up, ffn_down):
-    return (
-        lax.all_gather(ffn_gate, "seq", axis=0, tiled=True),
-        lax.all_gather(ffn_up, "seq", axis=0, tiled=True),
-        lax.all_gather(ffn_down, "seq", axis=1, tiled=True),
-    )
+def outer_exchange(blocks):
+    groups = blocks.shape[0]
+    outer = lax.axis_index("seq") // INNER
+    got = blocks
+    own = pick(blocks, outer)
+    received = []
+    for step in range(1, groups):
+        received.append(swap(pick(blocks, outer ^ step), "seq", step * INNER))
+    got = put(jnp.zeros_like(blocks), own, outer)
+    for step in range(1, groups):
+        got = put(got, received[step - 1], outer ^ step)
+    return got
+
+
+def weights_in(pack):
+    groups, kinds, rows, units = pack.shape
+    column = outer_exchange(pack)
+    inner = lax.axis_index("seq") % INNER
+    half = rows // 2
+    first, second = column[:, :, :half], column[:, :, half:]
+    first_x = swap(first, "seq", 1)
+    second_y = swap(second, "seq", 2)
+    first_y, first_xy = (swap(v, "seq", 2) for v in (first, first_x))
+    second_x, second_xy = (swap(v, "seq", 1) for v in (second, second_y))
+    whole = jnp.zeros((kinds, groups, INNER, rows, units), pack.dtype)
+    for mask, top, low in (
+        (0, first, second),
+        (1, first_x, second_x),
+        (2, first_y, second_y),
+        (3, first_xy, second_xy),
+    ):
+        place = inner ^ mask
+        for block, start in ((top, 0), (low, half)):
+            block = jnp.moveaxis(block, 0, 1)[:, :, None]
+            whole = lax.dynamic_update_slice(whole, block, (0, 0, place, start, 0))
+    return whole.reshape(kinds, groups * INNER * rows, units)
+
+
+def grads_out(terms, rows):
+    units = terms[0].shape[1]
+    groups = terms[0].shape[0] // (INNER * rows)
+    inner = lax.axis_index("seq") % INNER
+    half = rows // 2
+    parts = [t.reshape(groups, INNER, rows, units) for t in terms]
+
+    def mine(place, start):
+        return jnp.stack(
+            [lax.dynamic_slice(t, (0, place, start, 0), (groups, 1, half, units))[:, 0] for t in parts],
+            axis=1,
+        )
+
+    def reduce(start, near, far):
+        low = lambda place: mine(place, start).astype(BF16)
+        got_far = swap(low(inner ^ far), "seq", far)
+        got_both = swap(low(inner ^ far ^ near), "seq", far)
+        mid = (mine(inner ^ near, start) + got_both.astype(F32)).astype(BF16)
+        got_near = swap(mid, "seq", near)
+        return (mine(inner, start) + got_far.astype(F32) + got_near.astype(F32)).astype(BF16)
+
+    summed = jnp.concatenate([reduce(0, 1, 2), reduce(half, 2, 1)], axis=2)
+    got = outer_exchange(summed)
+    return jnp.transpose(got, (1, 2, 0, 3)).reshape(3, rows, groups * units).astype(F32)
+
+
+def tokens_in(values):
+    rows, width = values.shape
+    groups = lax.axis_size("seq") // INNER
+    outer = lax.axis_index("seq") // INNER
+    core = lax.axis_index("ch")
+    half = rows // 2
+    own = lax.dynamic_slice_in_dim(values, core * half, half, 0)
+    got = put(jnp.zeros((groups, half, width), values.dtype), own, outer)
+    for step in range(1, groups):
+        got = put(got, swap(own, "seq", step * INNER), outer ^ step)
+    other = swap(got, "ch", 1)
+    first = jnp.where(core == 0, got, other)
+    second = jnp.where(core == 0, other, got)
+    return jnp.stack([first, second], axis=1).reshape(groups * rows, width)
+
+
+def tokens_out(partial, rows):
+    width = partial.shape[1]
+    groups = lax.axis_size("seq") // INNER
+    outer = lax.axis_index("seq") // INNER
+    core = lax.axis_index("ch")
+    half = rows // 2
+    parts = partial.reshape(groups, 2, half, width)
+    theirs = pick(parts, 1 - core, 1).astype(BF16)
+    summed = (pick(parts, core, 1) + swap(theirs, "ch", 1).astype(F32)).astype(BF16)
+    total = pick(summed, outer).astype(F32)
+    for step in range(1, groups):
+        total = total + swap(pick(summed, outer ^ step), "seq", step * INNER).astype(F32)
+    other = swap(total, "ch", 1)
+    return jnp.concatenate(
+        [jnp.where(core == 0, total, other), jnp.where(core == 0, other, total)], axis=0
+    )
+
+
+def scatter(term):
+    return lax.psum_scatter(term.astype(BF16), "seq", scatter_dimension=0, tiled=True).astype(F32)
 
 
 def shards(
@@ -81,20 +181,35 @@
     ffn_down,
     cotangent,
 ):
-    f32 = jnp.float32
-    bf16 = jnp.bfloat16
+    f32 = F32
+    bf16 = BF16
     tok_rows = inputs.shape[0]
     heads_here = gate_x_blocks.shape[0]
     block_size = gate_x_blocks.shape[2]
     width_here = heads_here * block_size
+    depth = ffn_gate.shape[0]
+    groups = lax.axis_size("seq") // INNER
+    units = ffn_gate.shape[1] // groups
     first = jnp.logical_and(
         lax.axis_index("seq") == 0, lax.broadcasted_iota(jnp.int32, (tok_rows, 1), 0) == 0
     )
     x_float = inputs.astype(f32)
     n_one_f, norm_back_one = jax.vjp(scaled_norm, x_float, norm_gain)
     n_one = n_one_f.astype(bf16)
-    mixer_set = fetch_mixer(branch_weight, input_weight, gate_x_blocks, gate_a_blocks, out_weight)
-    full_branch, full_input, full_gx, full_ga, full_out = mixer_set
+
+    full_branch = lax.all_gather(branch_weight, "seq", axis=0, tiled=True)
+    full_input = lax.all_gather(input_weight, "seq", axis=0, tiled=True)
+    full_out = lax.all_gather(out_weight.T, "seq", axis=0, tiled=True)
+    full_gx = lax.all_gather(gate_x_blocks, "seq", axis=1, tiled=True)
+    full_ga = lax.all_gather(gate_a_blocks, "seq", axis=1, tiled=True)
+
+    pack = jnp.stack(
+        [w.reshape(depth, groups, units).transpose(1, 0, 2) for w in (ffn_gate, ffn_up, ffn_down.T)],
+        axis=1,
+    )
+    full_ffn = weights_in(pack)
+    all_cot = tokens_in(cotangent)
+
     y_pre = jnp.dot(n_one, full_branch, preferred_element_type=f32)
     gelu_y, gelu_back_y = jax.vjp(gelu_tanh, y_pre)
     x_branch = jnp.dot(n_one, full_input, preferred_element_type=f32).astype(bf16)
@@ -134,47 +249,34 @@
     )
     states = local_state + cum_decay * carry_state[None, :]
     branch_out = (states * gelu_y).astype(bf16)
-    mixed = lax.psum(jnp.dot(branch_out, full_out, preferred_element_type=f32), "ch")
+    mixed = lax.psum(jnp.einsum("tw,dw->td", branch_out, full_out, preferred_element_type=f32), "ch")
     resid = x_float + mixed
     n_two_f, norm_back_two = jax.vjp(scaled_norm, resid, ffn_gain)
-    n_two = n_two_f.astype(bf16)
-    ffn_set = fetch_ffn(ffn_gate, ffn_up, ffn_down)
-    full_gate, full_up, full_down = ffn_set
-    gate_pre = jnp.dot(n_two, full_gate, preferred_element_type=f32)
-    up_pre = jnp.dot(n_two, full_up, preferred_element_type=f32)
+    all_two = tokens_in(n_two_f.astype(bf16))
+    gate_pre = jnp.dot(all_two, full_ffn[0], preferred_element_type=f32)
+    up_pre = jnp.dot(all_two, full_ffn[1], preferred_element_type=f32)
     gate_act, gelu_back_gate = jax.vjp(gelu_tanh, gate_pre)
     hidden = (gate_act * up_pre).astype(bf16)
-    ffn_out = lax.psum(
-        jnp.dot(hidden, full_down, preferred_element_type=f32).astype(jnp.bfloat16), "ch"
-    ).astype(jnp.float32)
-    block_out = (resid + ffn_out).astype(bf16)
-    back_gate, back_up, back_down = fetch_ffn(ffn_gate, ffn_up, ffn_down)
-    d_hidden = jnp.einsum("td,fd->tf", cotangent, back_down, preferred_element_type=f32)
-    d_down_term = jnp.einsum("tf,td->fd", hidden, cotangent, preferred_element_type=f32)
+    ffn_term = jnp.einsum("tf,df->td", hidden, full_ffn[2], preferred_element_type=f32)
+    block_out = (resid + tokens_out(ffn_term, tok_rows)).astype(bf16)
+
+    d_hidden = jnp.einsum("td,df->tf", all_cot, full_ffn[2], preferred_element_type=f32)
     d_gate = gelu_back_gate(d_hidden * up_pre)[0].astype(bf16)
     d_up = (d_hidden * gate_act).astype(bf16)
-    d_n_two = lax.psum(
-        (
-            jnp.einsum("tf,df->td", d_gate, back_gate, preferred_element_type=f32)
-            + jnp.einsum("tf,df->td", d_up, back_up, preferred_element_type=f32)
-        ).astype(jnp.bfloat16),
-        "ch",
-    ).astype(jnp.float32)
-    d_gate_term = jnp.einsum("td,tf->df", n_two, d_gate, preferred_element_type=f32)
-    d_up_term = jnp.einsum("td,tf->df", n_two, d_up, preferred_element_type=f32)
-    ffn_grads = (
-        lax.psum_scatter(d_gate_term, "seq", scatter_dimension=0, tiled=True),
-        lax.psum_scatter(d_up_term, "seq", scatter_dimension=0, tiled=True),
-        lax.psum_scatter(d_down_term, "seq", scatter_dimension=1, tiled=True),
-    )
+    d_n_two = tokens_out(
+        jnp.einsum("tf,df->td", d_gate, full_ffn[0], preferred_element_type=f32)
+        + jnp.einsum("tf,df->td", d_up, full_ffn[1], preferred_element_type=f32),
+        tok_rows,
+    )
+    d_gate_term = jnp.einsum("td,tf->df", all_two, d_gate, preferred_element_type=f32)
+    d_up_term = jnp.einsum("td,tf->df", all_two, d_up, preferred_element_type=f32)
+    d_down_term = jnp.einsum("td,tf->df", all_cot, hidden, preferred_element_type=f32)
+    ffn_grads = grads_out([d_gate_term, d_up_term, d_down_term], depth)
     d_resid_norm, d_ffn_gain_term = norm_back_two(d_n_two)
     d_resid = cotangent.astype(f32) + d_resid_norm
     d_mixed = d_resid.astype(bf16)
-    back_branch, back_input, back_gx, back_ga, back_out = fetch_mixer(
-        branch_weight, input_weight, gate_x_blocks, gate_a_blocks, out_weight
-    )
-    d_branch_out = jnp.einsum("td,wd->tw", d_mixed, back_out, preferred_element_type=f32)
-    d_out_term = jnp.einsum("tw,td->wd", branch_out, d_mixed, preferred_element_type=f32)
+    d_branch_out = jnp.einsum("td,dw->tw", d_mixed, full_out, preferred_element_type=f32)
+    d_out_term = jnp.einsum("td,tw->dw", d_mixed, branch_out, preferred_element_type=f32)
     d_y = gelu_back_y(d_branch_out * states)[0].astype(bf16)
     direct_grad = d_branch_out * gelu_y
     shifted_decay = jnp.concatenate([decay[1:], jnp.ones((1, width_here), f32)], axis=0)
@@ -191,8 +293,8 @@
     d_px_low = d_pre_x.astype(bf16).reshape(tok_rows, heads_here, block_size)
     d_pa_low = d_pre_a.astype(bf16).reshape(tok_rows, heads_here, block_size)
     d_conv = d_conv_direct + (
-        jnp.einsum("thj,hij->thi", d_px_low, back_gx, preferred_element_type=f32)
-        + jnp.einsum("thj,hij->thi", d_pa_low, back_ga, preferred_element_type=f32)
+        jnp.einsum("thj,hij->thi", d_px_low, full_gx, preferred_element_type=f32)
+        + jnp.einsum("thj,hij->thi", d_pa_low, full_ga, preferred_element_type=f32)
     ).reshape(tok_rows, width_here)
     d_gx_term = jnp.einsum("thi,thj->hij", conv_blocks, d_px_low, preferred_element_type=f32)
     d_ga_term = jnp.einsum("thi,thj->hij", conv_blocks, d_pa_low, preferred_element_type=f32)
@@ -211,20 +313,13 @@
     )
     d_n_one = lax.psum(
         (
-            jnp.einsum("tw,dw->td", d_y, back_branch, preferred_element_type=f32)
-            + jnp.einsum("tw,dw->td", d_xb, back_input, preferred_element_type=f32)
+            jnp.einsum("tw,dw->td", d_y, full_branch, preferred_element_type=f32)
+            + jnp.einsum("tw,dw->td", d_xb, full_input, preferred_element_type=f32)
         ).astype(jnp.bfloat16),
         "ch",
     ).astype(jnp.float32)
     d_branch_term = jnp.einsum("td,tw->dw", n_one, d_y, preferred_element_type=f32)
     d_input_term = jnp.einsum("td,tw->dw", n_one, d_xb, preferred_element_type=f32)
-    mixer_grads = (
-        lax.psum_scatter(d_branch_term, "seq", scatter_dimension=0, tiled=True),
-        lax.psum_scatter(d_input_term, "seq", scatter_dimension=0, tiled=True),
-        lax.psum_scatter(d_gx_term, "seq", scatter_dimension=1, tiled=True),
-        lax.psum_scatter(d_ga_term, "seq", scatter_dimension=1, tiled=True),
-        lax.psum_scatter(d_out_term, "seq", scatter_dimension=1, tiled=True),
-    )
     d_x_norm, d_norm_gain_term = norm_back_one(d_n_one)
     d_inputs = d_resid + d_x_norm
     d_norm_gain, d_ffn_gain, d_channel = lax.psum(
@@ -234,16 +329,16 @@
         block_out,
         d_inputs,
         d_norm_gain,
-        mixer_grads[0],
-        mixer_grads[1],
+        scatter(d_branch_term),
+        scatter(d_input_term),
         d_channel,
-        mixer_grads[2],
-        mixer_grads[3],
-        mixer_grads[4],
+        lax.psum_scatter(d_gx_term, "seq", scatter_dimension=1, tiled=True),
+        lax.psum_scatter(d_ga_term, "seq", scatter_dimension=1, tiled=True),
+        scatter(d_out_term).T,
         d_ffn_gain,
         ffn_grads[0],
         ffn_grads[1],
-        ffn_grads[2],
+        ffn_grads[2].T,
     )
 
 

time: 4140 us -> 2010 us (0.49)
  waiting for transfers between devices: 3310 us -> 631 us
  local copies, waits for them, and re-layouts: 255 us -> 489 us
  blocking collectives: 252 us -> 398 us
  starting transfers between devices: 6.55 us -> 115 us
  other arithmetic: 94.8 us -> 174 us
  matrix products: 192 us -> 147 us
    reduce_scatter x6 -> x3, waiting for transfers between devices: 2580 us -> 63.8 us  [scatter(): lax.psum_scatter(term.astype(BF16), 'seq', scatter_dimension=0, tiled=True)]
    all_gather x6 -> x3, waiting for transfers between devices: 656 us -> 0.02 us  [the longest x1 0.02 us: shards(): full_branch = lax.all_gather(branch_weight, 'seq', axis=0, tiled=True)]
    ppermute x0 -> x36, waiting for transfers between devices: none -> 389 us  [swap(): lax.ppermute(value, axis, [(i, i ^ mask) for i in range(lax.axis_size(axi...]
    ppermute x0 -> x36, starting transfers between devices: none -> 109 us  [swap(): lax.ppermute(value, axis, [(i, i ^ mask) for i in range(lax.axis_size(axi...]
    all_gather x2, blocking collectives: 80.5 us -> 183 us  [the longest x1 146 us: shards(): full_gx = lax.all_gather(gate_x_blocks, 'seq', axis=1, tiled=True)]
    reduce_scatter x1, waiting for transfers between devices: 0.01 us -> 65.3 us  [shards(): lax.psum_scatter(d_gx_term, 'seq', scatter_dimension=1, tiled=True)]
    reduce_scatter x1, waiting for transfers between devices: 31.2 us -> 77.5 us  [shards(): lax.psum_scatter(d_ga_term, 'seq', scatter_dimension=1, tiled=True)]
    dynamic_update_slice x0 -> x22, local copies, waits for them, and re-layouts: none -> 45.7 us  [the longest x14 23.4 us: put(): return lax.dynamic_update_index_in_dim(array, block, index, axis)]
  transfers between devices with their start and end apart: 19 -> 48, of which waited for: 14 -> 14; matrix products, arithmetic and copies ran while one was open for 8% -> 27% of each run, Pallas kernels for 0% -> 0%
where the time goes in v1:
time: 2010 us; the launch traced here: 1970 us
  waiting for transfers between devices  631 us (31%)
  local copies, waits for them, and re-layouts  489 us (24%)
  blocking collectives  398 us (20%)
  other arithmetic  174 us (9%)
  matrix products  147 us (7%)
  starting transfers between devices  115 us (6%)
    ppermute x36, waiting for transfers between devices, swap(): lax.ppermute(value, axis, [(i, i ^ mask) for i in range(lax.axis_size(axi...  389 us
    all_gather x1, blocking collectives, shards(): full_gx = lax.all_gather(gate_x_blocks, 'seq', axis=1, tiled=True)  146 us
    all_gather x4, blocking collectives, prefix(): gathered = jax.tree.map(lambda a: lax.all_gather(a, axis), part)  132 us
    slice x57, local copies, waits for them, and re-layouts, shards(): lax.associative_scan(combine, (shifted_decay, direct_grad), reverse=True)  113 us
    ppermute x36, starting transfers between devices, swap(): lax.ppermute(value, axis, [(i, i ^ mask) for i in range(lax.axis_size(axi...  109 us
    psum x1, blocking collectives, shards(): lax.psum((d_norm_gain_term, d_ffn_gain_term, d_channel_term), 'seq')  82.4 us
    slice x52, local copies, waits for them, and re-layouts, shards(): cum_decay, local_state = lax.associative_scan(combine, (decay, driven))  80.2 us
    reduce_scatter x1, waiting for transfers between devices, shards(): lax.psum_scatter(d_ga_term, 'seq', scatter_dimension=1, tiled=True)  77.5 us
  transfers between devices with their start and end apart: 48, of which 14 were waited for; matrix products, arithmetic and copies ran while one was open for 27% of the time, Pallas kernels for 0%

profile of v1, /device:TPU:25, one launch (start us, length us, event | category | flops | bytes accessed | tf_op | source)
XLA Modules:
  0.0 1970.2 jit_solution(13536688465086983907)
XLA Ops:
  48.2 145.9 %all_gather.30 = bf16[5,256,256]{2,1,0:T(8,128)(2,1)} all-gather(bf16[5,16,256]{2,1,0:T(8,128)(2,1)S(1)} %copy-done.102), channel_id=1, replica_groups=mesh['seq'=16,'ch'=2] {'seq'}, dimensions={1}, use_global_device_ids=true | all-gather | bytes 696320 | tf_op jit(solution)/shard_map/all_gather | solution.py:203
  194.0 37.1 %all_gather.31 = bf16[5,256,256]{2,1,0:T(8,128)(2,1)} all-gather(bf16[5,16,256]{2,1,0:T(8,128)(2,1)S(1)} %copy-done.103), channel_id=1, replica_groups=mesh['seq'=16,'ch'=2] {'seq'}, dimensions={1}, use_global_device_ids=true | all-gather | bytes 696320 | tf_op jit(solution)/shard_map/all_gather | solution.py:204
  239.6 22.4 %collective-permute-start.22 = (bf16[4,128,2560]{2,1,0:T(8,128)(2,1)}, bf16[4,128,2560]{2,1,0:T(8,128)(2,1)}, u32[]{:S(2)}, u32[]{:S(2)}) collective-permute-start(bf16[4,128,2560]{2,1,0:T(8,128)(2,1)} %bitcast_dynamic-update-slice_fusion.14), channel_id=1, source_target_pairs={{0,1},{1,0},{2,3},{3,2},{4,5},{5,4},{6,7},{7,6},{8,9},{9,8},{10,11... | collective-permute-start | bytes 7864328 | tf_op jit(solution)/shard_map/ppermute | solution.py:18
  285.2 18.0 collective-permute-done
  467.9 50.3 %all-gather = f32[16,1,1280]{2,1,0:T(1,128)S(1)} all-gather(f32[1,1,1280]{2,1,0:T(1,128)S(1)} %add_bitcast_fusion.1), channel_id=1, replica_groups=mesh['seq'=16,'ch'=2] {'seq'}, dimensions={0}, use_global_device_ids=true | all-gather | bytes 87040 | tf_op jit(solution)/shard_map/all_gather | solution.py:33
  529.9 26.4 %all-gather.1 = f32[16,1,1280]{2,1,0:T(1,128)S(1)} all-gather(f32[1,1,1280]{2,1,0:T(1,128)S(1)} %add_bitcast_fusion), channel_id=1, replica_groups=mesh['seq'=16,'ch'=2] {'seq'}, dimensions={0}, use_global_device_ids=true | all-gather | bytes 87040 | tf_op jit(solution)/shard_map/all_gather | solution.py:33
  608.5 15.9 all-reduce.70.cloned.1.call-done
  647.4 38.2 %collective-permute-done.2 = bf16[128,2560]{1,0:T(8,128)(2,1)S(1)} collective-permute-done((bf16[128,2560]{1,0:T(8,128)(2,1)S(1)}, bf16[128,2560]{1,0:T(8,128)(2,1)S(1)}, u32[]{:S(2)}, u32[]{:S(2)}) %collective-permute-start.2) | collective-permute-done | bytes 655392 | tf_op jit(solution)/shard_map/ppermute | solution.py:18
  724.4 14.1 fusion.8
  807.9 28.9 %collective-permute-start.15 = (bf16[128,2560]{1,0:T(8,128)(2,1)}, bf16[128,2560]{1,0:T(8,128)(2,1)}, u32[]{:S(2)}, u32[]{:S(2)}) collective-permute-start(bf16[128,2560]{1,0:T(8,128)(2,1)} %get-tuple-element.261), channel_id=1, source_target_pairs={{0,8},{2,10},{4,12},{6,14},{8,0},{10,2},{12,4},{14,6},{16,24},{18,... | collective-permute-start | bytes 1966088 | tf_op jit(solution)/shard_map/ppermute | solution.py:18
  836.8 41.6 %collective-permute-done.25 = bf16[128,2560]{1,0:T(8,128)(2,1)S(1)} collective-permute-done((bf16[128,2560]{1,0:T(8,128)(2,1)S(1)}, bf16[128,2560]{1,0:T(8,128)(2,1)S(1)}, u32[]{:S(2)}, u32[]{:S(2)}) %collective-permute-start.25) | collective-permute-done | bytes 655392 | tf_op jit(solution)/shard_map/ppermute | solution.py:18
  1098.9 10.9 rev.9
  1109.8 25.0 %all-gather.2 = f32[16,1,1280]{2,1,0:T(1,128)S(1)} all-gather(f32[1,1,1280]{2,1,0:T(1,128)S(1)} %get-tuple-element.265), channel_id=1, replica_groups=mesh['seq'=16,'ch'=2] {'seq'}, dimensions={0}, use_global_device_ids=true | all-gather | bytes 87040 | tf_op jit(solution)/shard_map/all_gather | solution.py:33
  1134.8 30.6 %all-gather.3 = f32[16,1,1280]{2,1,0:T(1,128)S(1)} all-gather(f32[1,1,1280]{2,1,0:T(1,128)S(1)} %get-tuple-element.264), channel_id=1, replica_groups=mesh['seq'=16,'ch'=2] {'seq'}, dimensions={0}, use_global_device_ids=true | all-gather | bytes 87040 | tf_op jit(solution)/shard_map/all_gather | solution.py:33
  1278.7 36.6 %collective-permute-done.30 = bf16[4,3,80,960]{3,2,1,0:T(8,128)(2,1)} collective-permute-done((bf16[4,3,80,960]{3,2,1,0:T(8,128)(2,1)}, bf16[4,3,80,960]{3,2,1,0:T(8,128)(2,1)}, u32[]{:S(2)}, u32[]{:S(2)}) %collective-permute-start.30) | collective-permute-done | bytes 1843232 | tf_op jit(solution)/shard_map/ppermute | solution.py:18
  1326.2 42.4 %collective-permute-done.33 = bf16[4,3,80,960]{3,2,1,0:T(8,128)(2,1)} collective-permute-done((bf16[4,3,80,960]{3,2,1,0:T(8,128)(2,1)}, bf16[4,3,80,960]{3,2,1,0:T(8,128)(2,1)}, u32[]{:S(2)}, u32[]{:S(2)}) %collective-permute-start.33) | collective-permute-done | bytes 1843232 | tf_op jit(solution)/shard_map/ppermute | solution.py:18
  1373.8 78.7 %collective-permute-done.31 = bf16[4,3,80,960]{3,2,1,0:T(8,128)(2,1)} collective-permute-done((bf16[4,3,80,960]{3,2,1,0:T(8,128)(2,1)}, bf16[4,3,80,960]{3,2,1,0:T(8,128)(2,1)}, u32[]{:S(2)}, u32[]{:S(2)}) %collective-permute-start.31) | collective-permute-done | bytes 1843232 | tf_op jit(solution)/shard_map/ppermute | solution.py:18
  1457.2 47.8 %collective-permute-done.32 = bf16[4,3,80,960]{3,2,1,0:T(8,128)(2,1)} collective-permute-done((bf16[4,3,80,960]{3,2,1,0:T(8,128)(2,1)}, bf16[4,3,80,960]{3,2,1,0:T(8,128)(2,1)}, u32[]{:S(2)}, u32[]{:S(2)}) %collective-permute-start.32) | collective-permute-done | bytes 1843232 | tf_op jit(solution)/shard_map/ppermute | solution.py:18
  1518.6 69.7 %collective-permute-done.35 = bf16[3,160,960]{2,1,0:T(8,128)(2,1)} collective-permute-done((bf16[3,160,960]{2,1,0:T(8,128)(2,1)}, bf16[3,160,960]{2,1,0:T(8,128)(2,1)}, u32[]{:S(2)}, u32[]{:S(2)}) %collective-permute-start.35) | collective-permute-done | bytes 921632 | tf_op jit(solution)/shard_map/ppermute | solution.py:18
  1592.8 33.3 %collective-permute-done.37 = bf16[3,160,960]{2,1,0:T(8,128)(2,1)} collective-permute-done((bf16[3,160,960]{2,1,0:T(8,128)(2,1)}, bf16[3,160,960]{2,1,0:T(8,128)(2,1)}, u32[]{:S(2)}, u32[]{:S(2)}) %collective-permute-start.37) | collective-permute-done | bytes 921632 | tf_op jit(solution)/shard_map/ppermute | solution.py:18
  1664.0 82.4 %all-reduce.66 = (f32[2560]{0:T(1024)}, f32[8,1280]{1,0:T(8,128)}, f32[2560]{0:T(1024)}) all-reduce(f32[2560]{0:T(1024)S(1)} %get-tuple-element.151, f32[8,1280]{1,0:T(8,128)S(1)} %stack.94, f32[2560]{0:T(1024)S(1)} %copy-done.98), channel_id=1, replica_groups=mesh['seq'=16,'ch'=2] {'seq'}, use_global_device_ids=true, to_apply=%region_11.12 | all-reduce | flops 15360 | bytes 122880 | tf_op jit(solution)/shard_map/psum | solution.py:325
  1754.4 63.8 %reduce-scatter.8.cloned.1.call-done = bf16[160,1280]{1,0:T(8,128)(2,1)} async-done(((bf16[2560,1280]{1,0:T(8,128)(2,1)}), bf16[160,1280]{1,0:T(8,128)(2,1)}) %reduce-scatter.8.cloned.1.call-update) | async-done | bytes 409616 | tf_op jit(solution)/shard_map/reduce_scatter | solution.py:166
  1820.1 65.3 %reduce-scatter.10.cloned.1.call-done = f32[5,16,256]{2,1,0:T(8,128)} async-done(((f32[5,256,256]{2,1,0:T(8,128)}), f32[5,16,256]{2,1,0:T(8,128)}) %reduce-scatter.10.cloned.1.call-update) | async-done | bytes 81936 | tf_op jit(solution)/shard_map/reduce_scatter | solution.py:335
  1885.4 77.5 %reduce-scatter.12.cloned.1.call-done = f32[5,16,256]{2,1,0:T(8,128)} async-done(((f32[5,256,256]{2,1,0:T(8,128)}), f32[5,16,256]{2,1,0:T(8,128)}) %reduce-scatter.12.cloned.1.call-update) | async-done | bytes 81936 | tf_op jit(solution)/shard_map/reduce_scatter | solution.py:336
  (821 shorter events, 851.3 us)
Async XLA Ops:
  7.2 260.4 %all-gather.8.cloned.1.call-start = ((), (), s32[]{:S(2)}) async-start(), calls=%async_computation.5 | async-start | bytes 6963200 | tf_op jit(solution)/shard_map/all_gather | solution.py:201
  7.9 549.6 %all-gather.10.cloned.1.call-start = ((), (), s32[]{:S(2)}) async-start(), calls=%async_computation.6 | async-start | bytes 6963200 | tf_op jit(solution)/shard_map/all_gather | solution.py:200
  8.7 556.8 %all-gather.12.cloned.1.call-start = ((), (), s32[]{:S(2)}) async-start(), calls=%async_computation.7 | async-start | bytes 6963200 | tf_op jit(solution)/shard_map/all_gather | solution.py:202
  11.6 219.6 %collective-permute-start.19 = (bf16[128,2560]{1,0:T(8,128)(2,1)}, bf16[128,2560]{1,0:T(8,128)(2,1)}, u32[]{:S(2)}, u32[]{:S(2)}) collective-permute-start(bf16[128,2560]{1,0:T(8,128)(2,1)} %get-tuple-element.189), channel_id=1, source_target_pairs={{0,8},{2,10},{4,12},{6,14},{8,0},{10,2},{12,4},{14,6},{16,24},{18,... | collective-permute-start | bytes 1966088 | tf_op jit(solution)/shard_map/ppermute | solution.py:18
  11.8 223.9 %collective-permute-start.20 = (bf16[128,2560]{1,0:T(8,128)(2,1)}, bf16[128,2560]{1,0:T(8,128)(2,1)}, u32[]{:S(2)}, u32[]{:S(2)}) collective-permute-start(bf16[128,2560]{1,0:T(8,128)(2,1)} %get-tuple-element.189), channel_id=1, source_target_pairs={{0,16},{2,18},{4,20},{6,22},{8,24},{10,26},{12,28},{14,30},{16,0},... | collective-permute-start | bytes 1966088 | tf_op jit(solution)/shard_map/ppermute | solution.py:18
  11.8 225.9 %collective-permute-start.21 = (bf16[128,2560]{1,0:T(8,128)(2,1)}, bf16[128,2560]{1,0:T(8,128)(2,1)}, u32[]{:S(2)}, u32[]{:S(2)}) collective-permute-start(bf16[128,2560]{1,0:T(8,128)(2,1)} %get-tuple-element.189), channel_id=1, source_target_pairs={{0,24},{2,26},{4,28},{6,30},{8,16},{10,18},{12,20},{14,22},{16,8},... | collective-permute-start | bytes 1966088 | tf_op jit(solution)/shard_map/ppermute | solution.py:18
  39.8 222.3 %collective-permute-start.5 = (bf16[3,160,960]{2,1,0:T(8,128)(2,1)}, bf16[3,160,960]{2,1,0:T(8,128)(2,1)}, u32[]{:S(2)}, u32[]{:S(2)}) collective-permute-start(bf16[3,160,960]{2,1,0:T(8,128)(2,1)} %bitcast.267), channel_id=1, source_target_pairs={{0,8},{2,10},{4,12},{6,14},{8,0},{10,2},{12,4},{14,6},{16,24},{18,... | collective-permute-start | bytes 2764808 | tf_op jit(solution)/shard_map/ppermute | solution.py:18
  41.1 223.2 %collective-permute-start.6 = (bf16[3,160,960]{2,1,0:T(8,128)(2,1)}, bf16[3,160,960]{2,1,0:T(8,128)(2,1)}, u32[]{:S(2)}, u32[]{:S(2)}) collective-permute-start(bf16[3,160,960]{2,1,0:T(8,128)(2,1)} %bitcast.266), channel_id=1, source_target_pairs={{0,16},{2,18},{4,20},{6,22},{8,24},{10,26},{12,28},{14,30},{16,0},... | collective-permute-start | bytes 2764808 | tf_op jit(solution)/shard_map/ppermute | solution.py:18
  41.4 583.0 %all-reduce.70.cloned.1.call-start = ((), (), s32[]{:S(2)}) async-start(), calls=%async_computation.8 | async-start | bytes 5242880 | tf_op jit(solution)/shard_map/psum | solution.py:252
  239.6 363.6 %collective-permute-start.22 = (bf16[4,128,2560]{2,1,0:T(8,128)(2,1)}, bf16[4,128,2560]{2,1,0:T(8,128)(2,1)}, u32[]{:S(2)}, u32[]{:S(2)}) collective-permute-start(bf16[4,128,2560]{2,1,0:T(8,128)(2,1)} %bitcast_dynamic-update-slice_fusion.14), channel_id=1, source_target_pairs={{0,1},{1,0},{2,3},{3,2},{4,5},{5,4},{6,7},{7,6},{8,9},{9,8},{10,11... | collective-permute-start | bytes 7864328 | tf_op jit(solution)/shard_map/ppermute | solution.py:18
  279.5 306.2 %collective-permute-start.8 = (bf16[4,3,80,960]{3,2,0,1:T(8,128)(2,1)}, bf16[4,3,80,960]{3,2,0,1:T(8,128)(2,1)}, u32[]{:S(2)}, u32[]{:S(2)}) collective-permute-start(bf16[4,3,80,960]{3,2,0,1:T(8,128)(2,1)} %get-tuple-element.247), channel_id=1, source_target_pairs={{0,2},{2,0},{4,6},{6,4},{8,10},{10,8},{12,14},{14,12},{16,18},{18,... | collective-permute-start | bytes 5529608 | tf_op jit(solution)/shard_map/ppermute | solution.py:18
  279.5 317.7 %collective-permute-start.10 = (bf16[4,3,80,960]{3,2,0,1:T(8,128)(2,1)}, bf16[4,3,80,960]{3,2,0,1:T(8,128)(2,1)}, u32[]{:S(2)}, u32[]{:S(2)}) collective-permute-start(bf16[4,3,80,960]{3,2,0,1:T(8,128)(2,1)} %get-tuple-element.247), channel_id=1, source_target_pairs={{0,4},{2,6},{4,0},{6,2},{8,12},{10,14},{12,8},{14,10},{16,20},{18,... | collective-permute-start | bytes 5529608 | tf_op jit(solution)/shard_map/ppermute | solution.py:18
  283.7 310.5 %collective-permute-start.9 = (bf16[4,3,80,960]{3,2,0,1:T(8,128)(2,1)}, bf16[4,3,80,960]{3,2,0,1:T(8,128)(2,1)}, u32[]{:S(2)}, u32[]{:S(2)}) collective-permute-start(bf16[4,3,80,960]{3,2,0,1:T(8,128)(2,1)} %get-tuple-element.246), channel_id=1, source_target_pairs={{0,2},{2,0},{4,6},{6,4},{8,10},{10,8},{12,14},{14,12},{16,18},{18,... | collective-permute-start | bytes 5529608 | tf_op jit(solution)/shard_map/ppermute | solution.py:18
  303.2 286.1 %collective-permute-start.11 = (bf16[4,3,80,960]{3,2,0,1:T(8,128)(2,1)}, bf16[4,3,80,960]{3,2,0,1:T(8,128)(2,1)}, u32[]{:S(2)}, u32[]{:S(2)}) collective-permute-start(bf16[4,3,80,960]{3,2,0,1:T(8,128)(2,1)} %get-tuple-element.246), channel_id=1, source_target_pairs={{0,4},{2,6},{4,0},{6,2},{8,12},{10,14},{12,8},{14,10},{16,20},{18,... | collective-permute-start | bytes 5529608 | tf_op jit(solution)/shard_map/ppermute | solution.py:18
  572.0 1089.2 %all-reduce.72.cloned.1.call-start = ((), (), s32[]{:S(2)}) async-start(), calls=%async_computation.9 | async-start | bytes 2621440 | tf_op jit(solution)/shard_map/psum | solution.py:314
  1199.9 550.6 %reduce-scatter.6.cloned.1.call-start = ((), (), s32[]{:S(2)}) async-start(), calls=%async_computation.10 | async-start | bytes 6963200 | tf_op jit(solution)/shard_map/reduce_scatter | solution.py:166
  1204.8 547.6 %reduce-scatter.14.cloned.1.call-start = ((), (), s32[]{:S(2)}) async-start(), calls=%async_computation.14 | async-start | bytes 6963200 | tf_op jit(solution)/shard_map/reduce_scatter | solution.py:166
  1212.2 605.9 %reduce-scatter.8.cloned.1.call-start = ((), (), s32[]{:S(2)}) async-start(), calls=%async_computation.11 | async-start | bytes 6963200 | tf_op jit(solution)/shard_map/reduce_scatter | solution.py:166
  1217.1 668.3 %reduce-scatter.10.cloned.1.call-start = ((), (), s32[]{:S(2)}) async-start(), calls=%async_computation.12 | async-start | bytes 1392640 | tf_op jit(solution)/shard_map/reduce_scatter | solution.py:335
  1319.1 133.4 %collective-permute-start.31 = (bf16[4,3,80,960]{3,2,1,0:T(8,128)(2,1)}, bf16[4,3,80,960]{3,2,1,0:T(8,128)(2,1)}, u32[]{:S(2)}, u32[]{:S(2)}) collective-permute-start(bf16[4,3,80,960]{3,2,1,0:T(8,128)(2,1)} %fusion.11), channel_id=1, source_target_pairs={{0,2},{2,0},{4,6},{6,4},{8,10},{10,8},{12,14},{14,12},{16,18},{18,... | collective-permute-start | bytes 5529608 | tf_op jit(solution)/shard_map/ppermute | solution.py:18
  1326.2 178.8 %collective-permute-start.32 = (bf16[4,3,80,960]{3,2,1,0:T(8,128)(2,1)}, bf16[4,3,80,960]{3,2,1,0:T(8,128)(2,1)}, u32[]{:S(2)}, u32[]{:S(2)}) collective-permute-start(bf16[4,3,80,960]{3,2,1,0:T(8,128)(2,1)} %pad_maximum_fusion.6), channel_id=1, source_target_pairs={{0,2},{2,0},{4,6},{6,4},{8,10},{10,8},{12,14},{14,12},{16,18},{18,... | collective-permute-start | bytes 5529608 | tf_op jit(solution)/shard_map/ppermute | solution.py:18
  1372.3 132.6 %collective-permute-start.34 = (bf16[4,3,80,960]{3,2,1,0:T(8,128)(2,1)}, bf16[4,3,80,960]{3,2,1,0:T(8,128)(2,1)}, u32[]{:S(2)}, u32[]{:S(2)}) collective-permute-start(bf16[4,3,80,960]{3,2,1,0:T(8,128)(2,1)} %fusion.14), channel_id=1, source_target_pairs={{0,4},{2,6},{4,0},{6,2},{8,12},{10,14},{12,8},{14,10},{16,20},{18,... | collective-permute-start | bytes 5529608 | tf_op jit(solution)/shard_map/ppermute | solution.py:18
  1373.8 589.1 %reduce-scatter.12.cloned.1.call-start = ((), (), s32[]{:S(2)}) async-start(), calls=%async_computation.13 | async-start | bytes 1392640 | tf_op jit(solution)/shard_map/reduce_scatter | solution.py:336
  1510.3 115.8 %collective-permute-start.37 = (bf16[3,160,960]{2,1,0:T(8,128)(2,1)}, bf16[3,160,960]{2,1,0:T(8,128)(2,1)}, u32[]{:S(2)}, u32[]{:S(2)}) collective-permute-start(bf16[3,160,960]{2,1,0:T(8,128)(2,1)} %get-tuple-element.241), channel_id=1, source_target_pairs={{0,24},{2,26},{4,28},{6,30},{8,16},{10,18},{12,20},{14,22},{16,8},... | collective-permute-start | bytes 2764808 | tf_op jit(solution)/shard_map/ppermute | solution.py:18
  (166 other events, 5908.3 us)
Sparse Core Ops, SparseCore 0:
  10.7 171.6 all-gather.7
  185.1 132.6 all-gather.9
  320.5 133.6 all-gather.11
  572.1 52.1 all-reduce.69
  1200.0 40.7 all-reduce.71
  1242.9 246.8 reduce-scatter.5
  1492.2 174.2 reduce-scatter.13
  1668.8 149.2 reduce-scatter.7
  1821.1 64.2 reduce-scatter.9
  1888.2 74.6 reduce-scatter.11

commit v2 on v1

v2 whole, which is shorter than its diff:
```python
import functools

import jax
import jax.numpy as jnp
from jax import lax
from jax.experimental import pallas as pl
from jax.experimental.pallas import tpu as pltpu
from jax.sharding import PartitionSpec as P

F32 = jnp.float32
BF16 = jnp.bfloat16
INNER = 4
MESH = pl.DeviceIdType.MESH
VMEM = pl.BlockSpec(memory_space=pltpu.VMEM)
ANY = pl.BlockSpec(memory_space=pl.ANY)


def swap(value, axis, mask):
    return lax.ppermute(value, axis, [(i, i ^ mask) for i in range(lax.axis_size(axis))])


def pick(array, index, axis=0):
    return lax.dynamic_index_in_dim(array, index, axis, False)


def put(array, block, index, axis=0):
    return lax.dynamic_update_index_in_dim(array, block, index, axis)


def scaled_norm(values, gain):
    return values * lax.rsqrt(jnp.mean(values * values, axis=-1, keepdims=True) + 1e-06) * gain


def gelu_tanh(values):
    return jax.nn.gelu(values, approximate=True)


def whereabouts():
    me = lax.axis_index("seq")
    outer = me // INNER
    inner = me - outer * INNER
    y = inner // 2
    x = inner - 2 * y
    by_x = me + 1 - 2 * x
    by_y = me + 2 - 4 * y
    return me, outer, by_x, by_y, by_x + 2 - 4 * y


def when(condition, action):
    if condition is None:
        action()
    else:
        pl.when(condition)(action)


def both(one, other):
    if one is None or other is None:
        return one if other is None else other
    return jnp.logical_and(one, other)


def greet(peers):
    barrier = pltpu.get_barrier_semaphore()
    for condition, peer in peers:
        when(
            condition,
            lambda peer=peer: pl.semaphore_signal(
                barrier, inc=1, device_id={"seq": peer}, device_id_type=MESH
            ),
        )
    count = 0
    for condition, _ in peers:
        count = count + (1 if condition is None else condition.astype(jnp.int32))
    pl.semaphore_wait(barrier, count)


def greet_all(n, me):
    barrier = pltpu.get_barrier_semaphore()

    def hello(step, carry):
        pl.semaphore_signal(
            barrier, inc=1, device_id={"seq": lax.rem(me + step, n)}, device_id_type=MESH
        )
        return carry

    lax.fori_loop(1, n, hello, 0)
    pl.semaphore_wait(barrier, n - 1)


def remote(src, dst, send_sem, recv_sem, place):
    return pltpu.make_async_remote_copy(
        src_ref=src,
        dst_ref=dst,
        send_sem=send_sem,
        recv_sem=recv_sem,
        device_id={"seq": place},
        device_id_type=MESH,
    )


def params(collective_id, mib):
    return pltpu.CompilerParams(
        collective_id=collective_id, has_side_effects=True, vmem_limit_bytes=mib * 2**20
    )


def gather_body(n, w_ref, g_ref, wo_ref, go_ref, send_w, send_g, recv_w, recv_g, here):
    groups = n // INNER
    me, outer, by_x, by_y, by_xy = whereabouts()
    above, below = outer + 1 < groups, outer > 0
    greet([(below, me - INNER), (above, me + INNER), (None, by_x), (None, by_y)])
    half = w_ref.shape[2] // 2
    keep_w = pltpu.make_async_copy(w_ref, wo_ref.at[:, me], here.at[0])
    keep_g = pltpu.make_async_copy(g_ref, go_ref.at[me], here.at[1])
    keep_w.start()
    keep_g.start()
    sent = []

    def copies(h, source, kind, target, own):
        cols = pl.ds(h * half, half)
        w_dst = wo_ref.at[:, source, :, cols]
        g_dst = go_ref.at[source, :, cols]
        w_src = w_ref.at[:, :, cols] if own else w_dst
        g_src = g_ref.at[:, cols] if own else g_dst
        return (
            remote(w_src, w_dst, send_w.at[h, source, kind], recv_w.at[h, source], target),
            remote(g_src, g_dst, send_g.at[h, source, kind], recv_g.at[h, source], target),
        )

    def send(condition, *what):
        def go():
            for copy in copies(*what):
                copy.start()

        when(condition, go)
        sent.append((condition, what))

    def arrive(condition, h, source):
        def go():
            for copy in copies(h, source, 0, by_x, False):
                copy.wait_recv()

        when(condition, go)

    for step in range(groups):
        for h in range(2):
            flip_p, flip_q = (by_x, by_y) if h == 0 else (by_y, by_x)
            if step == 0:
                send(above, h, me, 0, me + INNER, True)
                send(below, h, me, 1, me - INNER, True)
                send(None, h, me, 2, flip_p, True)
                send(None, h, me, 3, flip_q, True)
                continue
            for source, there, onward, kind, to in (
                (me - step * INNER, outer >= step, above, 0, me + INNER),
                (me + step * INNER, outer + step < groups, below, 1, me - INNER),
            ):
                arrive(there, h, source)
                send(both(there, onward), h, source, kind, to, False)
                send(there, h, source, 2, flip_p, False)
                send(there, h, source, 3, flip_q, False)
        for h in range(2):
            flip_p, flip_q = (by_x, by_y) if h == 0 else (by_y, by_x)
            if step == 0:
                arrive(None, h, flip_p)
                send(None, h, flip_p, 3, flip_q, False)
                continue
            for source, there in (
                (flip_p - step * INNER, outer >= step),
                (flip_p + step * INNER, outer + step < groups),
            ):
                arrive(there, h, source)
                send(there, h, source, 3, flip_q, False)
    for place in range(groups):
        shift = (place - outer) * INNER
        for h in range(2):
            arrive(None, h, (by_y if h == 0 else by_x) + shift)
            arrive(None, h, by_xy + shift)
    for condition, what in sent:

        def finish(what=what):
            for copy in copies(*what):
                copy.wait_send()

        when(condition, finish)
    keep_w.wait()
    keep_g.wait()


def gather_mixer(weights, gates):
    n = lax.axis_size("seq")
    kinds, rows, width = weights.shape
    dma = pltpu.SemaphoreType.DMA
    return pl.pallas_call(
        functools.partial(gather_body, n),
        out_shape=(
            jax.ShapeDtypeStruct((kinds, n, rows, width), weights.dtype),
            jax.ShapeDtypeStruct((n,) + gates.shape, gates.dtype),
        ),
        in_specs=[ANY, ANY],
        out_specs=(ANY, ANY),
        scratch_shapes=[
            dma((2, n, 4)),
            dma((2, n, 4)),
            dma((2, n)),
            dma((2, n)),
            dma((2,)),
        ],
        compiler_params=params(1, 16),
        name="gather_mixer",
    )(weights, gates)


def scatter_body(
    n, one_ref, mixed_ref, dy_ref, dxb_ref, branch_ref, gate_ref, out_ref, made, got_q, got_p, got_z, *sems
):
    send_q, recv_q, send_p, recv_p, send_z, recv_z = sems
    groups = n // INNER
    me, outer, by_x, by_y, by_xy = whereabouts()
    rows = one_ref.shape[1]
    total, width = out_ref.shape
    half = width // 2

    def place_of(turn):
        return lax.rem(outer + 1 + turn, groups)

    def base_of(turn):
        return (place_of(turn) - outer) * INNER

    barrier = pltpu.get_barrier_semaphore()

    def hello(peer):
        pl.semaphore_signal(barrier, inc=1, device_id={"seq": peer}, device_id_type=MESH)

    hello(by_x)
    hello(by_y)

    def hello_outer(turn, carry):
        hello(me + base_of(turn))
        return carry

    lax.fori_loop(0, groups - 1, hello_outer, 0)
    pl.semaphore_wait(barrier, groups + 1)

    flips = ((by_x, by_y), (by_y, by_x))

    def cols(h):
        return pl.ds(h * half, half)

    def along_q(turn, h, other):
        source = (by_xy if other else flips[h][1]) + base_of(turn)
        return remote(
            made.at[source, :, cols(h)],
            got_q.at[h, turn, other],
            send_q.at[h, turn, other],
            recv_q.at[h, turn, other],
            flips[h][1],
        )

    def along_p(turn, h):
        return remote(
            made.at[flips[h][0] + base_of(turn), :, cols(h)],
            got_p.at[h, turn],
            send_p.at[h, turn],
            recv_p.at[h, turn],
            flips[h][0],
        )

    def along_z(turn, h):
        target = me + base_of(turn)
        return remote(
            made.at[target, :, cols(h)],
            got_z.at[h, turn],
            send_z.at[h, turn],
            recv_z.at[h, turn],
            target,
        )

    def make(block):
        left = one_ref[block]
        parts = [
            jnp.dot(left, dy_ref[...], preferred_element_type=F32),
            jnp.dot(left, dxb_ref[...], preferred_element_type=F32),
            jnp.dot(mixed_ref[block], branch_ref[...], preferred_element_type=F32),
        ]
        if rows % 16 == 0:
            for at, part in enumerate(parts):
                made[block, at * rows : (at + 1) * rows] = part.astype(BF16)
            made[block, 3 * rows :] = gate_ref[block]
        else:
            parts.append(gate_ref[block].astype(F32))
            made[block] = jnp.concatenate(parts, axis=0).astype(BF16)

    step = 32

    def add(block, h, ref, index):
        def one(at, carry):
            r = pl.ds(pl.multiple_of(at * step, step), step)
            made[block, r, cols(h)] = (
                made[block, r, cols(h)].astype(F32) + ref[index + (r,)].astype(F32)
            ).astype(BF16)
            return carry

        lax.fori_loop(0, total // step, one, 0)

    def turn_of(turn, carry):
        @pl.when(turn < groups)
        def _():
            base = base_of(turn)
            for h in range(2):
                make(flips[h][1] + base)
            make(by_xy + base)
            for h in range(2):
                for other in range(2):
                    along_q(turn, h, other).start()
            make(me + base)

        @pl.when(jnp.logical_and(turn >= 1, turn <= groups))
        def _():
            now = turn - 1
            base = base_of(now)
            for h in range(2):
                along_q(now, h, 1).wait_recv()
                add(flips[h][0] + base, h, got_q, (h, now, 1))
                along_p(now, h).start()
            for h in range(2):
                along_q(now, h, 0).wait_recv()
                add(me + base, h, got_q, (h, now, 0))

        @pl.when(turn >= 2)
        def _():
            now = turn - 2
            for h in range(2):
                along_p(now, h).wait_recv()
                add(me + base_of(now), h, got_p, (h, now))

                @pl.when(now < groups - 1)
                def _():
                    along_z(now, h).start()

        return carry

    lax.fori_loop(0, groups + 2, turn_of, 0)
    for h in range(2):

        def landed(turn, carry):
            along_z(turn, h).wait_recv()
            return carry

        lax.fori_loop(0, groups - 1, landed, 0)

        def finish(at, carry):
            r = pl.ds(pl.multiple_of(at * step, step), step)
            value = made[me, r, cols(h)].astype(F32)
            for turn in range(groups - 1):
                value = value + got_z[h, turn, r].astype(F32)
            out_ref[r, cols(h)] = value
            return carry

        lax.fori_loop(0, total // step, finish, 0)

    def clear(turn, carry):
        for h in range(2):
            along_q(turn, h, 0).wait_send()
            along_q(turn, h, 1).wait_send()
            along_p(turn, h).wait_send()

            @pl.when(turn < groups - 1)
            def _():
                along_z(turn, h).wait_send()

        return carry

    lax.fori_loop(0, groups, clear, 0)


def scatter_mixer(one, mixed, dy, dxb, branch, gates):
    n, rows, _ = one.shape
    groups = n // INNER
    width = dy.shape[1]
    total = 3 * rows + gates.shape[1]
    dma = pltpu.SemaphoreType.DMA
    return pl.pallas_call(
        functools.partial(scatter_body, n),
        out_shape=jax.ShapeDtypeStruct((total, width), F32),
        in_specs=[VMEM] * 6,
        out_specs=VMEM,
        scratch_shapes=[
            pltpu.VMEM((n, total, width), BF16),
            pltpu.VMEM((2, groups, 2, total, width // 2), BF16),
            pltpu.VMEM((2, groups, total, width // 2), BF16),
            pltpu.VMEM((2, groups, total, width // 2), BF16),
            dma((2, groups, 2)),
            dma((2, groups, 2)),
            dma((2, groups)),
            dma((2, groups)),
            dma((2, groups)),
            dma((2, groups)),
        ],
        compiler_params=params(2, 60),
        cost_estimate=pl.CostEstimate(
            flops=6 * 256 * 2560 * 1280, bytes_accessed=30 * 2**20, transcendentals=0
        ),
        name="scatter_mixer",
    )(one, mixed, dy, dxb, branch, gates)


def small_body(n, value_ref, out_ref, got, send_sem, recv_sem):
    me = lax.axis_index("seq")
    core = lax.axis_index("ch")
    masks = [1 << bit for bit in range(n.bit_length() - 1)]
    peers = [{"seq": me + mask * (1 - 2 * lax.rem(me // mask, 2))} for mask in masks]
    peers.append({"ch": 1 - core})
    barrier = pltpu.get_barrier_semaphore()
    for peer in peers:
        pl.semaphore_signal(barrier, inc=1, device_id=peer, device_id_type=MESH)
    pl.semaphore_wait(barrier, len(peers))
    out_ref[...] = value_ref[...]
    for turn, peer in enumerate(peers):
        copy = pltpu.make_async_remote_copy(
            src_ref=out_ref,
            dst_ref=got.at[turn],
            send_sem=send_sem.at[turn],
            recv_sem=recv_sem.at[turn],
            device_id=peer,
            device_id_type=MESH,
        )
        copy.start()
        copy.wait()
        if turn < len(masks):
            out_ref[...] = out_ref[...] + got[turn]
        else:
            out_ref[8:] = out_ref[8:] + got[turn, 8:]


def small_sums(value):
    n = lax.axis_size("seq")
    turns = n.bit_length()
    return pl.pallas_call(
        functools.partial(small_body, n),
        out_shape=jax.ShapeDtypeStruct(value.shape, F32),
        in_specs=[VMEM],
        out_specs=VMEM,
        scratch_shapes=[
            pltpu.VMEM((turns,) + value.shape, F32),
            pltpu.SemaphoreType.DMA((turns,)),
            pltpu.SemaphoreType.DMA((turns,)),
        ],
        compiler_params=params(3, 16),
        name="small_sums",
    )(value)


GELU_A = 0.7978845608028654
GELU_B = 0.044715


def gelu_parts(v):
    t = jnp.tanh(GELU_A * (v + GELU_B * v * v * v))
    value = 0.5 * v * (1.0 + t)
    slope = 0.5 * (1.0 + t) + 0.5 * v * (1.0 - t * t) * GELU_A * (1.0 + 3.0 * GELU_B * v * v)
    return value, slope


def gates_of(conv_low, gate_ref, par_ref, head, cols, first):
    pre_x = jnp.dot(conv_low, gate_ref[0, head], preferred_element_type=F32)
    pre_a = jnp.dot(conv_low, gate_ref[1, head], preferred_element_type=F32)
    gate_x = jax.nn.sigmoid(pre_x + par_ref[5:6, cols])
    gate_a = jax.nn.sigmoid(pre_a + par_ref[6:7, cols])
    decay = jnp.exp(-8.0 * gate_a * par_ref[8:9, cols])
    room = 1.0 - decay * decay
    mult = jnp.where(first, 1.0, jnp.sqrt(jnp.maximum(room, 0.001)))
    return gate_x, gate_a, decay, room, mult


def first_row(tokens):
    row = lax.broadcasted_iota(jnp.int32, (tokens, 1), 0)
    return jnp.logical_and(row == 0, lax.axis_index("seq") == 0)


def forward_body(
    n, xb_ref, yp_ref, gate_ref, par_ref, conv_ref, state_ref, branch_ref, edge_ref, wide, tail, fade, mine, theirs, *sems
):
    send_tail, recv_tail, send_tot, recv_tot = sems
    tokens, width = xb_ref.shape
    me = lax.axis_index("seq")
    size = gate_ref.shape[2]
    greet_all(n, me)
    tail_copy = remote(
        xb_ref.at[pl.ds(tokens - 16, 16)], tail, send_tail, recv_tail, lax.rem(me + 1, n)
    )
    pl.when(me + 1 < n)(tail_copy.start)
    wide[8:] = xb_ref[...].astype(F32)

    @pl.when(me > 0)
    def _():
        tail_copy.wait_recv()
        wide[:8] = tail[...].astype(F32)[8:]

    @pl.when(me == 0)
    def _():
        wide[:8] = jnp.zeros((8, width), F32)

    pl.when(me + 1 < n)(tail_copy.wait_send)
    edge_ref[:8] = wide[:8]
    first = first_row(tokens)
    for head in range(width // size):
        cols = slice(head * size, (head + 1) * size)
        conv = par_ref[4:5, cols]
        for tap in range(4):
            conv = conv + par_ref[tap : tap + 1, cols] * wide[8 - tap : 8 - tap + tokens, cols]
        conv_low = conv.astype(BF16)
        conv_ref[:, cols] = conv_low
        gate_x, _, decay, _, mult = gates_of(conv_low, gate_ref, par_ref, head, cols, first)
        fade[:, cols] = decay
        state_ref[:, cols] = conv_low.astype(F32) * gate_x * mult

    row = lax.broadcasted_iota(jnp.int32, (8, width), 0)

    def inside(at, carry):
        r = pl.ds(pl.multiple_of(at * 8, 8), 8)
        a, b = fade[r], state_ref[r]
        for by in (1, 2, 4):
            a_back = pltpu.roll(a, by, 0)
            b_back = pltpu.roll(b, by, 0)
            b = jnp.where(row >= by, a * b_back + b, b)
            a = jnp.where(row >= by, a * a_back, a)
        fade[r] = a
        state_ref[r] = b
        return a[7:8] * carry[0], a[7:8] * carry[1] + b[7:8]

    ones, zeros = jnp.ones((1, width), F32), jnp.zeros((1, width), F32)
    tot_a, tot_b = lax.fori_loop(0, tokens // 8, inside, (ones, zeros))
    mine[...] = jnp.where(row == 0, tot_a, tot_b)

    def told(place):
        return remote(mine, theirs.at[me], send_tot.at[place], recv_tot.at[me], place)

    def heard(place):
        return remote(mine, theirs.at[place], send_tot.at[place], recv_tot.at[place], place)

    def tell(place, carry):
        told(place).start()
        return carry

    lax.fori_loop(me + 1, n, tell, 0)

    def hear(place, state):
        heard(place).wait_recv()
        return theirs[place, 0:1] * state + theirs[place, 1:2]

    carry_in = lax.fori_loop(0, me, hear, zeros)
    edge_ref[8:] = jnp.broadcast_to(carry_in, (8, width))

    def finish(at, carry):
        r = pl.ds(pl.multiple_of(at * 16, 16), 16)
        a, b = fade[r], state_ref[r]
        top = b[:8] + a[:8] * carry
        low = b[8:] + a[8:] * top[7:8]
        states = jnp.concatenate([top, low], axis=0)
        state_ref[r] = states
        branch_ref[r] = (states * gelu_parts(yp_ref[r])[0]).astype(BF16)
        return low[7:8]

    lax.fori_loop(0, tokens // 16, finish, carry_in)

    def sent(place, carry):
        told(place).wait_send()
        return carry

    lax.fori_loop(me + 1, n, sent, 0)


def mixer_forward(x_branch, y_pre, gates, par):
    n = lax.axis_size("seq")
    tokens, width = x_branch.shape
    dma = pltpu.SemaphoreType.DMA
    return pl.pallas_call(
        functools.partial(forward_body, n),
        out_shape=(
            jax.ShapeDtypeStruct((tokens, width), BF16),
            jax.ShapeDtypeStruct((tokens, width), F32),
            jax.ShapeDtypeStruct((tokens, width), BF16),
            jax.ShapeDtypeStruct((16, width), F32),
        ),
        in_specs=[VMEM] * 4,
        out_specs=(VMEM,) * 4,
        scratch_shapes=[
            pltpu.VMEM((tokens + 8, width), F32),
            pltpu.VMEM((16, width), BF16),
            pltpu.VMEM((tokens, width), F32),
            pltpu.VMEM((8, width), F32),
            pltpu.VMEM((n, 8, width), F32),
            dma(()),
            dma(()),
            dma((n,)),
            dma((n,)),
        ],
        compiler_params=params(4, 40),
        name="mixer_forward",
    )(x_branch, y_pre, gates, par)


def backward_body(
    n,
    grad_ref,
    yp_ref,
    state_ref,
    edge_ref,
    conv_ref,
    xb_ref,
    gate_ref,
    par_ref,
    dy_ref,
    dxb_ref,
    dgate_ref,
    dpar_ref,
    fade,
    shift,
    adj,
    gate_x_s,
    gate_a_s,
    dconv,
    wide,
    mine,
    theirs,
    head_rows,
    *sems,
):
    send_rows, recv_rows, send_tot, recv_tot = sems
    tokens, width = xb_ref.shape
    me = lax.axis_index("seq")
    size = gate_ref.shape[2]
    greet_all(n, me)
    first = first_row(tokens)
    fade[tokens:] = jnp.ones((8, width), F32)
    for head in range(width // size):
        cols = slice(head * size, (head + 1) * size)
        gate_x, gate_a, decay, _, _ = gates_of(conv_ref[:, cols], gate_ref, par_ref, head, cols, first)
        gate_x_s[:, cols] = gate_x
        gate_a_s[:, cols] = gate_a
        fade[:tokens, cols] = decay
        value, slope = gelu_parts(yp_ref[:, cols])
        grad = grad_ref[:, cols]
        dy_ref[:, cols] = (grad * state_ref[:, cols] * slope).astype(BF16)
        adj[:, cols] = grad * value
        shift[:, cols] = fade[1 : tokens + 1, cols]

    row = lax.broadcasted_iota(jnp.int32, (8, width), 0)
    tiles = tokens // 8

    def inside(turn, carry):
        r = pl.ds(pl.multiple_of((tiles - 1 - turn) * 8, 8), 8)
        a, b = shift[r], adj[r]
        for by in (1, 2, 4):
            a_next = pltpu.roll(a, 8 - by, 0)
            b_next = pltpu.roll(b, 8 - by, 0)
            b = jnp.where(row < 8 - by, a * b_next + b, b)
            a = jnp.where(row < 8 - by, a * a_next, a)
        shift[r] = a
        adj[r] = b
        return a[0:1] * carry[0], a[0:1] * carry[1] + b[0:1]

    ones, zeros = jnp.ones((1, width), F32), jnp.zeros((1, width), F32)
    tot_a, tot_b = lax.fori_loop(0, tiles, inside, (ones, zeros))
    first_fade = fade[0:1]
    mine[...] = jnp.where(row == 0, first_fade * tot_a, first_fade * tot_b)

    def told(place):
        return remote(mine, theirs.at[me], send_tot.at[place], recv_tot.at[me], place)

    def heard(place):
        return remote(mine, theirs.at[place], send_tot.at[place], recv_tot.at[place], place)

    def tell(place, carry):
        told(place).start()
        return carry

    lax.fori_loop(0, me, tell, 0)

    def hear(turn, state):
        place = n - 1 - turn
        heard(place).wait_recv()
        return theirs[place, 0:1] * state + theirs[place, 1:2]

    carry_in = lax.fori_loop(0, n - 1 - me, hear, zeros)

    def finish(turn, carry):
        r = pl.ds(pl.multiple_of((tiles - 1 - turn) * 8, 8), 8)
        value = adj[r] + shift[r] * carry
        adj[r] = value
        return value[0:1]

    lax.fori_loop(0, tiles, finish, carry_in)

    wide[:8] = edge_ref[:8]
    wide[8:] = xb_ref[...].astype(F32)
    at_first = lax.broadcasted_iota(jnp.int32, (tokens, 1), 0) == 0
    for head in range(width // size):
        cols = slice(head * size, (head + 1) * size)
        conv_low = conv_ref[:, cols]
        conv = conv_low.astype(F32)
        gate_x, gate_a, decay = gate_x_s[:, cols], gate_a_s[:, cols], fade[:tokens, cols]
        room = 1.0 - decay * decay
        mult = jnp.where(first, 1.0, jnp.sqrt(jnp.maximum(room, 0.001)))
        back = adj[:, cols]
        before = jnp.where(at_first, edge_ref[8:9, cols], pltpu.roll(state_ref[:, cols], 1, 0))
        d_mult = back * conv * gate_x
        moves = jnp.logical_and(room > 0.001, jnp.logical_not(first))
        d_decay = back * before - jnp.where(moves, d_mult * decay / mult, 0.0)
        d_log = d_decay * decay
        d_pre_x = back * conv * mult * gate_x * (1.0 - gate_x)
        d_pre_a = d_log * (-8.0 * par_ref[8:9, cols]) * gate_a * (1.0 - gate_a)
        dpar_ref[5:6, cols] = jnp.sum(d_pre_x, axis=0, keepdims=True)
        dpar_ref[6:7, cols] = jnp.sum(d_pre_a, axis=0, keepdims=True)
        dpar_ref[7:8, cols] = (
            jnp.sum(d_log * (-8.0 * gate_a), axis=0, keepdims=True) * par_ref[9:10, cols]
        )
        low_x, low_a = d_pre_x.astype(BF16), d_pre_a.astype(BF16)
        flipped = (((1,), (1,)), ((), ()))
        d_conv = (
            back * gate_x * mult
            + lax.dot_general(low_x, gate_ref[0, head], flipped, preferred_element_type=F32)
            + lax.dot_general(low_a, gate_ref[1, head], flipped, preferred_element_type=F32)
        )
        dconv[:tokens, cols] = d_conv
        over_rows = (((0,), (0,)), ((), ()))
        dgate_ref[0, head] = lax.dot_general(
            conv_low, low_x, over_rows, preferred_element_type=F32
        ).astype(BF16)
        dgate_ref[1, head] = lax.dot_general(
            conv_low, low_a, over_rows, preferred_element_type=F32
        ).astype(BF16)
        dpar_ref[4:5, cols] = jnp.sum(d_conv, axis=0, keepdims=True)
        for tap in range(4):
            dpar_ref[tap : tap + 1, cols] = jnp.sum(
                d_conv * wide[8 - tap : 8 - tap + tokens, cols], axis=0, keepdims=True
            )

    rows_copy = remote(
        dconv.at[pl.ds(0, 8)], head_rows, send_rows, recv_rows, lax.rem(me + n - 1, n)
    )
    pl.when(me > 0)(rows_copy.start)

    @pl.when(me + 1 < n)
    def _():
        rows_copy.wait_recv()
        dconv[tokens:] = head_rows[...]

    @pl.when(me + 1 == n)
    def _():
        dconv[tokens:] = jnp.zeros((8, width), F32)

    for head in range(width // size):
        cols = slice(head * size, (head + 1) * size)
        total = par_ref[0:1, cols] * dconv[:tokens, cols]
        for tap in range(1, 4):
            total = total + par_ref[tap : tap + 1, cols] * dconv[tap : tap + tokens, cols]
        dxb_ref[:, cols] = total.astype(BF16)

    pl.when(me > 0)(rows_copy.wait_send)

    def sent(place, carry):
        told(place).wait_send()
        return carry

    lax.fori_loop(0, me, sent, 0)


def mixer_backward(grad, y_pre, states, edge, conv, x_branch, gates, par):
    n = lax.axis_size("seq")
    tokens, width = x_branch.shape
    dma = pltpu.SemaphoreType.DMA
    whole = pltpu.VMEM((tokens, width), F32)
    longer = pltpu.VMEM((tokens + 8, width), F32)
    return pl.pallas_call(
        functools.partial(backward_body, n),
        out_shape=(
            jax.ShapeDtypeStruct((tokens, width), BF16),
            jax.ShapeDtypeStruct((tokens, width), BF16),
            jax.ShapeDtypeStruct(gates.shape, BF16),
            jax.ShapeDtypeStruct((8, width), F32),
        ),
        in_specs=[VMEM] * 8,
        out_specs=(VMEM,) * 4,
        scratch_shapes=[
            longer,
            whole,
            whole,
            whole,
            whole,
            longer,
            longer,
            pltpu.VMEM((8, width), F32),
            pltpu.VMEM((n, 8, width), F32),
            pltpu.VMEM((8, width), F32),
            dma(()),
            dma(()),
            dma((n,)),
            dma((n,)),
        ],
        compiler_params=params(5, 48),
        name="mixer_backward",
    )(grad, y_pre, states, edge, conv, x_branch, gates, par)


def outer_exchange(blocks):
    groups = blocks.shape[0]
    outer = lax.axis_index("seq") // INNER
    got = blocks
    own = pick(blocks, outer)
    received = []
    for step in range(1, groups):
        received.append(swap(pick(blocks, outer ^ step), "seq", step * INNER))
    got = put(jnp.zeros_like(blocks), own, outer)
    for step in range(1, groups):
        got = put(got, received[step - 1], outer ^ step)
    return got


def weights_in(pack):
    groups, kinds, rows, units = pack.shape
    column = outer_exchange(pack)
    inner = lax.axis_index("seq") % INNER
    half = rows // 2
    first, second = column[:, :, :half], column[:, :, half:]
    first_x = swap(first, "seq", 1)
    second_y = swap(second, "seq", 2)
    first_y, first_xy = (swap(v, "seq", 2) for v in (first, first_x))
    second_x, second_xy = (swap(v, "seq", 1) for v in (second, second_y))
    whole = jnp.zeros((kinds, groups, INNER, rows, units), pack.dtype)
    for mask, top, low in (
        (0, first, second),
        (1, first_x, second_x),
        (2, first_y, second_y),
        (3, first_xy, second_xy),
    ):
        place = inner ^ mask
        for block, start in ((top, 0), (low, half)):
            block = jnp.moveaxis(block, 0, 1)[:, :, None]
            whole = lax.dynamic_update_slice(whole, block, (0, 0, place, start, 0))
    return whole.reshape(kinds, groups * INNER * rows, units)


def grads_out(terms, rows):
    units = terms[0].shape[1]
    groups = terms[0].shape[0] // (INNER * rows)
    inner = lax.axis_index("seq") % INNER
    half = rows // 2
    parts = [t.reshape(groups, INNER, rows, units) for t in terms]

    def mine(place, start):
        return jnp.stack(
            [lax.dynamic_slice(t, (0, place, start, 0), (groups, 1, half, units))[:, 0] for t in parts],
            axis=1,
        )

    def reduce(start, near, far):
        low = lambda place: mine(place, start).astype(BF16)
        got_far = swap(low(inner ^ far), "seq", far)
        got_both = swap(low(inner ^ far ^ near), "seq", far)
        mid = (mine(inner ^ near, start) + got_both.astype(F32)).astype(BF16)
        got_near = swap(mid, "seq", near)
        return (mine(inner, start) + got_far.astype(F32) + got_near.astype(F32)).astype(BF16)

    summed = jnp.concatenate([reduce(0, 1, 2), reduce(half, 2, 1)], axis=2)
    got = outer_exchange(summed)
    return jnp.transpose(got, (1, 2, 0, 3)).reshape(3, rows, groups * units).astype(F32)


def my_half(values):
    half = values.shape[0] // 2
    return lax.dynamic_slice_in_dim(values, lax.axis_index("ch") * half, half, 0)


def join(own):
    other = swap(own, "ch", 1)
    core = lax.axis_index("ch")
    return jnp.concatenate(
        [jnp.where(core == 0, own, other), jnp.where(core == 0, other, own)], axis=0
    )


def half_sum(partial):
    core = lax.axis_index("ch")
    parts = partial.reshape((2, partial.shape[0] // 2) + partial.shape[1:])
    theirs = swap(pick(parts, 1 - core), "ch", 1)
    return pick(parts, core).astype(F32) + theirs.astype(F32)


def tokens_in(own):
    half, width = own.shape
    groups = lax.axis_size("seq") // INNER
    outer = lax.axis_index("seq") // INNER
    core = lax.axis_index("ch")
    got = put(jnp.zeros((groups, half, width), own.dtype), own, outer)
    for step in range(1, groups):
        got = put(got, swap(own, "seq", step * INNER), outer ^ step)
    other = swap(got, "ch", 1)
    first = jnp.where(core == 0, got, other)
    second = jnp.where(core == 0, other, got)
    return jnp.stack([first, second], axis=1).reshape(groups * 2 * half, width)


def tokens_out(partial, half):
    width = partial.shape[1]
    groups = lax.axis_size("seq") // INNER
    outer = lax.axis_index("seq") // INNER
    core = lax.axis_index("ch")
    parts = partial.reshape(groups, 2, half, width)
    theirs = pick(parts, 1 - core, 1).astype(BF16)
    summed = (pick(parts, core, 1).astype(F32) + swap(theirs, "ch", 1).astype(F32)).astype(BF16)
    total = pick(summed, outer).astype(F32)
    for step in range(1, groups):
        total = total + swap(pick(summed, outer ^ step), "seq", step * INNER).astype(F32)
    return total


def gate_rows(blocks, n):
    _, heads, depth, size = blocks.shape
    part = depth // n
    rows = 2 * part
    split = blocks.reshape(2, heads, n, part, size).transpose(2, 0, 1, 3, 4)
    return split.reshape(n, 2, rows, heads * size // 2).transpose(0, 2, 1, 3).reshape(n, rows, heads * size)


def gate_blocks(rows, heads, size):
    n, count, width = rows.shape
    split = rows.reshape(n, count, 2, width // 2).transpose(0, 2, 1, 3)
    part = count * width // (2 * heads * size)
    return split.reshape(n, 2, heads, part, size).transpose(1, 2, 0, 3, 4).reshape(2, heads, n * part, size)


def shards(
    inputs,
    norm_gain,
    branch_weight,
    input_weight,
    channel_params,
    gate_x_blocks,
    gate_a_blocks,
    out_weight,
    ffn_gain,
    ffn_gate,
    ffn_up,
    ffn_down,
    cotangent,
):
    f32 = F32
    bf16 = BF16
    n = lax.axis_size("seq")
    tok_rows, model = inputs.shape
    half_rows = tok_rows // 2
    heads, part, size = gate_x_blocks.shape
    width = heads * size
    depth = ffn_gate.shape[0]
    groups = n // INNER
    units = ffn_gate.shape[1] // groups
    x_float = inputs.astype(f32)
    n_one = scaled_norm(x_float, norm_gain).astype(bf16)
    x_half = my_half(inputs).astype(f32)
    _, norm_back_one = jax.vjp(scaled_norm, x_half, norm_gain)

    mixer_pack = jnp.stack([branch_weight, input_weight, out_weight.T])
    gate_pack = gate_rows(jnp.stack([gate_x_blocks, gate_a_blocks]), 1)[0]
    full_mixer, full_gates = gather_mixer(mixer_pack, gate_pack)
    full_mixer = full_mixer.reshape(3, model, width)
    full_branch, full_input, full_out = full_mixer[0], full_mixer[1], full_mixer[2]
    gates = gate_blocks(full_gates, heads, size)
    par = jnp.concatenate(
        [
            channel_params,
            jax.nn.softplus(channel_params[7:8]),
            jax.nn.sigmoid(channel_params[7:8]),
            jnp.zeros((6, width), f32),
        ],
        axis=0,
    )

    pack = jnp.stack(
        [w.reshape(depth, groups, units).transpose(1, 0, 2) for w in (ffn_gate, ffn_up, ffn_down.T)],
        axis=1,
    )
    full_ffn = weights_in(pack)
    cot_half = my_half(cotangent)
    all_cot = tokens_in(cot_half)

    x_branch = jnp.dot(n_one, full_input, preferred_element_type=f32).astype(bf16)
    y_pre = jnp.dot(n_one, full_branch, preferred_element_type=f32)
    conv_out, states, branch_out, edge = mixer_forward(x_branch, y_pre, gates, par)
    mixed = half_sum(jnp.einsum("tw,dw->td", branch_out, full_out, preferred_element_type=f32))
    resid = x_half + mixed
    n_two_f, norm_back_two = jax.vjp(scaled_norm, resid, ffn_gain)
    all_two = tokens_in(n_two_f.astype(bf16))
    gate_pre = jnp.dot(all_two, full_ffn[0], preferred_element_type=f32)
    up_pre = jnp.dot(all_two, full_ffn[1], preferred_element_type=f32)
    gate_act, gelu_back_gate = jax.vjp(gelu_tanh, gate_pre)
    hidden = (gate_act * up_pre).astype(bf16)
    ffn_term = jnp.einsum("tf,df->td", hidden, full_ffn[2], preferred_element_type=f32)
    block_out = join((resid + tokens_out(ffn_term, half_rows)).astype(bf16))

    d_hidden = jnp.einsum("td,df->tf", all_cot, full_ffn[2], preferred_element_type=f32)
    d_gate = gelu_back_gate(d_hidden * up_pre)[0].astype(bf16)
    d_up = (d_hidden * gate_act).astype(bf16)
    d_n_two = tokens_out(
        jnp.einsum("tf,df->td", d_gate, full_ffn[0], preferred_element_type=f32)
        + jnp.einsum("tf,df->td", d_up, full_ffn[1], preferred_element_type=f32),
        half_rows,
    )
    d_gate_term = jnp.einsum("td,tf->df", all_two, d_gate, preferred_element_type=f32)
    d_up_term = jnp.einsum("td,tf->df", all_two, d_up, preferred_element_type=f32)
    d_down_term = jnp.einsum("td,tf->df", all_cot, hidden, preferred_element_type=f32)
    ffn_grads = grads_out([d_gate_term, d_up_term, d_down_term], depth)
    d_resid_norm, d_ffn_gain_term = norm_back_two(d_n_two)
    d_resid = cot_half.astype(f32) + d_resid_norm
    d_mixed = join(d_resid.astype(bf16))
    d_branch_out = jnp.einsum("td,dw->tw", d_mixed, full_out, preferred_element_type=f32)
    d_y, d_xb, d_gates, d_channel_term = mixer_backward(
        d_branch_out, y_pre, states, edge, conv_out, x_branch, gates, par
    )
    d_n_one = half_sum(
        (
            jnp.einsum("tw,dw->td", d_y, full_branch, preferred_element_type=f32)
            + jnp.einsum("tw,dw->td", d_xb, full_input, preferred_element_type=f32)
        ).astype(bf16)
    )
    d_x_norm, d_norm_gain_term = norm_back_one(d_n_one)
    d_inputs = join(d_resid + d_x_norm)
    small = small_sums(
        jnp.concatenate(
            [
                d_channel_term,
                d_norm_gain_term.reshape(-1, width),
                d_ffn_gain_term.reshape(-1, width),
                jnp.zeros((8 - 2 * (model // width), width), f32),
            ],
            axis=0,
        )
    )
    gain_rows = model // width
    scattered = scatter_mixer(
        n_one.T.reshape(n, depth, tok_rows),
        d_mixed.T.reshape(n, depth, tok_rows),
        d_y,
        d_xb,
        branch_out,
        gate_rows(d_gates, n),
    )
    d_gate_pair = gate_blocks(scattered[None, 3 * depth :], heads, size)
    return (
        block_out,
        d_inputs,
        small[8 : 8 + gain_rows].reshape(model),
        scattered[:depth],
        scattered[depth : 2 * depth],
        small[:8],
        d_gate_pair[0],
        d_gate_pair[1],
        scattered[2 * depth : 3 * depth].T,
        small[8 + gain_rows : 8 + 2 * gain_rows].reshape(model),
        ffn_grads[0],
        ffn_grads[1],
        ffn_grads[2].T,
    )


def solution(mesh):
    placed = (
        P("seq", None),
        P(),
        P("seq", "ch"),
        P("seq", "ch"),
        P(None, "ch"),
        P("ch", "seq", None),
        P("ch", "seq", None),
        P("ch", "seq"),
        P(),
        P("seq", "ch"),
        P("seq", "ch"),
        P("ch", "seq"),
        P("seq", None),
    )
    return jax.shard_map(
        shards,
        mesh=mesh,
        in_specs=placed,
        out_specs=(
            P("seq", None),
            P("seq", None),
            P(),
            P("seq", "ch"),
            P("seq", "ch"),
            P(None, "ch"),
            P("ch", "seq", None),
            P("ch", "seq", None),
            P("ch", "seq"),
            P(),
            P("seq", "ch"),
            P("seq", "ch"),
            P("ch", "seq"),
        ),
        check_vma=False,
    )
```

time: 2010 us -> 1250 us (0.62); the launches traced: 1970 us -> 1240 us
  Pallas kernels: 0 us -> 550 us
  blocking collectives: 398 us -> 0 us
  waiting for transfers between devices: 631 us -> 235 us
  local copies, waits for them, and re-layouts: 489 us -> 212 us
  other arithmetic: 174 us -> 63.1 us
  matrix products: 147 us -> 102 us
  starting transfers between devices: 115 us -> 73.6 us
    pallas_call x0 -> x5, Pallas kernels: none -> 550 us  [the longest x1 223 us: scatter_mixer(): pl.pallas_call(functools.partial(scatter_body, n), out_shape=jax.ShapeDty...]
    all_gather x6 -> x0, blocking collectives: 315 us -> none  [the longest x1 146 us: shards(): full_gx = lax.all_gather(gate_x_blocks, 'seq', axis=1, tiled=True)]
    reduce_scatter x5 -> x0, waiting for transfers between devices: 207 us -> none  [the longest x1 77.5 us: shards(): lax.psum_scatter(d_ga_term, 'seq', scatter_dimension=1, tiled=True)]
    slice x112 -> x5, local copies, waits for them, and re-layouts: 193 us -> 8.78 us  [the longest x1 5.12 us: shards(): full_mixer[2]]
    ppermute x36 -> x39, waiting for transfers between devices: 389 us -> 235 us  [swap(): lax.ppermute(value, axis, [(i, i ^ mask) for i in range(lax.axis_size(axi...]
    psum x1 -> x0, blocking collectives: 82.4 us -> none  [shards(): lax.psum((d_norm_gain_term, d_ffn_gain_term, d_channel_term), 'seq')]
    pad x56 -> x0, local copies, waits for them, and re-layouts: 72.6 us -> none  [the longest x28 37.3 us: shards(): cum_decay, local_state = lax.associative_scan(combine, (decay, driven))]
    add x63 -> x1, other arithmetic: 52.5 us -> 4.61 us  [shards(): d_inputs = join(d_resid + d_x_norm)]
  transfers between devices with their start and end apart: 48 -> 39, of which waited for: 14 -> 11; matrix products, arithmetic and copies ran while one was open for 27% -> 22% of each run, Pallas kernels for 0% -> 44%
where the time goes in v2:
time: 1250 us; the launch traced here: 1240 us
  Pallas kernels  550 us (44%)
  waiting for transfers between devices  235 us (19%)
  local copies, waits for them, and re-layouts  212 us (17%)
  matrix products  102 us (8%)
  starting transfers between devices  73.6 us (6%)
  other arithmetic  63.1 us (5%)
    ppermute x39, waiting for transfers between devices, swap(): lax.ppermute(value, axis, [(i, i ^ mask) for i in range(lax.axis_size(axi...  235 us
    pallas_call x1, Pallas kernels, scatter_mixer(): pl.pallas_call(functools.partial(scatter_body, n), out_shape=jax.ShapeDty...  223 us
    pallas_call x1, Pallas kernels, gather_mixer(): pl.pallas_call(functools.partial(gather_body, n), out_shape=(jax.ShapeDty...  180 us
    pallas_call x1, Pallas kernels, small_sums(): pl.pallas_call(functools.partial(small_body, n), out_shape=jax.ShapeDtype...  83.1 us
    ppermute x39, starting transfers between devices, swap(): lax.ppermute(value, axis, [(i, i ^ mask) for i in range(lax.axis_size(axi...  73.6 us
    pallas_call x1, Pallas kernels, mixer_forward(): pl.pallas_call(functools.partial(forward_body, n), out_shape=(jax.ShapeDt...  39 us
    pallas_call x1, Pallas kernels, mixer_backward(): pl.pallas_call(functools.partial(backward_body, n), out_shape=(jax.ShapeD...  25.1 us
  transfers between devices with their start and end apart: 39, of which 11 were waited for; matrix products, arithmetic and copies ran while one was open for 22% of the time, Pallas kernels for 44%

profile of v2, /device:TPU:25, one launch (start us, length us, event | category | flops | bytes accessed | tf_op | source)
XLA Modules:
  0.0 1238.5 jit_solution(10043277447799765056)
XLA Ops:
  7.7 179.6 %gather_mixer.1 = (bf16[3,16,160,1280]{3,2,1,0:T(8,128)(2,1)S(1)}, bf16[16,32,1280]{2,1,0:T(8,128)(2,1)S(1)}) custom-call(bf16[3,160,1280]{2,1,0:T(8,128)(2,1)S(1)} %pad_maximum_fusion.10.w_ref, bf16[32,1280]{1,0:T(8,128)(2,1)S(1)} %bitcast.282), custom_call_target="tpu_custom_call" | custom-call | tf_op jit(solution)/shard_map/gather_mixer/pallas_call | solution.py:194
  203.4 39.0 %mixer_forward.1 = (bf16[256,1280]{1,0:T(8,128)(2,1)S(1)}, f32[256,1280]{1,0:T(8,128)S(1)}, bf16[256,1280]{1,0:T(8,128)(2,1)S(1)}, f32[16,1280]{1,0:T(8,128)S(1)}) custom-call(bf16[256,1280]{1,0:T(8,128)(2,1)S(1)} %convolution_convert_fusion.xb_ref, f32[256,1280]{1,0:T(8,128)S(1)} %fusion.57.yp_ref, bf16[2,5,256,256]{3,2,1,0:T(8,128)(2,1)S(1)} %bitcast.278, ...), custom_call_target="tpu_custom_call" | custom-call | tf_op jit(solution)/shard_map/mixer_forward/pallas_call | solution.py:578
  271.9 9.3 constant_dynamic-slice_fusion.13
  302.9 12.3 collective-permute-done.5
  316.6 43.3 %collective-permute-done.6 = bf16[3,160,960]{2,1,0:T(8,128)(2,1)S(1)} collective-permute-done((bf16[3,160,960]{2,1,0:T(8,128)(2,1)S(1)}, bf16[3,160,960]{2,1,0:T(8,128)(2,1)S(1)}, u32[]{:S(2)}, u32[]{:S(2)}) %collective-permute-start.6) | collective-permute-done | bytes 921632 | tf_op jit(solution)/shard_map/ppermute | solution.py:19
  370.8 21.2 %collective-permute-start.1 = (bf16[128,2560]{1,0:T(8,128)(2,1)}, bf16[128,2560]{1,0:T(8,128)(2,1)}, u32[]{:S(2)}, u32[]{:S(2)}) collective-permute-start(bf16[128,2560]{1,0:T(8,128)(2,1)} %get-tuple-element.43), channel_id=1, source_target_pairs={{0,8},{2,10},{4,12},{6,14},{8,0},{10,2},{12,4},{14,6},{16,24},{18,... | collective-permute-start | bytes 1966088 | tf_op jit(solution)/shard_map/ppermute | solution.py:19
  408.3 40.8 %collective-permute-done.2 = bf16[128,2560]{1,0:T(8,128)(2,1)S(1)} collective-permute-done((bf16[128,2560]{1,0:T(8,128)(2,1)}, bf16[128,2560]{1,0:T(8,128)(2,1)S(1)}, u32[]{:S(2)}, u32[]{:S(2)}) %collective-permute-start.2) | collective-permute-done | bytes 655392 | tf_op jit(solution)/shard_map/ppermute | solution.py:19
  461.1 35.1 %collective-permute-done.10 = bf16[4,3,80,960]{3,2,0,1:T(8,128)(2,1)S(1)} collective-permute-done((bf16[4,3,80,960]{3,2,0,1:T(8,128)(2,1)}, bf16[4,3,80,960]{3,2,0,1:T(8,128)(2,1)S(1)}, u32[]{:S(2)}, u32[]{:S(2)}) %collective-permute-start.10) | collective-permute-done | bytes 1843232 | tf_op jit(solution)/shard_map/ppermute | solution.py:19
  527.4 10.9 collective-permute-done.12
  544.4 12.1 fusion.63
  563.8 9.9 fusion.68
  573.7 13.6 %fusion.8 = (bf16[1024,960]{0,1:T(8,128)(2,1)S(1)}, bf16[1024,960]{0,1:T(8,128)(2,1)}, bf16[1024,960]{0,1:T(8,128)(2,1)}) fusion(f32[1024,960]{0,1:T(8,128)} %fusion.69, f32[1024,960]{0,1:T(8,128)} %fusion.68, bf16[1024,2560]{1,0:T(8,128)(2,1)S(1)} %bitcast.292, bf16[2560,960]{1,0:T(8,128)(2,1)} %bitcast.327), kind=kOutput, calls=%fused_computation.27 | convolution fusion | flops 5058723840 | bytes 23920640 | tf_op jit(solution)/shard_map/dot_general | solution.py:995
  587.3 11.1 fusion.70
  598.5 8.2 fusion.23
  606.7 8.6 fusion.25
  615.3 10.0 convolution_add_fusion
  636.7 8.4 fusion.21
  682.5 17.2 %collective-permute-done.31 = bf16[4,3,80,960]{3,2,1,0:T(8,128)(2,1)} collective-permute-done((bf16[4,3,80,960]{3,2,1,0:T(8,128)(2,1)S(1)}, bf16[4,3,80,960]{3,2,1,0:T(8,128)(2,1)}, u32[]{:S(2)}, u32[]{:S(2)}) %collective-permute-start.31) | collective-permute-done | bytes 1843232 | tf_op jit(solution)/shard_map/ppermute | solution.py:19
  713.6 11.9 collective-permute-start.25
  728.8 43.8 %collective-permute-done.25 = bf16[128,2560]{1,0:T(8,128)(2,1)S(1)} collective-permute-done((bf16[128,2560]{1,0:T(8,128)(2,1)S(1)}, bf16[128,2560]{1,0:T(8,128)(2,1)S(1)}, u32[]{:S(2)}, u32[]{:S(2)}) %collective-permute-start.25) | collective-permute-done | bytes 655392 | tf_op jit(solution)/shard_map/ppermute | solution.py:19
  791.7 25.2 %collective-permute-done.35 = bf16[4,3,80,960]{3,2,1,0:T(8,128)(2,1)} collective-permute-done((bf16[4,3,80,960]{3,2,1,0:T(8,128)(2,1)}, bf16[4,3,80,960]{3,2,1,0:T(8,128)(2,1)}, u32[]{:S(2)}, u32[]{:S(2)}) %collective-permute-start.35) | collective-permute-done | bytes 1843232 | tf_op jit(solution)/shard_map/ppermute | solution.py:19
  828.9 25.1 %mixer_backward.1 = (bf16[256,1280]{1,0:T(8,128)(2,1)S(1)}, bf16[256,1280]{1,0:T(8,128)(2,1)S(1)}, bf16[2,5,256,256]{3,2,1,0:T(8,128)(2,1)S(1)}, f32[8,1280]{1,0:T(8,128)S(1)}) custom-call(f32[256,1280]{1,0:T(8,128)S(1)} %fusion.52.grad_ref, f32[256,1280]{1,0:T(8,128)} %copy-done.1, f32[256,1280]{1,0:T(8,128)} %copy-done.2, ...), custom_call_target="tpu_custom_call" | custom-call | tf_op jit(solution)/shard_map/mixer_backward/pallas_call | solution.py:776
  872.8 223.1 %scatter_mixer.1 = f32[512,1280]{1,0:T(8,128)} custom-call(bf16[16,160,256]{2,1,0:T(8,128)(2,1)} %bitcast.335, bf16[16,160,256]{2,1,0:T(8,128)(2,1)} %bitcast.336, bf16[256,1280]{1,0:T(8,128)(2,1)} %copy-done.8, bf16[256,1280]{1,0:T(8,128)(2,1)} %copy-done.9, bf16[256,1280]{1,0:T(8,128)(2,1)} %copy-done.7, bf16[16,32,1280]{2,1,0:T(8,128)(2,1)} %bitcast.337), custom_call_target="tpu_custom_call" | custom-call | flops 5033164800 | bytes 31457280 | tf_op jit(solution)/shard_map/scatter_mixer/pallas_call | solution.py:383
  1115.0 83.1 %small_sums.1 = f32[16,1280]{1,0:T(8,128)S(1)} custom-call(f32[16,1280]{1,0:T(8,128)S(1)} %maximum_maximum_fusion.1.value_ref), custom_call_target="tpu_custom_call" | custom-call | tf_op jit(solution)/shard_map/small_sums/pallas_call | solution.py:439
  (368 shorter events, 333.3 us)
Async XLA Ops:
  3.7 289.7 %collective-permute-start.19 = (bf16[128,2560]{1,0:T(8,128)(2,1)}, bf16[128,2560]{1,0:T(8,128)(2,1)}, u32[]{:S(2)}, u32[]{:S(2)}) collective-permute-start(bf16[128,2560]{1,0:T(8,128)(2,1)} %get-tuple-element.41), channel_id=1, source_target_pairs={{0,8},{2,10},{4,12},{6,14},{8,0},{10,2},{12,4},{14,6},{16,24},{18,... | collective-permute-start | bytes 1966088 | tf_op jit(solution)/shard_map/ppermute | solution.py:19
  3.8 291.6 %collective-permute-start.20 = (bf16[128,2560]{1,0:T(8,128)(2,1)}, bf16[128,2560]{1,0:T(8,128)(2,1)}, u32[]{:S(2)}, u32[]{:S(2)}) collective-permute-start(bf16[128,2560]{1,0:T(8,128)(2,1)} %get-tuple-element.41), channel_id=1, source_target_pairs={{0,16},{2,18},{4,20},{6,22},{8,24},{10,26},{12,28},{14,30},{16,0},... | collective-permute-start | bytes 1966088 | tf_op jit(solution)/shard_map/ppermute | solution.py:19
  3.8 297.1 %collective-permute-start.21 = (bf16[128,2560]{1,0:T(8,128)(2,1)}, bf16[128,2560]{1,0:T(8,128)(2,1)}, u32[]{:S(2)}, u32[]{:S(2)}) collective-permute-start(bf16[128,2560]{1,0:T(8,128)(2,1)} %get-tuple-element.41), channel_id=1, source_target_pairs={{0,24},{2,26},{4,28},{6,30},{8,16},{10,18},{12,20},{14,22},{16,8},... | collective-permute-start | bytes 1966088 | tf_op jit(solution)/shard_map/ppermute | solution.py:19
  254.0 113.3 %collective-permute-start = (f32[128,2560]{1,0:T(8,128)}, f32[128,2560]{1,0:T(8,128)}, u32[]{:S(2)}, u32[]{:S(2)}) collective-permute-start(f32[128,2560]{1,0:T(8,128)} %dynamic-slice_bitcast_fusion), channel_id=1, source_target_pairs={{0,1},{1,0},{2,3},{3,2},{4,5},{5,4},{6,7},{7,6},{8,9},{9,8},{10,11... | collective-permute-start | bytes 3932168 | tf_op jit(solution)/shard_map/ppermute | solution.py:19
  293.4 66.5 %collective-permute-start.6 = (bf16[3,160,960]{2,1,0:T(8,128)(2,1)S(1)}, bf16[3,160,960]{2,1,0:T(8,128)(2,1)S(1)}, u32[]{:S(2)}, u32[]{:S(2)}) collective-permute-start(bf16[3,160,960]{2,1,0:T(8,128)(2,1)S(1)} %bitcast.340), channel_id=1, source_target_pairs={{0,16},{2,18},{4,20},{6,22},{8,24},{10,26},{12,28},{14,30},{16,0},... | collective-permute-start | bytes 2764808 | tf_op jit(solution)/shard_map/ppermute | solution.py:19
  295.4 64.6 %collective-permute-start.7 = (bf16[3,160,960]{2,1,0:T(8,128)(2,1)S(1)}, bf16[3,160,960]{2,1,0:T(8,128)(2,1)S(1)}, u32[]{:S(2)}, u32[]{:S(2)}) collective-permute-start(bf16[3,160,960]{2,1,0:T(8,128)(2,1)S(1)} %bitcast.339), channel_id=1, source_target_pairs={{0,24},{2,26},{4,28},{6,30},{8,16},{10,18},{12,20},{14,22},{16,8},... | collective-permute-start | bytes 2764808 | tf_op jit(solution)/shard_map/ppermute | solution.py:19
  363.6 91.3 %collective-permute-start.9 = (bf16[4,3,80,960]{3,2,0,1:T(8,128)(2,1)}, bf16[4,3,80,960]{3,2,0,1:T(8,128)(2,1)}, u32[]{:S(2)}, u32[]{:S(2)}) collective-permute-start(bf16[4,3,80,960]{3,2,0,1:T(8,128)(2,1)} %get-tuple-element.89), channel_id=1, source_target_pairs={{0,2},{2,0},{4,6},{6,4},{8,10},{10,8},{12,14},{14,12},{16,18},{18,... | collective-permute-start | bytes 5529608 | tf_op jit(solution)/shard_map/ppermute | solution.py:19
  365.2 91.3 %collective-permute-start.11 = (bf16[4,3,80,960]{3,2,0,1:T(8,128)(2,1)}, bf16[4,3,80,960]{3,2,0,1:T(8,128)(2,1)}, u32[]{:S(2)}, u32[]{:S(2)}) collective-permute-start(bf16[4,3,80,960]{3,2,0,1:T(8,128)(2,1)} %get-tuple-element.89), channel_id=1, source_target_pairs={{0,4},{2,6},{4,0},{6,2},{8,12},{10,14},{12,8},{14,10},{16,20},{18,... | collective-permute-start | bytes 5529608 | tf_op jit(solution)/shard_map/ppermute | solution.py:19
  367.3 84.3 %collective-permute-start.8 = (bf16[4,3,80,960]{3,2,0,1:T(8,128)(2,1)}, bf16[4,3,80,960]{3,2,0,1:T(8,128)(2,1)}, u32[]{:S(2)}, u32[]{:S(2)}) collective-permute-start(bf16[4,3,80,960]{3,2,0,1:T(8,128)(2,1)} %get-tuple-element.90), channel_id=1, source_target_pairs={{0,2},{2,0},{4,6},{6,4},{8,10},{10,8},{12,14},{14,12},{16,18},{18,... | collective-permute-start | bytes 5529608 | tf_op jit(solution)/shard_map/ppermute | solution.py:19
  451.6 62.9 %collective-permute-start.4 = (bf16[4,128,2560]{2,1,0:T(8,128)(2,1)S(1)}, bf16[4,128,2560]{2,1,0:T(8,128)(2,1)}, u32[]{:S(2)}, u32[]{:S(2)}) collective-permute-start(bf16[4,128,2560]{2,1,0:T(8,128)(2,1)S(1)} %bitcast_dynamic-update-slice_fusion.18), channel_id=1, source_target_pairs={{0,1},{1,0},{2,3},{3,2},{4,5},{5,4},{6,7},{7,6},{8,9},{9,8},{10,11... | collective-permute-start | bytes 7864328 | tf_op jit(solution)/shard_map/ppermute | solution.py:19
  455.0 83.4 %collective-permute-start.12 = (bf16[4,3,80,960]{3,2,0,1:T(8,128)(2,1)}, bf16[4,3,80,960]{3,2,0,1:T(8,128)(2,1)}, u32[]{:S(2)}, u32[]{:S(2)}) collective-permute-start(bf16[4,3,80,960]{3,2,0,1:T(8,128)(2,1)} %collective-permute-done.8), channel_id=1, source_target_pairs={{0,4},{2,6},{4,0},{6,2},{8,12},{10,14},{12,8},{14,10},{16,20},{18,... | collective-permute-start | bytes 5529608 | tf_op jit(solution)/shard_map/ppermute | solution.py:19
  456.5 84.8 %collective-permute-start.13 = (bf16[4,3,80,960]{3,2,0,1:T(8,128)(2,1)}, bf16[4,3,80,960]{3,2,0,1:T(8,128)(2,1)}, u32[]{:S(2)}, u32[]{:S(2)}) collective-permute-start(bf16[4,3,80,960]{3,2,0,1:T(8,128)(2,1)} %collective-permute-done.11), channel_id=1, source_target_pairs={{0,2},{2,0},{4,6},{6,4},{8,10},{10,8},{12,14},{14,12},{16,18},{18,... | collective-permute-start | bytes 5529608 | tf_op jit(solution)/shard_map/ppermute | solution.py:19
  631.1 78.0 %collective-permute-start.23 = (bf16[4,128,2560]{2,1,0:T(8,128)(2,1)}, bf16[4,128,2560]{2,1,0:T(8,128)(2,1)}, u32[]{:S(2)}, u32[]{:S(2)}) collective-permute-start(bf16[4,128,2560]{2,1,0:T(8,128)(2,1)} %fusion.20), channel_id=1, source_target_pairs={{0,1},{1,0},{2,3},{3,2},{4,5},{5,4},{6,7},{7,6},{8,9},{9,8},{10,11... | collective-permute-start | bytes 7864328 | tf_op jit(solution)/shard_map/ppermute | solution.py:19
  667.7 110.9 %collective-permute-start.30 = (bf16[4,3,80,960]{3,2,1,0:T(8,128)(2,1)}, bf16[4,3,80,960]{3,2,1,0:T(8,128)(2,1)}, u32[]{:S(2)}, u32[]{:S(2)}) collective-permute-start(bf16[4,3,80,960]{3,2,1,0:T(8,128)(2,1)} %pad_maximum_fusion.4), channel_id=1, source_target_pairs={{0,4},{2,6},{4,0},{6,2},{8,12},{10,14},{12,8},{14,10},{16,20},{18,... | collective-permute-start | bytes 5529608 | tf_op jit(solution)/shard_map/ppermute | solution.py:19
  703.9 74.8 %collective-permute-start.32 = (bf16[4,3,80,960]{3,2,1,0:T(8,128)(2,1)}, bf16[4,3,80,960]{3,2,1,0:T(8,128)(2,1)}, u32[]{:S(2)}, u32[]{:S(2)}) collective-permute-start(bf16[4,3,80,960]{3,2,1,0:T(8,128)(2,1)} %fusion.11), channel_id=1, source_target_pairs={{0,2},{2,0},{4,6},{6,4},{8,10},{10,8},{12,14},{14,12},{16,18},{18,... | collective-permute-start | bytes 5529608 | tf_op jit(solution)/shard_map/ppermute | solution.py:19
  774.1 333.4 %collective-permute-start.17 = (bf16[128,2560]{1,0:T(8,128)(2,1)}, bf16[128,2560]{1,0:T(8,128)(2,1)}, u32[]{:S(2)}, u32[]{:S(2)}) collective-permute-start(bf16[128,2560]{1,0:T(8,128)(2,1)} %get-tuple-element.104), channel_id=1, source_target_pairs={{0,24},{2,26},{4,28},{6,30},{8,16},{10,18},{12,20},{14,22},{16,8},... | collective-permute-start | bytes 1966088 | tf_op jit(solution)/shard_map/ppermute | solution.py:19
  778.6 330.9 %collective-permute-start.16 = (bf16[128,2560]{1,0:T(8,128)(2,1)}, bf16[128,2560]{1,0:T(8,128)(2,1)}, u32[]{:S(2)}, u32[]{:S(2)}) collective-permute-start(bf16[128,2560]{1,0:T(8,128)(2,1)} %get-tuple-element.105), channel_id=1, source_target_pairs={{0,16},{2,18},{4,20},{6,22},{8,24},{10,26},{12,28},{14,30},{16,0},... | collective-permute-start | bytes 1966088 | tf_op jit(solution)/shard_map/ppermute | solution.py:19
  778.7 330.8 %collective-permute-start.15 = (bf16[128,2560]{1,0:T(8,128)(2,1)}, bf16[128,2560]{1,0:T(8,128)(2,1)}, u32[]{:S(2)}, u32[]{:S(2)}) collective-permute-start(bf16[128,2560]{1,0:T(8,128)(2,1)} %get-tuple-element.103), channel_id=1, source_target_pairs={{0,8},{2,10},{4,12},{6,14},{8,0},{10,2},{12,4},{14,6},{16,24},{18,... | collective-permute-start | bytes 1966088 | tf_op jit(solution)/shard_map/ppermute | solution.py:19
  822.0 378.0 %collective-permute-start.36 = (bf16[3,160,960]{2,1,0:T(8,128)(2,1)}, bf16[3,160,960]{2,1,0:T(8,128)(2,1)}, u32[]{:S(2)}, u32[]{:S(2)}) collective-permute-start(bf16[3,160,960]{2,1,0:T(8,128)(2,1)} %get-tuple-element.87), channel_id=1, source_target_pairs={{0,8},{2,10},{4,12},{6,14},{8,0},{10,2},{12,4},{14,6},{16,24},{18,... | collective-permute-start | bytes 2764808 | tf_op jit(solution)/shard_map/ppermute | solution.py:19
  863.2 242.1 %collective-permute-start.28 = (bf16[128,2560]{1,0:T(8,128)(2,1)}, bf16[128,2560]{1,0:T(8,128)(2,1)S(1)}, u32[]{:S(2)}, u32[]{:S(2)}) collective-permute-start(bf16[128,2560]{1,0:T(8,128)(2,1)} %dynamic-slice_bitcast_fusion.1), channel_id=1, source_target_pairs={{0,1},{1,0},{2,3},{3,2},{4,5},{5,4},{6,7},{7,6},{8,9},{9,8},{10,11... | collective-permute-start | bytes 1966088 | tf_op jit(solution)/shard_map/ppermute | solution.py:19
  1105.2 97.0 %collective-permute-start.37 = (bf16[3,160,960]{2,1,0:T(8,128)(2,1)}, bf16[3,160,960]{2,1,0:T(8,128)(2,1)}, u32[]{:S(2)}, u32[]{:S(2)}) collective-permute-start(bf16[3,160,960]{2,1,0:T(8,128)(2,1)} %get-tuple-element.88), channel_id=1, source_target_pairs={{0,16},{2,18},{4,20},{6,22},{8,24},{10,26},{12,28},{14,30},{16,0},... | collective-permute-start | bytes 2764808 | tf_op jit(solution)/shard_map/ppermute | solution.py:19
  1107.6 96.9 %collective-permute-start.38 = (bf16[3,160,960]{2,1,0:T(8,128)(2,1)}, bf16[3,160,960]{2,1,0:T(8,128)(2,1)}, u32[]{:S(2)}, u32[]{:S(2)}) collective-permute-start(bf16[3,160,960]{2,1,0:T(8,128)(2,1)} %get-tuple-element.86), channel_id=1, source_target_pairs={{0,24},{2,26},{4,28},{6,30},{8,16},{10,18},{12,20},{14,22},{16,8},... | collective-permute-start | bytes 2764808 | tf_op jit(solution)/shard_map/ppermute | solution.py:19
  1114.2 118.0 %collective-permute-start.18 = (bf16[128,2560]{1,0:T(8,128)(2,1)}, bf16[128,2560]{1,0:T(8,128)(2,1)}, u32[]{:S(2)}, u32[]{:S(2)}) collective-permute-start(bf16[128,2560]{1,0:T(8,128)(2,1)} %get-tuple-element.107), channel_id=1, source_target_pairs={{0,1},{1,0},{2,3},{3,2},{4,5},{5,4},{6,7},{7,6},{8,9},{9,8},{10,11... | collective-permute-start | bytes 1966088 | tf_op jit(solution)/shard_map/ppermute | solution.py:19
  1114.9 119.7 %collective-permute-start.29 = (f32[128,2560]{1,0:T(8,128)}, f32[128,2560]{1,0:T(8,128)}, u32[]{:S(2)}, u32[]{:S(2)}) collective-permute-start(f32[128,2560]{1,0:T(8,128)} %get-tuple-element.106), channel_id=1, source_target_pairs={{0,1},{1,0},{2,3},{3,2},{4,5},{5,4},{6,7},{7,6},{8,9},{9,8},{10,11... | collective-permute-start | bytes 3932168 | tf_op jit(solution)/shard_map/ppermute | solution.py:19
  (93 other events, 1607.3 us)

commit v3 on v2

--- a/solution.py
+++ b/solution.py
@@ -104,28 +104,64 @@
     )
 
 
-def gather_body(n, w_ref, g_ref, wo_ref, go_ref, send_w, send_g, recv_w, recv_g, here):
+def gather_body(n, *refs):
+    w_refs, g_ref, f_ref = refs[:3], refs[3], refs[4]
+    wo_refs, go_ref, column_ref = refs[5:8], refs[8], refs[9]
+    send_m, recv_m, send_f, recv_f, here = refs[10:]
     groups = n // INNER
     me, outer, by_x, by_y, by_xy = whereabouts()
     above, below = outer + 1 < groups, outer > 0
-    greet([(below, me - INNER), (above, me + INNER), (None, by_x), (None, by_y)])
-    half = w_ref.shape[2] // 2
-    keep_w = pltpu.make_async_copy(w_ref, wo_ref.at[:, me], here.at[0])
-    keep_g = pltpu.make_async_copy(g_ref, go_ref.at[me], here.at[1])
-    keep_w.start()
-    keep_g.start()
+    barrier = pltpu.get_barrier_semaphore()
+
+    def hello(peer):
+        pl.semaphore_signal(barrier, inc=1, device_id={"seq": peer}, device_id_type=MESH)
+
+    hello(by_x)
+    hello(by_y)
+
+    def column_peer(turn):
+        return lax.rem(outer + turn, groups)
+
+    def hello_column(turn, carry):
+        hello(me + (column_peer(turn) - outer) * INNER)
+        return carry
+
+    lax.fori_loop(1, groups, hello_column, 0)
+    pl.semaphore_wait(barrier, groups + 1)
+    units = column_ref.shape[3]
+    half = w_refs[0].shape[1] // 2
+
+    def units_of(place):
+        return pl.ds(pl.multiple_of(place * units, units), units)
+
+    keep = [
+        pltpu.make_async_copy(w_refs[kind], wo_refs[kind].at[me], here.at[kind])
+        for kind in range(3)
+    ]
+    keep.append(pltpu.make_async_copy(g_ref, go_ref.at[me], here.at[3]))
+    keep.append(
+        pltpu.make_async_copy(
+            f_ref.at[:, :, units_of(outer)], column_ref.at[:, outer], here.at[4]
+        )
+    )
+    for copy in keep:
+        copy.start()
     sent = []
 
-    def copies(h, source, kind, target, own):
+    def copies(h, source, way, target, own):
         cols = pl.ds(h * half, half)
-        w_dst = wo_ref.at[:, source, :, cols]
-        g_dst = go_ref.at[source, :, cols]
-        w_src = w_ref.at[:, :, cols] if own else w_dst
-        g_src = g_ref.at[:, cols] if own else g_dst
-        return (
-            remote(w_src, w_dst, send_w.at[h, source, kind], recv_w.at[h, source], target),
-            remote(g_src, g_dst, send_g.at[h, source, kind], recv_g.at[h, source], target),
-        )
+        pairs = [(w_refs[kind], wo_refs[kind].at[source]) for kind in range(3)]
+        pairs.append((g_ref, go_ref.at[source]))
+        return [
+            remote(
+                (given if own else dst).at[:, cols],
+                dst.at[:, cols],
+                send_m.at[kind, h, source, way],
+                recv_m.at[kind, h, source],
+                target,
+            )
+            for kind, (given, dst) in enumerate(pairs)
+        ]
 
     def send(condition, *what):
         def go():
@@ -141,6 +177,24 @@
                 copy.wait_recv()
 
         when(condition, go)
+
+    def exchange(turn, receive):
+        place = lax.rem(outer + groups - turn, groups) if receive else column_peer(turn)
+        target = me + (place - outer) * INNER
+        return remote(
+            f_ref.at[:, :, units_of(place)],
+            column_ref.at[:, place if receive else outer],
+            send_f.at[turn],
+            recv_f.at[turn],
+            target,
+        )
+
+    def each_turn(action):
+        def one(turn, carry):
+            action(turn)
+            return carry
+
+        lax.fori_loop(1, groups, one, 0)
 
     for step in range(groups):
         for h in range(2):
@@ -151,14 +205,16 @@
                 send(None, h, me, 2, flip_p, True)
                 send(None, h, me, 3, flip_q, True)
                 continue
-            for source, there, onward, kind, to in (
+            for source, there, onward, way, to in (
                 (me - step * INNER, outer >= step, above, 0, me + INNER),
                 (me + step * INNER, outer + step < groups, below, 1, me - INNER),
             ):
                 arrive(there, h, source)
-                send(both(there, onward), h, source, kind, to, False)
+                send(both(there, onward), h, source, way, to, False)
                 send(there, h, source, 2, flip_p, False)
                 send(there, h, source, 3, flip_q, False)
+        if step == groups - 1:
+            each_turn(lambda turn: exchange(turn, False).start())
         for h in range(2):
             flip_p, flip_q = (by_x, by_y) if h == 0 else (by_y, by_x)
             if step == 0:
@@ -176,6 +232,7 @@
         for h in range(2):
             arrive(None, h, (by_y if h == 0 else by_x) + shift)
             arrive(None, h, by_xy + shift)
+    each_turn(lambda turn: exchange(turn, True).wait_recv())
     for condition, what in sent:
 
         def finish(what=what):
@@ -183,38 +240,407 @@
                 copy.wait_send()
 
         when(condition, finish)
-    keep_w.wait()
-    keep_g.wait()
-
-
-def gather_mixer(weights, gates):
+    each_turn(lambda turn: exchange(turn, False).wait_send())
+    for copy in keep:
+        copy.wait()
+
+
+def gather_weights(weights, gates, ffn):
     n = lax.axis_size("seq")
-    kinds, rows, width = weights.shape
+    groups = n // INNER
+    kinds, rows, padded = ffn.shape
+    dma = pltpu.SemaphoreType.DMA
+    made = [jax.ShapeDtypeStruct((n,) + w.shape, w.dtype) for w in (*weights, gates)]
+    made.append(jax.ShapeDtypeStruct((kinds, groups, rows, padded // groups), ffn.dtype))
+    return pl.pallas_call(
+        functools.partial(gather_body, n),
+        out_shape=tuple(made),
+        in_specs=[ANY] * 5,
+        out_specs=(ANY,) * 5,
+        scratch_shapes=[
+            dma((4, 2, n, 4)),
+            dma((4, 2, n)),
+            dma((groups,)),
+            dma((groups,)),
+            dma((5,)),
+        ],
+        compiler_params=params(1, 16),
+        name="gather_weights",
+    )(*weights, gates, ffn)
+
+
+def tokens_body(n, *refs):
+    own_refs, column_ref, near_ref = refs[:2], refs[2], refs[3]
+    all_refs, w_refs = refs[4:6], refs[6:9]
+    send_t, recv_z, recv_c, send_w, recv_w, here = refs[9:]
+    groups = n // INNER
+    half = groups // 2
+    me, outer, by_x, by_y, by_xy = whereabouts()
+    base = outer * INNER
+    core = lax.axis_index("ch")
+    above, below = outer + 1 < groups, outer > 0
+    sibling = {"ch": 1 - core}
+    barrier = pltpu.get_barrier_semaphore()
+
+    def hello(peer):
+        pl.semaphore_signal(barrier, inc=1, device_id=peer, device_id_type=MESH)
+
+    hello({"seq": by_x})
+    hello({"seq": by_y})
+    hello(sibling)
+    pl.when(above)(lambda: hello({"seq": me + INNER}))
+    pl.when(below)(lambda: hello({"seq": me - INNER}))
+    pl.semaphore_wait(barrier, 3 + above.astype(jnp.int32) + below.astype(jnp.int32))
+
+    def token_copy(kind, source, way, own=False):
+        dst = all_refs[kind].at[source, core]
+        to = ({"seq": me + INNER}, {"seq": me - INNER}, sibling)[way]
+        return pltpu.make_async_remote_copy(
+            src_ref=own_refs[kind] if own else dst,
+            dst_ref=dst,
+            send_sem=send_t.at[kind, source, way],
+            recv_sem=(recv_c if way == 2 else recv_z).at[kind, source],
+            device_id=to,
+            device_id_type=MESH,
+        )
+
+    def from_sibling(kind, source):
+        dst = all_refs[kind].at[source, 1 - core]
+        return pltpu.make_async_remote_copy(
+            src_ref=own_refs[kind],
+            dst_ref=dst,
+            send_sem=send_t.at[kind, source, 2],
+            recv_sem=recv_c.at[kind, source],
+            device_id=sibling,
+            device_id_type=MESH,
+        )
+
+    def part(h):
+        return pl.ds(h * half, half)
+
+    flips = ((by_x, by_y), (by_y, by_x))
+
+    def weight_copy(kind, h, far, receive=False):
+        source = flips[h][0] if far else me
+        if receive:
+            source = by_xy if far else flips[h][1]
+        return remote(
+            near_ref.at[h, kind] if far else column_ref.at[kind, part(h)],
+            w_refs[kind].at[part(h), source - base],
+            send_w.at[kind, h, far],
+            recv_w.at[kind, h, far],
+            flips[h][1],
+        )
+
+    keep = []
+    for kind in range(2):
+        keep.append(
+            pltpu.make_async_copy(own_refs[kind], all_refs[kind].at[outer, core], here.at[kind])
+        )
+    for kind in range(3):
+        keep.append(
+            pltpu.make_async_copy(
+                column_ref.at[kind], w_refs[kind].at[:, me - base], here.at[2 + kind]
+            )
+        )
+        for h in range(2):
+            keep.append(
+                pltpu.make_async_copy(
+                    near_ref.at[h, kind],
+                    w_refs[kind].at[part(h), flips[h][0] - base],
+                    here.at[5 + 2 * kind + h],
+                )
+            )
+    every_w = [(kind, h, far) for kind in range(3) for h in range(2) for far in range(2)]
+
+    for kind in range(2):
+        pl.when(above)(token_copy(kind, outer, 0, True).start)
+        pl.when(below)(token_copy(kind, outer, 1, True).start)
+        token_copy(kind, outer, 2, True).start()
+    for what in every_w:
+        weight_copy(*what).start()
+    for copy in keep:
+        copy.start()
+    for kind in range(2):
+        for step in range(1, groups):
+            for source, there, onward, way in (
+                (outer - step, outer >= step, above, 0),
+                (outer + step, outer + step < groups, below, 1),
+            ):
+                pl.when(there)(token_copy(kind, source, way).wait_recv)
+                pl.when(both(there, onward))(token_copy(kind, source, way).start)
+                pl.when(there)(token_copy(kind, source, 2).start)
+    for kind in range(2):
+        for source in range(groups):
+            from_sibling(kind, source).wait_recv()
+    for what in every_w:
+        weight_copy(*what, receive=True).wait_recv()
+    for kind in range(2):
+        pl.when(above)(token_copy(kind, outer, 0, True).wait_send)
+        pl.when(below)(token_copy(kind, outer, 1, True).wait_send)
+        token_copy(kind, outer, 2, True).wait_send()
+        for step in range(1, groups):
+            for source, there, onward, way in (
+                (outer - step, outer >= step, above, 0),
+                (outer + step, outer + step < groups, below, 1),
+            ):
+                pl.when(both(there, onward))(token_copy(kind, source, way).wait_send)
+                pl.when(there)(token_copy(kind, source, 2).wait_send)
+    for what in every_w:
+        weight_copy(*what).wait_send()
+    for copy in keep:
+        copy.wait()
+
+
+def gather_tokens(tokens, cotangent, column, near):
+    n = lax.axis_size("seq")
+    groups = n // INNER
+    kinds, _, rows, units = column.shape
+    dma = pltpu.SemaphoreType.DMA
+    wide = jax.ShapeDtypeStruct((groups, 2) + tokens.shape, tokens.dtype)
+    weight = jax.ShapeDtypeStruct((groups, INNER, rows, units), column.dtype)
+    return pl.pallas_call(
+        functools.partial(tokens_body, n),
+        out_shape=(wide, wide, weight, weight, weight),
+        in_specs=[ANY] * 4,
+        out_specs=(ANY,) * 5,
+        scratch_shapes=[
+            dma((2, groups, 3)),
+            dma((2, groups)),
+            dma((2, groups)),
+            dma((kinds, 2, 2)),
+            dma((kinds, 2, 2)),
+            dma((11,)),
+        ],
+        compiler_params=params(6, 16),
+        name="gather_tokens",
+    )(tokens, cotangent, column, near)
+
+
+def reduce_body(n, kinds, *refs):
+    p_refs, t_refs = refs[:kinds], refs[kinds : kinds + 3]
+    out_refs, far_ref = refs[kinds + 3 : 2 * kinds + 3], refs[2 * kinds + 3]
+    summed, got, send_c, recv_c, send_z, recv_z, send_f, recv_f = refs[2 * kinds + 4 :]
+    groups = n // INNER
+    half = groups // 2
+    me, outer, by_x, by_y, by_xy = whereabouts()
+    base = outer * INNER
+    core = lax.axis_index("ch")
+    above, below = outer + 1 < groups, outer > 0
+    sibling = {"ch": 1 - core}
+    barrier = pltpu.get_barrier_semaphore()
+
+    def hello(peer):
+        pl.semaphore_signal(barrier, inc=1, device_id=peer, device_id_type=MESH)
+
+    hello({"seq": by_x})
+    hello({"seq": by_y})
+    hello(sibling)
+    pl.when(above)(lambda: hello({"seq": me + INNER}))
+    pl.when(below)(lambda: hello({"seq": me - INNER}))
+    pl.semaphore_wait(barrier, 3 + above.astype(jnp.int32) + below.astype(jnp.int32))
+    flips = ((by_x, by_y), (by_y, by_x))
+
+    def gradient_copy(kind, h, far):
+        source = by_xy if far else flips[h][1]
+        return remote(
+            t_refs[kind].at[pl.ds(h * half, half), source - base],
+            far_ref.at[h, far, kind],
+            send_f.at[kind, h, far],
+            recv_f.at[kind, h, far],
+            flips[h][1],
+        )
+
+    def to_sibling(kind, place):
+        return pltpu.make_async_remote_copy(
+            src_ref=p_refs[kind].at[place, 1 - core],
+            dst_ref=summed.at[kind, place],
+            send_sem=send_c.at[kind, place],
+            recv_sem=recv_c.at[kind, place],
+            device_id=sibling,
+            device_id_type=MESH,
+        )
+
+    def along(kind, place, up):
+        last = place == (outer + 1 if up else outer - 1)
+        slot = place if up else jnp.where(last, groups, place)
+        return remote(
+            summed.at[kind, place],
+            got.at[kind, slot],
+            send_z.at[kind, place],
+            recv_z.at[kind, slot],
+            me + (INNER if up else -INNER),
+        )
+
+    def landed(kind, slot):
+        return remote(
+            summed.at[kind, 0], got.at[kind, slot], send_z.at[kind, 0], recv_z.at[kind, slot], by_x
+        )
+
+    def each(limit, action):
+        def one(turn, carry):
+            action(turn)
+            return carry
+
+        lax.fori_loop(0, limit, one, 0)
+
+    every_f = [(kind, h, far) for far in (1, 0) for kind in range(3) for h in range(2)]
+    for kind in range(kinds):
+        each(groups, lambda place, kind=kind: to_sibling(kind, place).start())
+    for what in every_f:
+        gradient_copy(*what).start()
+
+    tall = summed.shape[2]
+    chunk = 16
+
+    def rows_of(at):
+        return pl.ds(pl.multiple_of(at * chunk, chunk), chunk)
+
+    def ready(kind, place, incoming):
+        to_sibling(kind, place).wait_recv()
+
+        def local(at):
+            r = rows_of(at)
+            summed[kind, place, r] = (
+                summed[kind, place, r].astype(F32) + p_refs[kind][place, core, r].astype(F32)
+            ).astype(BF16)
+
+        def more(at):
+            r = rows_of(at)
+            summed[kind, place, r] = (
+                summed[kind, place, r].astype(F32)
+                + p_refs[kind][place, core, r].astype(F32)
+                + got[kind, place, r].astype(F32)
+            ).astype(BF16)
+
+        @pl.when(incoming)
+        def _():
+            landed(kind, place).wait_recv()
+            each(tall // chunk, more)
+
+        @pl.when(jnp.logical_not(incoming))
+        def _():
+            each(tall // chunk, local)
+
+    for kind in range(kinds):
+
+        def climb(turn, kind=kind):
+            place = groups - 1 - turn
+
+            @pl.when(place > outer)
+            def _():
+                ready(kind, place, below)
+                along(kind, place, True).start()
+
+        def sink(turn, kind=kind):
+            place = turn
+
+            @pl.when(place < outer)
+            def _():
+                ready(kind, place, above)
+                along(kind, place, False).start()
+
+        def turns(turn):
+            @pl.when(outer < half)
+            def _():
+                climb(turn)
+                sink(turn)
+
+            @pl.when(outer >= half)
+            def _():
+                sink(turn)
+                climb(turn)
+
+        each(groups - 1, turns)
+    for kind in range(kinds):
+        to_sibling(kind, outer).wait_recv()
+
+        def own(at, kind=kind):
+            r = rows_of(at)
+            out_refs[kind][r] = summed[kind, outer, r].astype(F32) + p_refs[kind][
+                outer, core, r
+            ].astype(F32)
+
+        each(tall // chunk, own)
+        for there, slot in ((below, outer), (above, groups)):
+
+            @pl.when(there)
+            def _():
+                landed(kind, slot).wait_recv()
+
+                def plus(at):
+                    r = rows_of(at)
+                    out_refs[kind][r] = out_refs[kind][r] + got[kind, slot, r].astype(F32)
+
+                each(tall // chunk, plus)
+
+    for kind in range(kinds):
+
+        def clear(place, kind=kind):
+            to_sibling(kind, place).wait_send()
+
+            @pl.when(place > outer)
+            def _():
+                along(kind, place, True).wait_send()
+
+            @pl.when(place < outer)
+            def _():
+                along(kind, place, False).wait_send()
+
+        each(groups, clear)
+    for what in every_f:
+        gradient_copy(*what).wait()
+
+
+def reduce_tokens(partials, gradients):
+    n = lax.axis_size("seq")
+    groups = n // INNER
+    kinds = len(partials)
+    _, _, tall, width = partials[0].shape
+    _, _, rows, units = gradients[0].shape
     dma = pltpu.SemaphoreType.DMA
     return pl.pallas_call(
-        functools.partial(gather_body, n),
-        out_shape=(
-            jax.ShapeDtypeStruct((kinds, n, rows, width), weights.dtype),
-            jax.ShapeDtypeStruct((n,) + gates.shape, gates.dtype),
-        ),
-        in_specs=[ANY, ANY],
-        out_specs=(ANY, ANY),
+        functools.partial(reduce_body, n, kinds),
+        out_shape=(jax.ShapeDtypeStruct((tall, width), F32),) * kinds
+        + (jax.ShapeDtypeStruct((2, 2, 3, groups // 2, rows, units), BF16),),
+        in_specs=[VMEM] * kinds + [ANY] * 3,
+        out_specs=(VMEM,) * kinds + (ANY,),
         scratch_shapes=[
-            dma((2, n, 4)),
-            dma((2, n, 4)),
-            dma((2, n)),
-            dma((2, n)),
-            dma((2,)),
+            pltpu.VMEM((kinds, groups, tall, width), BF16),
+            pltpu.VMEM((kinds, groups + 1, tall, width), BF16),
+            dma((kinds, groups)),
+            dma((kinds, groups)),
+            dma((kinds, groups)),
+            dma((kinds, groups + 1)),
+            dma((3, 2, 2)),
+            dma((3, 2, 2)),
         ],
-        compiler_params=params(1, 16),
-        name="gather_mixer",
-    )(weights, gates)
+        compiler_params=params(7, 60),
+        name="reduce_tokens",
+    )(*partials, *gradients)
 
 
 def scatter_body(
-    n, one_ref, mixed_ref, dy_ref, dxb_ref, branch_ref, gate_ref, out_ref, made, got_q, got_p, got_z, *sems
+    n,
+    one_ref,
+    mixed_ref,
+    dy_ref,
+    dxb_ref,
+    branch_ref,
+    gate_ref,
+    small_ref,
+    column_ref,
+    out_ref,
+    small_out,
+    spread_ref,
+    made,
+    got_q,
+    got_p,
+    got_z,
+    got_s,
+    *sems,
 ):
-    send_q, recv_q, send_p, recv_p, send_z, recv_z = sems
+    send_q, recv_q, send_p, recv_p, send_z, recv_z, send_s, recv_s, send_f, recv_f, here = sems
     groups = n // INNER
     me, outer, by_x, by_y, by_xy = whereabouts()
     rows = one_ref.shape[1]
@@ -240,9 +666,44 @@
         return carry
 
     lax.fori_loop(0, groups - 1, hello_outer, 0)
-    pl.semaphore_wait(barrier, groups + 1)
+    core = lax.axis_index("ch")
+    masks = [1 << bit for bit in range(n.bit_length() - 1)]
+    pl.semaphore_signal(barrier, inc=1, device_id={"ch": 1 - core}, device_id_type=MESH)
+    pl.semaphore_wait(barrier, groups + 2)
 
     flips = ((by_x, by_y), (by_y, by_x))
+    units = column_ref.shape[3]
+
+    def units_of(place):
+        return pl.ds(pl.multiple_of(place * units, units), units)
+
+    def exchange(turn, receive=False):
+        place = lax.rem(outer + groups - 1 - turn, groups) if receive else place_of(turn)
+        return remote(
+            column_ref.at[:, place],
+            spread_ref.at[:, :, units_of(place if receive else outer)],
+            send_f.at[turn],
+            recv_f.at[turn],
+            me + (place - outer) * INNER,
+        )
+
+    def small(turn):
+        place = me
+        for at, mask in enumerate(masks):
+            flipped = me + mask * (1 - 2 * lax.rem(me // mask, 2))
+            place = jnp.where(turn == at, flipped, place)
+        other = jnp.where(turn == len(masks), 1 - core, core)
+        return pltpu.make_async_remote_copy(
+            src_ref=small_out,
+            dst_ref=got_s.at[turn],
+            send_sem=send_s.at[turn],
+            recv_sem=recv_s.at[turn],
+            device_id=(place, other),
+            device_id_type=MESH,
+        )
+
+    small_out[...] = small_ref[...]
+    small_row = lax.broadcasted_iota(jnp.int32, small_ref.shape, 0)
 
     def cols(h):
         return pl.ds(h * half, half)
@@ -303,7 +764,14 @@
 
         lax.fori_loop(0, total // step, one, 0)
 
+    keep = pltpu.make_async_copy(
+        column_ref.at[:, outer], spread_ref.at[:, :, units_of(outer)], here
+    )
+    keep.start()
+
     def turn_of(turn, carry):
+        pl.when(turn <= len(masks))(lambda: small(turn).start())
+
         @pl.when(turn < groups)
         def _():
             base = base_of(turn)
@@ -313,6 +781,7 @@
             for h in range(2):
                 for other in range(2):
                     along_q(turn, h, other).start()
+            pl.when(turn < groups - 1)(lambda: exchange(turn).start())
             make(me + base)
 
         @pl.when(jnp.logical_and(turn >= 1, turn <= groups))
@@ -338,8 +807,15 @@
                 def _():
                     along_z(now, h).start()
 
+        @pl.when(turn <= len(masks))
+        def _():
+            small(turn).wait()
+            counts = jnp.logical_or(turn < len(masks), small_row >= 8)
+            small_out[...] = small_out[...] + jnp.where(counts, got_s[turn], 0.0)
+
         return carry
 
+    assert len(masks) < groups + 2
     lax.fori_loop(0, groups + 2, turn_of, 0)
     for h in range(2):
 
@@ -369,86 +845,55 @@
             def _():
                 along_z(turn, h).wait_send()
 
+        @pl.when(turn < groups - 1)
+        def _():
+            exchange(turn, True).wait_recv()
+            exchange(turn).wait_send()
+
         return carry
 
     lax.fori_loop(0, groups, clear, 0)
-
-
-def scatter_mixer(one, mixed, dy, dxb, branch, gates):
+    keep.wait()
+
+
+def scatter_mixer(one, mixed, dy, dxb, branch, gates, small, column):
     n, rows, _ = one.shape
     groups = n // INNER
     width = dy.shape[1]
     total = 3 * rows + gates.shape[1]
+    kinds, _, _, units = column.shape
+    turns = n.bit_length()
     dma = pltpu.SemaphoreType.DMA
     return pl.pallas_call(
         functools.partial(scatter_body, n),
-        out_shape=jax.ShapeDtypeStruct((total, width), F32),
-        in_specs=[VMEM] * 6,
-        out_specs=VMEM,
+        out_shape=(
+            jax.ShapeDtypeStruct((total, width), F32),
+            jax.ShapeDtypeStruct(small.shape, F32),
+            jax.ShapeDtypeStruct((kinds, rows, groups * units), BF16),
+        ),
+        in_specs=[VMEM] * 7 + [ANY],
+        out_specs=(VMEM, VMEM, ANY),
         scratch_shapes=[
             pltpu.VMEM((n, total, width), BF16),
             pltpu.VMEM((2, groups, 2, total, width // 2), BF16),
             pltpu.VMEM((2, groups, total, width // 2), BF16),
             pltpu.VMEM((2, groups, total, width // 2), BF16),
+            pltpu.VMEM((turns,) + small.shape, F32),
             dma((2, groups, 2)),
             dma((2, groups, 2)),
             dma((2, groups)),
             dma((2, groups)),
             dma((2, groups)),
             dma((2, groups)),
+            dma((turns,)),
+            dma((turns,)),
+            dma((groups,)),
+            dma((groups,)),
+            dma(()),
         ],
-        compiler_params=params(2, 60),
-        cost_estimate=pl.CostEstimate(
-            flops=6 * 256 * 2560 * 1280, bytes_accessed=30 * 2**20, transcendentals=0
-        ),
+        compiler_params=params(2, 62),
         name="scatter_mixer",
-    )(one, mixed, dy, dxb, branch, gates)
-
-
-def small_body(n, value_ref, out_ref, got, send_sem, recv_sem):
-    me = lax.axis_index("seq")
-    core = lax.axis_index("ch")
-    masks = [1 << bit for bit in range(n.bit_length() - 1)]
-    peers = [{"seq": me + mask * (1 - 2 * lax.rem(me // mask, 2))} for mask in masks]
-    peers.append({"ch": 1 - core})
-    barrier = pltpu.get_barrier_semaphore()
-    for peer in peers:
-        pl.semaphore_signal(barrier, inc=1, device_id=peer, device_id_type=MESH)
-    pl.semaphore_wait(barrier, len(peers))
-    out_ref[...] = value_ref[...]
-    for turn, peer in enumerate(peers):
-        copy = pltpu.make_async_remote_copy(
-            src_ref=out_ref,
-            dst_ref=got.at[turn],
-            send_sem=send_sem.at[turn],
-            recv_sem=recv_sem.at[turn],
-            device_id=peer,
-            device_id_type=MESH,
-        )
-        copy.start()
-        copy.wait()
-        if turn < len(masks):
-            out_ref[...] = out_ref[...] + got[turn]
-        else:
-            out_ref[8:] = out_ref[8:] + got[turn, 8:]
-
-
-def small_sums(value):
-    n = lax.axis_size("seq")
-    turns = n.bit_length()
-    return pl.pallas_call(
-        functools.partial(small_body, n),
-        out_shape=jax.ShapeDtypeStruct(value.shape, F32),
-        in_specs=[VMEM],
-        out_specs=VMEM,
-        scratch_shapes=[
-            pltpu.VMEM((turns,) + value.shape, F32),
-            pltpu.SemaphoreType.DMA((turns,)),
-            pltpu.SemaphoreType.DMA((turns,)),
-        ],
-        compiler_params=params(3, 16),
-        name="small_sums",
-    )(value)
+    )(one, mixed, dy, dxb, branch, gates, small, column)
 
 
 GELU_A = 0.7978845608028654
@@ -479,9 +924,25 @@
 
 
 def forward_body(
-    n, xb_ref, yp_ref, gate_ref, par_ref, conv_ref, state_ref, branch_ref, edge_ref, wide, tail, fade, mine, theirs, *sems
+    n,
+    xb_ref,
+    yp_ref,
+    gate_ref,
+    par_ref,
+    column_ref,
+    conv_ref,
+    state_ref,
+    branch_ref,
+    edge_ref,
+    near_ref,
+    wide,
+    tail,
+    fade,
+    mine,
+    theirs,
+    *sems,
 ):
-    send_tail, recv_tail, send_tot, recv_tot = sems
+    send_tail, recv_tail, send_tot, recv_tot, send_f, recv_f = sems
     tokens, width = xb_ref.shape
     me = lax.axis_index("seq")
     size = gate_ref.shape[2]
@@ -490,6 +951,18 @@
         xb_ref.at[pl.ds(tokens - 16, 16)], tail, send_tail, recv_tail, lax.rem(me + 1, n)
     )
     pl.when(me + 1 < n)(tail_copy.start)
+    _, _, by_x, by_y, _ = whereabouts()
+    part = column_ref.shape[1] // 2
+    hosted = [
+        remote(
+            column_ref.at[:, pl.ds(h * part, part)],
+            near_ref.at[h],
+            send_f.at[h],
+            recv_f.at[h],
+            (by_x, by_y)[h],
+        )
+        for h in range(2)
+    ]
     wide[8:] = xb_ref[...].astype(F32)
 
     @pl.when(me > 0)
@@ -502,6 +975,8 @@
         wide[:8] = jnp.zeros((8, width), F32)
 
     pl.when(me + 1 < n)(tail_copy.wait_send)
+    for copy in hosted:
+        copy.start()
     edge_ref[:8] = wide[:8]
     first = first_row(tokens)
     for head in range(width // size):
@@ -569,11 +1044,14 @@
         return carry
 
     lax.fori_loop(me + 1, n, sent, 0)
-
-
-def mixer_forward(x_branch, y_pre, gates, par):
+    for copy in hosted:
+        copy.wait()
+
+
+def mixer_forward(x_branch, y_pre, gates, par, column):
     n = lax.axis_size("seq")
     tokens, width = x_branch.shape
+    kinds, groups, rows, units = column.shape
     dma = pltpu.SemaphoreType.DMA
     return pl.pallas_call(
         functools.partial(forward_body, n),
@@ -582,9 +1060,10 @@
             jax.ShapeDtypeStruct((tokens, width), F32),
             jax.ShapeDtypeStruct((tokens, width), BF16),
             jax.ShapeDtypeStruct((16, width), F32),
+            jax.ShapeDtypeStruct((2, kinds, groups // 2, rows, units), column.dtype),
         ),
-        in_specs=[VMEM] * 4,
-        out_specs=(VMEM,) * 4,
+        in_specs=[VMEM] * 4 + [ANY],
+        out_specs=(VMEM,) * 4 + (ANY,),
         scratch_shapes=[
             pltpu.VMEM((tokens + 8, width), F32),
             pltpu.VMEM((16, width), BF16),
@@ -595,10 +1074,12 @@
             dma(()),
             dma((n,)),
             dma((n,)),
+            dma((2,)),
+            dma((2,)),
         ],
         compiler_params=params(4, 40),
         name="mixer_forward",
-    )(x_branch, y_pre, gates, par)
+    )(x_branch, y_pre, gates, par, column)
 
 
 def backward_body(
@@ -611,10 +1092,12 @@
     xb_ref,
     gate_ref,
     par_ref,
+    half_ref,
     dy_ref,
     dxb_ref,
     dgate_ref,
     dpar_ref,
+    near_ref,
     fade,
     shift,
     adj,
@@ -627,11 +1110,18 @@
     head_rows,
     *sems,
 ):
-    send_rows, recv_rows, send_tot, recv_tot = sems
+    send_rows, recv_rows, send_tot, recv_tot, send_f, recv_f = sems
     tokens, width = xb_ref.shape
     me = lax.axis_index("seq")
     size = gate_ref.shape[2]
     greet_all(n, me)
+    _, _, by_x, by_y, _ = whereabouts()
+    hosted = [
+        remote(half_ref.at[h], near_ref.at[h], send_f.at[h], recv_f.at[h], (by_x, by_y)[h])
+        for h in range(2)
+    ]
+    for copy in hosted:
+        copy.start()
     first = first_row(tokens)
     fade[tokens:] = jnp.ones((8, width), F32)
     for head in range(width // size):
@@ -765,9 +1255,11 @@
         return carry
 
     lax.fori_loop(0, me, sent, 0)
-
-
-def mixer_backward(grad, y_pre, states, edge, conv, x_branch, gates, par):
+    for copy in hosted:
+        copy.wait()
+
+
+def mixer_backward(grad, y_pre, states, edge, conv, x_branch, gates, par, halves):
     n = lax.axis_size("seq")
     tokens, width = x_branch.shape
     dma = pltpu.SemaphoreType.DMA
@@ -780,9 +1272,10 @@
             jax.ShapeDtypeStruct((tokens, width), BF16),
             jax.ShapeDtypeStruct(gates.shape, BF16),
             jax.ShapeDtypeStruct((8, width), F32),
+            jax.ShapeDtypeStruct(halves.shape, BF16),
         ),
-        in_specs=[VMEM] * 8,
-        out_specs=(VMEM,) * 4,
+        in_specs=[VMEM] * 8 + [ANY],
+        out_specs=(VMEM,) * 4 + (ANY,),
         scratch_shapes=[
             longer,
             whole,
@@ -798,74 +1291,12 @@
             dma(()),
             dma((n,)),
             dma((n,)),
+            dma((2,)),
+            dma((2,)),
         ],
         compiler_params=params(5, 48),
         name="mixer_backward",
-    )(grad, y_pre, states, edge, conv, x_branch, gates, par)
-
-
-def outer_exchange(blocks):
-    groups = blocks.shape[0]
-    outer = lax.axis_index("seq") // INNER
-    got = blocks
-    own = pick(blocks, outer)
-    received = []
-    for step in range(1, groups):
-        received.append(swap(pick(blocks, outer ^ step), "seq", step * INNER))
-    got = put(jnp.zeros_like(blocks), own, outer)
-    for step in range(1, groups):
-        got = put(got, received[step - 1], outer ^ step)
-    return got
-
-
-def weights_in(pack):
-    groups, kinds, rows, units = pack.shape
-    column = outer_exchange(pack)
-    inner = lax.axis_index("seq") % INNER
-    half = rows // 2
-    first, second = column[:, :, :half], column[:, :, half:]
-    first_x = swap(first, "seq", 1)
-    second_y = swap(second, "seq", 2)
-    first_y, first_xy = (swap(v, "seq", 2) for v in (first, first_x))
-    second_x, second_xy = (swap(v, "seq", 1) for v in (second, second_y))
-    whole = jnp.zeros((kinds, groups, INNER, rows, units), pack.dtype)
-    for mask, top, low in (
-        (0, first, second),
-        (1, first_x, second_x),
-        (2, first_y, second_y),
-        (3, first_xy, second_xy),
-    ):
-        place = inner ^ mask
-        for block, start in ((top, 0), (low, half)):
-            block = jnp.moveaxis(block, 0, 1)[:, :, None]
-            whole = lax.dynamic_update_slice(whole, block, (0, 0, place, start, 0))
-    return whole.reshape(kinds, groups * INNER * rows, units)
-
-
-def grads_out(terms, rows):
-    units = terms[0].shape[1]
-    groups = terms[0].shape[0] // (INNER * rows)
-    inner = lax.axis_index("seq") % INNER
-    half = rows // 2
-    parts = [t.reshape(groups, INNER, rows, units) for t in terms]
-
-    def mine(place, start):
-        return jnp.stack(
-            [lax.dynamic_slice(t, (0, place, start, 0), (groups, 1, half, units))[:, 0] for t in parts],
-            axis=1,
-        )
-
-    def reduce(start, near, far):
-        low = lambda place: mine(place, start).astype(BF16)
-        got_far = swap(low(inner ^ far), "seq", far)
-        got_both = swap(low(inner ^ far ^ near), "seq", far)
-        mid = (mine(inner ^ near, start) + got_both.astype(F32)).astype(BF16)
-        got_near = swap(mid, "seq", near)
-        return (mine(inner, start) + got_far.astype(F32) + got_near.astype(F32)).astype(BF16)
-
-    summed = jnp.concatenate([reduce(0, 1, 2), reduce(half, 2, 1)], axis=2)
-    got = outer_exchange(summed)
-    return jnp.transpose(got, (1, 2, 0, 3)).reshape(3, rows, groups * units).astype(F32)
+    )(grad, y_pre, states, edge, conv, x_branch, gates, par, halves)
 
 
 def my_half(values):
@@ -886,20 +1317,6 @@
     parts = partial.reshape((2, partial.shape[0] // 2) + partial.shape[1:])
     theirs = swap(pick(parts, 1 - core), "ch", 1)
     return pick(parts, core).astype(F32) + theirs.astype(F32)
-
-
-def tokens_in(own):
-    half, width = own.shape
-    groups = lax.axis_size("seq") // INNER
-    outer = lax.axis_index("seq") // INNER
-    core = lax.axis_index("ch")
-    got = put(jnp.zeros((groups, half, width), own.dtype), own, outer)
-    for step in range(1, groups):
-        got = put(got, swap(own, "seq", step * INNER), outer ^ step)
-    other = swap(got, "ch", 1)
-    first = jnp.where(core == 0, got, other)
-    second = jnp.where(core == 0, other, got)
-    return jnp.stack([first, second], axis=1).reshape(groups * 2 * half, width)
 
 
 def tokens_out(partial, half):
@@ -955,17 +1372,21 @@
     width = heads * size
     depth = ffn_gate.shape[0]
     groups = n // INNER
-    units = ffn_gate.shape[1] // groups
+    hidden_units = ffn_gate.shape[1]
+    units = -(-hidden_units // (groups * 128)) * 128
     x_float = inputs.astype(f32)
     n_one = scaled_norm(x_float, norm_gain).astype(bf16)
     x_half = my_half(inputs).astype(f32)
     _, norm_back_one = jax.vjp(scaled_norm, x_half, norm_gain)
 
-    mixer_pack = jnp.stack([branch_weight, input_weight, out_weight.T])
     gate_pack = gate_rows(jnp.stack([gate_x_blocks, gate_a_blocks]), 1)[0]
-    full_mixer, full_gates = gather_mixer(mixer_pack, gate_pack)
-    full_mixer = full_mixer.reshape(3, model, width)
-    full_branch, full_input, full_out = full_mixer[0], full_mixer[1], full_mixer[2]
+    ffn_pack = jnp.pad(
+        jnp.stack([ffn_gate, ffn_up, ffn_down.T]), ((0, 0), (0, 0), (0, groups * units - hidden_units))
+    )
+    *full_mixer, full_gates, column = gather_weights(
+        [branch_weight, input_weight, out_weight.T], gate_pack, ffn_pack
+    )
+    full_branch, full_input, full_out = (w.reshape(model, width) for w in full_mixer)
     gates = gate_blocks(full_gates, heads, size)
     par = jnp.concatenate(
         [
@@ -977,46 +1398,64 @@
         axis=0,
     )
 
-    pack = jnp.stack(
-        [w.reshape(depth, groups, units).transpose(1, 0, 2) for w in (ffn_gate, ffn_up, ffn_down.T)],
-        axis=1,
-    )
-    full_ffn = weights_in(pack)
     cot_half = my_half(cotangent)
-    all_cot = tokens_in(cot_half)
 
     x_branch = jnp.dot(n_one, full_input, preferred_element_type=f32).astype(bf16)
     y_pre = jnp.dot(n_one, full_branch, preferred_element_type=f32)
-    conv_out, states, branch_out, edge = mixer_forward(x_branch, y_pre, gates, par)
+    conv_out, states, branch_out, edge, near = mixer_forward(x_branch, y_pre, gates, par, column)
     mixed = half_sum(jnp.einsum("tw,dw->td", branch_out, full_out, preferred_element_type=f32))
     resid = x_half + mixed
     n_two_f, norm_back_two = jax.vjp(scaled_norm, resid, ffn_gain)
-    all_two = tokens_in(n_two_f.astype(bf16))
+    all_two, all_cot, *full_ffn = gather_tokens(n_two_f.astype(bf16), cot_half, column, near)
+    all_two, all_cot = (v.reshape(groups * tok_rows, model) for v in (all_two, all_cot))
+    full_ffn = [w.reshape(model, units) for w in full_ffn]
     gate_pre = jnp.dot(all_two, full_ffn[0], preferred_element_type=f32)
     up_pre = jnp.dot(all_two, full_ffn[1], preferred_element_type=f32)
     gate_act, gelu_back_gate = jax.vjp(gelu_tanh, gate_pre)
     hidden = (gate_act * up_pre).astype(bf16)
-    ffn_term = jnp.einsum("tf,df->td", hidden, full_ffn[2], preferred_element_type=f32)
-    block_out = join((resid + tokens_out(ffn_term, half_rows)).astype(bf16))
-
+    ffn_term = jnp.einsum("tf,df->td", hidden, full_ffn[2], preferred_element_type=f32).astype(bf16)
     d_hidden = jnp.einsum("td,df->tf", all_cot, full_ffn[2], preferred_element_type=f32)
     d_gate = gelu_back_gate(d_hidden * up_pre)[0].astype(bf16)
     d_up = (d_hidden * gate_act).astype(bf16)
-    d_n_two = tokens_out(
+    d_n_two = (
         jnp.einsum("tf,df->td", d_gate, full_ffn[0], preferred_element_type=f32)
-        + jnp.einsum("tf,df->td", d_up, full_ffn[1], preferred_element_type=f32),
-        half_rows,
-    )
-    d_gate_term = jnp.einsum("td,tf->df", all_two, d_gate, preferred_element_type=f32)
-    d_up_term = jnp.einsum("td,tf->df", all_two, d_up, preferred_element_type=f32)
-    d_down_term = jnp.einsum("td,tf->df", all_cot, hidden, preferred_element_type=f32)
-    ffn_grads = grads_out([d_gate_term, d_up_term, d_down_term], depth)
+        + jnp.einsum("tf,df->td", d_up, full_ffn[1], preferred_element_type=f32)
+    ).astype(bf16)
+    terms = [
+        jnp.einsum("td,tf->df", left, right, preferred_element_type=f32)
+        .astype(bf16)
+        .reshape(groups, INNER, depth, units)
+        for left, right in ((all_two, d_gate), (all_two, d_up), (all_cot, hidden))
+    ]
+    split = [v.reshape(groups, 2, half_rows, model) for v in (d_n_two, ffn_term)]
+    if groups <= 4:
+        d_n_two, ffn_out, far = reduce_tokens(split, terms)
+    else:
+        d_n_two, far = reduce_tokens(split[:1], terms)
+        ffn_out = tokens_out(ffn_term, half_rows)
+    block_out = join((resid + ffn_out).astype(bf16))
+    inner = lax.axis_index("seq") % INNER
+    by_half = [t.reshape(2, groups // 2, INNER, depth, units) for t in terms]
+
+    def block_at(h, place):
+        return jnp.stack([pick(t[h], place, 1) for t in by_half]).astype(f32)
+
+    halves = jnp.stack(
+        [(block_at(h, inner ^ (1, 2)[h]) + far[h, 1].astype(f32)).astype(bf16) for h in range(2)]
+    )
     d_resid_norm, d_ffn_gain_term = norm_back_two(d_n_two)
     d_resid = cot_half.astype(f32) + d_resid_norm
     d_mixed = join(d_resid.astype(bf16))
     d_branch_out = jnp.einsum("td,dw->tw", d_mixed, full_out, preferred_element_type=f32)
-    d_y, d_xb, d_gates, d_channel_term = mixer_backward(
-        d_branch_out, y_pre, states, edge, conv_out, x_branch, gates, par
+    d_y, d_xb, d_gates, d_channel_term, near_back = mixer_backward(
+        d_branch_out, y_pre, states, edge, conv_out, x_branch, gates, par, halves
+    )
+    column_back = jnp.concatenate(
+        [
+            (block_at(h, inner) + far[h, 0].astype(f32) + near_back[h].astype(f32)).astype(bf16)
+            for h in range(2)
+        ],
+        axis=1,
     )
     d_n_one = half_sum(
         (
@@ -1026,26 +1465,27 @@
     )
     d_x_norm, d_norm_gain_term = norm_back_one(d_n_one)
     d_inputs = join(d_resid + d_x_norm)
-    small = small_sums(
-        jnp.concatenate(
-            [
-                d_channel_term,
-                d_norm_gain_term.reshape(-1, width),
-                d_ffn_gain_term.reshape(-1, width),
-                jnp.zeros((8 - 2 * (model // width), width), f32),
-            ],
-            axis=0,
-        )
+    small_terms = jnp.concatenate(
+        [
+            d_channel_term,
+            d_norm_gain_term.reshape(-1, width),
+            d_ffn_gain_term.reshape(-1, width),
+            jnp.zeros((8 - 2 * (model // width), width), f32),
+        ],
+        axis=0,
     )
     gain_rows = model // width
-    scattered = scatter_mixer(
+    scattered, small, spread = scatter_mixer(
         n_one.T.reshape(n, depth, tok_rows),
         d_mixed.T.reshape(n, depth, tok_rows),
         d_y,
         d_xb,
         branch_out,
         gate_rows(d_gates, n),
-    )
+        small_terms,
+        column_back,
+    )
+    ffn_grads = [spread[kind, :, :hidden_units].astype(f32) for kind in range(3)]
     d_gate_pair = gate_blocks(scattered[None, 3 * depth :], heads, size)
     return (
         block_out,

time: 1250 us -> 960 us (0.77)
  waiting for transfers between devices: 235 us -> 0.01 us
  Pallas kernels: 550 us -> 752 us
  local copies, waits for them, and re-layouts: 212 us -> 55.4 us
  starting transfers between devices: 73.6 us -> 8.02 us
  other arithmetic: 63.1 us -> 42.9 us
  matrix products: 102 us -> 87.8 us
    ppermute x39 -> x5, waiting for transfers between devices: 235 us -> 0.01 us  [swap(): lax.ppermute(value, axis, [(i, i ^ mask) for i in range(lax.axis_size(axi...]
    pallas_call x3 -> x4, Pallas kernels: 486 us -> 644 us  [the longest x1 235 us: gather_weights(): pl.pallas_call(functools.partial(gather_body, n), out_shape=tuple(made),...]
    ppermute x39 -> x5, starting transfers between devices: 73.6 us -> 8.02 us  [swap(): lax.ppermute(value, axis, [(i, i ^ mask) for i in range(lax.axis_size(axi...]
    dynamic_update_slice x22 -> x0, local copies, waits for them, and re-layouts: 38.3 us -> none  [the longest x8 21.3 us: weights_in(): whole = lax.dynamic_update_slice(whole, block, (0, 0, place, start, 0))]
    pallas_call x1, Pallas kernels: 25.1 us -> 56.8 us  [mixer_backward(): pl.pallas_call(functools.partial(backward_body, n), out_shape=(jax.ShapeD...]
    slice x7 -> x3, local copies, waits for them, and re-layouts: 31.6 us -> 8.87 us  [block_at(): return jnp.stack([pick(t[h], place, 1) for t in by_half]).astype(f32)]
    dot_general x3 -> x0, local copies, waits for them, and re-layouts: 20.8 us -> none  [the longest x1 7.98 us: shards(): jnp.einsum('td,tf->df', all_cot, hidden, preferred_element_type=f32)]
    dynamic_slice x4 -> x1, local copies, waits for them, and re-layouts: 21.1 us -> 1.28 us  [my_half(): lax.dynamic_slice_in_dim(values, lax.axis_index('ch') * half, half, 0)]
  transfers between devices with their start and end apart: 39 -> 5, of which waited for: 11 -> 0; matrix products, arithmetic and copies ran while one was open for 22% -> 5% of each run, Pallas kernels for 44% -> 23%
where the time goes in v3:
time: 960 us; the launch traced here: 948 us
  Pallas kernels  752 us (78%)
  matrix products  87.8 us (9%)
  local copies, waits for them, and re-layouts  55.4 us (6%)
  other arithmetic  42.9 us (4%)
    pallas_call x1, Pallas kernels, gather_weights(): pl.pallas_call(functools.partial(gather_body, n), out_shape=tuple(made),...  235 us
    pallas_call x1, Pallas kernels, scatter_mixer(): pl.pallas_call(functools.partial(scatter_body, n), out_shape=(jax.ShapeDt...  215 us
    pallas_call x1, Pallas kernels, reduce_tokens(): pl.pallas_call(functools.partial(reduce_body, n, kinds), out_shape=(jax.S...  103 us
    pallas_call x1, Pallas kernels, gather_tokens(): pl.pallas_call(functools.partial(tokens_body, n), out_shape=(wide, wide,...  91 us
    pallas_call x1, Pallas kernels, mixer_backward(): pl.pallas_call(functools.partial(backward_body, n), out_shape=(jax.ShapeD...  56.8 us
    pallas_call x1, Pallas kernels, mixer_forward(): pl.pallas_call(functools.partial(forward_body, n), out_shape=(jax.ShapeDt...  51.7 us
    dot_general x3, matrix products, shards(): jnp.einsum('td,tf->df', left, right, preferred_element_type=f32)  21 us
  transfers between devices with their start and end apart: 5, of which 0 were waited for; matrix products, arithmetic and copies ran while one was open for 5% of the time, Pallas kernels for 23%

profile of v3, /device:TPU:25, one launch (start us, length us, event | category | flops | bytes accessed | tf_op | source)
XLA Modules:
  0.0 948.1 jit_solution(6793513837805113543)
XLA Ops:
  6.3 234.7 %gather_weights.1 = (bf16[16,160,1280]{2,1,0:T(8,128)(2,1)S(1)}, bf16[16,160,1280]{2,1,0:T(8,128)(2,1)S(1)}, bf16[16,160,1280]{2,1,0:T(8,128)(2,1)S(1)}, bf16[16...) custom-call(bf16[160,1280]{1,0:T(8,128)(2,1)S(1)} %copy-done.13, bf16[160,1280]{1,0:T(8,128)(2,1)S(1)} %copy-done.14, ...), custom_call_target="tpu_custom_call" | custom-call | tf_op jit(solution)/shard_map/gather_weights/pallas_call | solution.py:255
  255.8 51.7 %mixer_forward.1 = (bf16[256,1280]{1,0:T(8,128)(2,1)S(1)}, f32[256,1280]{1,0:T(8,128)S(1)}, bf16[256,1280]{1,0:T(8,128)(2,1)S(1)}, f32[16,1280]{1,0:T(8,128)S(1)}, bf16[2,3,2,160,1024]{4,3,2,1,0:T(8,128)(2,1)S(1)}) custom-call(bf16[256,1280]{1,0:T(8,128)(2,1)S(1)} %convolution_convert_fusion.4.xb_ref, f32[256,1280]{1,0:T(8,128)S(1)} %fusion.33.yp_ref, ...), custom_call_target="tpu_custom_call" | custom-call | tf_op jit(solution)/shard_map/mixer_forward/pallas_call | solution.py:1056
  312.3 3.4 fusion.41
  318.3 3.8 collective-permute-start
  329.1 91.0 %gather_tokens.1 = (bf16[4,2,128,2560]{3,2,1,0:T(8,128)(2,1)S(1)}, bf16[4,2,128,2560]{3,2,1,0:T(8,128)(2,1)S(1)}, bf16[4,4,160,1024]{3,2,1,0:T(8,128)(2,1)S(1)},...) custom-call(bf16[128,2560]{1,0:T(8,128)(2,1)S(1)} %multiply_convert_fusion.2.refs_0_, ...), custom_call_target="tpu_custom_call" | custom-call | tf_op jit(solution)/shard_map/gather_tokens/pallas_call | solution.py:402
  420.1 5.6 fusion.43
  425.7 7.2 fusion.42
  432.8 11.9 %multiply_convert_fusion = (bf16[1024,1024]{1,0:T(8,128)(2,1)}, bf16[1024,1024]{1,0:T(8,128)(2,1)}, bf16[1024,1024]{1,0:T(8,128)(2,1)}) fusion(f32[1024,1024]{1,0:T(8,128)S(1)} %fusion.43, f32[1024,1024]{1,0:T(8,128)} %fusion.42, bf16[1024,2560]{1,0:T(8,128)(2,1)S(1)} %bitcast.202, bf16[2560,1024]{1,0:T(8,128)(2,1)S(1)} %bitcast.199), kind=kOutput, calls=%fused_computation.18 | convolution fusion | flops 5395972096 | bytes 25165824 | tf_op jit(solution)/shard_map/dot_general | solution.py:1413
  444.8 11.2 %fusion.44 = f32[1024,2560]{1,0:T(8,128)} fusion(bf16[1024,1024]{1,0:T(8,128)(2,1)} %get-tuple-element.76, bf16[2560,1024]{1,0:T(8,128)(2,1)} %bitcast.210), kind=kOutput, calls=%fused_computation.121 | convolution fusion | flops 5368709120 | bytes 17825792 | tf_op jit(solution)/shard_map/tf,df->td/dot_general | solution.py:1421
  455.9 7.7 convolution_convert_fusion.2
  463.6 7.4 convolution_convert_fusion.3
  471.0 5.9 convolution_convert_fusion
  477.0 7.4 convolution_convert_fusion.1
  484.4 10.6 %add_convert_fusion = bf16[1024,2560]{1,0:T(8,128)(2,1)} fusion(f32[1024,2560]{1,0:T(8,128)} %fusion.44, bf16[1024,1024]{1,0:T(8,128)(2,1)} %get-tuple-element.77, bf16[2560,1024]{1,0:T(8,128)(2,1)S(1)} %bitcast.200), kind=kOutput, calls=%fused_computation | convolution fusion | flops 5373952000 | bytes 23068672 | tf_op jit(solution)/shard_map/tf,df->td/dot_general | solution.py:1422
  495.1 3.1 fusion.37
  498.2 2.9 fusion.39
  504.0 103.0 %reduce_tokens.1 = (f32[128,2560]{1,0:T(8,128)}, f32[128,2560]{1,0:T(8,128)}, bf16[2,2,3,2,160,1024]{5,4,3,2,1,0:T(8,128)(2,1)}) custom-call(bf16[4,2,128,2560]{3,2,1,0:T(8,128)(2,1)} %bitcast.234, bf16[4,2,128,2560]{3,2,1,0:T(8,128)(2,1)} %bitcast.233, bf16[4,4,160,1024]{3,2,1,0:T(8,128)(2,1)} %bitcast.211, bf16[4,4,160,1024]{3,2,1,0:T(8,128)(2,1)} %bitcast.215, ...), custom_call_target="tpu_custom_call" | custom-call | tf_op jit(solution)/shard_map/reduce_tokens/pallas_call | solution.py:602
  612.4 3.2 dynamic-slice_bitcast_fusion.5
  619.6 3.2 fusion.15
  622.8 4.7 pad_maximum_fusion.half_ref
  632.3 56.8 %mixer_backward.1 = (bf16[256,1280]{1,0:T(8,128)(2,1)S(1)}, bf16[256,1280]{1,0:T(8,128)(2,1)S(1)}, bf16[2,5,256,256]{3,2,1,0:T(8,128)(2,1)S(1)}, f32[8,1280]{1,0:T(8,128)S(1)}, bf16[2,3,2,160,1024]{4,3,2,1,0:T(8,128)(2,1)}) custom-call(f32[256,1280]{1,0:T(8,128)S(1)} %fusion.28.grad_ref, f32[256,1280]{1,0:T(8,128)} %copy-done.4, f32[256,1280]{1,0:T(8,128)} %copy-done.7, ...), custom_call_target="tpu_custom_call" | custom-call | tf_op jit(solution)/shard_map/mixer_backward/pallas_call | solution.py:1268
  703.1 5.1 fusion.13
  716.4 215.0 %scatter_mixer.1 = (f32[512,1280]{1,0:T(8,128)}, f32[16,1280]{1,0:T(8,128)}, bf16[3,160,4096]{2,1,0:T(8,128)(2,1)}) custom-call(bf16[16,160,256]{2,1,0:T(8,128)(2,1)} %bitcast.226, bf16[16,160,256]{2,1,0:T(8,128)(2,1)} %bitcast.227, bf16[256,1280]{1,0:T(8,128)(2,1)} %copy-done.9, bf16[256,1280]{1,0:T(8,128)(2,1)} %copy-done.10, bf16[256,1280]{1,0:T(8,128)(2,1)} %copy-done.8, ...), custom_call_target="tpu_custom_call" | custom-call | tf_op jit(solution)/shard_map/scatter_mixer/pallas_call | solution.py:867
  931.4 5.4 convert_bitcast_fusion
  (210 shorter events, 84.5 us)
Async XLA Ops:
  6.3 237.5 %copy-start.25 = (bf16[256,2560]{1,0:T(8,128)(2,1)S(1)}, bf16[256,2560]{1,0:T(8,128)(2,1)}, u32[]{:S(2)}) copy-start(bf16[256,2560]{1,0:T(8,128)(2,1)} %param.13) | copy-start | bytes 3932164
  6.3 237.5 %copy-start.46 = (f32[2560]{0:T(1024)S(1)}, f32[2560]{0:T(1024)}, u32[]{:S(2)}) copy-start(f32[2560]{0:T(1024)} %param.14) | copy-start | bytes 30724
  253.2 54.3 %copy-start.3 = (bf16[2,5,16,16,256]{4,3,2,1,0:T(8,128)(2,1)}, bf16[2,5,16,16,256]{4,3,2,1,0:T(8,128)(2,1)S(1)}, u32[]{:S(2)}) copy-start(bf16[2,5,16,16,256]{4,3,2,1,0:T(8,128)(2,1)S(1)} %copy.45) | copy-start | bytes 3932164
  255.8 56.5 %copy-start.19 = (bf16[16,160,1280]{2,1,0:T(8,128)(2,1)S(1)}, bf16[16,160,1280]{2,1,0:T(8,128)(2,1)}, u32[]{:S(2)}) copy-start(bf16[16,160,1280]{2,1,0:T(8,128)(2,1)} %copy-done.18) | copy-start | bytes 19660804
  318.3 7.6 collective-permute-start
  328.1 92.0 %copy-start.21 = (f32[128,2560]{1,0:T(8,128)}, f32[128,2560]{1,0:T(8,128)S(1)}, u32[]{:S(2)}) copy-start(f32[128,2560]{1,0:T(8,128)S(1)} %get-tuple-element.72) | copy-start | bytes 3932164
  444.8 11.2 %copy-start.52 = (bf16[1024,1024]{1,0:T(8,128)(2,1)S(1)}, bf16[1024,1024]{1,0:T(8,128)(2,1)}, u32[]{:S(2)}) copy-start(bf16[1024,1024]{1,0:T(8,128)(2,1)} %get-tuple-element.76) | copy-start | bytes 6291460
  455.9 7.7 copy-start.53
  471.0 24.0 %slice-start.6 = ((s8[5242880]{0:T(1024)(128)(4,1)}), s8[1048576]{0:T(1024)(128)(4,1)S(1)}, s32[]{:S(2)}) async-start(s8[5242880]{0:T(1024)(128)(4,1)} %bitcast.212), calls=%async_computation.6 | async-start | bytes 2097152
  477.0 21.2 %copy-start.24 = (bf16[2560,1024]{1,0:T(8,128)(2,1)}, bf16[2560,1024]{1,0:T(8,128)(2,1)S(1)}, u32[]{:S(2)}) copy-start(bf16[2560,1024]{1,0:T(8,128)(2,1)S(1)} %convolution_convert_fusion) | copy-start | bytes 15728644
  477.0 18.1 %slice-start.7 = ((s8[5242880]{0:T(1024)(128)(4,1)}), s8[4194304]{0:T(1024)(128)(4,1)S(1)}, s32[]{:S(2)}) async-start(s8[5242880]{0:T(1024)(128)(4,1)} %bitcast.212), calls=%async_computation.7 | async-start | bytes 8388608
  503.9 103.1 %copy-start.22 = (f32[128,2560]{1,0:T(8,128)S(1)}, f32[128,2560]{1,0:T(8,128)}, u32[]{:S(2)}) copy-start(f32[128,2560]{1,0:T(8,128)} %copy-done.21) | copy-start | bytes 3932164
  504.0 105.0 %copy-start.36 = (bf16[256,2560]{1,0:T(8,128)(2,1)S(1)}, bf16[256,2560]{1,0:T(8,128)(2,1)}, u32[]{:S(2)}) copy-start(bf16[256,2560]{1,0:T(8,128)(2,1)} %param.25) | copy-start | bytes 3932164
  607.0 8.6 copy-start.33
  608.9 6.6 copy-start.32
  610.3 17.2 %collective-permute-start.2 = (bf16[128,2560]{1,0:T(8,128)(2,1)}, bf16[128,2560]{1,0:T(8,128)(2,1)}, u32[]{:S(2)}, u32[]{:S(2)}) collective-permute-start(bf16[128,2560]{1,0:T(8,128)(2,1)} %fusion.36), channel_id=1, source_target_pairs={{0,1},{1,0},{2,3},{3,2},{4,5},{5,4},{6,7},{7,6},{8,9},{9,8},{10,11... | collective-permute-start | bytes 1966088 | tf_op jit(solution)/shard_map/ppermute | solution.py:19
  619.6 10.8 %slice-start.4 = ((s8[6553600]{0:T(1024)(128)(4,1)}), s8[2359296]{0:T(1024)(128)(4,1)S(1)}, s32[]{:S(2)}) async-start(s8[6553600]{0:T(1024)(128)(4,1)} %bitcast.196), calls=%async_computation.4 | async-start | bytes 4718592
  622.8 7.6 slice-start.5
  622.8 66.3 %slice-start.2 = ((s8[6553600]{0:T(1024)(128)(4,1)}), s8[4194304]{0:T(1024)(128)(4,1)S(1)}, s32[]{:S(2)}) async-start(s8[6553600]{0:T(1024)(128)(4,1)} %bitcast.192), calls=%async_computation.2 | async-start | bytes 8388608
  630.4 58.8 %slice-start.3 = ((s8[6553600]{0:T(1024)(128)(4,1)}), s8[2359296]{0:T(1024)(128)(4,1)S(1)}, s32[]{:S(2)}) async-start(s8[6553600]{0:T(1024)(128)(4,1)} %bitcast.192), calls=%async_computation.3 | async-start | bytes 4718592
  632.3 58.8 %slice-start = ((s8[6553600]{0:T(1024)(128)(4,1)}), s8[2359296]{0:T(1024)(128)(4,1)S(1)}, s32[]{:S(2)}) async-start(s8[6553600]{0:T(1024)(128)(4,1)} %bitcast.188), calls=%async_computation | async-start | bytes 4718592
  695.7 15.0 %collective-permute-start.3 = (bf16[128,2560]{1,0:T(8,128)(2,1)}, bf16[128,2560]{1,0:T(8,128)(2,1)S(1)}, u32[]{:S(2)}, u32[]{:S(2)}) collective-permute-start(bf16[128,2560]{1,0:T(8,128)(2,1)} %dynamic-slice_bitcast_fusion.7), channel_id=1, source_target_pairs={{0,1},{1,0},{2,3},{3,2},{4,5},{5,4},{6,7},{7,6},{8,9},{9,8},{10,11... | collective-permute-start | bytes 1966088 | tf_op jit(solution)/shard_map/ppermute | solution.py:19
  715.2 226.9 %collective-permute-start.1 = (bf16[128,2560]{1,0:T(8,128)(2,1)S(1)}, bf16[128,2560]{1,0:T(8,128)(2,1)}, u32[]{:S(2)}, u32[]{:S(2)}) collective-permute-start(bf16[128,2560]{1,0:T(8,128)(2,1)S(1)} %get-tuple-element.107), channel_id=1, source_target_pairs={{0,1},{1,0},{2,3},{3,2},{4,5},{5,4},{6,7},{7,6},{8,9},{9,8},{10,11... | collective-permute-start | bytes 1966088 | tf_op jit(solution)/shard_map/ppermute | solution.py:19
  715.2 229.2 %collective-permute-start.4 = (f32[128,2560]{1,0:T(8,128)}, f32[128,2560]{1,0:T(8,128)}, u32[]{:S(2)}, u32[]{:S(2)}) collective-permute-start(f32[128,2560]{1,0:T(8,128)} %get-tuple-element.106), channel_id=1, source_target_pairs={{0,1},{1,0},{2,3},{3,2},{4,5},{5,4},{6,7},{7,6},{8,9},{9,8},{10,11... | collective-permute-start | bytes 3932168 | tf_op jit(solution)/shard_map/ppermute | solution.py:19
  (47 other events, 144.7 us)

commit v4 on v3

--- a/solution.py
+++ b/solution.py
@@ -13,6 +13,7 @@
 MESH = pl.DeviceIdType.MESH
 VMEM = pl.BlockSpec(memory_space=pltpu.VMEM)
 ANY = pl.BlockSpec(memory_space=pl.ANY)
+HBM = pl.BlockSpec(memory_space=pltpu.HBM)
 
 
 def swap(value, axis, mask):
@@ -74,7 +75,7 @@
     pl.semaphore_wait(barrier, count)
 
 
-def greet_all(n, me):
+def greet_all(n, me, sibling=False):
     barrier = pltpu.get_barrier_semaphore()
 
     def hello(step, carry):
@@ -84,7 +85,11 @@
         return carry
 
     lax.fori_loop(1, n, hello, 0)
-    pl.semaphore_wait(barrier, n - 1)
+    if sibling:
+        pl.semaphore_signal(
+            barrier, inc=1, device_id={"ch": 1 - lax.axis_index("ch")}, device_id_type=MESH
+        )
+    pl.semaphore_wait(barrier, n if sibling else n - 1)
 
 
 def remote(src, dst, send_sem, recv_sem, place):
@@ -138,7 +143,7 @@
         pltpu.make_async_copy(w_refs[kind], wo_refs[kind].at[me], here.at[kind])
         for kind in range(3)
     ]
-    keep.append(pltpu.make_async_copy(g_ref, go_ref.at[me], here.at[3]))
+    keep.append(pltpu.make_async_copy(g_ref, go_ref.at[:, :, me], here.at[3]))
     keep.append(
         pltpu.make_async_copy(
             f_ref.at[:, :, units_of(outer)], column_ref.at[:, outer], here.at[4]
@@ -150,12 +155,14 @@
 
     def copies(h, source, way, target, own):
         cols = pl.ds(h * half, half)
-        pairs = [(w_refs[kind], wo_refs[kind].at[source]) for kind in range(3)]
-        pairs.append((g_ref, go_ref.at[source]))
+        pairs = [
+            (w_refs[kind].at[:, cols], wo_refs[kind].at[source, :, cols]) for kind in range(3)
+        ]
+        pairs.append((g_ref.at[h], go_ref.at[h, :, source]))
         return [
             remote(
-                (given if own else dst).at[:, cols],
-                dst.at[:, cols],
+                given if own else dst,
+                dst,
                 send_m.at[kind, h, source, way],
                 recv_m.at[kind, h, source],
                 target,
@@ -213,8 +220,8 @@
                 send(both(there, onward), h, source, way, to, False)
                 send(there, h, source, 2, flip_p, False)
                 send(there, h, source, 3, flip_q, False)
-        if step == groups - 1:
-            each_turn(lambda turn: exchange(turn, False).start())
+    each_turn(lambda turn: exchange(turn, False).start())
+    for step in range(groups):
         for h in range(2):
             flip_p, flip_q = (by_x, by_y) if h == 0 else (by_y, by_x)
             if step == 0:
@@ -250,7 +257,8 @@
     groups = n // INNER
     kinds, rows, padded = ffn.shape
     dma = pltpu.SemaphoreType.DMA
-    made = [jax.ShapeDtypeStruct((n,) + w.shape, w.dtype) for w in (*weights, gates)]
+    made = [jax.ShapeDtypeStruct((n,) + w.shape, w.dtype) for w in weights]
+    made.append(jax.ShapeDtypeStruct(gates.shape[:2] + (n,) + gates.shape[2:], gates.dtype))
     made.append(jax.ShapeDtypeStruct((kinds, groups, rows, padded // groups), ffn.dtype))
     return pl.pallas_call(
         functools.partial(gather_body, n),
@@ -269,10 +277,80 @@
     )(*weights, gates, ffn)
 
 
+class Chain:
+    def __init__(self, n, own, whole, send, recv_z, recv_c):
+        me = lax.axis_index("seq")
+        self.groups = n // INNER
+        self.outer = outer = me // INNER
+        self.core = lax.axis_index("ch")
+        self.above, self.below = outer + 1 < self.groups, outer > 0
+        self.sibling = {"ch": 1 - self.core}
+        self.to = ({"seq": me + INNER}, {"seq": me - INNER}, self.sibling)
+        self.own, self.whole = own, whole
+        self.send, self.recv_z, self.recv_c = send, recv_z, recv_c
+
+    def copy(self, source, way, own=False):
+        dst = self.whole.at[source, self.core]
+        return pltpu.make_async_remote_copy(
+            src_ref=self.own if own else dst,
+            dst_ref=dst,
+            send_sem=self.send.at[source, way],
+            recv_sem=(self.recv_c if way == 2 else self.recv_z).at[source],
+            device_id=self.to[way],
+            device_id_type=MESH,
+        )
+
+    def from_sibling(self, source):
+        return pltpu.make_async_remote_copy(
+            src_ref=self.own,
+            dst_ref=self.whole.at[source, 1 - self.core],
+            send_sem=self.send.at[source, 2],
+            recv_sem=self.recv_c.at[source],
+            device_id=self.sibling,
+            device_id_type=MESH,
+        )
+
+    def keep(self, sem):
+        return pltpu.make_async_copy(self.own, self.whole.at[self.outer, self.core], sem)
+
+    def ways(self, step):
+        return (
+            (self.outer - step, self.outer >= step, self.above, 0),
+            (self.outer + step, self.outer + step < self.groups, self.below, 1),
+        )
+
+    def start(self):
+        pl.when(self.above)(self.copy(self.outer, 0, True).start)
+        pl.when(self.below)(self.copy(self.outer, 1, True).start)
+        self.copy(self.outer, 2, True).start()
+
+    def step(self, step):
+        for source, there, onward, way in self.ways(step):
+            pl.when(there)(self.copy(source, way).wait_recv)
+            pl.when(both(there, onward))(self.copy(source, way).start)
+            pl.when(there)(self.copy(source, 2).start)
+
+    def finish(self):
+        for source in range(self.groups):
+            self.from_sibling(source).wait_recv()
+        pl.when(self.above)(self.copy(self.outer, 0, True).wait_send)
+        pl.when(self.below)(self.copy(self.outer, 1, True).wait_send)
+        self.copy(self.outer, 2, True).wait_send()
+        for step in range(1, self.groups):
+            for source, there, onward, way in self.ways(step):
+                pl.when(both(there, onward))(self.copy(source, way).wait_send)
+                pl.when(there)(self.copy(source, 2).wait_send)
+
+
+def chain_semaphores(groups):
+    dma = pltpu.SemaphoreType.DMA
+    return [dma((groups, 3)), dma((groups,)), dma((groups,))]
+
+
 def tokens_body(n, *refs):
-    own_refs, column_ref, near_ref = refs[:2], refs[2], refs[3]
-    all_refs, w_refs = refs[4:6], refs[6:9]
-    send_t, recv_z, recv_c, send_w, recv_w, here = refs[9:]
+    own_ref, column_ref, near_ref = refs[:3]
+    all_ref, w_refs = refs[3], refs[4:7]
+    send_t, recv_z, recv_c, send_w, recv_w, here = refs[7:]
     groups = n // INNER
     half = groups // 2
     me, outer, by_x, by_y, by_xy = whereabouts()
@@ -292,28 +370,7 @@
     pl.when(below)(lambda: hello({"seq": me - INNER}))
     pl.semaphore_wait(barrier, 3 + above.astype(jnp.int32) + below.astype(jnp.int32))
 
-    def token_copy(kind, source, way, own=False):
-        dst = all_refs[kind].at[source, core]
-        to = ({"seq": me + INNER}, {"seq": me - INNER}, sibling)[way]
-        return pltpu.make_async_remote_copy(
-            src_ref=own_refs[kind] if own else dst,
-            dst_ref=dst,
-            send_sem=send_t.at[kind, source, way],
-            recv_sem=(recv_c if way == 2 else recv_z).at[kind, source],
-            device_id=to,
-            device_id_type=MESH,
-        )
-
-    def from_sibling(kind, source):
-        dst = all_refs[kind].at[source, 1 - core]
-        return pltpu.make_async_remote_copy(
-            src_ref=own_refs[kind],
-            dst_ref=dst,
-            send_sem=send_t.at[kind, source, 2],
-            recv_sem=recv_c.at[kind, source],
-            device_id=sibling,
-            device_id_type=MESH,
-        )
+    chain = Chain(n, own_ref, all_ref, send_t, recv_z, recv_c)
 
     def part(h):
         return pl.ds(h * half, half)
@@ -332,15 +389,11 @@
             flips[h][1],
         )
 
-    keep = []
-    for kind in range(2):
-        keep.append(
-            pltpu.make_async_copy(own_refs[kind], all_refs[kind].at[outer, core], here.at[kind])
-        )
+    keep = [chain.keep(here.at[0])]
     for kind in range(3):
         keep.append(
             pltpu.make_async_copy(
-                column_ref.at[kind], w_refs[kind].at[:, me - base], here.at[2 + kind]
+                column_ref.at[kind], w_refs[kind].at[:, me - base], here.at[1 + kind]
             )
         )
         for h in range(2):
@@ -348,51 +401,28 @@
                 pltpu.make_async_copy(
                     near_ref.at[h, kind],
                     w_refs[kind].at[part(h), flips[h][0] - base],
-                    here.at[5 + 2 * kind + h],
+                    here.at[4 + 2 * kind + h],
                 )
             )
     every_w = [(kind, h, far) for kind in range(3) for h in range(2) for far in range(2)]
 
-    for kind in range(2):
-        pl.when(above)(token_copy(kind, outer, 0, True).start)
-        pl.when(below)(token_copy(kind, outer, 1, True).start)
-        token_copy(kind, outer, 2, True).start()
+    chain.start()
     for what in every_w:
         weight_copy(*what).start()
     for copy in keep:
         copy.start()
-    for kind in range(2):
-        for step in range(1, groups):
-            for source, there, onward, way in (
-                (outer - step, outer >= step, above, 0),
-                (outer + step, outer + step < groups, below, 1),
-            ):
-                pl.when(there)(token_copy(kind, source, way).wait_recv)
-                pl.when(both(there, onward))(token_copy(kind, source, way).start)
-                pl.when(there)(token_copy(kind, source, 2).start)
-    for kind in range(2):
-        for source in range(groups):
-            from_sibling(kind, source).wait_recv()
+    for step in range(1, groups):
+        chain.step(step)
     for what in every_w:
         weight_copy(*what, receive=True).wait_recv()
-    for kind in range(2):
-        pl.when(above)(token_copy(kind, outer, 0, True).wait_send)
-        pl.when(below)(token_copy(kind, outer, 1, True).wait_send)
-        token_copy(kind, outer, 2, True).wait_send()
-        for step in range(1, groups):
-            for source, there, onward, way in (
-                (outer - step, outer >= step, above, 0),
-                (outer + step, outer + step < groups, below, 1),
-            ):
-                pl.when(both(there, onward))(token_copy(kind, source, way).wait_send)
-                pl.when(there)(token_copy(kind, source, 2).wait_send)
+    chain.finish()
     for what in every_w:
         weight_copy(*what).wait_send()
     for copy in keep:
         copy.wait()
 
 
-def gather_tokens(tokens, cotangent, column, near):
+def gather_tokens(tokens, column, near):
     n = lax.axis_size("seq")
     groups = n // INNER
     kinds, _, rows, units = column.shape
@@ -401,20 +431,14 @@
     weight = jax.ShapeDtypeStruct((groups, INNER, rows, units), column.dtype)
     return pl.pallas_call(
         functools.partial(tokens_body, n),
-        out_shape=(wide, wide, weight, weight, weight),
-        in_specs=[ANY] * 4,
-        out_specs=(ANY,) * 5,
-        scratch_shapes=[
-            dma((2, groups, 3)),
-            dma((2, groups)),
-            dma((2, groups)),
-            dma((kinds, 2, 2)),
-            dma((kinds, 2, 2)),
-            dma((11,)),
-        ],
+        out_shape=(wide, weight, weight, weight),
+        in_specs=[ANY] * 3,
+        out_specs=(ANY,) * 4,
+        scratch_shapes=chain_semaphores(groups)
+        + [dma((kinds, 2, 2)), dma((kinds, 2, 2)), dma((10,))],
         compiler_params=params(6, 16),
         name="gather_tokens",
-    )(tokens, cotangent, column, near)
+    )(tokens, column, near)
 
 
 def reduce_body(n, kinds, *refs):
@@ -628,7 +652,9 @@
     dxb_ref,
     branch_ref,
     gate_ref,
-    small_ref,
+    dpar_ref,
+    gain_one_ref,
+    gain_two_ref,
     column_ref,
     out_ref,
     small_out,
@@ -644,6 +670,7 @@
     groups = n // INNER
     me, outer, by_x, by_y, by_xy = whereabouts()
     rows = one_ref.shape[1]
+    part_rows = gate_ref.shape[2]
     total, width = out_ref.shape
     half = width // 2
 
@@ -702,8 +729,14 @@
             device_id_type=MESH,
         )
 
-    small_out[...] = small_ref[...]
-    small_row = lax.broadcasted_iota(jnp.int32, small_ref.shape, 0)
+    small_out[:8] = dpar_ref[...]
+    small_out[8:] = jnp.zeros((8, width), F32)
+    at = 8
+    for gain_ref in (gain_one_ref, gain_two_ref):
+        for start in range(0, gain_ref.shape[1], width):
+            small_out[at : at + 1] = gain_ref[:, start : start + width]
+            at += 1
+    small_row = lax.broadcasted_iota(jnp.int32, small_out.shape, 0)
 
     def cols(h):
         return pl.ds(h * half, half)
@@ -747,9 +780,11 @@
         if rows % 16 == 0:
             for at, part in enumerate(parts):
                 made[block, at * rows : (at + 1) * rows] = part.astype(BF16)
-            made[block, 3 * rows :] = gate_ref[block]
+            for gate in range(2):
+                at = 3 * rows + gate * part_rows
+                made[block, at : at + part_rows] = gate_ref[block, gate]
         else:
-            parts.append(gate_ref[block].astype(F32))
+            parts.extend(gate_ref[block, gate].astype(F32) for gate in range(2))
             made[block] = jnp.concatenate(parts, axis=0).astype(BF16)
 
     step = 32
@@ -856,11 +891,11 @@
     keep.wait()
 
 
-def scatter_mixer(one, mixed, dy, dxb, branch, gates, small, column):
+def scatter_mixer(one, mixed, dy, dxb, branch, gates, dpar, gain_one, gain_two, column):
     n, rows, _ = one.shape
     groups = n // INNER
     width = dy.shape[1]
-    total = 3 * rows + gates.shape[1]
+    total = 3 * rows + 2 * gates.shape[2]
     kinds, _, _, units = column.shape
     turns = n.bit_length()
     dma = pltpu.SemaphoreType.DMA
@@ -868,17 +903,17 @@
         functools.partial(scatter_body, n),
         out_shape=(
             jax.ShapeDtypeStruct((total, width), F32),
-            jax.ShapeDtypeStruct(small.shape, F32),
+            jax.ShapeDtypeStruct((16, width), F32),
             jax.ShapeDtypeStruct((kinds, rows, groups * units), BF16),
         ),
-        in_specs=[VMEM] * 7 + [ANY],
+        in_specs=[VMEM] * 9 + [ANY],
         out_specs=(VMEM, VMEM, ANY),
         scratch_shapes=[
             pltpu.VMEM((n, total, width), BF16),
             pltpu.VMEM((2, groups, 2, total, width // 2), BF16),
             pltpu.VMEM((2, groups, total, width // 2), BF16),
             pltpu.VMEM((2, groups, total, width // 2), BF16),
-            pltpu.VMEM((turns,) + small.shape, F32),
+            pltpu.VMEM((turns, 16, width), F32),
             dma((2, groups, 2)),
             dma((2, groups, 2)),
             dma((2, groups)),
@@ -893,7 +928,7 @@
         ],
         compiler_params=params(2, 62),
         name="scatter_mixer",
-    )(one, mixed, dy, dxb, branch, gates, small, column)
+    )(one, mixed, dy, dxb, branch, gates, dpar, gain_one, gain_two, column)
 
 
 GELU_A = 0.7978845608028654
@@ -918,6 +953,9 @@
     return gate_x, gate_a, decay, room, mult
 
 
+FLIPPED = (((1,), (1,)), ((), ()))
+
+
 def first_row(tokens):
     row = lax.broadcasted_iota(jnp.int32, (tokens, 1), 0)
     return jnp.logical_and(row == 0, lax.axis_index("seq") == 0)
@@ -925,16 +963,31 @@
 
 def forward_body(
     n,
+    one_ref,
+    w_in_ref,
+    w_branch_ref,
+    w_out_ref,
+    gate_ref,
+    par_ref,
+    x_ref,
+    gain_ref,
+    column_ref,
+    cot_ref,
     xb_ref,
     yp_ref,
-    gate_ref,
-    par_ref,
-    column_ref,
     conv_ref,
     state_ref,
     branch_ref,
     edge_ref,
+    resid_ref,
+    two_ref,
     near_ref,
+    cots_ref,
+    w_in,
+    w_branch,
+    w_out,
+    mixed,
+    mixed_got,
     wide,
     tail,
     fade,
@@ -942,28 +995,61 @@
     theirs,
     *sems,
 ):
-    send_tail, recv_tail, send_tot, recv_tot, send_f, recv_f = sems
+    send_tail, recv_tail, send_tot, recv_tot, send_f, recv_f, here, send_m, recv_m, loaded = sems[:10]
     tokens, width = xb_ref.shape
+    model = one_ref.shape[1]
     me = lax.axis_index("seq")
     size = gate_ref.shape[2]
-    greet_all(n, me)
+    loads = [
+        pltpu.make_async_copy(src, dst, loaded.at[at])
+        for at, (src, dst) in enumerate(
+            ((w_in_ref, w_in), (w_branch_ref, w_branch), (w_out_ref, w_out))
+        )
+    ]
+    for load in loads:
+        load.start()
+    greet_all(n, me, True)
     tail_copy = remote(
         xb_ref.at[pl.ds(tokens - 16, 16)], tail, send_tail, recv_tail, lax.rem(me + 1, n)
     )
-    pl.when(me + 1 < n)(tail_copy.start)
     _, _, by_x, by_y, _ = whereabouts()
     part = column_ref.shape[1] // 2
+    kinds = column_ref.shape[0]
     hosted = [
-        remote(
-            column_ref.at[:, pl.ds(h * part, part)],
-            near_ref.at[h],
-            send_f.at[h],
-            recv_f.at[h],
-            (by_x, by_y)[h],
-        )
-        for h in range(2)
+        [
+            remote(
+                column_ref.at[kind, pl.ds(h * part, part)],
+                near_ref.at[h, kind],
+                send_f.at[kind, h],
+                recv_f.at[kind, h],
+                (by_x, by_y)[h],
+            )
+            for h in range(2)
+        ]
+        for kind in range(kinds)
     ]
+    chain = Chain(n, cot_ref, cots_ref, *sems[10:])
+    keep = chain.keep(here)
+
+    def host(kind):
+        for copy in hosted[kind]:
+            copy.start()
+
+    host(0)
+    chain.start()
+    keep.start()
+    loads[0].wait()
+    for start in range(0, width, size):
+        cols = slice(start, start + size)
+        xb_ref[:, cols] = jnp.dot(
+            one_ref[...], w_in[:, cols], preferred_element_type=F32
+        ).astype(BF16)
+    pl.when(me + 1 < n)(tail_copy.start)
     wide[8:] = xb_ref[...].astype(F32)
+    loads[1].wait()
+    for start in range(0, width, size):
+        cols = slice(start, start + size)
+        yp_ref[:, cols] = jnp.dot(one_ref[...], w_branch[:, cols], preferred_element_type=F32)
 
     @pl.when(me > 0)
     def _():
@@ -975,8 +1061,6 @@
         wide[:8] = jnp.zeros((8, width), F32)
 
     pl.when(me + 1 < n)(tail_copy.wait_send)
-    for copy in hosted:
-        copy.start()
     edge_ref[:8] = wide[:8]
     first = first_row(tokens)
     for head in range(width // size):
@@ -1006,7 +1090,8 @@
 
     ones, zeros = jnp.ones((1, width), F32), jnp.zeros((1, width), F32)
     tot_a, tot_b = lax.fori_loop(0, tokens // 8, inside, (ones, zeros))
-    mine[...] = jnp.where(row == 0, tot_a, tot_b)
+    mine[0:1] = tot_a
+    mine[1:2] = tot_b
 
     def told(place):
         return remote(mine, theirs.at[me], send_tot.at[place], recv_tot.at[me], place)
@@ -1019,6 +1104,7 @@
         return carry
 
     lax.fori_loop(me + 1, n, tell, 0)
+    host(1)
 
     def hear(place, state):
         heard(place).wait_recv()
@@ -1026,6 +1112,9 @@
 
     carry_in = lax.fori_loop(0, me, hear, zeros)
     edge_ref[8:] = jnp.broadcast_to(carry_in, (8, width))
+    for kind in range(2, kinds):
+        host(kind)
+    chain.step(1)
 
     def finish(at, carry):
         r = pl.ds(pl.multiple_of(at * 16, 16), 16)
@@ -1044,47 +1133,106 @@
         return carry
 
     lax.fori_loop(me + 1, n, sent, 0)
-    for copy in hosted:
-        copy.wait()
-
-
-def mixer_forward(x_branch, y_pre, gates, par, column):
+    loads[2].wait()
+    core = lax.axis_index("ch")
+    half = tokens // 2
+    for start in range(0, model, size):
+        cols = slice(start, start + size)
+        part = lax.dot_general(branch_ref[...], w_out[cols], FLIPPED, preferred_element_type=F32)
+        mixed[0, :, cols] = part[:half]
+        mixed[1, :, cols] = part[half:]
+    exchange = pltpu.make_async_remote_copy(
+        src_ref=mixed.at[1 - core],
+        dst_ref=mixed_got,
+        send_sem=send_m,
+        recv_sem=recv_m,
+        device_id={"ch": 1 - core},
+        device_id_type=MESH,
+    )
+    exchange.start()
+    exchange.wait_recv()
+
+    def norm(at, carry):
+        r = pl.ds(pl.multiple_of(at * 16, 16), 16)
+        resid = x_ref[r].astype(F32) + (mixed[core, r] + mixed_got[r])
+        resid_ref[r] = resid
+        scale = lax.rsqrt(jnp.mean(resid * resid, axis=-1, keepdims=True) + 1e-06)
+        two_ref[r] = (resid * scale * gain_ref[...]).astype(BF16)
+        return carry
+
+    lax.fori_loop(0, half // 16, norm, 0)
+    exchange.wait_send()
+    for step in range(2, n // INNER):
+        chain.step(step)
+    for pair in hosted:
+        for copy in pair:
+            copy.wait()
+    chain.finish()
+    keep.wait()
+
+
+def mixer_forward(one, weights, gates, par, x_half, gain, column, cotangent):
     n = lax.axis_size("seq")
-    tokens, width = x_branch.shape
+    tokens, model = one.shape
+    width = par.shape[1]
+    half = tokens // 2
     kinds, groups, rows, units = column.shape
     dma = pltpu.SemaphoreType.DMA
+    whole = jax.ShapeDtypeStruct((tokens, width), F32)
+    low = jax.ShapeDtypeStruct((tokens, width), BF16)
     return pl.pallas_call(
         functools.partial(forward_body, n),
         out_shape=(
-            jax.ShapeDtypeStruct((tokens, width), BF16),
-            jax.ShapeDtypeStruct((tokens, width), F32),
-            jax.ShapeDtypeStruct((tokens, width), BF16),
+            low,
+            whole,
+            low,
+            whole,
+            low,
             jax.ShapeDtypeStruct((16, width), F32),
+            jax.ShapeDtypeStruct((half, model), F32),
+            jax.ShapeDtypeStruct((half, model), BF16),
             jax.ShapeDtypeStruct((2, kinds, groups // 2, rows, units), column.dtype),
+            jax.ShapeDtypeStruct((groups, 2) + cotangent.shape, cotangent.dtype),
         ),
-        in_specs=[VMEM] * 4 + [ANY],
-        out_specs=(VMEM,) * 4 + (ANY,),
+        in_specs=[VMEM] + [HBM] * 3 + [VMEM] * 4 + [HBM, HBM],
+        out_specs=(VMEM,) * 8 + (ANY, ANY),
         scratch_shapes=[
+            pltpu.VMEM((model, width), BF16),
+            pltpu.VMEM((model, width), BF16),
+            pltpu.VMEM((model, width), BF16),
+            pltpu.VMEM((2, half, model), F32),
+            pltpu.VMEM((half, model), F32),
             pltpu.VMEM((tokens + 8, width), F32),
             pltpu.VMEM((16, width), BF16),
             pltpu.VMEM((tokens, width), F32),
-            pltpu.VMEM((8, width), F32),
-            pltpu.VMEM((n, 8, width), F32),
+            pltpu.VMEM((2, width), F32),
+            pltpu.VMEM((n, 2, width), F32),
             dma(()),
             dma(()),
             dma((n,)),
             dma((n,)),
-            dma((2,)),
-            dma((2,)),
+            dma((kinds, 2)),
+            dma((kinds, 2)),
+            dma(()),
+            dma(()),
+            dma(()),
+            dma((3,)),
+            *chain_semaphores(groups),
         ],
-        compiler_params=params(4, 40),
+        compiler_params=params(4, 60),
         name="mixer_forward",
-    )(x_branch, y_pre, gates, par, column)
+    )(one, *weights, gates, par, x_half, gain, column, cotangent)
 
 
 def backward_body(
     n,
-    grad_ref,
+    mixed_ref,
+    w_in_ref,
+    w_branch_ref,
+    w_out_ref,
+    x_ref,
+    gain_ref,
+    resid_ref,
     yp_ref,
     state_ref,
     edge_ref,
@@ -1097,7 +1245,14 @@
     dxb_ref,
     dgate_ref,
     dpar_ref,
+    dx_ref,
+    dgain_ref,
     near_ref,
+    w_in,
+    w_branch,
+    w_out,
+    d_one,
+    d_one_got,
     fade,
     shift,
     adj,
@@ -1110,11 +1265,20 @@
     head_rows,
     *sems,
 ):
-    send_rows, recv_rows, send_tot, recv_tot, send_f, recv_f = sems
+    send_rows, recv_rows, send_tot, recv_tot, send_f, recv_f, send_m, recv_m, loaded = sems
     tokens, width = xb_ref.shape
+    model = gain_ref.shape[1]
     me = lax.axis_index("seq")
     size = gate_ref.shape[2]
-    greet_all(n, me)
+    loads = [
+        pltpu.make_async_copy(src, dst, loaded.at[at])
+        for at, (src, dst) in enumerate(
+            ((w_out_ref, w_out), (w_in_ref, w_in), (w_branch_ref, w_branch))
+        )
+    ]
+    for load in loads:
+        load.start()
+    greet_all(n, me, True)
     _, _, by_x, by_y, _ = whereabouts()
     hosted = [
         remote(half_ref.at[h], near_ref.at[h], send_f.at[h], recv_f.at[h], (by_x, by_y)[h])
@@ -1124,6 +1288,7 @@
         copy.start()
     first = first_row(tokens)
     fade[tokens:] = jnp.ones((8, width), F32)
+    loads[0].wait()
     for head in range(width // size):
         cols = slice(head * size, (head + 1) * size)
         gate_x, gate_a, decay, _, _ = gates_of(conv_ref[:, cols], gate_ref, par_ref, head, cols, first)
@@ -1131,7 +1296,7 @@
         gate_a_s[:, cols] = gate_a
         fade[:tokens, cols] = decay
         value, slope = gelu_parts(yp_ref[:, cols])
-        grad = grad_ref[:, cols]
+        grad = jnp.dot(mixed_ref[...], w_out[:, cols], preferred_element_type=F32)
         dy_ref[:, cols] = (grad * state_ref[:, cols] * slope).astype(BF16)
         adj[:, cols] = grad * value
         shift[:, cols] = fade[1 : tokens + 1, cols]
@@ -1154,7 +1319,8 @@
     ones, zeros = jnp.ones((1, width), F32), jnp.zeros((1, width), F32)
     tot_a, tot_b = lax.fori_loop(0, tiles, inside, (ones, zeros))
     first_fade = fade[0:1]
-    mine[...] = jnp.where(row == 0, first_fade * tot_a, first_fade * tot_b)
+    mine[0:1] = first_fade * tot_a
+    mine[1:2] = first_fade * tot_b
 
     def told(place):
         return remote(mine, theirs.at[me], send_tot.at[place], recv_tot.at[me], place)
@@ -1207,20 +1373,16 @@
             jnp.sum(d_log * (-8.0 * gate_a), axis=0, keepdims=True) * par_ref[9:10, cols]
         )
         low_x, low_a = d_pre_x.astype(BF16), d_pre_a.astype(BF16)
-        flipped = (((1,), (1,)), ((), ()))
         d_conv = (
             back * gate_x * mult
-            + lax.dot_general(low_x, gate_ref[0, head], flipped, preferred_element_type=F32)
-            + lax.dot_general(low_a, gate_ref[1, head], flipped, preferred_element_type=F32)
+            + lax.dot_general(low_x, gate_ref[0, head], FLIPPED, preferred_element_type=F32)
+            + lax.dot_general(low_a, gate_ref[1, head], FLIPPED, preferred_element_type=F32)
         )
         dconv[:tokens, cols] = d_conv
         over_rows = (((0,), (0,)), ((), ()))
-        dgate_ref[0, head] = lax.dot_general(
-            conv_low, low_x, over_rows, preferred_element_type=F32
-        ).astype(BF16)
-        dgate_ref[1, head] = lax.dot_general(
-            conv_low, low_a, over_rows, preferred_element_type=F32
-        ).astype(BF16)
+        for gate, low in enumerate((low_x, low_a)):
+            d_gate = lax.dot_general(conv_low, low, over_rows, preferred_element_type=F32)
+            dgate_ref[:, gate, :, cols] = d_gate.astype(BF16).reshape(n, size // n, size)
         dpar_ref[4:5, cols] = jnp.sum(d_conv, axis=0, keepdims=True)
         for tap in range(4):
             dpar_ref[tap : tap + 1, cols] = jnp.sum(
@@ -1255,28 +1417,76 @@
         return carry
 
     lax.fori_loop(0, me, sent, 0)
+    core = lax.axis_index("ch")
+    half = tokens // 2
+    loads[1].wait()
+    loads[2].wait()
+    for start in range(0, model, size):
+        cols = slice(start, start + size)
+        part = (
+            lax.dot_general(dy_ref[...], w_branch[cols], FLIPPED, preferred_element_type=F32)
+            + lax.dot_general(dxb_ref[...], w_in[cols], FLIPPED, preferred_element_type=F32)
+        ).astype(BF16)
+        d_one[0, :, cols] = part[:half]
+        d_one[1, :, cols] = part[half:]
+    exchange = pltpu.make_async_remote_copy(
+        src_ref=d_one.at[1 - core],
+        dst_ref=d_one_got,
+        send_sem=send_m,
+        recv_sem=recv_m,
+        device_id={"ch": 1 - core},
+        device_id_type=MESH,
+    )
+    exchange.start()
+    exchange.wait_recv()
+
+    def norm(at, total):
+        r = pl.ds(pl.multiple_of(at * 16, 16), 16)
+        x = x_ref[r].astype(F32)
+        scale = lax.rsqrt(jnp.mean(x * x, axis=-1, keepdims=True) + 1e-06)
+        grad = d_one[core, r].astype(F32) + d_one_got[r].astype(F32)
+        back = grad * gain_ref[...]
+        shrink = scale * scale * scale * jnp.mean(x * back, axis=-1, keepdims=True)
+        dx_ref[r] = resid_ref[r] + (scale * back - x * shrink)
+        return total + jnp.sum(grad * (x * scale), axis=0, keepdims=True)
+
+    dgain_ref[...] = lax.fori_loop(0, half // 16, norm, jnp.zeros((1, model), F32))
+    exchange.wait_send()
     for copy in hosted:
         copy.wait()
 
 
-def mixer_backward(grad, y_pre, states, edge, conv, x_branch, gates, par, halves):
+def mixer_backward(
+    mixed, weights, x_half, gain, d_resid, y_pre, states, edge, conv, x_branch, gates, par, halves
+):
     n = lax.axis_size("seq")
     tokens, width = x_branch.shape
+    model = mixed.shape[1]
+    size = gates.shape[2]
+    half = tokens // 2
     dma = pltpu.SemaphoreType.DMA
     whole = pltpu.VMEM((tokens, width), F32)
     longer = pltpu.VMEM((tokens + 8, width), F32)
+    weight = pltpu.VMEM((model, width), BF16)
     return pl.pallas_call(
         functools.partial(backward_body, n),
         out_shape=(
             jax.ShapeDtypeStruct((tokens, width), BF16),
             jax.ShapeDtypeStruct((tokens, width), BF16),
-            jax.ShapeDtypeStruct(gates.shape, BF16),
+            jax.ShapeDtypeStruct((n, 2, size // n, width), BF16),
             jax.ShapeDtypeStruct((8, width), F32),
+            jax.ShapeDtypeStruct((half, model), F32),
+            jax.ShapeDtypeStruct((1, model), F32),
             jax.ShapeDtypeStruct(halves.shape, BF16),
         ),
-        in_specs=[VMEM] * 8 + [ANY],
-        out_specs=(VMEM,) * 4 + (ANY,),
+        in_specs=[VMEM] + [HBM] * 3 + [VMEM] * 10 + [HBM],
+        out_specs=(VMEM,) * 6 + (ANY,),
         scratch_shapes=[
+            weight,
+            weight,
+            weight,
+            pltpu.VMEM((2, half, model), BF16),
+            pltpu.VMEM((half, model), BF16),
             longer,
             whole,
             whole,
@@ -1284,8 +1494,8 @@
             whole,
             longer,
             longer,
-            pltpu.VMEM((8, width), F32),
-            pltpu.VMEM((n, 8, width), F32),
+            pltpu.VMEM((2, width), F32),
+            pltpu.VMEM((n, 2, width), F32),
             pltpu.VMEM((8, width), F32),
             dma(()),
             dma(()),
@@ -1293,10 +1503,458 @@
             dma((n,)),
             dma((2,)),
             dma((2,)),
+            dma(()),
+            dma(()),
+            dma((3,)),
         ],
-        compiler_params=params(5, 48),
+        compiler_params=params(5, 60),
         name="mixer_backward",
-    )(grad, y_pre, states, edge, conv, x_branch, gates, par, halves)
+    )(mixed, *weights, x_half, gain, d_resid, y_pre, states, edge, conv, x_branch, gates, par, halves)
+
+
+def ffn_body(n, *refs):
+    own_ref, column_ref, near_ref, cots_ref, resid_ref, gain_ref = refs[:6]
+    block_ref, d_resid_ref, mixed_ref, d_gain_ref, halves_ref, mine_ref, far_ref = refs[6:13]
+    tokens, cots, w, hidden, box, sib, got, d_hidden, stage, turned = refs[13:23]
+    send_t, recv_z, recv_c, send_w, recv_w, keep_w, keep_c, keep_t = refs[23:31]
+    send_c, recv_s, send_z, recv_r, send_f, recv_f, send_m, recv_m, move, out_sem = refs[31:]
+    groups = n // INNER
+    half = groups // 2
+    me, outer, by_x, by_y, by_xy = whereabouts()
+    base = outer * INNER
+    core = lax.axis_index("ch")
+    above, below = outer + 1 < groups, outer > 0
+    sibling = {"ch": 1 - core}
+    barrier = pltpu.get_barrier_semaphore()
+
+    def hello(peer):
+        pl.semaphore_signal(barrier, inc=1, device_id=peer, device_id_type=MESH)
+
+    hello({"seq": by_x})
+    hello({"seq": by_y})
+    hello(sibling)
+    pl.when(above)(lambda: hello({"seq": me + INNER}))
+    pl.when(below)(lambda: hello({"seq": me - INNER}))
+    pl.semaphore_wait(barrier, 3 + above.astype(jnp.int32) + below.astype(jnp.int32))
+    flips = ((by_x, by_y), (by_y, by_x))
+    rows, units = w.shape[3], w.shape[4]
+    tall, model = own_ref.shape
+    count = 2 * tall
+    deep = INNER * rows
+    tile = 256
+
+    def part(h):
+        return pl.ds(h * half, half)
+
+
+    chain = Chain(n, own_ref, tokens, send_t, recv_z, recv_c)
+
+    def weight_copy(kind, h, far, receive=False):
+        source = flips[h][0] if far else me
+        if receive:
+            source = by_xy if far else flips[h][1]
+        return remote(
+            near_ref.at[h, kind] if far else column_ref.at[kind, part(h)],
+            w.at[kind, part(h), source - base],
+            send_w.at[kind, h, far],
+            recv_w.at[kind, h, far],
+            flips[h][1],
+        )
+
+    keep = [
+        [
+            pltpu.make_async_copy(
+                column_ref.at[kind], w.at[kind, :, me - base], keep_w.at[kind, 0]
+            ),
+            *(
+                pltpu.make_async_copy(
+                    near_ref.at[h, kind],
+                    w.at[kind, part(h), flips[h][0] - base],
+                    keep_w.at[kind, 1 + h],
+                )
+                for h in range(2)
+            ),
+        ]
+        for kind in range(3)
+    ]
+    every = [(h, far) for far in range(2) for h in range(2)]
+    load_c = pltpu.make_async_copy(cots_ref, cots, keep_c)
+    own = chain.keep(keep_t)
+    chain.start()
+    for kind in (2, 0, 1):
+        for h, far in every:
+            weight_copy(kind, h, far).start()
+    load_c.start()
+    own.start()
+    for kind in (2, 0, 1):
+        for copy in keep[kind]:
+            copy.start()
+    for step in range(1, groups):
+        chain.step(step)
+    chain.finish()
+    own.wait()
+    load_c.wait()
+
+    def weights_landed(kind):
+        for h, far in every:
+            weight_copy(kind, h, far, True).wait_recv()
+        for copy in keep[kind]:
+            copy.wait()
+
+    def columns(kind, at):
+        return w[kind, :, :, :, at : at + tile].reshape(model, tile)
+
+    def token_rows(place):
+        return pl.ds(pl.multiple_of(place * count, count), count)
+
+    def each(limit, action):
+        def one(turn, carry):
+            action(turn)
+            return carry
+
+        lax.fori_loop(0, limit, one, 0)
+
+    weights_landed(2)
+
+    def back_hidden(place):
+        left = cots[place].reshape(count, model)
+        for at in range(0, units, tile):
+            d_hidden[token_rows(place), at : at + tile] = jnp.dot(
+                left, columns(2, at), preferred_element_type=F32
+            )
+
+    each(groups, back_hidden)
+    weights_landed(0)
+    weights_landed(1)
+
+    def middle(place):
+        left = tokens[place].reshape(count, model)
+        r = token_rows(place)
+        for at in range(0, units, tile):
+            c = slice(at, at + tile)
+            gate = jnp.dot(left, columns(0, at), preferred_element_type=F32)
+            up = jnp.dot(left, columns(1, at), preferred_element_type=F32)
+            value, slope = gelu_parts(gate)
+            back = d_hidden[r, c]
+            hidden[0, r, c] = (value * up).astype(BF16)
+            hidden[1, r, c] = (back * up * slope).astype(BF16)
+            hidden[2, r, c] = (back * value).astype(BF16)
+
+    each(groups, middle)
+    for kind in range(3):
+        for h, far in every:
+            weight_copy(kind, h, far).wait_send()
+
+
+    def partial(kind, place):
+        r = token_rows(place)
+        for at in range(groups):
+            pairs = ((1, 0), (2, 1)) if kind == 0 else ((0, 2),)
+            value = 0.0
+            for left, right in pairs:
+                value = value + lax.dot_general(
+                    hidden[left, r],
+                    w[right, at].reshape(deep, units),
+                    FLIPPED,
+                    preferred_element_type=F32,
+                )
+            value = value.astype(BF16)
+            box[place, 0, :, at * deep : (at + 1) * deep] = value[:tall]
+            box[place, 1, :, at * deep : (at + 1) * deep] = value[tall:]
+        to_sibling(kind, place).start()
+
+    def to_sibling(kind, place):
+        return pltpu.make_async_remote_copy(
+            src_ref=box.at[place, 1 - core],
+            dst_ref=sib.at[kind, place],
+            send_sem=send_c.at[kind, place],
+            recv_sem=recv_s.at[kind, place],
+            device_id=sibling,
+            device_id_type=MESH,
+        )
+
+    def along(kind, place, up):
+        last = place == (outer + 1 if up else outer - 1)
+        slot = place if up else jnp.where(last, groups, place)
+        return remote(
+            box.at[place, core],
+            got.at[kind, slot],
+            send_z.at[kind, place],
+            recv_r.at[kind, slot],
+            me + (INNER if up else -INNER),
+        )
+
+    def landed(kind, slot):
+        return remote(
+            box.at[0, core], got.at[kind, slot], send_z.at[kind, 0], recv_r.at[kind, slot], by_x
+        )
+
+    chunk = 16
+
+    def rows_of(at):
+        return pl.ds(pl.multiple_of(at * chunk, chunk), chunk)
+
+    def ready(kind, place, incoming):
+        to_sibling(kind, place).wait_recv()
+
+        def add(at, with_got):
+            r = rows_of(at)
+            value = box[place, core, r].astype(F32) + sib[kind, place, r].astype(F32)
+            if with_got:
+                value = value + got[kind, place, r].astype(F32)
+            box[place, core, r] = value.astype(BF16)
+
+        @pl.when(incoming)
+        def _():
+            landed(kind, place).wait_recv()
+            each(tall // chunk, lambda at: add(at, True))
+
+        @pl.when(jnp.logical_not(incoming))
+        def _():
+            each(tall // chunk, lambda at: add(at, False))
+
+    def climb(kind, turn):
+        place = groups - 1 - turn
+
+        @pl.when(place > outer)
+        def _():
+            ready(kind, place, below)
+            along(kind, place, True).start()
+
+    def sink(kind, turn):
+        @pl.when(turn < outer)
+        def _():
+            ready(kind, turn, above)
+            along(kind, turn, False).start()
+
+    def pass_on(kind):
+        def turns(turn):
+            @pl.when(outer < half)
+            def _():
+                climb(kind, turn)
+                sink(kind, turn)
+
+            @pl.when(outer >= half)
+            def _():
+                sink(kind, turn)
+                climb(kind, turn)
+
+        each(groups - 1, turns)
+
+    def totals(kind, use):
+        to_sibling(kind, outer).wait_recv()
+        for condition, slots in (
+            (jnp.logical_and(below, above), (outer, groups)),
+            (jnp.logical_and(below, jnp.logical_not(above)), (outer,)),
+            (jnp.logical_and(jnp.logical_not(below), above), (groups,)),
+        ):
+
+            @pl.when(condition)
+            def _(slots=slots):
+                for slot in slots:
+                    landed(kind, slot).wait_recv()
+
+                def one(at):
+                    r = rows_of(at)
+                    value = box[outer, core, r].astype(F32) + sib[kind, outer, r].astype(F32)
+                    for slot in slots:
+                        value = value + got[kind, slot, r].astype(F32)
+                    use(r, value)
+
+                each(tall // chunk, one)
+
+    def clear(kind):
+        def one(place):
+            to_sibling(kind, place).wait_send()
+
+            @pl.when(place > outer)
+            def _():
+                along(kind, place, True).wait_send()
+
+            @pl.when(place < outer)
+            def _():
+                along(kind, place, False).wait_send()
+
+        each(groups, one)
+
+
+    def gradient_copy(kind, h, far):
+        source = by_xy if far else flips[h][1]
+        return remote(
+            w.at[kind, part(h), source - base],
+            far_ref.at[h, far, kind],
+            send_f.at[kind, h, far],
+            recv_f.at[kind, h, far],
+            flips[h][1],
+        )
+
+    def gradients(kinds, source):
+        for h in range(2):
+            for at in range(h * half, (h + 1) * half):
+                left = source[:, :, :, at * deep : (at + 1) * deep].reshape(groups * count, deep)
+                turned[...] = left.T
+                for kind, right in kinds:
+                    for start in range(0, units, tile):
+                        c = slice(start, start + tile)
+                        w[kind, at, :, :, c] = (
+                            jnp.dot(
+                                turned[...], hidden[right, :, c], preferred_element_type=F32
+                            )
+                            .astype(BF16)
+                            .reshape(INNER, rows, tile)
+                        )
+            for kind, _ in kinds:
+                for far in (1, 0):
+                    gradient_copy(kind, h, far).start()
+
+    def collect(kind, h, far):
+        inner = (flips[h][0] if far else me) - base
+        gradient_copy(kind, h, far).wait_recv()
+        load = pltpu.make_async_copy(far_ref.at[h, far, kind], stage, move)
+        load.start()
+        load.wait()
+        for place in range(half):
+            at = h * half + place
+
+            def one(turn, place=place, at=at):
+                r = rows_of(turn)
+                w[kind, at, inner, r] = (
+                    w[kind, at, inner, r].astype(F32) + stage[place, r].astype(F32)
+                ).astype(BF16)
+
+            each(rows // chunk, one)
+        out_copy(kind, h, far).start()
+
+    def out_copy(kind, h, far):
+        inner = (flips[h][0] if far else me) - base
+        return pltpu.make_async_copy(
+            w.at[kind, part(h), inner],
+            (halves_ref if far else mine_ref).at[h, kind],
+            out_sem.at[kind, h, far],
+        )
+
+    def in_order(action):
+        @pl.when(outer < half)
+        def _():
+            for turn in range(half):
+                action(groups - 1 - turn)
+                action(turn)
+
+        @pl.when(outer >= half)
+        def _():
+            for turn in range(half):
+                action(turn)
+                action(groups - 1 - turn)
+
+    in_order(lambda place: partial(0, place))
+    gradients(((0, 1), (1, 2)), tokens)
+    pass_on(0)
+    d_gain_ref[...] = jnp.zeros((1, model), F32)
+
+    def norm(r, grad):
+        resid = resid_ref[r]
+        scale = lax.rsqrt(jnp.mean(resid * resid, axis=-1, keepdims=True) + 1e-06)
+        back = grad * gain_ref[...]
+        shrink = scale * scale * scale * jnp.mean(resid * back, axis=-1, keepdims=True)
+        value = cots[outer, core, r].astype(F32) + (scale * back - resid * shrink)
+        d_resid_ref[r] = value
+        mixed_ref[core, r] = value.astype(BF16)
+        d_gain_ref[...] = d_gain_ref[...] + jnp.sum(grad * (resid * scale), axis=0, keepdims=True)
+
+    totals(0, norm)
+    share = pltpu.make_async_remote_copy(
+        src_ref=mixed_ref.at[core],
+        dst_ref=mixed_ref.at[core],
+        send_sem=send_m,
+        recv_sem=recv_m,
+        device_id=sibling,
+        device_id_type=MESH,
+    )
+    share.start()
+    clear(0)
+    in_order(lambda place: partial(1, place))
+    gradients(((2, 0),), cots)
+    pass_on(1)
+    for far in (1, 0):
+        for kind in range(2):
+            for h in range(2):
+                collect(kind, h, far)
+
+    def finish(r, value):
+        block_ref[r] = (resid_ref[r] + value).astype(BF16)
+
+    totals(1, finish)
+    clear(1)
+    for far in (1, 0):
+        for h in range(2):
+            collect(2, h, far)
+    pltpu.make_async_remote_copy(
+        src_ref=mixed_ref.at[core],
+        dst_ref=mixed_ref.at[1 - core],
+        send_sem=send_m,
+        recv_sem=recv_m,
+        device_id=sibling,
+        device_id_type=MESH,
+    ).wait_recv()
+    share.wait_send()
+    for kind in range(3):
+        for h, far in every:
+            gradient_copy(kind, h, far).wait_send()
+            out_copy(kind, h, far).wait()
+
+
+def feed_forward(own, column, near, cots, resid, gain):
+    n = lax.axis_size("seq")
+    groups = n // INNER
+    tall, model = own.shape
+    kinds, _, rows, units = column.shape
+    half = groups // 2
+    dma = pltpu.SemaphoreType.DMA
+    part = jax.ShapeDtypeStruct((2, kinds, half, rows, units), BF16)
+    return pl.pallas_call(
+        functools.partial(ffn_body, n),
+        out_shape=(
+            jax.ShapeDtypeStruct((tall, model), BF16),
+            jax.ShapeDtypeStruct((tall, model), F32),
+            jax.ShapeDtypeStruct((2, tall, model), BF16),
+            jax.ShapeDtypeStruct((1, model), F32),
+            part,
+            part,
+            jax.ShapeDtypeStruct((2, 2, kinds, half, rows, units), BF16),
+        ),
+        in_specs=[HBM] * 4 + [VMEM] * 2,
+        out_specs=(VMEM,) * 4 + (HBM,) * 3,
+        scratch_shapes=[
+            pltpu.VMEM((groups, 2, tall, model), BF16),
+            pltpu.VMEM((groups, 2, tall, model), BF16),
+            pltpu.VMEM((kinds, groups, INNER, rows, units), BF16),
+            pltpu.VMEM((3, groups * 2 * tall, units), BF16),
+            pltpu.VMEM((groups, 2, tall, model), BF16),
+            pltpu.VMEM((2, groups, tall, model), BF16),
+            pltpu.VMEM((2, groups + 1, tall, model), BF16),
+            pltpu.VMEM((groups * 2 * tall, units), F32),
+            pltpu.VMEM((half, rows, units), BF16),
+            pltpu.VMEM((INNER * rows, groups * 2 * tall), BF16),
+            *chain_semaphores(groups),
+            dma((kinds, 2, 2)),
+            dma((kinds, 2, 2)),
+            dma((kinds, 3)),
+            dma(()),
+            dma(()),
+            dma((2, groups)),
+            dma((2, groups)),
+            dma((2, groups)),
+            dma((2, groups + 1)),
+            dma((kinds, 2, 2)),
+            dma((kinds, 2, 2)),
+            dma(()),
+            dma(()),
+            dma(()),
+            dma((kinds, 2, 2)),
+        ],
+        compiler_params=params(8, 63),
+        name="feed_forward",
+    )(own, column, near, cots, resid, gain)
 
 
 def my_half(values):
@@ -1310,13 +1968,6 @@
     return jnp.concatenate(
         [jnp.where(core == 0, own, other), jnp.where(core == 0, other, own)], axis=0
     )
-
-
-def half_sum(partial):
-    core = lax.axis_index("ch")
-    parts = partial.reshape((2, partial.shape[0] // 2) + partial.shape[1:])
-    theirs = swap(pick(parts, 1 - core), "ch", 1)
-    return pick(parts, core).astype(F32) + theirs.astype(F32)
 
 
 def tokens_out(partial, half):
@@ -1333,19 +1984,56 @@
     return total
 
 
-def gate_rows(blocks, n):
-    _, heads, depth, size = blocks.shape
-    part = depth // n
-    rows = 2 * part
-    split = blocks.reshape(2, heads, n, part, size).transpose(2, 0, 1, 3, 4)
-    return split.reshape(n, 2, rows, heads * size // 2).transpose(0, 2, 1, 3).reshape(n, rows, heads * size)
-
-
-def gate_blocks(rows, heads, size):
-    n, count, width = rows.shape
-    split = rows.reshape(n, count, 2, width // 2).transpose(0, 2, 1, 3)
-    part = count * width // (2 * heads * size)
-    return split.reshape(n, 2, heads, part, size).transpose(1, 2, 0, 3, 4).reshape(2, heads, n * part, size)
+def feed_forward_parts(n_two, column, near, all_cot, resid, ffn_gain, cot_half):
+    f32, bf16 = F32, BF16
+    _, groups, depth, units = column.shape
+    half_rows, model = n_two.shape
+    tok_rows = 2 * half_rows
+    _, norm_back_two = jax.vjp(scaled_norm, resid, ffn_gain)
+    all_two, *full_ffn = gather_tokens(n_two, column, near)
+    all_two, all_cot = (v.reshape(groups * tok_rows, model) for v in (all_two, all_cot))
+    full_ffn = [w.reshape(model, units) for w in full_ffn]
+    gate_pre = jnp.dot(all_two, full_ffn[0], preferred_element_type=f32)
+    up_pre = jnp.dot(all_two, full_ffn[1], preferred_element_type=f32)
+    gate_act, gelu_back_gate = jax.vjp(gelu_tanh, gate_pre)
+    hidden = (gate_act * up_pre).astype(bf16)
+    ffn_term = jnp.einsum("tf,df->td", hidden, full_ffn[2], preferred_element_type=f32).astype(bf16)
+    d_hidden = jnp.einsum("td,df->tf", all_cot, full_ffn[2], preferred_element_type=f32)
+    d_gate = gelu_back_gate(d_hidden * up_pre)[0].astype(bf16)
+    d_up = (d_hidden * gate_act).astype(bf16)
+    d_n_two = (
+        jnp.einsum("tf,df->td", d_gate, full_ffn[0], preferred_element_type=f32)
+        + jnp.einsum("tf,df->td", d_up, full_ffn[1], preferred_element_type=f32)
+    ).astype(bf16)
+    terms = [
+        jnp.einsum("td,tf->df", left, right, preferred_element_type=f32)
+        .astype(bf16)
+        .reshape(groups, INNER, depth, units)
+        for left, right in ((all_two, d_gate), (all_two, d_up), (all_cot, hidden))
+    ]
+    split = [v.reshape(groups, 2, half_rows, model) for v in (d_n_two, ffn_term)]
+    if groups <= 4:
+        d_n_two, ffn_out, far = reduce_tokens(split, terms)
+    else:
+        d_n_two, far = reduce_tokens(split[:1], terms)
+        ffn_out = tokens_out(ffn_term, half_rows)
+    block_half = (resid + ffn_out).astype(bf16)
+    inner = lax.axis_index("seq") % INNER
+    by_half = [t.reshape(2, groups // 2, INNER, depth, units) for t in terms]
+
+    def block_at(h, place):
+        return jnp.stack([pick(t[h], place, 1) for t in by_half]).astype(f32)
+
+    mine = jnp.stack(
+        [(block_at(h, inner) + far[h, 0].astype(f32)).astype(bf16) for h in range(2)]
+    )
+    halves = jnp.stack(
+        [(block_at(h, inner ^ (1, 2)[h]) + far[h, 1].astype(f32)).astype(bf16) for h in range(2)]
+    )
+    d_resid_norm, d_ffn_gain_term = norm_back_two(d_n_two)
+    d_resid = cot_half.astype(f32) + d_resid_norm
+    d_mixed = join(d_resid.astype(bf16))
+    return block_half, d_resid, d_mixed, d_ffn_gain_term.reshape(1, model), halves, mine
 
 
 def shards(
@@ -1376,18 +2064,17 @@
     units = -(-hidden_units // (groups * 128)) * 128
     x_float = inputs.astype(f32)
     n_one = scaled_norm(x_float, norm_gain).astype(bf16)
-    x_half = my_half(inputs).astype(f32)
-    _, norm_back_one = jax.vjp(scaled_norm, x_half, norm_gain)
-
-    gate_pack = gate_rows(jnp.stack([gate_x_blocks, gate_a_blocks]), 1)[0]
+    x_half = my_half(inputs)
+
+    gate_pack = jnp.stack([gate_x_blocks, gate_a_blocks])
     ffn_pack = jnp.pad(
         jnp.stack([ffn_gate, ffn_up, ffn_down.T]), ((0, 0), (0, 0), (0, groups * units - hidden_units))
     )
     *full_mixer, full_gates, column = gather_weights(
-        [branch_weight, input_weight, out_weight.T], gate_pack, ffn_pack
+        [input_weight, branch_weight, out_weight.T], gate_pack, ffn_pack
     )
-    full_branch, full_input, full_out = (w.reshape(model, width) for w in full_mixer)
-    gates = gate_blocks(full_gates, heads, size)
+    full_mixer = [w.reshape(model, width) for w in full_mixer]
+    gates = full_gates.reshape(2, heads, size, size)
     par = jnp.concatenate(
         [
             channel_params,
@@ -1400,80 +2087,48 @@
 
     cot_half = my_half(cotangent)
 
-    x_branch = jnp.dot(n_one, full_input, preferred_element_type=f32).astype(bf16)
-    y_pre = jnp.dot(n_one, full_branch, preferred_element_type=f32)
-    conv_out, states, branch_out, edge, near = mixer_forward(x_branch, y_pre, gates, par, column)
-    mixed = half_sum(jnp.einsum("tw,dw->td", branch_out, full_out, preferred_element_type=f32))
-    resid = x_half + mixed
-    n_two_f, norm_back_two = jax.vjp(scaled_norm, resid, ffn_gain)
-    all_two, all_cot, *full_ffn = gather_tokens(n_two_f.astype(bf16), cot_half, column, near)
-    all_two, all_cot = (v.reshape(groups * tok_rows, model) for v in (all_two, all_cot))
-    full_ffn = [w.reshape(model, units) for w in full_ffn]
-    gate_pre = jnp.dot(all_two, full_ffn[0], preferred_element_type=f32)
-    up_pre = jnp.dot(all_two, full_ffn[1], preferred_element_type=f32)
-    gate_act, gelu_back_gate = jax.vjp(gelu_tanh, gate_pre)
-    hidden = (gate_act * up_pre).astype(bf16)
-    ffn_term = jnp.einsum("tf,df->td", hidden, full_ffn[2], preferred_element_type=f32).astype(bf16)
-    d_hidden = jnp.einsum("td,df->tf", all_cot, full_ffn[2], preferred_element_type=f32)
-    d_gate = gelu_back_gate(d_hidden * up_pre)[0].astype(bf16)
-    d_up = (d_hidden * gate_act).astype(bf16)
-    d_n_two = (
-        jnp.einsum("tf,df->td", d_gate, full_ffn[0], preferred_element_type=f32)
-        + jnp.einsum("tf,df->td", d_up, full_ffn[1], preferred_element_type=f32)
-    ).astype(bf16)
-    terms = [
-        jnp.einsum("td,tf->df", left, right, preferred_element_type=f32)
-        .astype(bf16)
-        .reshape(groups, INNER, depth, units)
-        for left, right in ((all_two, d_gate), (all_two, d_up), (all_cot, hidden))
-    ]
-    split = [v.reshape(groups, 2, half_rows, model) for v in (d_n_two, ffn_term)]
-    if groups <= 4:
-        d_n_two, ffn_out, far = reduce_tokens(split, terms)
+    x_branch, y_pre, conv_out, states, branch_out, edge, resid, n_two, near, all_cot = mixer_forward(
+        n_one,
+        full_mixer,
+        gates,
+        par,
+        x_half,
+        ffn_gain.reshape(1, model),
+        column,
+        cot_half,
+    )
+    if groups <= 4 and depth % 16 == 0:
+        block_half, d_resid, d_mixed, d_ffn_gain_term, halves, mine, _ = feed_forward(
+            n_two, column, near, all_cot, resid, ffn_gain.reshape(1, model)
+        )
+        d_mixed = d_mixed.reshape(tok_rows, model)
     else:
-        d_n_two, far = reduce_tokens(split[:1], terms)
-        ffn_out = tokens_out(ffn_term, half_rows)
-    block_out = join((resid + ffn_out).astype(bf16))
-    inner = lax.axis_index("seq") % INNER
-    by_half = [t.reshape(2, groups // 2, INNER, depth, units) for t in terms]
-
-    def block_at(h, place):
-        return jnp.stack([pick(t[h], place, 1) for t in by_half]).astype(f32)
-
-    halves = jnp.stack(
-        [(block_at(h, inner ^ (1, 2)[h]) + far[h, 1].astype(f32)).astype(bf16) for h in range(2)]
-    )
-    d_resid_norm, d_ffn_gain_term = norm_back_two(d_n_two)
-    d_resid = cot_half.astype(f32) + d_resid_norm
-    d_mixed = join(d_resid.astype(bf16))
-    d_branch_out = jnp.einsum("td,dw->tw", d_mixed, full_out, preferred_element_type=f32)
-    d_y, d_xb, d_gates, d_channel_term, near_back = mixer_backward(
-        d_branch_out, y_pre, states, edge, conv_out, x_branch, gates, par, halves
+        block_half, d_resid, d_mixed, d_ffn_gain_term, halves, mine = feed_forward_parts(
+            n_two, column, near, all_cot, resid, ffn_gain, cot_half
+        )
+    block_out = join(block_half)
+    d_y, d_xb, d_gates, d_par, d_inputs, d_norm_gain_term, near_back = mixer_backward(
+        d_mixed,
+        full_mixer,
+        x_half,
+        norm_gain.reshape(1, model),
+        d_resid,
+        y_pre,
+        states,
+        edge,
+        conv_out,
+        x_branch,
+        gates,
+        par,
+        halves,
     )
     column_back = jnp.concatenate(
         [
-            (block_at(h, inner) + far[h, 0].astype(f32) + near_back[h].astype(f32)).astype(bf16)
-            for h in range(2)
+            (mine[h].astype(f32) + near_back[h].astype(f32)).astype(bf16) for h in range(2)
         ],
         axis=1,
     )
-    d_n_one = half_sum(
-        (
-            jnp.einsum("tw,dw->td", d_y, full_branch, preferred_element_type=f32)
-            + jnp.einsum("tw,dw->td", d_xb, full_input, preferred_element_type=f32)
-        ).astype(bf16)
-    )
-    d_x_norm, d_norm_gain_term = norm_back_one(d_n_one)
-    d_inputs = join(d_resid + d_x_norm)
-    small_terms = jnp.concatenate(
-        [
-            d_channel_term,
-            d_norm_gain_term.reshape(-1, width),
-            d_ffn_gain_term.reshape(-1, width),
-            jnp.zeros((8 - 2 * (model // width), width), f32),
-        ],
-        axis=0,
-    )
+    d_inputs = join(d_inputs)
     gain_rows = model // width
     scattered, small, spread = scatter_mixer(
         n_one.T.reshape(n, depth, tok_rows),
@@ -1481,12 +2136,14 @@
         d_y,
         d_xb,
         branch_out,
-        gate_rows(d_gates, n),
-        small_terms,
+        d_gates,
+        d_par,
+        d_norm_gain_term,
+        d_ffn_gain_term,
         column_back,
     )
     ffn_grads = [spread[kind, :, :hidden_units].astype(f32) for kind in range(3)]
-    d_gate_pair = gate_blocks(scattered[None, 3 * depth :], heads, size)
+    d_gate_pair = scattered[3 * depth :].reshape(2, part, heads, size).transpose(0, 2, 1, 3)
     return (
         block_out,
         d_inputs,

time: 960 us -> 841 us (0.88)
  matrix products: 87.8 us -> 0 us
  local copies, waits for them, and re-layouts: 55.4 us -> 26.3 us
  Pallas kernels: 752 us -> 780 us
  other arithmetic: 42.9 us -> 25.6 us
    dot_general x15 -> x0, matrix products: 87.8 us -> none  [the longest x3 21 us: shards(): jnp.einsum('td,tf->df', left, right, preferred_element_type=f32)]
    pallas_call x3 -> x2, Pallas kernels: 246 us -> 311 us  [the longest x1 247 us: feed_forward(): pl.pallas_call(functools.partial(ffn_body, n), out_shape=(jax.ShapeDtypeS...]
    pallas_call x1, Pallas kernels: 235 us -> 184 us  [gather_weights(): pl.pallas_call(functools.partial(gather_body, n), out_shape=tuple(made),...]
    pallas_call x1, Pallas kernels: 56.8 us -> 70 us  [mixer_backward(): pl.pallas_call(functools.partial(backward_body, n), out_shape=(jax.ShapeD...]
  transfers between devices with their start and end apart: 5 -> 2, of which waited for: 0 -> 0; matrix products, arithmetic and copies ran while one was open for 5% -> 3% of each run, Pallas kernels for 23% -> 26%
where the time goes in v4:
time: 841 us; the launch traced here: 833 us
  Pallas kernels  780 us (93%)
  local copies, waits for them, and re-layouts  26.3 us (3%)
  other arithmetic  25.6 us (3%)
    pallas_call x1, Pallas kernels, feed_forward(): pl.pallas_call(functools.partial(ffn_body, n), out_shape=(jax.ShapeDtypeS...  247 us
    pallas_call x1, Pallas kernels, scatter_mixer(): pl.pallas_call(functools.partial(scatter_body, n), out_shape=(jax.ShapeDt...  215 us
    pallas_call x1, Pallas kernels, gather_weights(): pl.pallas_call(functools.partial(gather_body, n), out_shape=tuple(made),...  184 us
    pallas_call x1, Pallas kernels, mixer_backward(): pl.pallas_call(functools.partial(backward_body, n), out_shape=(jax.ShapeD...  70 us
    pallas_call x1, Pallas kernels, mixer_forward(): pl.pallas_call(functools.partial(forward_body, n), out_shape=(low, whole,...  64.1 us
  transfers between devices with their start and end apart: 2, of which 0 were waited for; matrix products, arithmetic and copies ran while one was open for 3% of the time, Pallas kernels for 26%

profile of v4, /device:TPU:25, one launch (start us, length us, event | category | flops | bytes accessed | tf_op | source)
XLA Modules:
  0.0 833.3 jit_solution(7932047153982896468)
XLA Ops:
  1.6 1.7 fusion.5
  3.3 1.3 broadcast_in_dim.8.gain_ref
  4.6 2.8 fusion.7.one_ref
  8.0 2.4 constant_dynamic-slice_fusion
  12.0 183.7 %gather_weights.1 = (bf16[16,160,1280]{2,1,0:T(8,128)(2,1)S(1)}, bf16[16,160,1280]{2,1,0:T(8,128)(2,1)S(1)}, bf16[16,160,1280]{2,1,0:T(8,128)(2,1)S(1)}, bf16[2,...) custom-call(bf16[160,1280]{1,0:T(8,128)(2,1)S(1)} %copy-done.5, bf16[160,1280]{1,0:T(8,128)(2,1)S(1)} %copy-done.6, ...), custom_call_target="tpu_custom_call" | custom-call | tf_op jit(solution)/shard_map/gather_weights/pallas_call | solution.py:263
  195.7 2.8 copy-done
  198.5 2.7 copy-done.1
  201.1 2.8 copy-done.2
  203.9 1.9 copy-done.3
  205.8 1.1 copy-done.4
  206.9 64.1 %mixer_forward.1 = (bf16[256,1280]{1,0:T(8,128)(2,1)}, f32[256,1280]{1,0:T(8,128)}, bf16[256,1280]{1,0:T(8,128)(2,1)}, f32[256,1280]{1,0:T(8,128)}, bf16[256,128...) custom-call(bf16[256,2560]{1,0:T(8,128)(2,1)} %fusion.7.one_ref, ...), custom_call_target="tpu_custom_call" | custom-call | tf_op jit(solution)/shard_map/mixer_forward/pallas_call | solution.py:1183
  270.9 247.3 %feed_forward.1 = (bf16[128,2560]{1,0:T(8,128)(2,1)}, f32[128,2560]{1,0:T(8,128)}, bf16[2,128,2560]{2,1,0:T(8,128)(2,1)}, f32[1,2560]{1,0:T(1,128)}, bf16[2,3,2,...) custom-call(bf16[128,2560]{1,0:T(8,128)(2,1)} %get-tuple-element.49.refs, ...), custom_call_target="tpu_custom_call" | custom-call | tf_op jit(solution)/shard_map/feed_forward/pallas_call | solution.py:1914
  518.3 70.0 %mixer_backward.1 = (bf16[256,1280]{1,0:T(8,128)(2,1)}, bf16[256,1280]{1,0:T(8,128)(2,1)}, bf16[16,2,16,1280]{3,2,1,0:T(8,128)(2,1)}, f32[8,1280]{1,0:T(8,128)},...) custom-call(bf16[256,2560]{1,0:T(8,128)(2,1)} %bitcast.50, ...), custom_call_target="tpu_custom_call" | custom-call | tf_op jit(solution)/shard_map/mixer_backward/pallas_call | solution.py:1471
  589.7 1.4 copy.30
  591.1 1.4 copy.29
  592.5 5.3 fusion.8
  597.8 2.2 pad_maximum_fusion.column_ref
  600.1 214.5 %scatter_mixer.1 = (f32[512,1280]{1,0:T(8,128)}, f32[16,1280]{1,0:T(8,128)}, bf16[3,160,4096]{2,1,0:T(8,128)(2,1)}) custom-call(bf16[16,160,256]{2,1,0:T(8,128)(2,1)} %bitcast.53, bf16[16,160,256]{2,1,0:T(8,128)(2,1)} %bitcast.52, bf16[256,1280]{1,0:T(8,128)(2,1)} %get-tuple-element.63.dy_ref, bf16[256,1280]{1,0:T(8,128)(2,1)} %get-tuple-element.64.dxb_ref, ...), custom_call_target="tpu_custom_call" | custom-call | tf_op jit(solution)/shard_map/scatter_mixer/pallas_call | solution.py:902
  814.6 3.1 slice_bitcast_fusion
  818.7 5.3 convert_bitcast_fusion
  827.2 1.5 broadcast_select_fusion.3
  828.7 1.1 pad_maximum_fusion.2
  829.9 1.5 broadcast_select_fusion.1
  831.4 1.7 pad_maximum_fusion.1
  (59 shorter events, 8.6 us)
Async XLA Ops:
  0.6 7.4 copy-start.8
  0.7 6.8 copy-start.20
  4.6 5.8 copy-start.18
  4.6 5.8 copy-start.19
  4.6 5.9 copy-start.12
  8.0 2.5 copy-start.13
  8.0 2.5 copy-start.14
  10.5 0.8 copy-start.16
  10.5 1.5 copy-start.5
  10.5 1.5 copy-start.6
  10.6 1.5 copy-start.7
  195.7 2.8 copy-start
  198.5 2.7 copy-start.1
  201.1 2.8 copy-start.2
  203.9 1.9 copy-start.3
  205.8 1.1 copy-start.4
  518.3 70.7 %copy-start.9 = (bf16[256,2560]{1,0:T(8,128)(2,1)S(1)}, bf16[256,2560]{1,0:T(8,128)(2,1)}, u32[]{:S(2)}) copy-start(bf16[256,2560]{1,0:T(8,128)(2,1)} %param.13) | copy-start | bytes 3932164
  518.3 70.7 %copy-start.15 = (f32[2560]{0:T(1024)S(1)}, f32[2560]{0:T(1024)}, u32[]{:S(2)}) copy-start(f32[2560]{0:T(1024)} %param.14) | copy-start | bytes 30724
  588.4 1.3 copy-start.10
  588.4 241.5 %collective-permute-start.1 = (f32[128,2560]{1,0:T(8,128)}, f32[128,2560]{1,0:T(8,128)}, u32[]{:S(2)}, u32[]{:S(2)}) collective-permute-start(f32[128,2560]{1,0:T(8,128)} %get-tuple-element.62), channel_id=1, source_target_pairs={{0,1},{1,0},{2,3},{3,2},{4,5},{5,4},{6,7},{7,6},{8,9},{9,8},{10,11... | collective-permute-start | bytes 3932168 | tf_op jit(solution)/shard_map/ppermute | solution.py:20
  588.4 238.8 %collective-permute-start = (bf16[128,2560]{1,0:T(8,128)(2,1)}, bf16[128,2560]{1,0:T(8,128)(2,1)}, u32[]{:S(2)}, u32[]{:S(2)}) collective-permute-start(bf16[128,2560]{1,0:T(8,128)(2,1)} %get-tuple-element.53), channel_id=1, source_target_pairs={{0,1},{1,0},{2,3},{3,2},{4,5},{5,4},{6,7},{7,6},{8,9},{9,8},{10,11... | collective-permute-start | bytes 1966088 | tf_op jit(solution)/shard_map/ppermute | solution.py:20
  818.7 5.3 copy-start.17
  827.2 2.6 copy-start.11

commit v5 on v4

--- a/solution.py
+++ b/solution.py
@@ -263,8 +263,8 @@
     return pl.pallas_call(
         functools.partial(gather_body, n),
         out_shape=tuple(made),
-        in_specs=[ANY] * 5,
-        out_specs=(ANY,) * 5,
+        in_specs=[HBM] * 5,
+        out_specs=(HBM,) * 5,
         scratch_shapes=[
             dma((4, 2, n, 4)),
             dma((4, 2, n)),
@@ -275,6 +275,20 @@
         compiler_params=params(1, 16),
         name="gather_weights",
     )(*weights, gates, ffn)
+
+
+def far_first(groups, outer, turn):
+    def order(at):
+        alone = groups - 1 - 2 * at
+        later = turn - alone
+        step = later // 2
+        return jnp.where(
+            turn < alone, groups - 1 - turn, jnp.where(later - 2 * step == 0, step, 2 * at - step)
+        )
+
+    return jnp.where(
+        outer < groups // 2, order(outer), groups - 1 - order(groups - 1 - outer)
+    )
 
 
 class Chain:
@@ -675,7 +689,7 @@
     half = width // 2
 
     def place_of(turn):
-        return lax.rem(outer + 1 + turn, groups)
+        return far_first(groups, outer, turn)
 
     def base_of(turn):
         return (place_of(turn) - outer) * INNER
@@ -705,7 +719,7 @@
         return pl.ds(pl.multiple_of(place * units, units), units)
 
     def exchange(turn, receive=False):
-        place = lax.rem(outer + groups - 1 - turn, groups) if receive else place_of(turn)
+        place = lax.rem(outer + (groups - 1 - turn if receive else turn + 1), groups)
         return remote(
             column_ref.at[:, place],
             spread_ref.at[:, :, units_of(place if receive else outer)],
@@ -761,14 +775,36 @@
         )
 
     def along_z(turn, h):
-        target = me + base_of(turn)
+        place = place_of(turn)
+        up = place > outer
+        onto = jnp.where(up, outer + 1, outer - 1)
+        slot = jnp.where(jnp.logical_and(place == onto, jnp.logical_not(up)), groups, place)
         return remote(
-            made.at[target, :, cols(h)],
-            got_z.at[h, turn],
+            made.at[me + base_of(turn), :, cols(h)],
+            got_z.at[h, slot],
             send_z.at[h, turn],
-            recv_z.at[h, turn],
-            target,
-        )
+            recv_z.at[h, slot],
+            me + (onto - outer) * INNER,
+        )
+
+    def landed(slot, h):
+        return remote(
+            made.at[me, :, cols(h)], got_z.at[h, slot], send_z.at[h, 0], recv_z.at[h, slot], by_x
+        )
+
+    def has_incoming(turn):
+        return jnp.where(place_of(turn) > outer, outer > 0, outer < groups - 1)
+
+    def pass_on(turn):
+        incoming = has_incoming(turn)
+        for h in range(2):
+
+            @pl.when(incoming)
+            def _():
+                landed(place_of(turn), h).wait_recv()
+                add(me + base_of(turn), h, got_z, (h, place_of(turn)))
+
+            along_z(turn, h).start()
 
     def make(block):
         left = one_ref[block]
@@ -804,43 +840,56 @@
     )
     keep.start()
 
+    def begin(turn, other):
+        base = base_of(turn)
+        if other:
+            make(by_xy + base)
+        else:
+            for h in range(2):
+                make(flips[h][1] + base)
+        for h in range(2):
+            along_q(turn, h, other).start()
+
+    begin(0, 1)
+    begin(0, 0)
+    make(me + base_of(0))
+
     def turn_of(turn, carry):
         pl.when(turn <= len(masks))(lambda: small(turn).start())
+        pl.when(turn < groups - 1)(lambda: exchange(turn).start())
 
         @pl.when(turn < groups)
         def _():
             base = base_of(turn)
             for h in range(2):
-                make(flips[h][1] + base)
-            make(by_xy + base)
+                along_q(turn, h, 1).wait_recv()
+                add(flips[h][0] + base, h, got_q, (h, turn, 1))
+                along_p(turn, h).start()
+            pl.when(turn < groups - 1)(lambda: begin(turn + 1, 1))
             for h in range(2):
-                for other in range(2):
-                    along_q(turn, h, other).start()
-            pl.when(turn < groups - 1)(lambda: exchange(turn).start())
-            make(me + base)
-
-        @pl.when(jnp.logical_and(turn >= 1, turn <= groups))
-        def _():
-            now = turn - 1
-            base = base_of(now)
+                along_q(turn, h, 0).wait_recv()
+                add(me + base, h, got_q, (h, turn, 0))
+
+            @pl.when(turn < groups - 1)
+            def _():
+                begin(turn + 1, 0)
+                make(me + base_of(turn + 1))
+
             for h in range(2):
-                along_q(now, h, 1).wait_recv()
-                add(flips[h][0] + base, h, got_q, (h, now, 1))
-                along_p(now, h).start()
-            for h in range(2):
-                along_q(now, h, 0).wait_recv()
-                add(me + base, h, got_q, (h, now, 0))
-
-        @pl.when(turn >= 2)
-        def _():
-            now = turn - 2
-            for h in range(2):
-                along_p(now, h).wait_recv()
-                add(me + base_of(now), h, got_p, (h, now))
-
-                @pl.when(now < groups - 1)
-                def _():
-                    along_z(now, h).start()
+                along_p(turn, h).wait_recv()
+                add(me + base, h, got_p, (h, turn))
+
+            @pl.when(jnp.logical_and(turn < groups - 1, jnp.logical_not(has_incoming(turn))))
+            def _():
+                pass_on(turn)
+
+            @pl.when(jnp.logical_and(turn >= 1, turn < groups - 1))
+            def _():
+                pl.when(has_incoming(turn - 1))(lambda: pass_on(turn - 1))
+
+            @pl.when(jnp.logical_and(turn == groups - 2, has_incoming(turn)))
+            def _():
+                pass_on(turn)
 
         @pl.when(turn <= len(masks))
         def _():
@@ -852,23 +901,27 @@
 
     assert len(masks) < groups + 2
     lax.fori_loop(0, groups + 2, turn_of, 0)
-    for h in range(2):
-
-        def landed(turn, carry):
-            along_z(turn, h).wait_recv()
-            return carry
-
-        lax.fori_loop(0, groups - 1, landed, 0)
-
-        def finish(at, carry):
-            r = pl.ds(pl.multiple_of(at * step, step), step)
-            value = made[me, r, cols(h)].astype(F32)
-            for turn in range(groups - 1):
-                value = value + got_z[h, turn, r].astype(F32)
-            out_ref[r, cols(h)] = value
-            return carry
-
-        lax.fori_loop(0, total // step, finish, 0)
+    for condition, slots in (
+        (jnp.logical_and(outer > 0, outer < groups - 1), (outer, groups)),
+        (outer == groups - 1, (outer,)),
+        (outer == 0, (groups,)),
+    ):
+
+        @pl.when(condition)
+        def _(slots=slots):
+            for h in range(2):
+                for slot in slots:
+                    landed(slot, h).wait_recv()
+
+                def finish(at, carry):
+                    r = pl.ds(pl.multiple_of(at * step, step), step)
+                    value = made[me, r, cols(h)].astype(F32)
+                    for slot in slots:
+                        value = value + got_z[h, slot, r].astype(F32)
+                    out_ref[r, cols(h)] = value
+                    return carry
+
+                lax.fori_loop(0, total // step, finish, 0)
 
     def clear(turn, carry):
         for h in range(2):
@@ -912,14 +965,14 @@
             pltpu.VMEM((n, total, width), BF16),
             pltpu.VMEM((2, groups, 2, total, width // 2), BF16),
             pltpu.VMEM((2, groups, total, width // 2), BF16),
-            pltpu.VMEM((2, groups, total, width // 2), BF16),
+            pltpu.VMEM((2, groups + 1, total, width // 2), BF16),
             pltpu.VMEM((turns, 16, width), F32),
             dma((2, groups, 2)),
             dma((2, groups, 2)),
             dma((2, groups)),
             dma((2, groups)),
             dma((2, groups)),
-            dma((2, groups)),
+            dma((2, groups + 1)),
             dma((turns,)),
             dma((turns,)),
             dma((groups,)),
@@ -972,7 +1025,6 @@
     x_ref,
     gain_ref,
     column_ref,
-    cot_ref,
     xb_ref,
     yp_ref,
     conv_ref,
@@ -982,7 +1034,6 @@
     resid_ref,
     two_ref,
     near_ref,
-    cots_ref,
     w_in,
     w_branch,
     w_out,
@@ -995,7 +1046,7 @@
     theirs,
     *sems,
 ):
-    send_tail, recv_tail, send_tot, recv_tot, send_f, recv_f, here, send_m, recv_m, loaded = sems[:10]
+    send_tail, recv_tail, send_tot, recv_tot, send_f, recv_f, send_m, recv_m, loaded = sems
     tokens, width = xb_ref.shape
     model = one_ref.shape[1]
     me = lax.axis_index("seq")
@@ -1028,16 +1079,11 @@
         ]
         for kind in range(kinds)
     ]
-    chain = Chain(n, cot_ref, cots_ref, *sems[10:])
-    keep = chain.keep(here)
 
     def host(kind):
         for copy in hosted[kind]:
             copy.start()
 
-    host(0)
-    chain.start()
-    keep.start()
     loads[0].wait()
     for start in range(0, width, size):
         cols = slice(start, start + size)
@@ -1045,6 +1091,7 @@
             one_ref[...], w_in[:, cols], preferred_element_type=F32
         ).astype(BF16)
     pl.when(me + 1 < n)(tail_copy.start)
+    host(0)
     wide[8:] = xb_ref[...].astype(F32)
     loads[1].wait()
     for start in range(0, width, size):
@@ -1104,7 +1151,8 @@
         return carry
 
     lax.fori_loop(me + 1, n, tell, 0)
-    host(1)
+    for kind in range(1, kinds):
+        host(kind)
 
     def hear(place, state):
         heard(place).wait_recv()
@@ -1112,9 +1160,6 @@
 
     carry_in = lax.fori_loop(0, me, hear, zeros)
     edge_ref[8:] = jnp.broadcast_to(carry_in, (8, width))
-    for kind in range(2, kinds):
-        host(kind)
-    chain.step(1)
 
     def finish(at, carry):
         r = pl.ds(pl.multiple_of(at * 16, 16), 16)
@@ -1162,16 +1207,12 @@
 
     lax.fori_loop(0, half // 16, norm, 0)
     exchange.wait_send()
-    for step in range(2, n // INNER):
-        chain.step(step)
     for pair in hosted:
         for copy in pair:
             copy.wait()
-    chain.finish()
-    keep.wait()
-
-
-def mixer_forward(one, weights, gates, par, x_half, gain, column, cotangent):
+
+
+def mixer_forward(one, weights, gates, par, x_half, gain, column):
     n = lax.axis_size("seq")
     tokens, model = one.shape
     width = par.shape[1]
@@ -1192,10 +1233,9 @@
             jax.ShapeDtypeStruct((half, model), F32),
             jax.ShapeDtypeStruct((half, model), BF16),
             jax.ShapeDtypeStruct((2, kinds, groups // 2, rows, units), column.dtype),
-            jax.ShapeDtypeStruct((groups, 2) + cotangent.shape, cotangent.dtype),
         ),
-        in_specs=[VMEM] + [HBM] * 3 + [VMEM] * 4 + [HBM, HBM],
-        out_specs=(VMEM,) * 8 + (ANY, ANY),
+        in_specs=[VMEM] + [HBM] * 3 + [VMEM] * 4 + [HBM],
+        out_specs=(VMEM,) * 8 + (HBM,),
         scratch_shapes=[
             pltpu.VMEM((model, width), BF16),
             pltpu.VMEM((model, width), BF16),
@@ -1215,13 +1255,11 @@
             dma((kinds, 2)),
             dma(()),
             dma(()),
-            dma(()),
             dma((3,)),
-            *chain_semaphores(groups),
         ],
         compiler_params=params(4, 60),
         name="mixer_forward",
-    )(one, *weights, gates, par, x_half, gain, column, cotangent)
+    )(one, *weights, gates, par, x_half, gain, column)
 
 
 def backward_body(
@@ -1265,7 +1303,7 @@
     head_rows,
     *sems,
 ):
-    send_rows, recv_rows, send_tot, recv_tot, send_f, recv_f, send_m, recv_m, loaded = sems
+    send_rows, recv_rows, send_tot, recv_tot, send_f, recv_f, send_m, recv_m, send_x, recv_x, loaded = sems
     tokens, width = xb_ref.shape
     model = gain_ref.shape[1]
     me = lax.axis_index("seq")
@@ -1280,12 +1318,26 @@
         load.start()
     greet_all(n, me, True)
     _, _, by_x, by_y, _ = whereabouts()
+    kinds = half_ref.shape[1]
     hosted = [
-        remote(half_ref.at[h], near_ref.at[h], send_f.at[h], recv_f.at[h], (by_x, by_y)[h])
-        for h in range(2)
+        [
+            remote(
+                half_ref.at[h, kind],
+                near_ref.at[h, kind],
+                send_f.at[kind, h],
+                recv_f.at[kind, h],
+                (by_x, by_y)[h],
+            )
+            for h in range(2)
+        ]
+        for kind in range(kinds)
     ]
-    for copy in hosted:
-        copy.start()
+
+    def host(kind):
+        for copy in hosted[kind]:
+            copy.start()
+
+    host(0)
     first = first_row(tokens)
     fade[tokens:] = jnp.ones((8, width), F32)
     loads[0].wait()
@@ -1333,6 +1385,7 @@
         return carry
 
     lax.fori_loop(0, me, tell, 0)
+    host(1)
 
     def hear(turn, state):
         place = n - 1 - turn
@@ -1393,6 +1446,8 @@
         dconv.at[pl.ds(0, 8)], head_rows, send_rows, recv_rows, lax.rem(me + n - 1, n)
     )
     pl.when(me > 0)(rows_copy.start)
+    for kind in range(2, kinds):
+        host(kind)
 
     @pl.when(me + 1 < n)
     def _():
@@ -1447,13 +1502,32 @@
         grad = d_one[core, r].astype(F32) + d_one_got[r].astype(F32)
         back = grad * gain_ref[...]
         shrink = scale * scale * scale * jnp.mean(x * back, axis=-1, keepdims=True)
-        dx_ref[r] = resid_ref[r] + (scale * back - x * shrink)
+        dx_ref[core, r] = resid_ref[r] + (scale * back - x * shrink)
         return total + jnp.sum(grad * (x * scale), axis=0, keepdims=True)
 
     dgain_ref[...] = lax.fori_loop(0, half // 16, norm, jnp.zeros((1, model), F32))
+    share = pltpu.make_async_remote_copy(
+        src_ref=dx_ref.at[core],
+        dst_ref=dx_ref.at[core],
+        send_sem=send_x,
+        recv_sem=recv_x,
+        device_id={"ch": 1 - core},
+        device_id_type=MESH,
+    )
+    share.start()
     exchange.wait_send()
-    for copy in hosted:
-        copy.wait()
+    for pair in hosted:
+        for copy in pair:
+            copy.wait()
+    pltpu.make_async_remote_copy(
+        src_ref=dx_ref.at[core],
+        dst_ref=dx_ref.at[1 - core],
+        send_sem=send_x,
+        recv_sem=recv_x,
+        device_id={"ch": 1 - core},
+        device_id_type=MESH,
+    ).wait_recv()
+    share.wait_send()
 
 
 def mixer_backward(
@@ -1475,12 +1549,12 @@
             jax.ShapeDtypeStruct((tokens, width), BF16),
             jax.ShapeDtypeStruct((n, 2, size // n, width), BF16),
             jax.ShapeDtypeStruct((8, width), F32),
-            jax.ShapeDtypeStruct((half, model), F32),
+            jax.ShapeDtypeStruct((2, half, model), F32),
             jax.ShapeDtypeStruct((1, model), F32),
             jax.ShapeDtypeStruct(halves.shape, BF16),
         ),
         in_specs=[VMEM] + [HBM] * 3 + [VMEM] * 10 + [HBM],
-        out_specs=(VMEM,) * 6 + (ANY,),
+        out_specs=(VMEM,) * 6 + (HBM,),
         scratch_shapes=[
             weight,
             weight,
@@ -1501,8 +1575,10 @@
             dma(()),
             dma((n,)),
             dma((n,)),
-            dma((2,)),
-            dma((2,)),
+            dma((halves.shape[1], 2)),
+            dma((halves.shape[1], 2)),
+            dma(()),
+            dma(()),
             dma(()),
             dma(()),
             dma((3,)),
@@ -1513,11 +1589,12 @@
 
 
 def ffn_body(n, *refs):
-    own_ref, column_ref, near_ref, cots_ref, resid_ref, gain_ref = refs[:6]
+    own_ref, cot_ref, column_ref, near_ref, resid_ref, gain_ref = refs[:6]
     block_ref, d_resid_ref, mixed_ref, d_gain_ref, halves_ref, mine_ref, far_ref = refs[6:13]
     tokens, cots, w, hidden, box, sib, got, d_hidden, stage, turned = refs[13:23]
-    send_t, recv_z, recv_c, send_w, recv_w, keep_w, keep_c, keep_t = refs[23:31]
-    send_c, recv_s, send_z, recv_r, send_f, recv_f, send_m, recv_m, move, out_sem = refs[31:]
+    token_sems, cot_sems = refs[23:26], refs[26:29]
+    send_w, recv_w, keep_w, keep_c, keep_t = refs[29:34]
+    send_c, recv_s, send_z, recv_r, send_f, recv_f, send_m, recv_m, move, out_sem = refs[34:]
     groups = n // INNER
     half = groups // 2
     me, outer, by_x, by_y, by_xy = whereabouts()
@@ -1547,7 +1624,8 @@
         return pl.ds(h * half, half)
 
 
-    chain = Chain(n, own_ref, tokens, send_t, recv_z, recv_c)
+    chain_t = Chain(n, own_ref, tokens, *token_sems)
+    chain_c = Chain(n, cot_ref, cots, *cot_sems)
 
     def weight_copy(kind, h, far, receive=False):
         source = flips[h][0] if far else me
@@ -1578,22 +1656,22 @@
         for kind in range(3)
     ]
     every = [(h, far) for far in range(2) for h in range(2)]
-    load_c = pltpu.make_async_copy(cots_ref, cots, keep_c)
-    own = chain.keep(keep_t)
-    chain.start()
+    own_t, own_c = chain_t.keep(keep_t), chain_c.keep(keep_c)
+    chain_c.start()
     for kind in (2, 0, 1):
         for h, far in every:
             weight_copy(kind, h, far).start()
-    load_c.start()
-    own.start()
+    own_c.start()
+    own_t.start()
     for kind in (2, 0, 1):
         for copy in keep[kind]:
             copy.start()
-    for step in range(1, groups):
-        chain.step(step)
-    chain.finish()
-    own.wait()
-    load_c.wait()
+    for step in range(1, groups - 1):
+        chain_c.step(step)
+    chain_t.start()
+    chain_c.step(groups - 1)
+    chain_c.finish()
+    own_c.wait()
 
     def weights_landed(kind):
         for h, far in every:
@@ -1624,6 +1702,10 @@
             )
 
     each(groups, back_hidden)
+    for step in range(1, groups):
+        chain_t.step(step)
+    chain_t.finish()
+    own_t.wait()
     weights_landed(0)
     weights_landed(1)
 
@@ -1645,6 +1727,8 @@
         for h, far in every:
             weight_copy(kind, h, far).wait_send()
 
+
+    boxes = (box, tokens)
 
     def partial(kind, place):
         r = token_rows(place)
@@ -1659,13 +1743,13 @@
                     preferred_element_type=F32,
                 )
             value = value.astype(BF16)
-            box[place, 0, :, at * deep : (at + 1) * deep] = value[:tall]
-            box[place, 1, :, at * deep : (at + 1) * deep] = value[tall:]
+            boxes[kind][place, 0, :, at * deep : (at + 1) * deep] = value[:tall]
+            boxes[kind][place, 1, :, at * deep : (at + 1) * deep] = value[tall:]
         to_sibling(kind, place).start()
 
     def to_sibling(kind, place):
         return pltpu.make_async_remote_copy(
-            src_ref=box.at[place, 1 - core],
+            src_ref=boxes[kind].at[place, 1 - core],
             dst_ref=sib.at[kind, place],
             send_sem=send_c.at[kind, place],
             recv_sem=recv_s.at[kind, place],
@@ -1677,7 +1761,7 @@
         last = place == (outer + 1 if up else outer - 1)
         slot = place if up else jnp.where(last, groups, place)
         return remote(
-            box.at[place, core],
+            boxes[kind].at[place, core],
             got.at[kind, slot],
             send_z.at[kind, place],
             recv_r.at[kind, slot],
@@ -1699,10 +1783,10 @@
 
         def add(at, with_got):
             r = rows_of(at)
-            value = box[place, core, r].astype(F32) + sib[kind, place, r].astype(F32)
+            value = boxes[kind][place, core, r].astype(F32) + sib[kind, place, r].astype(F32)
             if with_got:
                 value = value + got[kind, place, r].astype(F32)
-            box[place, core, r] = value.astype(BF16)
+            boxes[kind][place, core, r] = value.astype(BF16)
 
         @pl.when(incoming)
         def _():
@@ -1713,33 +1797,40 @@
         def _():
             each(tall // chunk, lambda at: add(at, False))
 
-    def climb(kind, turn):
-        place = groups - 1 - turn
-
-        @pl.when(place > outer)
+    def pass_on(kind, turn):
+        ups = groups - 1 - outer
+        upper = jnp.where(outer < half, turn < ups, turn >= outer)
+        later = jnp.where(outer < half, turn, turn - outer)
+        earlier = jnp.where(outer < half, turn - ups, turn)
+
+        @pl.when(upper)
         def _():
+            place = groups - 1 - later
             ready(kind, place, below)
             along(kind, place, True).start()
 
-    def sink(kind, turn):
-        @pl.when(turn < outer)
+        @pl.when(jnp.logical_not(upper))
         def _():
-            ready(kind, turn, above)
-            along(kind, turn, False).start()
-
-    def pass_on(kind):
-        def turns(turn):
-            @pl.when(outer < half)
+            ready(kind, earlier, above)
+            along(kind, earlier, False).start()
+
+    at_end = jnp.logical_or(outer == 0, outer == groups - 1)
+
+    def partials(kind):
+        def one(turn):
+            partial(kind, far_first(groups, outer, turn))
+
+            @pl.when(jnp.logical_and(at_end, turn >= 1))
             def _():
-                climb(kind, turn)
-                sink(kind, turn)
-
-            @pl.when(outer >= half)
-            def _():
-                sink(kind, turn)
-                climb(kind, turn)
-
-        each(groups - 1, turns)
+                pass_on(kind, turn - 1)
+
+        each(groups, one)
+
+    def between(kind, turns):
+        @pl.when(jnp.logical_not(at_end))
+        def _():
+            for turn in turns:
+                pass_on(kind, turn)
 
     def totals(kind, use):
         to_sibling(kind, outer).wait_recv()
@@ -1756,7 +1847,7 @@
 
                 def one(at):
                     r = rows_of(at)
-                    value = box[outer, core, r].astype(F32) + sib[kind, outer, r].astype(F32)
+                    value = boxes[kind][outer, core, r].astype(F32) + sib[kind, outer, r].astype(F32)
                     for slot in slots:
                         value = value + got[kind, slot, r].astype(F32)
                     use(r, value)
@@ -1788,24 +1879,21 @@
             flips[h][1],
         )
 
-    def gradients(kinds, source):
-        for h in range(2):
-            for at in range(h * half, (h + 1) * half):
-                left = source[:, :, :, at * deep : (at + 1) * deep].reshape(groups * count, deep)
-                turned[...] = left.T
-                for kind, right in kinds:
-                    for start in range(0, units, tile):
-                        c = slice(start, start + tile)
-                        w[kind, at, :, :, c] = (
-                            jnp.dot(
-                                turned[...], hidden[right, :, c], preferred_element_type=F32
-                            )
-                            .astype(BF16)
-                            .reshape(INNER, rows, tile)
-                        )
-            for kind, _ in kinds:
-                for far in (1, 0):
-                    gradient_copy(kind, h, far).start()
+    def gradients(kinds, source, h):
+        for at in range(h * half, (h + 1) * half):
+            left = source[:, :, :, at * deep : (at + 1) * deep].reshape(groups * count, deep)
+            turned[...] = left.T
+            for kind, right in kinds:
+                for start in range(0, units, tile):
+                    c = slice(start, start + tile)
+                    w[kind, at, :, :, c] = (
+                        jnp.dot(turned[...], hidden[right, :, c], preferred_element_type=F32)
+                        .astype(BF16)
+                        .reshape(INNER, rows, tile)
+                    )
+        for kind, _ in kinds:
+            for far in (1, 0):
+                gradient_copy(kind, h, far).start()
 
     def collect(kind, h, far):
         inner = (flips[h][0] if far else me) - base
@@ -1833,22 +1921,19 @@
             out_sem.at[kind, h, far],
         )
 
-    def in_order(action):
-        @pl.when(outer < half)
-        def _():
-            for turn in range(half):
-                action(groups - 1 - turn)
-                action(turn)
-
-        @pl.when(outer >= half)
-        def _():
-            for turn in range(half):
-                action(turn)
-                action(groups - 1 - turn)
-
-    in_order(lambda place: partial(0, place))
-    gradients(((0, 1), (1, 2)), tokens)
-    pass_on(0)
+    first, second = range(groups // 2), range(groups // 2, groups - 1)
+    pair = ((0, 1), (1, 2))
+    partials(0)
+    gradients(pair, tokens, 0)
+    between(0, first[:1])
+    gradients(pair, tokens, 1)
+    between(0, first[1:])
+    between(0, second)
+    partials(1)
+    gradients(((2, 0),), cots, 0)
+    between(1, first[:1])
+    gradients(((2, 0),), cots, 1)
+    between(1, first[1:])
     d_gain_ref[...] = jnp.zeros((1, model), F32)
 
     def norm(r, grad):
@@ -1862,48 +1947,47 @@
         d_gain_ref[...] = d_gain_ref[...] + jnp.sum(grad * (resid * scale), axis=0, keepdims=True)
 
     totals(0, norm)
-    share = pltpu.make_async_remote_copy(
-        src_ref=mixed_ref.at[core],
-        dst_ref=mixed_ref.at[core],
-        send_sem=send_m,
-        recv_sem=recv_m,
-        device_id=sibling,
-        device_id_type=MESH,
-    )
+
+    def shared(ref, at, part):
+        return pltpu.make_async_remote_copy(
+            src_ref=ref.at[core],
+            dst_ref=ref.at[part],
+            send_sem=send_m.at[at],
+            recv_sem=recv_m.at[at],
+            device_id=sibling,
+            device_id_type=MESH,
+        )
+
+    share = shared(mixed_ref, 0, core)
     share.start()
+    between(1, second)
+    for far in (1, 0):
+        for h in range(2):
+            for kind in range(2):
+                collect(kind, h, far)
+
+    def finish(r, value):
+        block_ref[core, r] = (resid_ref[r] + value).astype(BF16)
+
+    totals(1, finish)
+    show = shared(block_ref, 1, core)
+    show.start()
     clear(0)
-    in_order(lambda place: partial(1, place))
-    gradients(((2, 0),), cots)
-    pass_on(1)
-    for far in (1, 0):
-        for kind in range(2):
-            for h in range(2):
-                collect(kind, h, far)
-
-    def finish(r, value):
-        block_ref[r] = (resid_ref[r] + value).astype(BF16)
-
-    totals(1, finish)
     clear(1)
     for far in (1, 0):
         for h in range(2):
             collect(2, h, far)
-    pltpu.make_async_remote_copy(
-        src_ref=mixed_ref.at[core],
-        dst_ref=mixed_ref.at[1 - core],
-        send_sem=send_m,
-        recv_sem=recv_m,
-        device_id=sibling,
-        device_id_type=MESH,
-    ).wait_recv()
+    shared(mixed_ref, 0, 1 - core).wait_recv()
+    shared(block_ref, 1, 1 - core).wait_recv()
     share.wait_send()
+    show.wait_send()
     for kind in range(3):
         for h, far in every:
             gradient_copy(kind, h, far).wait_send()
             out_copy(kind, h, far).wait()
 
 
-def feed_forward(own, column, near, cots, resid, gain):
+def feed_forward(own, cotangent, column, near, resid, gain):
     n = lax.axis_size("seq")
     groups = n // INNER
     tall, model = own.shape
@@ -1914,7 +1998,7 @@
     return pl.pallas_call(
         functools.partial(ffn_body, n),
         out_shape=(
-            jax.ShapeDtypeStruct((tall, model), BF16),
+            jax.ShapeDtypeStruct((2, tall, model), BF16),
             jax.ShapeDtypeStruct((tall, model), F32),
             jax.ShapeDtypeStruct((2, tall, model), BF16),
             jax.ShapeDtypeStruct((1, model), F32),
@@ -1936,6 +2020,7 @@
             pltpu.VMEM((half, rows, units), BF16),
             pltpu.VMEM((INNER * rows, groups * 2 * tall), BF16),
             *chain_semaphores(groups),
+            *chain_semaphores(groups),
             dma((kinds, 2, 2)),
             dma((kinds, 2, 2)),
             dma((kinds, 3)),
@@ -1947,14 +2032,14 @@
             dma((2, groups + 1)),
             dma((kinds, 2, 2)),
             dma((kinds, 2, 2)),
-            dma(()),
-            dma(()),
+            dma((2,)),
+            dma((2,)),
             dma(()),
             dma((kinds, 2, 2)),
         ],
         compiler_params=params(8, 63),
         name="feed_forward",
-    )(own, column, near, cots, resid, gain)
+    )(own, cotangent, column, near, resid, gain)
 
 
 def my_half(values):
@@ -1968,6 +2053,17 @@
     return jnp.concatenate(
         [jnp.where(core == 0, own, other), jnp.where(core == 0, other, own)], axis=0
     )
+
+
+def tokens_in(own):
+    groups = lax.axis_size("seq") // INNER
+    outer = lax.axis_index("seq") // INNER
+    got = put(jnp.zeros((groups,) + own.shape, own.dtype), own, outer)
+    for step in range(1, groups):
+        got = put(got, swap(own, "seq", step * INNER), outer ^ step)
+    other = swap(got, "ch", 1)
+    first = lax.axis_index("ch") == 0
+    return jnp.stack([jnp.where(first, got, other), jnp.where(first, other, got)], axis=1)
 
 
 def tokens_out(partial, half):
@@ -1984,13 +2080,14 @@
     return total
 
 
-def feed_forward_parts(n_two, column, near, all_cot, resid, ffn_gain, cot_half):
+def feed_forward_parts(n_two, cot_half, column, near, resid, ffn_gain):
     f32, bf16 = F32, BF16
     _, groups, depth, units = column.shape
     half_rows, model = n_two.shape
     tok_rows = 2 * half_rows
     _, norm_back_two = jax.vjp(scaled_norm, resid, ffn_gain)
     all_two, *full_ffn = gather_tokens(n_two, column, near)
+    all_cot = tokens_in(cot_half)
     all_two, all_cot = (v.reshape(groups * tok_rows, model) for v in (all_two, all_cot))
     full_ffn = [w.reshape(model, units) for w in full_ffn]
     gate_pre = jnp.dot(all_two, full_ffn[0], preferred_element_type=f32)
@@ -2017,7 +2114,7 @@
     else:
         d_n_two, far = reduce_tokens(split[:1], terms)
         ffn_out = tokens_out(ffn_term, half_rows)
-    block_half = (resid + ffn_out).astype(bf16)
+    block_out = join((resid + ffn_out).astype(bf16))
     inner = lax.axis_index("seq") % INNER
     by_half = [t.reshape(2, groups // 2, INNER, depth, units) for t in terms]
 
@@ -2033,7 +2130,7 @@
     d_resid_norm, d_ffn_gain_term = norm_back_two(d_n_two)
     d_resid = cot_half.astype(f32) + d_resid_norm
     d_mixed = join(d_resid.astype(bf16))
-    return block_half, d_resid, d_mixed, d_ffn_gain_term.reshape(1, model), halves, mine
+    return block_out, d_resid, d_mixed, d_ffn_gain_term.reshape(1, model), halves, mine
 
 
 def shards(
@@ -2087,7 +2184,7 @@
 
     cot_half = my_half(cotangent)
 
-    x_branch, y_pre, conv_out, states, branch_out, edge, resid, n_two, near, all_cot = mixer_forward(
+    x_branch, y_pre, conv_out, states, branch_out, edge, resid, n_two, near = mixer_forward(
         n_one,
         full_mixer,
         gates,
@@ -2095,18 +2192,17 @@
         x_half,
         ffn_gain.reshape(1, model),
         column,
-        cot_half,
     )
     if groups <= 4 and depth % 16 == 0:
-        block_half, d_resid, d_mixed, d_ffn_gain_term, halves, mine, _ = feed_forward(
-            n_two, column, near, all_cot, resid, ffn_gain.reshape(1, model)
-        )
+        block_out, d_resid, d_mixed, d_ffn_gain_term, halves, mine, _ = feed_forward(
+            n_two, cot_half, column, near, resid, ffn_gain.reshape(1, model)
+        )
+        block_out = block_out.reshape(tok_rows, model)
         d_mixed = d_mixed.reshape(tok_rows, model)
     else:
-        block_half, d_resid, d_mixed, d_ffn_gain_term, halves, mine = feed_forward_parts(
-            n_two, column, near, all_cot, resid, ffn_gain, cot_half
-        )
-    block_out = join(block_half)
+        block_out, d_resid, d_mixed, d_ffn_gain_term, halves, mine = feed_forward_parts(
+            n_two, cot_half, column, near, resid, ffn_gain
+        )
     d_y, d_xb, d_gates, d_par, d_inputs, d_norm_gain_term, near_back = mixer_backward(
         d_mixed,
         full_mixer,
@@ -2128,7 +2224,7 @@
         ],
         axis=1,
     )
-    d_inputs = join(d_inputs)
+    d_inputs = d_inputs.reshape(tok_rows, model)
     gain_rows = model // width
     scattered, small, spread = scatter_mixer(
         n_one.T.reshape(n, depth, tok_rows),

time: 841 us -> 761 us (0.905)
  Pallas kernels: 780 us -> 708 us
  other arithmetic: 25.6 us -> 16.3 us
    pallas_call x1, Pallas kernels: 215 us -> 190 us  [scatter_mixer(): pl.pallas_call(functools.partial(scatter_body, n), out_shape=(jax.ShapeDt...]
    pallas_call x1, Pallas kernels: 247 us -> 224 us  [feed_forward(): pl.pallas_call(functools.partial(ffn_body, n), out_shape=(jax.ShapeDtypeS...]
    pallas_call x1, Pallas kernels: 70 us -> 56.7 us  [mixer_backward(): pl.pallas_call(functools.partial(backward_body, n), out_shape=(jax.ShapeD...]
    pallas_call x1, Pallas kernels: 64.1 us -> 54.6 us  [mixer_forward(): pl.pallas_call(functools.partial(forward_body, n), out_shape=(low, whole,...]
  transfers between devices with their start and end apart: 2 -> 0, of which waited for: 0 -> 0; matrix products, arithmetic and copies ran while one was open for 3% -> 0% of each run, Pallas kernels for 26% -> 0%
where the time goes in v5:
time: 761 us; the launch traced here: 753 us
  Pallas kernels  708 us (93%)
  local copies, waits for them, and re-layouts  26.6 us (3%)
  other arithmetic  16.3 us (2%)
    pallas_call x1, Pallas kernels, feed_forward(): pl.pallas_call(functools.partial(ffn_body, n), out_shape=(jax.ShapeDtypeS...  224 us
    pallas_call x1, Pallas kernels, scatter_mixer(): pl.pallas_call(functools.partial(scatter_body, n), out_shape=(jax.ShapeDt...  190 us
    pallas_call x1, Pallas kernels, gather_weights(): pl.pallas_call(functools.partial(gather_body, n), out_shape=tuple(made),...  184 us
    pallas_call x1, Pallas kernels, mixer_backward(): pl.pallas_call(functools.partial(backward_body, n), out_shape=(jax.ShapeD...  56.7 us
    pallas_call x1, Pallas kernels, mixer_forward(): pl.pallas_call(functools.partial(forward_body, n), out_shape=(low, whole,...  54.6 us
    unnamed x48, local copies, waits for them, and re-layouts  16.5 us

profile of v5, /device:TPU:25, one launch (start us, length us, event | category | flops | bytes accessed | tf_op | source)
XLA Modules:
  0.0 752.8 jit_solution(11013432964551540158)
XLA Ops:
  0.7 2.6 constant_dynamic-slice_fusion
  3.3 1.7 fusion.4.refs_4_
  5.1 183.7 %gather_weights.1 = (bf16[16,160,1280]{2,1,0:T(8,128)(2,1)S(1)}, bf16[16,160,1280]{2,1,0:T(8,128)(2,1)S(1)}, bf16[16,160,1280]{2,1,0:T(8,128)(2,1)S(1)}, bf16[2,...) custom-call(bf16[160,1280]{1,0:T(8,128)(2,1)S(1)} %copy-done.5, bf16[160,1280]{1,0:T(8,128)(2,1)S(1)} %copy-done.6, ...), custom_call_target="tpu_custom_call" | custom-call | tf_op jit(solution)/shard_map/gather_weights/pallas_call | solution.py:263
  188.8 2.8 copy-done
  191.5 2.7 copy-done.1
  194.2 2.8 copy-done.2
  196.9 1.9 copy-done.3
  198.8 1.1 copy-done.4
  200.0 0.7 maximum_maximum_fusion.par_ref
  201.1 1.4 fusion.7.one_ref
  203.1 54.6 %mixer_forward.1 = (bf16[256,1280]{1,0:T(8,128)(2,1)}, f32[256,1280]{1,0:T(8,128)}, bf16[256,1280]{1,0:T(8,128)(2,1)}, f32[256,1280]{1,0:T(8,128)}, bf16[256,128...) custom-call(bf16[256,2560]{1,0:T(8,128)(2,1)} %fusion.7.one_ref, ...), custom_call_target="tpu_custom_call" | custom-call | tf_op jit(solution)/shard_map/mixer_forward/pallas_call | solution.py:1224
  257.7 224.0 %feed_forward.1 = (bf16[2,128,2560]{2,1,0:T(8,128)(2,1)}, f32[128,2560]{1,0:T(8,128)}, bf16[2,128,2560]{2,1,0:T(8,128)(2,1)}, f32[1,2560]{1,0:T(1,128)}, bf16[2,...) custom-call(bf16[128,2560]{1,0:T(8,128)(2,1)} %get-tuple-element.48., ...), custom_call_target="tpu_custom_call" | custom-call | tf_op jit(solution)/shard_map/feed_forward/pallas_call | solution.py:1998
  482.4 56.7 %mixer_backward.1 = (bf16[256,1280]{1,0:T(8,128)(2,1)}, bf16[256,1280]{1,0:T(8,128)(2,1)}, bf16[16,2,16,1280]{3,2,1,0:T(8,128)(2,1)}, f32[8,1280]{1,0:T(8,128)},...) custom-call(bf16[256,2560]{1,0:T(8,128)(2,1)} %bitcast.52, ...), custom_call_target="tpu_custom_call" | custom-call | tf_op jit(solution)/shard_map/mixer_backward/pallas_call | solution.py:1545
  539.1 4.1 fusion.8
  543.2 2.2 pad_maximum_fusion.column_ref
  545.4 1.4 copy.30
  547.2 1.4 copy.29
  548.7 189.5 %scatter_mixer.1 = (f32[512,1280]{1,0:T(8,128)}, f32[16,1280]{1,0:T(8,128)}, bf16[3,160,4096]{2,1,0:T(8,128)(2,1)}) custom-call(bf16[16,160,256]{2,1,0:T(8,128)(2,1)} %bitcast.55, bf16[16,160,256]{2,1,0:T(8,128)(2,1)} %bitcast.54, bf16[256,1280]{1,0:T(8,128)(2,1)} %get-tuple-element.61.dy_ref, bf16[256,1280]{1,0:T(8,128)(2,1)} %get-tuple-element.62.dxb_ref, ...), custom_call_target="tpu_custom_call" | custom-call | tf_op jit(solution)/shard_map/scatter_mixer/pallas_call | solution.py:955
  738.2 5.4 convert_bitcast_fusion
  743.6 1.5 slice_bitcast_fusion
  745.2 0.7 copy.31
  745.9 0.7 copy.32
  748.4 2.5 copy.35
  750.9 1.5 copy.36
  (55 shorter events, 4.1 us)
Async XLA Ops:
  0.6 2.6 copy-start.15
  0.7 2.6 copy-start.14
  3.3 1.7 copy-start.19
  3.3 1.7 copy-start.20
  3.3 1.7 copy-start.5
  3.3 1.7 copy-start.6
  3.3 1.7 copy-start.7
  5.0 194.8 %copy-start.17 = (f32[8,1280]{1,0:T(8,128)S(1)}, f32[8,1280]{1,0:T(8,128)}, u32[]{:S(2)}) copy-start(f32[8,1280]{1,0:T(8,128)} %param.17) | copy-start | bytes 122884
  5.1 195.7 %copy-start.8 = (bf16[256,2560]{1,0:T(8,128)(2,1)S(1)}, bf16[256,2560]{1,0:T(8,128)(2,1)}, u32[]{:S(2)}) copy-start(bf16[256,2560]{1,0:T(8,128)(2,1)} %param.13) | copy-start | bytes 3932164
  5.1 196.0 %copy-start.16 = (f32[2560]{0:T(1024)S(1)}, f32[2560]{0:T(1024)}, u32[]{:S(2)}) copy-start(f32[2560]{0:T(1024)} %param.14) | copy-start | bytes 30724
  188.7 2.8 copy-start
  191.5 2.7 copy-start.1
  194.2 2.8 copy-start.2
  196.9 1.9 copy-start.3
  198.8 1.1 copy-start.4
  199.9 2.6 copy-start.21
  482.4 56.7 %copy-start.11 = (bf16[2,3,2,160,1024]{4,3,2,1,0:T(8,128)(2,1)S(1)}, bf16[2,3,2,160,1024]{4,3,2,1,0:T(8,128)(2,1)}, u32[]{:S(2)}) copy-start(bf16[2,3,2,160,1024]{4,3,2,1,0:T(8,128)(2,1)} %get-tuple-element.68) | copy-start | bytes 11796484
  543.2 2.2 copy-start.10
  545.4 1.4 copy-start.9
  738.2 5.4 copy-start.13
  743.6 2.9 copy-start.18
  745.1 5.7 copy-start.12

commit v6 on v5

--- a/solution.py
+++ b/solution.py
@@ -110,9 +110,9 @@
 
 
 def gather_body(n, *refs):
-    w_refs, g_ref, f_ref = refs[:3], refs[3], refs[4]
-    wo_refs, go_ref, column_ref = refs[5:8], refs[8], refs[9]
-    send_m, recv_m, send_f, recv_f, here = refs[10:]
+    w_refs, g_refs, f_refs, x_ref, gain_ref = refs[:3], refs[3:5], refs[5:8], refs[8], refs[9]
+    wo_refs, go_ref, column_ref, one_ref, turned_ref, last_ref = refs[10:13], *refs[13:18]
+    send_m, recv_m, send_f, recv_f, here, send_l, recv_l = refs[18:]
     groups = n // INNER
     me, outer, by_x, by_y, by_xy = whereabouts()
     above, below = outer + 1 < groups, outer > 0
@@ -132,23 +132,31 @@
         return carry
 
     lax.fori_loop(1, groups, hello_column, 0)
-    pl.semaphore_wait(barrier, groups + 1)
-    units = column_ref.shape[3]
+    pl.when(me + 1 < n)(lambda: hello(me + 1))
+    pl.when(me > 0)(lambda: hello(me - 1))
+    neighbours = (me + 1 < n).astype(jnp.int32) + (me > 0).astype(jnp.int32)
+    pl.semaphore_wait(barrier, groups + 1 + neighbours)
+    units = Units(f_refs[0].shape[1], groups, lax.axis_index("ch"))
     half = w_refs[0].shape[1] // 2
-
-    def units_of(place):
-        return pl.ds(pl.multiple_of(place * units, units), units)
 
     keep = [
         pltpu.make_async_copy(w_refs[kind], wo_refs[kind].at[me], here.at[kind])
         for kind in range(3)
     ]
-    keep.append(pltpu.make_async_copy(g_ref, go_ref.at[:, :, me], here.at[3]))
-    keep.append(
-        pltpu.make_async_copy(
-            f_ref.at[:, :, units_of(outer)], column_ref.at[:, outer], here.at[4]
-        )
-    )
+    for gate in range(2):
+        keep.append(pltpu.make_async_copy(g_refs[gate], go_ref.at[gate, :, me], here.at[3 + gate]))
+    for kind in range(3):
+        keep.append(
+            Sized(
+                units,
+                outer,
+                lambda width, kind=kind: pltpu.make_async_copy(
+                    f_refs[kind].at[:, units.columns(outer, width)],
+                    column_ref.at[kind, outer, :, pl.ds(0, width)],
+                    here.at[5 + kind],
+                ),
+            )
+        )
     for copy in keep:
         copy.start()
     sent = []
@@ -158,7 +166,7 @@
         pairs = [
             (w_refs[kind].at[:, cols], wo_refs[kind].at[source, :, cols]) for kind in range(3)
         ]
-        pairs.append((g_ref.at[h], go_ref.at[h, :, source]))
+        pairs.append((g_refs[h], go_ref.at[h, :, source]))
         return [
             remote(
                 given if own else dst,
@@ -187,14 +195,21 @@
 
     def exchange(turn, receive):
         place = lax.rem(outer + groups - turn, groups) if receive else column_peer(turn)
-        target = me + (place - outer) * INNER
-        return remote(
-            f_ref.at[:, :, units_of(place)],
-            column_ref.at[:, place if receive else outer],
-            send_f.at[turn],
-            recv_f.at[turn],
-            target,
-        )
+        owner = outer if receive else place
+        return [
+            Sized(
+                units,
+                owner,
+                lambda width, kind=kind: remote(
+                    f_refs[kind].at[:, units.columns(owner, width)],
+                    column_ref.at[kind, place if receive else outer, :, pl.ds(0, width)],
+                    send_f.at[kind, turn],
+                    recv_f.at[kind, turn],
+                    me + (place - outer) * INNER,
+                ),
+            )
+            for kind in range(3)
+        ]
 
     def each_turn(action):
         def one(turn, carry):
@@ -203,7 +218,31 @@
 
         lax.fori_loop(1, groups, one, 0)
 
+    tokens, model = x_ref.shape
+    tall = last_ref.shape[0]
+    last_copy = remote(one_ref.at[pl.ds(tokens - tall, tall)], last_ref, send_l, recv_l, me + 1)
+
+    def norm(at, carry):
+        r = pl.ds(pl.multiple_of(at * 16, 16), 16)
+        x = x_ref[r].astype(F32)
+        scale = lax.rsqrt(jnp.mean(x * x, axis=-1, keepdims=True) + 1e-06)
+        one_ref[r] = (x * scale * gain_ref[...]).astype(BF16)
+        return carry
+
+    def norm_all():
+        lax.fori_loop(0, tokens // 16, norm, 0)
+        pl.when(me + 1 < n)(last_copy.start)
+        for start in range(0, model, 256):
+            cols = slice(start, start + 256)
+            turned_ref[cols] = one_ref[:, cols].T
+
+        @pl.when(me == 0)
+        def _():
+            last_ref[...] = jnp.zeros(last_ref.shape, BF16)
+
     for step in range(groups):
+        if step == 1:
+            norm_all()
         for h in range(2):
             flip_p, flip_q = (by_x, by_y) if h == 0 else (by_y, by_x)
             if step == 0:
@@ -220,7 +259,7 @@
                 send(both(there, onward), h, source, way, to, False)
                 send(there, h, source, 2, flip_p, False)
                 send(there, h, source, 3, flip_q, False)
-    each_turn(lambda turn: exchange(turn, False).start())
+    each_turn(lambda turn: [copy.start() for copy in exchange(turn, False)])
     for step in range(groups):
         for h in range(2):
             flip_p, flip_q = (by_x, by_y) if h == 0 else (by_y, by_x)
@@ -239,7 +278,7 @@
         for h in range(2):
             arrive(None, h, (by_y if h == 0 else by_x) + shift)
             arrive(None, h, by_xy + shift)
-    each_turn(lambda turn: exchange(turn, True).wait_recv())
+    each_turn(lambda turn: [copy.wait_recv() for copy in exchange(turn, True)])
     for condition, what in sent:
 
         def finish(what=what):
@@ -247,34 +286,92 @@
                 copy.wait_send()
 
         when(condition, finish)
-    each_turn(lambda turn: exchange(turn, False).wait_send())
+    each_turn(lambda turn: [copy.wait_send() for copy in exchange(turn, False)])
     for copy in keep:
         copy.wait()
-
-
-def gather_weights(weights, gates, ffn):
+    pl.when(me > 0)(last_copy.wait_recv)
+    pl.when(me + 1 < n)(last_copy.wait_send)
+
+
+def gather_weights(weights, gates, ffn, x, gain):
     n = lax.axis_size("seq")
     groups = n // INNER
-    kinds, rows, padded = ffn.shape
+    rows, hidden_units = ffn[0].shape
+    most = Units(hidden_units, groups, 0).most
     dma = pltpu.SemaphoreType.DMA
     made = [jax.ShapeDtypeStruct((n,) + w.shape, w.dtype) for w in weights]
-    made.append(jax.ShapeDtypeStruct(gates.shape[:2] + (n,) + gates.shape[2:], gates.dtype))
-    made.append(jax.ShapeDtypeStruct((kinds, groups, rows, padded // groups), ffn.dtype))
+    heads, part, size = gates[0].shape
+    made.append(jax.ShapeDtypeStruct((2, heads, n, part, size), BF16))
+    made.append(jax.ShapeDtypeStruct((3, groups, rows, most), BF16))
+    made.append(jax.ShapeDtypeStruct(x.shape, BF16))
+    made.append(jax.ShapeDtypeStruct(x.shape[::-1], BF16))
+    made.append(jax.ShapeDtypeStruct((16, x.shape[1]), BF16))
     return pl.pallas_call(
         functools.partial(gather_body, n),
         out_shape=tuple(made),
-        in_specs=[HBM] * 5,
-        out_specs=(HBM,) * 5,
+        in_specs=[HBM] * 8 + [VMEM] * 2,
+        out_specs=(HBM,) * 5 + (VMEM,) * 3,
         scratch_shapes=[
             dma((4, 2, n, 4)),
             dma((4, 2, n)),
-            dma((groups,)),
-            dma((groups,)),
-            dma((5,)),
+            dma((3, groups)),
+            dma((3, groups)),
+            dma((8,)),
+            dma(()),
+            dma(()),
         ],
-        compiler_params=params(1, 16),
+        compiler_params=params(1, 60),
         name="gather_weights",
-    )(*weights, gates, ffn)
+    )(*weights, *gates, *ffn, x, gain)
+
+
+LANES = 128
+
+
+class Units:
+    def __init__(self, total, groups, core):
+        self.tiles, self.groups, self.core = total // LANES, groups, core
+        self.most = -(-self.tiles // groups) * LANES
+        self.even = self.tiles % groups == 0
+
+    def start(self, place):
+        up = (1 - self.core) * (self.groups - 1)
+        return (place * self.tiles + up) // self.groups
+
+    def full(self, place):
+        return (self.start(place + 1) - self.start(place)) * LANES == self.most
+
+    def width(self, place):
+        return (self.start(place + 1) - self.start(place)) * LANES
+
+    def columns(self, place, width):
+        return pl.ds(pl.multiple_of(self.start(place) * LANES, LANES), width)
+
+
+class Sized:
+    def __init__(self, units, place, make):
+        self.units, self.place, self.make = units, place, make
+
+    def each(self, action):
+        most = self.units.most
+        if self.units.even:
+            action(self.make(most))
+            return
+        full = self.units.full(self.place)
+        pl.when(full)(lambda: action(self.make(most)))
+        pl.when(jnp.logical_not(full))(lambda: action(self.make(most - LANES)))
+
+    def start(self):
+        self.each(lambda copy: copy.start())
+
+    def wait(self):
+        self.each(lambda copy: copy.wait())
+
+    def wait_send(self):
+        self.each(lambda copy: copy.wait_send())
+
+    def wait_recv(self):
+        self.each(lambda copy: copy.wait_recv())
 
 
 def far_first(groups, outer, turn):
@@ -713,19 +810,21 @@
     pl.semaphore_wait(barrier, groups + 2)
 
     flips = ((by_x, by_y), (by_y, by_x))
-    units = column_ref.shape[3]
-
-    def units_of(place):
-        return pl.ds(pl.multiple_of(place * units, units), units)
+    units = Units(spread_ref.shape[2], groups, core)
 
     def exchange(turn, receive=False):
         place = lax.rem(outer + (groups - 1 - turn if receive else turn + 1), groups)
-        return remote(
-            column_ref.at[:, place],
-            spread_ref.at[:, :, units_of(place if receive else outer)],
-            send_f.at[turn],
-            recv_f.at[turn],
-            me + (place - outer) * INNER,
+        owner = place if receive else outer
+        return Sized(
+            units,
+            owner,
+            lambda width: remote(
+                column_ref.at[:, place, :, pl.ds(0, width)],
+                spread_ref.at[:, :, units.columns(owner, width)],
+                send_f.at[turn],
+                recv_f.at[turn],
+                me + (place - outer) * INNER,
+            ),
         )
 
     def small(turn):
@@ -835,8 +934,14 @@
 
         lax.fori_loop(0, total // step, one, 0)
 
-    keep = pltpu.make_async_copy(
-        column_ref.at[:, outer], spread_ref.at[:, :, units_of(outer)], here
+    keep = Sized(
+        units,
+        outer,
+        lambda width: pltpu.make_async_copy(
+            column_ref.at[:, outer, :, pl.ds(0, width)],
+            spread_ref.at[:, :, units.columns(outer, width)],
+            here,
+        ),
     )
     keep.start()
 
@@ -944,12 +1049,12 @@
     keep.wait()
 
 
-def scatter_mixer(one, mixed, dy, dxb, branch, gates, dpar, gain_one, gain_two, column):
+def scatter_mixer(one, mixed, dy, dxb, branch, gates, dpar, gain_one, gain_two, column, hidden_units):
     n, rows, _ = one.shape
     groups = n // INNER
     width = dy.shape[1]
     total = 3 * rows + 2 * gates.shape[2]
-    kinds, _, _, units = column.shape
+    kinds = column.shape[0]
     turns = n.bit_length()
     dma = pltpu.SemaphoreType.DMA
     return pl.pallas_call(
@@ -957,7 +1062,7 @@
         out_shape=(
             jax.ShapeDtypeStruct((total, width), F32),
             jax.ShapeDtypeStruct((16, width), F32),
-            jax.ShapeDtypeStruct((kinds, rows, groups * units), BF16),
+            jax.ShapeDtypeStruct((kinds, rows, hidden_units), BF16),
         ),
         in_specs=[VMEM] * 9 + [ANY],
         out_specs=(VMEM, VMEM, ANY),
@@ -1016,7 +1121,9 @@
 
 def forward_body(
     n,
+    hidden_units,
     one_ref,
+    last_ref,
     w_in_ref,
     w_branch_ref,
     w_out_ref,
@@ -1040,13 +1147,12 @@
     mixed,
     mixed_got,
     wide,
-    tail,
     fade,
     mine,
     theirs,
     *sems,
 ):
-    send_tail, recv_tail, send_tot, recv_tot, send_f, recv_f, send_m, recv_m, loaded = sems
+    send_tot, recv_tot, send_f, recv_f, send_m, recv_m, loaded = sems
     tokens, width = xb_ref.shape
     model = one_ref.shape[1]
     me = lax.axis_index("seq")
@@ -1060,54 +1166,48 @@
     for load in loads:
         load.start()
     greet_all(n, me, True)
-    tail_copy = remote(
-        xb_ref.at[pl.ds(tokens - 16, 16)], tail, send_tail, recv_tail, lax.rem(me + 1, n)
-    )
     _, _, by_x, by_y, _ = whereabouts()
     part = column_ref.shape[1] // 2
     kinds = column_ref.shape[0]
+    units = Units(hidden_units, n // INNER, lax.axis_index("ch"))
+    outer = me // INNER
     hosted = [
         [
-            remote(
-                column_ref.at[kind, pl.ds(h * part, part)],
-                near_ref.at[h, kind],
-                send_f.at[kind, h],
-                recv_f.at[kind, h],
-                (by_x, by_y)[h],
+            Sized(
+                units,
+                outer,
+                lambda width, kind=kind, h=h, part=part: remote(
+                    column_ref.at[kind, pl.ds(h * part, part), :, pl.ds(0, width)],
+                    near_ref.at[h, kind, :, :, pl.ds(0, width)],
+                    send_f.at[kind, h],
+                    recv_f.at[kind, h],
+                    (by_x, by_y)[h],
+                ),
             )
             for h in range(2)
         ]
         for kind in range(kinds)
     ]
 
-    def host(kind):
-        for copy in hosted[kind]:
-            copy.start()
-
+    def host(pieces):
+        for pair in pieces:
+            for copy in pair:
+                copy.start()
+
+    host(hosted[:1])
     loads[0].wait()
     for start in range(0, width, size):
         cols = slice(start, start + size)
-        xb_ref[:, cols] = jnp.dot(
-            one_ref[...], w_in[:, cols], preferred_element_type=F32
-        ).astype(BF16)
-    pl.when(me + 1 < n)(tail_copy.start)
-    host(0)
-    wide[8:] = xb_ref[...].astype(F32)
+        low = jnp.dot(one_ref[...], w_in[:, cols], preferred_element_type=F32).astype(BF16)
+        xb_ref[:, cols] = low
+        wide[8:, cols] = low.astype(F32)
+        low = jnp.dot(last_ref[...], w_in[:, cols], preferred_element_type=F32).astype(BF16)
+        wide[:8, cols] = low.astype(F32)[8:]
     loads[1].wait()
     for start in range(0, width, size):
         cols = slice(start, start + size)
         yp_ref[:, cols] = jnp.dot(one_ref[...], w_branch[:, cols], preferred_element_type=F32)
 
-    @pl.when(me > 0)
-    def _():
-        tail_copy.wait_recv()
-        wide[:8] = tail[...].astype(F32)[8:]
-
-    @pl.when(me == 0)
-    def _():
-        wide[:8] = jnp.zeros((8, width), F32)
-
-    pl.when(me + 1 < n)(tail_copy.wait_send)
     edge_ref[:8] = wide[:8]
     first = first_row(tokens)
     for head in range(width // size):
@@ -1151,8 +1251,7 @@
         return carry
 
     lax.fori_loop(me + 1, n, tell, 0)
-    for kind in range(1, kinds):
-        host(kind)
+    host(hosted[1:])
 
     def hear(place, state):
         heard(place).wait_recv()
@@ -1212,7 +1311,7 @@
             copy.wait()
 
 
-def mixer_forward(one, weights, gates, par, x_half, gain, column):
+def mixer_forward(one, last, weights, gates, par, x_half, gain, column, hidden_units):
     n = lax.axis_size("seq")
     tokens, model = one.shape
     width = par.shape[1]
@@ -1222,7 +1321,7 @@
     whole = jax.ShapeDtypeStruct((tokens, width), F32)
     low = jax.ShapeDtypeStruct((tokens, width), BF16)
     return pl.pallas_call(
-        functools.partial(forward_body, n),
+        functools.partial(forward_body, n, hidden_units),
         out_shape=(
             low,
             whole,
@@ -1234,7 +1333,7 @@
             jax.ShapeDtypeStruct((half, model), BF16),
             jax.ShapeDtypeStruct((2, kinds, groups // 2, rows, units), column.dtype),
         ),
-        in_specs=[VMEM] + [HBM] * 3 + [VMEM] * 4 + [HBM],
+        in_specs=[VMEM] * 2 + [HBM] * 3 + [VMEM] * 4 + [HBM],
         out_specs=(VMEM,) * 8 + (HBM,),
         scratch_shapes=[
             pltpu.VMEM((model, width), BF16),
@@ -1243,12 +1342,9 @@
             pltpu.VMEM((2, half, model), F32),
             pltpu.VMEM((half, model), F32),
             pltpu.VMEM((tokens + 8, width), F32),
-            pltpu.VMEM((16, width), BF16),
             pltpu.VMEM((tokens, width), F32),
             pltpu.VMEM((2, width), F32),
             pltpu.VMEM((n, 2, width), F32),
-            dma(()),
-            dma(()),
             dma((n,)),
             dma((n,)),
             dma((kinds, 2)),
@@ -1259,11 +1355,12 @@
         ],
         compiler_params=params(4, 60),
         name="mixer_forward",
-    )(one, *weights, gates, par, x_half, gain, column)
+    )(one, last, *weights, gates, par, x_half, gain, column)
 
 
 def backward_body(
     n,
+    hidden_units,
     mixed_ref,
     w_in_ref,
     w_branch_ref,
@@ -1279,18 +1376,22 @@
     gate_ref,
     par_ref,
     half_ref,
+    own_ref,
     dy_ref,
     dxb_ref,
     dgate_ref,
     dpar_ref,
     dx_ref,
     dgain_ref,
+    column_ref,
     near_ref,
+    own,
     w_in,
     w_branch,
     w_out,
     d_one,
     d_one_got,
+    d_one_part,
     fade,
     shift,
     adj,
@@ -1303,7 +1404,7 @@
     head_rows,
     *sems,
 ):
-    send_rows, recv_rows, send_tot, recv_tot, send_f, recv_f, send_m, recv_m, send_x, recv_x, loaded = sems
+    send_rows, recv_rows, send_tot, recv_tot, send_f, recv_f, send_m, recv_m, send_x, recv_x, loaded, own_sem, out_sem = sems
     tokens, width = xb_ref.shape
     model = gain_ref.shape[1]
     me = lax.axis_index("seq")
@@ -1318,26 +1419,36 @@
         load.start()
     greet_all(n, me, True)
     _, _, by_x, by_y, _ = whereabouts()
-    kinds = half_ref.shape[1]
+    kinds, pieces = half_ref.shape[1:3]
+    units = Units(hidden_units, n // INNER, lax.axis_index("ch"))
+    outer = me // INNER
     hosted = [
         [
-            remote(
-                half_ref.at[h, kind],
-                near_ref.at[h, kind],
-                send_f.at[kind, h],
-                recv_f.at[kind, h],
-                (by_x, by_y)[h],
+            Sized(
+                units,
+                outer,
+                lambda width, kind=kind, at=at, h=h: remote(
+                    half_ref.at[h, kind, at, :, pl.ds(0, width)],
+                    near_ref.at[h, kind, at, :, pl.ds(0, width)],
+                    send_f.at[kind, at, h],
+                    recv_f.at[kind, at, h],
+                    (by_x, by_y)[h],
+                ),
             )
             for h in range(2)
         ]
         for kind in range(kinds)
+        for at in range(pieces)
     ]
 
-    def host(kind):
-        for copy in hosted[kind]:
-            copy.start()
-
-    host(0)
+    def host(some):
+        for pair in some:
+            for copy in pair:
+                copy.start()
+
+    host(hosted[:2])
+    own_load = pltpu.make_async_copy(own_ref, own, own_sem)
+    own_load.start()
     first = first_row(tokens)
     fade[tokens:] = jnp.ones((8, width), F32)
     loads[0].wait()
@@ -1385,7 +1496,7 @@
         return carry
 
     lax.fori_loop(0, me, tell, 0)
-    host(1)
+    host(hosted[2:3])
 
     def hear(turn, state):
         place = n - 1 - turn
@@ -1446,8 +1557,13 @@
         dconv.at[pl.ds(0, 8)], head_rows, send_rows, recv_rows, lax.rem(me + n - 1, n)
     )
     pl.when(me > 0)(rows_copy.start)
-    for kind in range(2, kinds):
-        host(kind)
+    host(hosted[3:])
+    loads[2].wait()
+    for start in range(0, model, size):
+        cols = slice(start, start + size)
+        d_one_part[:, cols] = lax.dot_general(
+            dy_ref[...], w_branch[cols], FLIPPED, preferred_element_type=F32
+        )
 
     @pl.when(me + 1 < n)
     def _():
@@ -1475,11 +1591,10 @@
     core = lax.axis_index("ch")
     half = tokens // 2
     loads[1].wait()
-    loads[2].wait()
     for start in range(0, model, size):
         cols = slice(start, start + size)
         part = (
-            lax.dot_general(dy_ref[...], w_branch[cols], FLIPPED, preferred_element_type=F32)
+            d_one_part[:, cols]
             + lax.dot_general(dxb_ref[...], w_in[cols], FLIPPED, preferred_element_type=F32)
         ).astype(BF16)
         d_one[0, :, cols] = part[:half]
@@ -1516,9 +1631,33 @@
     )
     share.start()
     exchange.wait_send()
-    for pair in hosted:
-        for copy in pair:
-            copy.wait()
+    own_load.wait()
+    part, rows = own.shape[2:4]
+    chunk = 16 if rows % 16 == 0 else rows
+    outs = []
+    for kind in range(kinds):
+        for h in range(2):
+            for place in range(part):
+                hosted[kind * part + place][h].wait()
+
+                def add(at, carry, kind=kind, h=h, place=place):
+                    r = pl.ds(pl.multiple_of(at * chunk, chunk), chunk)
+                    own[h, kind, place, r] = (
+                        own[h, kind, place, r].astype(F32) + near_ref[h, kind, place, r].astype(F32)
+                    ).astype(BF16)
+                    return carry
+
+                lax.fori_loop(0, rows // chunk, add, 0)
+            outs.append(
+                pltpu.make_async_copy(
+                    own.at[h, kind],
+                    column_ref.at[kind, pl.ds(h * part, part)],
+                    out_sem.at[kind, h],
+                )
+            )
+            outs[-1].start()
+    for copy in outs:
+        copy.wait()
     pltpu.make_async_remote_copy(
         src_ref=dx_ref.at[core],
         dst_ref=dx_ref.at[1 - core],
@@ -1531,19 +1670,20 @@
 
 
 def mixer_backward(
-    mixed, weights, x_half, gain, d_resid, y_pre, states, edge, conv, x_branch, gates, par, halves
+    mixed, weights, x_half, gain, d_resid, y_pre, states, edge, conv, x_branch, gates, par, halves, own, hidden_units
 ):
     n = lax.axis_size("seq")
     tokens, width = x_branch.shape
     model = mixed.shape[1]
     size = gates.shape[2]
     half = tokens // 2
+    _, kinds, part, rows, units = halves.shape
     dma = pltpu.SemaphoreType.DMA
     whole = pltpu.VMEM((tokens, width), F32)
     longer = pltpu.VMEM((tokens + 8, width), F32)
     weight = pltpu.VMEM((model, width), BF16)
     return pl.pallas_call(
-        functools.partial(backward_body, n),
+        functools.partial(backward_body, n, hidden_units),
         out_shape=(
             jax.ShapeDtypeStruct((tokens, width), BF16),
             jax.ShapeDtypeStruct((tokens, width), BF16),
@@ -1551,16 +1691,19 @@
             jax.ShapeDtypeStruct((8, width), F32),
             jax.ShapeDtypeStruct((2, half, model), F32),
             jax.ShapeDtypeStruct((1, model), F32),
-            jax.ShapeDtypeStruct(halves.shape, BF16),
+            jax.ShapeDtypeStruct((kinds, 2 * part, rows, units), BF16),
         ),
-        in_specs=[VMEM] + [HBM] * 3 + [VMEM] * 10 + [HBM],
+        in_specs=[VMEM] + [HBM] * 3 + [VMEM] * 10 + [HBM, HBM],
         out_specs=(VMEM,) * 6 + (HBM,),
         scratch_shapes=[
+            pltpu.VMEM(halves.shape, BF16),
+            pltpu.VMEM(halves.shape, BF16),
             weight,
             weight,
             weight,
             pltpu.VMEM((2, half, model), BF16),
             pltpu.VMEM((half, model), BF16),
+            pltpu.VMEM((tokens, model), F32),
             longer,
             whole,
             whole,
@@ -1575,26 +1718,29 @@
             dma(()),
             dma((n,)),
             dma((n,)),
-            dma((halves.shape[1], 2)),
-            dma((halves.shape[1], 2)),
+            dma((kinds, part, 2)),
+            dma((kinds, part, 2)),
             dma(()),
             dma(()),
             dma(()),
             dma(()),
             dma((3,)),
+            dma(()),
+            dma((kinds, 2)),
         ],
         compiler_params=params(5, 60),
         name="mixer_backward",
-    )(mixed, *weights, x_half, gain, d_resid, y_pre, states, edge, conv, x_branch, gates, par, halves)
-
-
-def ffn_body(n, *refs):
+    )(mixed, *weights, x_half, gain, d_resid, y_pre, states, edge, conv, x_branch, gates, par, halves, own)
+
+
+def ffn_body(n, hidden_units, *refs):
     own_ref, cot_ref, column_ref, near_ref, resid_ref, gain_ref = refs[:6]
-    block_ref, d_resid_ref, mixed_ref, d_gain_ref, halves_ref, mine_ref, far_ref = refs[6:13]
-    tokens, cots, w, hidden, box, sib, got, d_hidden, stage, turned = refs[13:23]
-    token_sems, cot_sems = refs[23:26], refs[26:29]
-    send_w, recv_w, keep_w, keep_c, keep_t = refs[29:34]
-    send_c, recv_s, send_z, recv_r, send_f, recv_f, send_m, recv_m, move, out_sem = refs[34:]
+    block_ref, d_resid_ref, mixed_ref, d_gain_ref, turned_ref = refs[6:11]
+    halves_ref, mine_ref, far_ref = refs[11:14]
+    tokens, cots, w, extra, hidden, box, sib, got, stage, turned, my_cot = refs[14:25]
+    token_sems, cot_sems = refs[25:28], refs[28:31]
+    send_w, recv_w, keep_w, keep_c, keep_t, keep_m = refs[31:37]
+    send_c, recv_s, send_z, recv_r, send_f, recv_f, send_m, recv_m, move, out_sem = refs[37:]
     groups = n // INNER
     half = groups // 2
     me, outer, by_x, by_y, by_xy = whereabouts()
@@ -1615,6 +1761,7 @@
     pl.semaphore_wait(barrier, 3 + above.astype(jnp.int32) + below.astype(jnp.int32))
     flips = ((by_x, by_y), (by_y, by_x))
     rows, units = w.shape[3], w.shape[4]
+    split = Units(hidden_units, groups, core)
     tall, model = own_ref.shape
     count = 2 * tall
     deep = INNER * rows
@@ -1631,12 +1778,17 @@
         source = flips[h][0] if far else me
         if receive:
             source = by_xy if far else flips[h][1]
-        return remote(
-            near_ref.at[h, kind] if far else column_ref.at[kind, part(h)],
-            w.at[kind, part(h), source - base],
-            send_w.at[kind, h, far],
-            recv_w.at[kind, h, far],
-            flips[h][1],
+        src = near_ref.at[h, kind] if far else column_ref.at[kind, part(h)]
+        return Sized(
+            split,
+            outer,
+            lambda width: remote(
+                src.at[:, :, pl.ds(0, width)],
+                w.at[kind, part(h), source - base, :, pl.ds(0, width)],
+                send_w.at[kind, h, far],
+                recv_w.at[kind, h, far],
+                flips[h][1],
+            ),
         )
 
     keep = [
@@ -1657,27 +1809,35 @@
     ]
     every = [(h, far) for far in range(2) for h in range(2)]
     own_t, own_c = chain_t.keep(keep_t), chain_c.keep(keep_c)
-    chain_c.start()
-    for kind in (2, 0, 1):
+    load_m = pltpu.make_async_copy(cot_ref, my_cot, keep_m)
+    chain_t.start()
+    for kind in range(3):
         for h, far in every:
             weight_copy(kind, h, far).start()
+    own_t.start()
     own_c.start()
-    own_t.start()
-    for kind in (2, 0, 1):
+    load_m.start()
+    for kind in range(3):
         for copy in keep[kind]:
             copy.start()
     for step in range(1, groups - 1):
-        chain_c.step(step)
-    chain_t.start()
-    chain_c.step(groups - 1)
-    chain_c.finish()
-    own_c.wait()
+        chain_t.step(step)
+    chain_c.start()
+    chain_t.step(groups - 1)
+    chain_t.finish()
+    own_t.wait()
 
     def weights_landed(kind):
         for h, far in every:
             weight_copy(kind, h, far, True).wait_recv()
         for copy in keep[kind]:
             copy.wait()
+        if not split.even:
+
+            @pl.when(jnp.logical_not(split.full(outer)))
+            def _():
+                rest = jnp.zeros((groups, INNER, rows, LANES), BF16)
+                w[kind, :, :, :, units - LANES :] = rest
 
     def columns(kind, at):
         return w[kind, :, :, :, at : at + tile].reshape(model, tile)
@@ -1692,22 +1852,9 @@
 
         lax.fori_loop(0, limit, one, 0)
 
-    weights_landed(2)
-
-    def back_hidden(place):
-        left = cots[place].reshape(count, model)
-        for at in range(0, units, tile):
-            d_hidden[token_rows(place), at : at + tile] = jnp.dot(
-                left, columns(2, at), preferred_element_type=F32
-            )
-
-    each(groups, back_hidden)
-    for step in range(1, groups):
-        chain_t.step(step)
-    chain_t.finish()
-    own_t.wait()
     weights_landed(0)
     weights_landed(1)
+    chain_c.step(1)
 
     def middle(place):
         left = tokens[place].reshape(count, model)
@@ -1717,18 +1864,31 @@
             gate = jnp.dot(left, columns(0, at), preferred_element_type=F32)
             up = jnp.dot(left, columns(1, at), preferred_element_type=F32)
             value, slope = gelu_parts(gate)
-            back = d_hidden[r, c]
             hidden[0, r, c] = (value * up).astype(BF16)
-            hidden[1, r, c] = (back * up * slope).astype(BF16)
-            hidden[2, r, c] = (back * value).astype(BF16)
+            hidden[1, r, c] = (up * slope).astype(BF16)
+            hidden[2, r, c] = value.astype(BF16)
 
     each(groups, middle)
+    for step in range(2, groups):
+        chain_c.step(step)
+    chain_c.finish()
+    own_c.wait()
+    weights_landed(2)
     for kind in range(3):
         for h, far in every:
             weight_copy(kind, h, far).wait_send()
 
-
-    boxes = (box, tokens)
+    def back_hidden(place):
+        left = cots[place].reshape(count, model)
+        r = token_rows(place)
+        for at in range(0, units, tile):
+            c = slice(at, at + tile)
+            back = jnp.dot(left, columns(2, at), preferred_element_type=F32)
+            for kind in (1, 2):
+                hidden[kind, r, c] = (back * hidden[kind, r, c].astype(F32)).astype(BF16)
+
+
+    boxes = (cots, box)
 
     def partial(kind, place):
         r = token_rows(place)
@@ -1816,15 +1976,17 @@
 
     at_end = jnp.logical_or(outer == 0, outer == groups - 1)
 
-    def partials(kind):
-        def one(turn):
+    def partials(kind, start, stop):
+        def one(turn, carry):
             partial(kind, far_first(groups, outer, turn))
 
             @pl.when(jnp.logical_and(at_end, turn >= 1))
             def _():
                 pass_on(kind, turn - 1)
 
-        each(groups, one)
+            return carry
+
+        lax.fori_loop(start, stop, one, 0)
 
     def between(kind, turns):
         @pl.when(jnp.logical_not(at_end))
@@ -1869,14 +2031,20 @@
         each(groups, one)
 
 
+    made = (w.at[0], w.at[1], extra)
+
     def gradient_copy(kind, h, far):
         source = by_xy if far else flips[h][1]
-        return remote(
-            w.at[kind, part(h), source - base],
-            far_ref.at[h, far, kind],
-            send_f.at[kind, h, far],
-            recv_f.at[kind, h, far],
-            flips[h][1],
+        return Sized(
+            split,
+            outer,
+            lambda width: remote(
+                made[kind].at[part(h), source - base, :, pl.ds(0, width)],
+                far_ref.at[h, far, kind, :, :, pl.ds(0, width)],
+                send_f.at[kind, h, far],
+                recv_f.at[kind, h, far],
+                flips[h][1],
+            ),
         )
 
     def gradients(kinds, source, h):
@@ -1886,7 +2054,7 @@
             for kind, right in kinds:
                 for start in range(0, units, tile):
                     c = slice(start, start + tile)
-                    w[kind, at, :, :, c] = (
+                    made[kind][at, :, :, c] = (
                         jnp.dot(turned[...], hidden[right, :, c], preferred_element_type=F32)
                         .astype(BF16)
                         .reshape(INNER, rows, tile)
@@ -1906,8 +2074,8 @@
 
             def one(turn, place=place, at=at):
                 r = rows_of(turn)
-                w[kind, at, inner, r] = (
-                    w[kind, at, inner, r].astype(F32) + stage[place, r].astype(F32)
+                made[kind][at, inner, r] = (
+                    made[kind][at, inner, r].astype(F32) + stage[place, r].astype(F32)
                 ).astype(BF16)
 
             each(rows // chunk, one)
@@ -1916,37 +2084,28 @@
     def out_copy(kind, h, far):
         inner = (flips[h][0] if far else me) - base
         return pltpu.make_async_copy(
-            w.at[kind, part(h), inner],
+            made[kind].at[part(h), inner],
             (halves_ref if far else mine_ref).at[h, kind],
             out_sem.at[kind, h, far],
         )
 
-    first, second = range(groups // 2), range(groups // 2, groups - 1)
-    pair = ((0, 1), (1, 2))
-    partials(0)
-    gradients(pair, tokens, 0)
-    between(0, first[:1])
-    gradients(pair, tokens, 1)
-    between(0, first[1:])
-    between(0, second)
-    partials(1)
+    partials(1, 0, 2)
     gradients(((2, 0),), cots, 0)
-    between(1, first[:1])
+    partials(1, 2, groups)
     gradients(((2, 0),), cots, 1)
-    between(1, first[1:])
-    d_gain_ref[...] = jnp.zeros((1, model), F32)
-
-    def norm(r, grad):
-        resid = resid_ref[r]
-        scale = lax.rsqrt(jnp.mean(resid * resid, axis=-1, keepdims=True) + 1e-06)
-        back = grad * gain_ref[...]
-        shrink = scale * scale * scale * jnp.mean(resid * back, axis=-1, keepdims=True)
-        value = cots[outer, core, r].astype(F32) + (scale * back - resid * shrink)
-        d_resid_ref[r] = value
-        mixed_ref[core, r] = value.astype(BF16)
-        d_gain_ref[...] = d_gain_ref[...] + jnp.sum(grad * (resid * scale), axis=0, keepdims=True)
-
-    totals(0, norm)
+    each(groups, back_hidden)
+    load_m.wait()
+    partials(0, 0, groups)
+    gradients(((0, 1),), tokens, 0)
+    between(1, range(1))
+    gradients(((0, 1),), tokens, 1)
+    between(1, range(1, groups // 2))
+    between(0, range(1))
+    gradients(((1, 2),), tokens, 0)
+    between(1, range(groups // 2, groups - 1))
+    between(0, range(1, groups // 2))
+    gradients(((1, 2),), tokens, 1)
+    between(0, range(groups // 2, groups - 1))
 
     def shared(ref, at, part):
         return pltpu.make_async_remote_copy(
@@ -1958,26 +2117,43 @@
             device_id_type=MESH,
         )
 
-    share = shared(mixed_ref, 0, core)
-    share.start()
-    between(1, second)
+    def finish(r, value):
+        block_ref[core, r] = (resid_ref[r] + value).astype(BF16)
+
+    d_gain_ref[...] = jnp.zeros((1, model), F32)
+
+    def norm(r, grad):
+        resid = resid_ref[r]
+        scale = lax.rsqrt(jnp.mean(resid * resid, axis=-1, keepdims=True) + 1e-06)
+        back = grad * gain_ref[...]
+        shrink = scale * scale * scale * jnp.mean(resid * back, axis=-1, keepdims=True)
+        value = my_cot[r].astype(F32) + (scale * back - resid * shrink)
+        d_resid_ref[r] = value
+        mixed_ref[core, r] = value.astype(BF16)
+        d_gain_ref[...] = d_gain_ref[...] + jnp.sum(grad * (resid * scale), axis=0, keepdims=True)
+
     for far in (1, 0):
         for h in range(2):
-            for kind in range(2):
-                collect(kind, h, far)
-
-    def finish(r, value):
-        block_ref[core, r] = (resid_ref[r] + value).astype(BF16)
-
+            collect(2, h, far)
     totals(1, finish)
     show = shared(block_ref, 1, core)
     show.start()
+    for far in (1, 0):
+        for h in range(2):
+            collect(0, h, far)
+    totals(0, norm)
+    share = shared(mixed_ref, 0, core)
+    share.start()
+    shared(mixed_ref, 0, 1 - core).wait_recv()
+    for start in range(0, model, tile):
+        c = slice(start, start + tile)
+        turned_ref[c, :tall] = mixed_ref[0, :, c].T
+        turned_ref[c, tall:] = mixed_ref[1, :, c].T
+    for far in (1, 0):
+        for h in range(2):
+            collect(1, h, far)
     clear(0)
     clear(1)
-    for far in (1, 0):
-        for h in range(2):
-            collect(2, h, far)
-    shared(mixed_ref, 0, 1 - core).wait_recv()
     shared(block_ref, 1, 1 - core).wait_recv()
     share.wait_send()
     show.wait_send()
@@ -1987,7 +2163,7 @@
             out_copy(kind, h, far).wait()
 
 
-def feed_forward(own, cotangent, column, near, resid, gain):
+def feed_forward(own, cotangent, column, near, resid, gain, hidden_units):
     n = lax.axis_size("seq")
     groups = n // INNER
     tall, model = own.shape
@@ -1996,34 +2172,37 @@
     dma = pltpu.SemaphoreType.DMA
     part = jax.ShapeDtypeStruct((2, kinds, half, rows, units), BF16)
     return pl.pallas_call(
-        functools.partial(ffn_body, n),
+        functools.partial(ffn_body, n, hidden_units),
         out_shape=(
             jax.ShapeDtypeStruct((2, tall, model), BF16),
             jax.ShapeDtypeStruct((tall, model), F32),
             jax.ShapeDtypeStruct((2, tall, model), BF16),
             jax.ShapeDtypeStruct((1, model), F32),
+            jax.ShapeDtypeStruct((model, 2 * tall), BF16),
             part,
             part,
             jax.ShapeDtypeStruct((2, 2, kinds, half, rows, units), BF16),
         ),
         in_specs=[HBM] * 4 + [VMEM] * 2,
-        out_specs=(VMEM,) * 4 + (HBM,) * 3,
+        out_specs=(VMEM,) * 5 + (HBM,) * 3,
         scratch_shapes=[
             pltpu.VMEM((groups, 2, tall, model), BF16),
             pltpu.VMEM((groups, 2, tall, model), BF16),
             pltpu.VMEM((kinds, groups, INNER, rows, units), BF16),
+            pltpu.VMEM((groups, INNER, rows, units), BF16),
             pltpu.VMEM((3, groups * 2 * tall, units), BF16),
             pltpu.VMEM((groups, 2, tall, model), BF16),
             pltpu.VMEM((2, groups, tall, model), BF16),
             pltpu.VMEM((2, groups + 1, tall, model), BF16),
-            pltpu.VMEM((groups * 2 * tall, units), F32),
             pltpu.VMEM((half, rows, units), BF16),
             pltpu.VMEM((INNER * rows, groups * 2 * tall), BF16),
+            pltpu.VMEM((tall, model), BF16),
             *chain_semaphores(groups),
             *chain_semaphores(groups),
             dma((kinds, 2, 2)),
             dma((kinds, 2, 2)),
             dma((kinds, 3)),
+            dma(()),
             dma(()),
             dma(()),
             dma((2, groups)),
@@ -2080,7 +2259,7 @@
     return total
 
 
-def feed_forward_parts(n_two, cot_half, column, near, resid, ffn_gain):
+def feed_forward_parts(n_two, cot_half, column, near, resid, ffn_gain, hidden_units):
     f32, bf16 = F32, BF16
     _, groups, depth, units = column.shape
     half_rows, model = n_two.shape
@@ -2089,7 +2268,9 @@
     all_two, *full_ffn = gather_tokens(n_two, column, near)
     all_cot = tokens_in(cot_half)
     all_two, all_cot = (v.reshape(groups * tok_rows, model) for v in (all_two, all_cot))
-    full_ffn = [w.reshape(model, units) for w in full_ffn]
+    own = Units(hidden_units, groups, lax.axis_index("ch")).width(lax.axis_index("seq") // INNER)
+    valid = lax.broadcasted_iota(jnp.int32, (1, units), 1) < own
+    full_ffn = [jnp.where(valid, w.reshape(model, units), 0) for w in full_ffn]
     gate_pre = jnp.dot(all_two, full_ffn[0], preferred_element_type=f32)
     up_pre = jnp.dot(all_two, full_ffn[1], preferred_element_type=f32)
     gate_act, gelu_back_gate = jax.vjp(gelu_tanh, gate_pre)
@@ -2158,17 +2339,13 @@
     depth = ffn_gate.shape[0]
     groups = n // INNER
     hidden_units = ffn_gate.shape[1]
-    units = -(-hidden_units // (groups * 128)) * 128
-    x_float = inputs.astype(f32)
-    n_one = scaled_norm(x_float, norm_gain).astype(bf16)
     x_half = my_half(inputs)
-
-    gate_pack = jnp.stack([gate_x_blocks, gate_a_blocks])
-    ffn_pack = jnp.pad(
-        jnp.stack([ffn_gate, ffn_up, ffn_down.T]), ((0, 0), (0, 0), (0, groups * units - hidden_units))
-    )
-    *full_mixer, full_gates, column = gather_weights(
-        [input_weight, branch_weight, out_weight.T], gate_pack, ffn_pack
+    *full_mixer, full_gates, column, n_one, n_one_turned, last_rows = gather_weights(
+        [input_weight, branch_weight, out_weight.T],
+        [gate_x_blocks, gate_a_blocks],
+        [ffn_gate, ffn_up, ffn_down.T],
+        inputs,
+        norm_gain.reshape(1, model),
     )
     full_mixer = [w.reshape(model, width) for w in full_mixer]
     gates = full_gates.reshape(2, heads, size, size)
@@ -2186,24 +2363,27 @@
 
     x_branch, y_pre, conv_out, states, branch_out, edge, resid, n_two, near = mixer_forward(
         n_one,
+        last_rows,
         full_mixer,
         gates,
         par,
         x_half,
         ffn_gain.reshape(1, model),
         column,
+        hidden_units,
     )
     if groups <= 4 and depth % 16 == 0:
-        block_out, d_resid, d_mixed, d_ffn_gain_term, halves, mine, _ = feed_forward(
-            n_two, cot_half, column, near, resid, ffn_gain.reshape(1, model)
+        block_out, d_resid, d_mixed, d_ffn_gain_term, d_mixed_turned, halves, mine, _ = feed_forward(
+            n_two, cot_half, column, near, resid, ffn_gain.reshape(1, model), hidden_units
         )
         block_out = block_out.reshape(tok_rows, model)
         d_mixed = d_mixed.reshape(tok_rows, model)
     else:
         block_out, d_resid, d_mixed, d_ffn_gain_term, halves, mine = feed_forward_parts(
-            n_two, cot_half, column, near, resid, ffn_gain
-        )
-    d_y, d_xb, d_gates, d_par, d_inputs, d_norm_gain_term, near_back = mixer_backward(
+            n_two, cot_half, column, near, resid, ffn_gain, hidden_units
+        )
+        d_mixed_turned = d_mixed.T
+    d_y, d_xb, d_gates, d_par, d_inputs, d_norm_gain_term, column_back = mixer_backward(
         d_mixed,
         full_mixer,
         x_half,
@@ -2217,18 +2397,14 @@
         gates,
         par,
         halves,
-    )
-    column_back = jnp.concatenate(
-        [
-            (mine[h].astype(f32) + near_back[h].astype(f32)).astype(bf16) for h in range(2)
-        ],
-        axis=1,
+        mine,
+        hidden_units,
     )
     d_inputs = d_inputs.reshape(tok_rows, model)
     gain_rows = model // width
     scattered, small, spread = scatter_mixer(
-        n_one.T.reshape(n, depth, tok_rows),
-        d_mixed.T.reshape(n, depth, tok_rows),
+        n_one_turned.reshape(n, depth, tok_rows),
+        d_mixed_turned.reshape(n, depth, tok_rows),
         d_y,
         d_xb,
         branch_out,
@@ -2237,8 +2413,9 @@
         d_norm_gain_term,
         d_ffn_gain_term,
         column_back,
+        hidden_units,
     )
-    ffn_grads = [spread[kind, :, :hidden_units].astype(f32) for kind in range(3)]
+    ffn_grads = [spread[kind].astype(f32) for kind in range(3)]
     d_gate_pair = scattered[3 * depth :].reshape(2, part, heads, size).transpose(0, 2, 1, 3)
     return (
         block_out,

time: 761 us -> 721 us (0.947)
  Pallas kernels: 708 us -> 685 us
  local copies, waits for them, and re-layouts: 26.6 us -> 17.8 us
  other arithmetic: 16.3 us -> 7.65 us
    pallas_call x3, Pallas kernels: 335 us -> 313 us  [the longest x1 201 us: feed_forward(): pl.pallas_call(functools.partial(ffn_body, n, hidden_units), out_shape=(j...]
    unnamed x48 -> x8, local copies, waits for them, and re-layouts: 16.5 us -> 5.03 us
where the time goes in v6:
time: 721 us; the launch traced here: 712 us
  Pallas kernels  685 us (95%)
  local copies, waits for them, and re-layouts  17.8 us (2%)
  other arithmetic  7.65 us (1%)
    pallas_call x1, Pallas kernels, feed_forward(): pl.pallas_call(functools.partial(ffn_body, n, hidden_units), out_shape=(j...  201 us
    pallas_call x1, Pallas kernels, scatter_mixer(): pl.pallas_call(functools.partial(scatter_body, n), out_shape=(jax.ShapeDt...  187 us
    pallas_call x1, Pallas kernels, gather_weights(): pl.pallas_call(functools.partial(gather_body, n), out_shape=tuple(made),...  185 us
    pallas_call x1, Pallas kernels, mixer_backward(): pl.pallas_call(functools.partial(backward_body, n, hidden_units), out_sha...  58.3 us
    pallas_call x1, Pallas kernels, mixer_forward(): pl.pallas_call(functools.partial(forward_body, n, hidden_units), out_shap...  53.8 us

profile of v6, /device:TPU:25, one launch (start us, length us, event | category | flops | bytes accessed | tf_op | source)
XLA Modules:
  0.0 711.8 jit_solution(11143123721203506026)
XLA Ops:
  0.7 0.1 pad.3.clone
  0.7 1.3 reshape.76.refs_9_.gain_ref
  2.0 1.3 reshape.81.gain_ref.refs_5_
  3.4 0.8 compare_select_fusion
  4.2 1.5 maximum_maximum_fusion.par_ref
  5.7 2.4 constant_dynamic-slice_fusion
  8.1 185.3 %gather_weights.1 = (bf16[16,160,1280]{2,1,0:T(8,128)(2,1)}, bf16[16,160,1280]{2,1,0:T(8,128)(2,1)}, bf16[16,160,1280]{2,1,0:T(8,128)(2,1)}, bf16[2,5,16,16,256]...) custom-call(bf16[160,1280]{1,0:T(8,128)(2,1)} %refs_0_.1, ...), custom_call_target="tpu_custom_call" | custom-call | tf_op jit(solution)/shard_map/gather_weights/pallas_call | solution.py:309
  193.4 53.8 %mixer_forward.1 = (bf16[256,1280]{1,0:T(8,128)(2,1)}, f32[256,1280]{1,0:T(8,128)}, bf16[256,1280]{1,0:T(8,128)(2,1)}, f32[256,1280]{1,0:T(8,128)}, bf16[256,128...) custom-call(bf16[256,2560]{1,0:T(8,128)(2,1)} %get-tuple-element.47., ...), custom_call_target="tpu_custom_call" | custom-call | tf_op jit(solution)/shard_map/mixer_forward/pallas_call | solution.py:1323
  247.2 200.6 %feed_forward.1 = (bf16[2,128,2560]{2,1,0:T(8,128)(2,1)}, f32[128,2560]{1,0:T(8,128)}, bf16[2,128,2560]{2,1,0:T(8,128)(2,1)}, f32[1,2560]{1,0:T(1,128)}, bf16[25...) custom-call(bf16[128,2560]{1,0:T(8,128)(2,1)} %get-tuple-element.54., ...), custom_call_target="tpu_custom_call" | custom-call | tf_op jit(solution)/shard_map/feed_forward/pallas_call | solution.py:2174
  447.8 58.3 %mixer_backward.1 = (bf16[256,1280]{1,0:T(8,128)(2,1)}, bf16[256,1280]{1,0:T(8,128)(2,1)}, bf16[16,2,16,1280]{3,2,1,0:T(8,128)(2,1)}, f32[8,1280]{1,0:T(8,128)},...) custom-call(bf16[256,2560]{1,0:T(8,128)(2,1)} %bitcast.38, ...), custom_call_target="tpu_custom_call" | custom-call | tf_op jit(solution)/shard_map/mixer_backward/pallas_call | solution.py:1685
  506.2 187.2 %scatter_mixer.1 = (f32[512,1280]{1,0:T(8,128)}, f32[16,1280]{1,0:T(8,128)}, bf16[3,160,3840]{2,1,0:T(8,128)(2,1)}) custom-call(bf16[16,160,256]{2,1,0:T(8,128)(2,1)} %bitcast.40, bf16[16,160,256]{2,1,0:T(8,128)(2,1)} %bitcast.41, bf16[256,1280]{1,0:T(8,128)(2,1)} %get-tuple-element.70.dy_ref, bf16[256,1280]{1,0:T(8,128)(2,1)} %get-tuple-element.71.dxb_ref, ...), custom_call_target="tpu_custom_call" | custom-call | tf_op jit(solution)/shard_map/scatter_mixer/pallas_call | solution.py:1060
  693.4 0.9 fusion
  694.2 1.4 slice.44
  695.6 0.6 reshape.89
  696.2 0.6 reshape.87
  696.8 0.9 slice.45
  697.8 3.1 slice_bitcast_fusion
  701.0 0.7 copy.28
  701.6 0.7 copy.27
  702.3 5.3 convert_bitcast_fusion
  707.6 0.0 copy-done.1
  707.6 1.1 copy.31
  708.7 1.2 copy-done
  709.9 1.5 copy.32
  (5 shorter events, 0.1 us)
Async XLA Ops:
  702.3 5.3 copy-start.1
  707.6 2.2 copy-start

commit v7 on v6

--- a/solution.py
+++ b/solution.py
@@ -22,10 +22,6 @@
 
 def pick(array, index, axis=0):
     return lax.dynamic_index_in_dim(array, index, axis, False)
-
-
-def put(array, block, index, axis=0):
-    return lax.dynamic_update_index_in_dim(array, block, index, axis)
 
 
 def scaled_norm(values, gain):
@@ -109,33 +105,34 @@
     )
 
 
-def gather_body(n, *refs):
+def gather_begin(n, refs, greeted):
     w_refs, g_refs, f_refs, x_ref, gain_ref = refs[:3], refs[3:5], refs[5:8], refs[8], refs[9]
     wo_refs, go_ref, column_ref, one_ref, turned_ref, last_ref = refs[10:13], *refs[13:18]
     send_m, recv_m, send_f, recv_f, here, send_l, recv_l = refs[18:]
     groups = n // INNER
     me, outer, by_x, by_y, by_xy = whereabouts()
     above, below = outer + 1 < groups, outer > 0
-    barrier = pltpu.get_barrier_semaphore()
-
-    def hello(peer):
-        pl.semaphore_signal(barrier, inc=1, device_id={"seq": peer}, device_id_type=MESH)
-
-    hello(by_x)
-    hello(by_y)
-
     def column_peer(turn):
         return lax.rem(outer + turn, groups)
 
-    def hello_column(turn, carry):
-        hello(me + (column_peer(turn) - outer) * INNER)
-        return carry
-
-    lax.fori_loop(1, groups, hello_column, 0)
-    pl.when(me + 1 < n)(lambda: hello(me + 1))
-    pl.when(me > 0)(lambda: hello(me - 1))
-    neighbours = (me + 1 < n).astype(jnp.int32) + (me > 0).astype(jnp.int32)
-    pl.semaphore_wait(barrier, groups + 1 + neighbours)
+    if not greeted:
+        barrier = pltpu.get_barrier_semaphore()
+
+        def hello(peer):
+            pl.semaphore_signal(barrier, inc=1, device_id={"seq": peer}, device_id_type=MESH)
+
+        hello(by_x)
+        hello(by_y)
+
+        def hello_column(turn, carry):
+            hello(me + (column_peer(turn) - outer) * INNER)
+            return carry
+
+        lax.fori_loop(1, groups, hello_column, 0)
+        pl.when(me + 1 < n)(lambda: hello(me + 1))
+        pl.when(me > 0)(lambda: hello(me - 1))
+        neighbours = (me + 1 < n).astype(jnp.int32) + (me > 0).astype(jnp.int32)
+        pl.semaphore_wait(barrier, groups + 1 + neighbours)
     units = Units(f_refs[0].shape[1], groups, lax.axis_index("ch"))
     half = w_refs[0].shape[1] // 2
 
@@ -161,7 +158,7 @@
         copy.start()
     sent = []
 
-    def copies(h, source, way, target, own):
+    def copies(h, source, way, target, own, kinds=range(4)):
         cols = pl.ds(h * half, half)
         pairs = [
             (w_refs[kind].at[:, cols], wo_refs[kind].at[source, :, cols]) for kind in range(3)
@@ -176,6 +173,7 @@
                 target,
             )
             for kind, (given, dst) in enumerate(pairs)
+            if kind in kinds
         ]
 
     def send(condition, *what):
@@ -186,9 +184,9 @@
         when(condition, go)
         sent.append((condition, what))
 
-    def arrive(condition, h, source):
+    def arrive(condition, h, source, kinds=range(4)):
         def go():
-            for copy in copies(h, source, 0, by_x, False):
+            for copy in copies(h, source, 0, by_x, False, kinds):
                 copy.wait_recv()
 
         when(condition, go)
@@ -273,24 +271,45 @@
             ):
                 arrive(there, h, source)
                 send(there, h, source, 3, flip_q, False)
-    for place in range(groups):
-        shift = (place - outer) * INNER
-        for h in range(2):
-            arrive(None, h, (by_y if h == 0 else by_x) + shift)
-            arrive(None, h, by_xy + shift)
-    each_turn(lambda turn: [copy.wait_recv() for copy in exchange(turn, True)])
-    for condition, what in sent:
-
-        def finish(what=what):
-            for copy in copies(*what):
-                copy.wait_send()
-
-        when(condition, finish)
-    each_turn(lambda turn: [copy.wait_send() for copy in exchange(turn, False)])
-    for copy in keep:
-        copy.wait()
-    pl.when(me > 0)(last_copy.wait_recv)
-    pl.when(me + 1 < n)(last_copy.wait_send)
+
+    def last(kind):
+        for place in range(groups):
+            shift = (place - outer) * INNER
+            for h in range(2):
+                arrive(None, h, (by_y if h == 0 else by_x) + shift, (kind,))
+                arrive(None, h, by_xy + shift, (kind,))
+        for copy in keep[kind : kind + 1] if kind < 3 else keep[3:5]:
+            copy.wait()
+
+    def columns():
+        each_turn(lambda turn: [copy.wait_recv() for copy in exchange(turn, True)])
+        for copy in keep[5:]:
+            copy.wait()
+
+    def rows_before():
+        pl.when(me > 0)(last_copy.wait_recv)
+
+    def finish():
+        for condition, what in sent:
+
+            def done(what=what):
+                for copy in copies(*what):
+                    copy.wait_send()
+
+            when(condition, done)
+        each_turn(lambda turn: [copy.wait_send() for copy in exchange(turn, False)])
+        pl.when(me + 1 < n)(last_copy.wait_send)
+
+    return last, columns, rows_before, finish
+
+
+def gather_body(n, *refs):
+    last, columns, rows_before, finish = gather_begin(n, refs, False)
+    for kind in range(4):
+        last(kind)
+    columns()
+    rows_before()
+    finish()
 
 
 def gather_weights(weights, gates, ffn, x, gain):
@@ -1101,8 +1120,10 @@
 
 
 def gates_of(conv_low, gate_ref, par_ref, head, cols, first):
-    pre_x = jnp.dot(conv_low, gate_ref[0, head], preferred_element_type=F32)
-    pre_a = jnp.dot(conv_low, gate_ref[1, head], preferred_element_type=F32)
+    size = gate_ref.shape[-1]
+    weight_x, weight_a = (gate_ref[gate, head].reshape(size, size) for gate in range(2))
+    pre_x = jnp.dot(conv_low, weight_x, preferred_element_type=F32)
+    pre_a = jnp.dot(conv_low, weight_a, preferred_element_type=F32)
     gate_x = jax.nn.sigmoid(pre_x + par_ref[5:6, cols])
     gate_a = jax.nn.sigmoid(pre_a + par_ref[6:7, cols])
     decay = jnp.exp(-8.0 * gate_a * par_ref[8:9, cols])
@@ -1114,6 +1135,25 @@
 FLIPPED = (((1,), (1,)), ((), ()))
 
 
+def by_columns(ref, cols):
+    if len(ref.shape) == 2:
+        return ref[:, cols]
+    return ref[:, :, cols].reshape(ref.shape[0] * ref.shape[1], -1)
+
+
+def by_rows(ref, start, size):
+    if len(ref.shape) == 2:
+        return ref[start : start + size]
+    rows = ref.shape[1]
+    parts, at = [], start
+    while at < start + size:
+        block, inside = divmod(at, rows)
+        upto = min(rows, inside + start + size - at)
+        parts.append(ref[block, inside:upto])
+        at += upto - inside
+    return jnp.concatenate(parts, axis=0)
+
+
 def first_row(tokens):
     row = lax.broadcasted_iota(jnp.int32, (tokens, 1), 0)
     return jnp.logical_and(row == 0, lax.axis_index("seq") == 0)
@@ -1122,6 +1162,7 @@
 def forward_body(
     n,
     hidden_units,
+    gathered,
     one_ref,
     last_ref,
     w_in_ref,
@@ -1132,6 +1173,7 @@
     x_ref,
     gain_ref,
     column_ref,
+    cot_ref,
     xb_ref,
     yp_ref,
     conv_ref,
@@ -1141,6 +1183,7 @@
     resid_ref,
     two_ref,
     near_ref,
+    cots_ref,
     w_in,
     w_branch,
     w_out,
@@ -1152,20 +1195,30 @@
     theirs,
     *sems,
 ):
-    send_tot, recv_tot, send_f, recv_f, send_m, recv_m, loaded = sems
+    send_tot, recv_tot, send_f, recv_f, send_m, recv_m, loaded, kept = sems[:8]
     tokens, width = xb_ref.shape
     model = one_ref.shape[1]
     me = lax.axis_index("seq")
-    size = gate_ref.shape[2]
+    size = gate_ref.shape[-1]
     loads = [
         pltpu.make_async_copy(src, dst, loaded.at[at])
         for at, (src, dst) in enumerate(
             ((w_in_ref, w_in), (w_branch_ref, w_branch), (w_out_ref, w_out))
         )
     ]
-    for load in loads:
-        load.start()
-    greet_all(n, me, True)
+    core = lax.axis_index("ch")
+    half = tokens // 2
+    if gathered is None:
+        for load in loads:
+            load.start()
+        greet_all(n, me, True)
+        x_start = 0
+    else:
+        last, columns, rows_before, gather_finish, gates_load = gathered
+        last(0)
+        loads[0].start()
+        rows_before()
+        x_start = core * half
     _, _, by_x, by_y, _ = whereabouts()
     part = column_ref.shape[1] // 2
     kinds = column_ref.shape[0]
@@ -1194,20 +1247,36 @@
             for copy in pair:
                 copy.start()
 
-    host(hosted[:1])
+    chain = Chain(n, cot_ref, cots_ref, *sems[8:])
+    keep = chain.keep(kept)
+    chain.start()
+    keep.start()
+    if gathered is None:
+        host(hosted[:1])
     loads[0].wait()
     for start in range(0, width, size):
         cols = slice(start, start + size)
-        low = jnp.dot(one_ref[...], w_in[:, cols], preferred_element_type=F32).astype(BF16)
+        low = jnp.dot(one_ref[...], by_columns(w_in, cols), preferred_element_type=F32).astype(BF16)
         xb_ref[:, cols] = low
         wide[8:, cols] = low.astype(F32)
-        low = jnp.dot(last_ref[...], w_in[:, cols], preferred_element_type=F32).astype(BF16)
+        low = jnp.dot(last_ref[...], by_columns(w_in, cols), preferred_element_type=F32).astype(BF16)
         wide[:8, cols] = low.astype(F32)[8:]
+    if gathered is not None:
+        last(1)
+        loads[1].start()
+        last(3)
+        gates_load.start()
+        columns()
+        host(hosted[:1])
+        gates_load.wait()
     loads[1].wait()
     for start in range(0, width, size):
         cols = slice(start, start + size)
-        yp_ref[:, cols] = jnp.dot(one_ref[...], w_branch[:, cols], preferred_element_type=F32)
-
+        yp_ref[:, cols] = jnp.dot(one_ref[...], by_columns(w_branch, cols), preferred_element_type=F32)
+
+    if gathered is not None:
+        last(2)
+        loads[2].start()
     edge_ref[:8] = wide[:8]
     first = first_row(tokens)
     for head in range(width // size):
@@ -1259,6 +1328,7 @@
 
     carry_in = lax.fori_loop(0, me, hear, zeros)
     edge_ref[8:] = jnp.broadcast_to(carry_in, (8, width))
+    chain.step(1)
 
     def finish(at, carry):
         r = pl.ds(pl.multiple_of(at * 16, 16), 16)
@@ -1278,11 +1348,9 @@
 
     lax.fori_loop(me + 1, n, sent, 0)
     loads[2].wait()
-    core = lax.axis_index("ch")
-    half = tokens // 2
     for start in range(0, model, size):
         cols = slice(start, start + size)
-        part = lax.dot_general(branch_ref[...], w_out[cols], FLIPPED, preferred_element_type=F32)
+        part = lax.dot_general(branch_ref[...], by_rows(w_out, start, size), FLIPPED, preferred_element_type=F32)
         mixed[0, :, cols] = part[:half]
         mixed[1, :, cols] = part[half:]
     exchange = pltpu.make_async_remote_copy(
@@ -1298,7 +1366,8 @@
 
     def norm(at, carry):
         r = pl.ds(pl.multiple_of(at * 16, 16), 16)
-        resid = x_ref[r].astype(F32) + (mixed[core, r] + mixed_got[r])
+        x = x_ref[pl.ds(pl.multiple_of(x_start + at * 16, 16), 16)]
+        resid = x.astype(F32) + (mixed[core, r] + mixed_got[r])
         resid_ref[r] = resid
         scale = lax.rsqrt(jnp.mean(resid * resid, axis=-1, keepdims=True) + 1e-06)
         two_ref[r] = (resid * scale * gain_ref[...]).astype(BF16)
@@ -1306,12 +1375,56 @@
 
     lax.fori_loop(0, half // 16, norm, 0)
     exchange.wait_send()
+    for step in range(2, n // INNER):
+        chain.step(step)
     for pair in hosted:
         for copy in pair:
             copy.wait()
-
-
-def mixer_forward(one, last, weights, gates, par, x_half, gain, column, hidden_units):
+    chain.finish()
+    keep.wait()
+    if gathered is not None:
+        gather_finish()
+
+
+def first_body(n, hidden_units, *refs):
+    given, refs = refs[:13], refs[13:]
+    weights, gates, ffn, (x_ref, norm_ref, par_ref, gain_ref, cot_ref) = (
+        given[:3],
+        given[3:5],
+        given[5:8],
+        given[8:],
+    )
+    outs, refs = refs[:18], refs[18:]
+    scratch, sems = refs[:10], refs[10:]
+    gather_sems, forward_sems, gate_sem = sems[:7], sems[7:-1], sems[-1]
+    me = lax.axis_index("seq")
+    greet_all(n, me, True)
+    steps = gather_begin(
+        n, (*weights, *gates, *ffn, x_ref, norm_ref, *outs[:8], *gather_sems), True
+    )
+    gate_s, scratch = scratch[0], scratch[1:]
+    full_gates, column_ref, one_ref, _, last_ref = outs[3:8]
+    gates_load = pltpu.make_async_copy(full_gates, gate_s, gate_sem)
+    forward_body(
+        n,
+        hidden_units,
+        (*steps, gates_load),
+        one_ref,
+        last_ref,
+        *outs[:3],
+        gate_s,
+        par_ref,
+        x_ref,
+        gain_ref,
+        column_ref,
+        cot_ref,
+        *outs[8:],
+        *scratch,
+        *forward_sems,
+    )
+
+
+def mixer_forward(one, last, weights, gates, par, x_half, gain, column, cotangent, hidden_units):
     n = lax.axis_size("seq")
     tokens, model = one.shape
     width = par.shape[1]
@@ -1321,7 +1434,7 @@
     whole = jax.ShapeDtypeStruct((tokens, width), F32)
     low = jax.ShapeDtypeStruct((tokens, width), BF16)
     return pl.pallas_call(
-        functools.partial(forward_body, n, hidden_units),
+        functools.partial(forward_body, n, hidden_units, None),
         out_shape=(
             low,
             whole,
@@ -1332,9 +1445,10 @@
             jax.ShapeDtypeStruct((half, model), F32),
             jax.ShapeDtypeStruct((half, model), BF16),
             jax.ShapeDtypeStruct((2, kinds, groups // 2, rows, units), column.dtype),
+            jax.ShapeDtypeStruct((groups, 2) + cotangent.shape, cotangent.dtype),
         ),
-        in_specs=[VMEM] * 2 + [HBM] * 3 + [VMEM] * 4 + [HBM],
-        out_specs=(VMEM,) * 8 + (HBM,),
+        in_specs=[VMEM] * 2 + [HBM] * 3 + [VMEM] * 4 + [HBM, HBM],
+        out_specs=(VMEM,) * 8 + (HBM, HBM),
         scratch_shapes=[
             pltpu.VMEM((model, width), BF16),
             pltpu.VMEM((model, width), BF16),
@@ -1352,10 +1466,81 @@
             dma(()),
             dma(()),
             dma((3,)),
+            dma(()),
+            *chain_semaphores(groups),
         ],
         compiler_params=params(4, 60),
         name="mixer_forward",
-    )(one, last, *weights, gates, par, x_half, gain, column)
+    )(one, last, *weights, gates, par, x_half, gain, column, cotangent)
+
+
+def gather_forward(weights, gates, ffn, x, norm_gain, par, gain, cotangent):
+    n = lax.axis_size("seq")
+    groups = n // INNER
+    tokens, model = x.shape
+    rows, width = weights[0].shape
+    half = tokens // 2
+    hidden_units = ffn[0].shape[1]
+    most = Units(hidden_units, groups, 0).most
+    heads, part, size = gates[0].shape
+    dma = pltpu.SemaphoreType.DMA
+    shape = jax.ShapeDtypeStruct
+    whole, low = shape((tokens, width), F32), shape((tokens, width), BF16)
+    weight = pltpu.VMEM((n, rows, width), BF16)
+    return pl.pallas_call(
+        functools.partial(first_body, n, hidden_units),
+        out_shape=(
+            *(shape((n, rows, width), BF16) for _ in range(3)),
+            shape((2, heads, n, part, size), BF16),
+            shape((3, groups, rows, most), BF16),
+            shape((tokens, model), BF16),
+            shape((model, tokens), BF16),
+            shape((16, model), BF16),
+            low,
+            whole,
+            low,
+            whole,
+            low,
+            shape((16, width), F32),
+            shape((half, model), F32),
+            shape((half, model), BF16),
+            shape((2, 3, groups // 2, rows, most), BF16),
+            shape((groups, 2, half, model), BF16),
+        ),
+        in_specs=[HBM] * 8 + [VMEM] * 4 + [HBM],
+        out_specs=(HBM,) * 5 + (VMEM,) * 11 + (HBM,) * 2,
+        scratch_shapes=[
+            pltpu.VMEM((2, heads, n, part, size), BF16),
+            weight,
+            weight,
+            weight,
+            pltpu.VMEM((2, half, model), F32),
+            pltpu.VMEM((half, model), F32),
+            pltpu.VMEM((tokens + 8, width), F32),
+            pltpu.VMEM((tokens, width), F32),
+            pltpu.VMEM((2, width), F32),
+            pltpu.VMEM((n, 2, width), F32),
+            dma((4, 2, n, 4)),
+            dma((4, 2, n)),
+            dma((3, groups)),
+            dma((3, groups)),
+            dma((8,)),
+            dma(()),
+            dma(()),
+            dma((n,)),
+            dma((n,)),
+            dma((3, 2)),
+            dma((3, 2)),
+            dma(()),
+            dma(()),
+            dma((3,)),
+            dma(()),
+            *chain_semaphores(groups),
+            dma(()),
+        ],
+        compiler_params=params(9, 60),
+        name="gather_forward",
+    )(*weights, *gates, *ffn, x, norm_gain, par, gain, cotangent)
 
 
 def backward_body(
@@ -1734,13 +1919,13 @@
 
 
 def ffn_body(n, hidden_units, *refs):
-    own_ref, cot_ref, column_ref, near_ref, resid_ref, gain_ref = refs[:6]
+    own_ref, cots_ref, column_ref, near_ref, resid_ref, gain_ref = refs[:6]
     block_ref, d_resid_ref, mixed_ref, d_gain_ref, turned_ref = refs[6:11]
     halves_ref, mine_ref, far_ref = refs[11:14]
     tokens, cots, w, extra, hidden, box, sib, got, stage, turned, my_cot = refs[14:25]
-    token_sems, cot_sems = refs[25:28], refs[28:31]
-    send_w, recv_w, keep_w, keep_c, keep_t, keep_m = refs[31:37]
-    send_c, recv_s, send_z, recv_r, send_f, recv_f, send_m, recv_m, move, out_sem = refs[37:]
+    token_sems = refs[25:28]
+    send_w, recv_w, keep_w, keep_c, keep_t, keep_m = refs[28:34]
+    send_c, recv_s, send_z, recv_r, send_f, recv_f, send_m, recv_m, move, out_sem = refs[34:]
     groups = n // INNER
     half = groups // 2
     me, outer, by_x, by_y, by_xy = whereabouts()
@@ -1772,7 +1957,6 @@
 
 
     chain_t = Chain(n, own_ref, tokens, *token_sems)
-    chain_c = Chain(n, cot_ref, cots, *cot_sems)
 
     def weight_copy(kind, h, far, receive=False):
         source = flips[h][0] if far else me
@@ -1808,22 +1992,21 @@
         for kind in range(3)
     ]
     every = [(h, far) for far in range(2) for h in range(2)]
-    own_t, own_c = chain_t.keep(keep_t), chain_c.keep(keep_c)
-    load_m = pltpu.make_async_copy(cot_ref, my_cot, keep_m)
+    own_t = chain_t.keep(keep_t)
+    load_c = pltpu.make_async_copy(cots_ref, cots, keep_c)
+    load_m = pltpu.make_async_copy(cots_ref.at[outer, core], my_cot, keep_m)
     chain_t.start()
     for kind in range(3):
         for h, far in every:
             weight_copy(kind, h, far).start()
     own_t.start()
-    own_c.start()
+    load_c.start()
     load_m.start()
     for kind in range(3):
         for copy in keep[kind]:
             copy.start()
-    for step in range(1, groups - 1):
+    for step in range(1, groups):
         chain_t.step(step)
-    chain_c.start()
-    chain_t.step(groups - 1)
     chain_t.finish()
     own_t.wait()
 
@@ -1854,7 +2037,6 @@
 
     weights_landed(0)
     weights_landed(1)
-    chain_c.step(1)
 
     def middle(place):
         left = tokens[place].reshape(count, model)
@@ -1869,15 +2051,6 @@
             hidden[2, r, c] = value.astype(BF16)
 
     each(groups, middle)
-    for step in range(2, groups):
-        chain_c.step(step)
-    chain_c.finish()
-    own_c.wait()
-    weights_landed(2)
-    for kind in range(3):
-        for h, far in every:
-            weight_copy(kind, h, far).wait_send()
-
     def back_hidden(place):
         left = cots[place].reshape(count, model)
         r = token_rows(place)
@@ -2089,23 +2262,25 @@
             out_sem.at[kind, h, far],
         )
 
-    partials(1, 0, 2)
+    load_c.wait()
     gradients(((2, 0),), cots, 0)
-    partials(1, 2, groups)
     gradients(((2, 0),), cots, 1)
+    weights_landed(2)
+    for kind in range(3):
+        for h, far in every:
+            weight_copy(kind, h, far).wait_send()
+    partials(1, 0, groups)
     each(groups, back_hidden)
     load_m.wait()
-    partials(0, 0, groups)
+    partials(0, 0, half)
+    between(1, range(1))
+    partials(0, half, groups)
     gradients(((0, 1),), tokens, 0)
-    between(1, range(1))
+    between(1, range(1, half))
     gradients(((0, 1),), tokens, 1)
-    between(1, range(1, groups // 2))
-    between(0, range(1))
     gradients(((1, 2),), tokens, 0)
-    between(1, range(groups // 2, groups - 1))
-    between(0, range(1, groups // 2))
+    between(1, range(half, groups - 1))
     gradients(((1, 2),), tokens, 1)
-    between(0, range(groups // 2, groups - 1))
 
     def shared(ref, at, part):
         return pltpu.make_async_remote_copy(
@@ -2135,12 +2310,14 @@
     for far in (1, 0):
         for h in range(2):
             collect(2, h, far)
+    between(0, range(1))
     totals(1, finish)
     show = shared(block_ref, 1, core)
     show.start()
     for far in (1, 0):
         for h in range(2):
             collect(0, h, far)
+    between(0, range(1, groups - 1))
     totals(0, norm)
     share = shared(mixed_ref, 0, core)
     share.start()
@@ -2163,7 +2340,7 @@
             out_copy(kind, h, far).wait()
 
 
-def feed_forward(own, cotangent, column, near, resid, gain, hidden_units):
+def feed_forward(own, cots, column, near, resid, gain, hidden_units):
     n = lax.axis_size("seq")
     groups = n // INNER
     tall, model = own.shape
@@ -2198,7 +2375,6 @@
             pltpu.VMEM((INNER * rows, groups * 2 * tall), BF16),
             pltpu.VMEM((tall, model), BF16),
             *chain_semaphores(groups),
-            *chain_semaphores(groups),
             dma((kinds, 2, 2)),
             dma((kinds, 2, 2)),
             dma((kinds, 3)),
@@ -2218,7 +2394,7 @@
         ],
         compiler_params=params(8, 63),
         name="feed_forward",
-    )(own, cotangent, column, near, resid, gain)
+    )(own, cots, column, near, resid, gain)
 
 
 def my_half(values):
@@ -2232,17 +2408,6 @@
     return jnp.concatenate(
         [jnp.where(core == 0, own, other), jnp.where(core == 0, other, own)], axis=0
     )
-
-
-def tokens_in(own):
-    groups = lax.axis_size("seq") // INNER
-    outer = lax.axis_index("seq") // INNER
-    got = put(jnp.zeros((groups,) + own.shape, own.dtype), own, outer)
-    for step in range(1, groups):
-        got = put(got, swap(own, "seq", step * INNER), outer ^ step)
-    other = swap(got, "ch", 1)
-    first = lax.axis_index("ch") == 0
-    return jnp.stack([jnp.where(first, got, other), jnp.where(first, other, got)], axis=1)
 
 
 def tokens_out(partial, half):
@@ -2259,14 +2424,13 @@
     return total
 
 
-def feed_forward_parts(n_two, cot_half, column, near, resid, ffn_gain, hidden_units):
+def feed_forward_parts(n_two, cot_half, all_cot, column, near, resid, ffn_gain, hidden_units):
     f32, bf16 = F32, BF16
     _, groups, depth, units = column.shape
     half_rows, model = n_two.shape
     tok_rows = 2 * half_rows
     _, norm_back_two = jax.vjp(scaled_norm, resid, ffn_gain)
     all_two, *full_ffn = gather_tokens(n_two, column, near)
-    all_cot = tokens_in(cot_half)
     all_two, all_cot = (v.reshape(groups * tok_rows, model) for v in (all_two, all_cot))
     own = Units(hidden_units, groups, lax.axis_index("ch")).width(lax.axis_index("seq") // INNER)
     valid = lax.broadcasted_iota(jnp.int32, (1, units), 1) < own
@@ -2340,15 +2504,7 @@
     groups = n // INNER
     hidden_units = ffn_gate.shape[1]
     x_half = my_half(inputs)
-    *full_mixer, full_gates, column, n_one, n_one_turned, last_rows = gather_weights(
-        [input_weight, branch_weight, out_weight.T],
-        [gate_x_blocks, gate_a_blocks],
-        [ffn_gate, ffn_up, ffn_down.T],
-        inputs,
-        norm_gain.reshape(1, model),
-    )
-    full_mixer = [w.reshape(model, width) for w in full_mixer]
-    gates = full_gates.reshape(2, heads, size, size)
+    cot_half = my_half(cotangent)
     par = jnp.concatenate(
         [
             channel_params,
@@ -2358,29 +2514,46 @@
         ],
         axis=0,
     )
-
-    cot_half = my_half(cotangent)
-
-    x_branch, y_pre, conv_out, states, branch_out, edge, resid, n_two, near = mixer_forward(
-        n_one,
-        last_rows,
-        full_mixer,
-        gates,
-        par,
-        x_half,
-        ffn_gain.reshape(1, model),
-        column,
-        hidden_units,
-    )
+    mixer_set = [input_weight, branch_weight, out_weight.T]
+    gate_set = [gate_x_blocks, gate_a_blocks]
+    ffn_set = [ffn_gate, ffn_up, ffn_down.T]
+    gain_one, gain_two = norm_gain.reshape(1, model), ffn_gain.reshape(1, model)
+    if depth % 16 == 0 and part % 16 == 0:
+        made = gather_forward(
+            mixer_set, gate_set, ffn_set, inputs, gain_one, par, gain_two, cot_half
+        )
+        *full_mixer, full_gates, column, n_one, n_one_turned, _ = made[:8]
+        full_mixer = [w.reshape(model, width) for w in full_mixer]
+        gates = full_gates.reshape(2, heads, size, size)
+        made = made[8:]
+    else:
+        *full_mixer, full_gates, column, n_one, n_one_turned, last_rows = gather_weights(
+            mixer_set, gate_set, ffn_set, inputs, gain_one
+        )
+        full_mixer = [w.reshape(model, width) for w in full_mixer]
+        gates = full_gates.reshape(2, heads, size, size)
+        made = mixer_forward(
+            n_one,
+            last_rows,
+            full_mixer,
+            gates,
+            par,
+            x_half,
+            gain_two,
+            column,
+            cot_half,
+            hidden_units,
+        )
+    x_branch, y_pre, conv_out, states, branch_out, edge, resid, n_two, near, cots = made
     if groups <= 4 and depth % 16 == 0:
         block_out, d_resid, d_mixed, d_ffn_gain_term, d_mixed_turned, halves, mine, _ = feed_forward(
-            n_two, cot_half, column, near, resid, ffn_gain.reshape(1, model), hidden_units
+            n_two, cots, column, near, resid, ffn_gain.reshape(1, model), hidden_units
         )
         block_out = block_out.reshape(tok_rows, model)
         d_mixed = d_mixed.reshape(tok_rows, model)
     else:
         block_out, d_resid, d_mixed, d_ffn_gain_term, halves, mine = feed_forward_parts(
-            n_two, cot_half, column, near, resid, ffn_gain, hidden_units
+            n_two, cot_half, cots, column, near, resid, ffn_gain, hidden_units
         )
         d_mixed_turned = d_mixed.T
     d_y, d_xb, d_gates, d_par, d_inputs, d_norm_gain_term, column_back = mixer_backward(

time: 721 us -> 706 us (0.979)
  Pallas kernels: 685 us -> 670 us
    pallas_call x1, Pallas kernels: 58.3 us -> 50.9 us  [mixer_backward(): pl.pallas_call(functools.partial(backward_body, n, hidden_units), out_sha...]
    pallas_call x2 -> x1, Pallas kernels: 239 us -> 233 us  [gather_forward(): pl.pallas_call(functools.partial(first_body, n, hidden_units), out_shape=...]
where the time goes in v7:
time: 706 us; the launch traced here: 696 us
  Pallas kernels  670 us (95%)
  local copies, waits for them, and re-layouts  17.7 us (3%)
  other arithmetic  7.65 us (1%)
    pallas_call x1, Pallas kernels, gather_forward(): pl.pallas_call(functools.partial(first_body, n, hidden_units), out_shape=...  233 us
    pallas_call x1, Pallas kernels, feed_forward(): pl.pallas_call(functools.partial(ffn_body, n, hidden_units), out_shape=(j...  199 us
    pallas_call x1, Pallas kernels, scatter_mixer(): pl.pallas_call(functools.partial(scatter_body, n), out_shape=(jax.ShapeDt...  187 us
    pallas_call x1, Pallas kernels, mixer_backward(): pl.pallas_call(functools.partial(backward_body, n, hidden_units), out_sha...  50.9 us

profile of v7, /device:TPU:25, one launch (start us, length us, event | category | flops | bytes accessed | tf_op | source)
XLA Modules:
  0.0 696.3 jit_solution(11305760671408598244)
XLA Ops:
  0.7 0.1 pad.3.clone
  0.7 1.3 reshape.76.refs_9_.gain_ref
  2.0 1.3 reshape.77.refs_11_.refs_5_
  3.4 0.8 compare_select_fusion
  4.2 1.5 maximum_maximum_fusion.refs_10_.par_ref
  5.7 2.4 constant_dynamic-slice_fusion
  8.1 233.0 %gather_forward.1 = (bf16[16,160,1280]{2,1,0:T(8,128)(2,1)}, bf16[16,160,1280]{2,1,0:T(8,128)(2,1)}, bf16[16,160,1280]{2,1,0:T(8,128)(2,1)}, bf16[2,5,16,16,256]...) custom-call(bf16[160,1280]{1,0:T(8,128)(2,1)} %refs_0_.1, ...), custom_call_target="tpu_custom_call" | custom-call | tf_op jit(solution)/shard_map/gather_forward/pallas_call | solution.py:1490
  241.1 198.7 %feed_forward.1 = (bf16[2,128,2560]{2,1,0:T(8,128)(2,1)}, f32[128,2560]{1,0:T(8,128)}, bf16[2,128,2560]{2,1,0:T(8,128)(2,1)}, f32[1,2560]{1,0:T(1,128)}, bf16[25...) custom-call(bf16[128,2560]{1,0:T(8,128)(2,1)} %get-tuple-element.46., ...), custom_call_target="tpu_custom_call" | custom-call | tf_op jit(solution)/shard_map/feed_forward/pallas_call | solution.py:2351
  439.8 50.9 %mixer_backward.1 = (bf16[256,1280]{1,0:T(8,128)(2,1)}, bf16[256,1280]{1,0:T(8,128)(2,1)}, bf16[16,2,16,1280]{3,2,1,0:T(8,128)(2,1)}, f32[8,1280]{1,0:T(8,128)},...) custom-call(bf16[256,2560]{1,0:T(8,128)(2,1)} %bitcast.34, ...), custom_call_target="tpu_custom_call" | custom-call | tf_op jit(solution)/shard_map/mixer_backward/pallas_call | solution.py:1870
  490.8 187.1 %scatter_mixer.1 = (f32[512,1280]{1,0:T(8,128)}, f32[16,1280]{1,0:T(8,128)}, bf16[3,160,3840]{2,1,0:T(8,128)(2,1)}) custom-call(bf16[16,160,256]{2,1,0:T(8,128)(2,1)} %bitcast.36, bf16[16,160,256]{2,1,0:T(8,128)(2,1)} %bitcast.37, bf16[256,1280]{1,0:T(8,128)(2,1)} %get-tuple-element.68.dy_ref, bf16[256,1280]{1,0:T(8,128)(2,1)} %get-tuple-element.69.dxb_ref, ...), custom_call_target="tpu_custom_call" | custom-call | tf_op jit(solution)/shard_map/scatter_mixer/pallas_call | solution.py:1079
  677.8 0.9 fusion
  678.7 1.4 slice.44
  680.1 0.6 reshape.89
  680.7 0.6 reshape.87
  681.3 0.9 slice.45
  682.2 3.1 slice_bitcast_fusion
  685.4 0.7 copy.28
  686.1 0.7 copy.27
  686.8 0.0 copy-start.1
  686.8 5.3 convert_bitcast_fusion
  692.1 0.0 copy-done.1
  692.1 1.1 copy.31
  693.2 1.2 copy-done
  694.3 1.5 copy.32
  (4 shorter events, 0.1 us)
Async XLA Ops:
  686.8 5.4 copy-start.1
  692.1 2.2 copy-start

commit v8 on v7

--- a/solution.py
+++ b/solution.py
@@ -456,9 +456,9 @@
 
     def step(self, step):
         for source, there, onward, way in self.ways(step):
-            pl.when(there)(self.copy(source, way).wait_recv)
-            pl.when(both(there, onward))(self.copy(source, way).start)
-            pl.when(there)(self.copy(source, 2).start)
+            pl.when(there)(lambda: self.copy(source, way).wait_recv())
+            pl.when(both(there, onward))(lambda: self.copy(source, way).start())
+            pl.when(there)(lambda: self.copy(source, 2).start())
 
     def finish(self):
         for source in range(self.groups):
@@ -468,8 +468,8 @@
         self.copy(self.outer, 2, True).wait_send()
         for step in range(1, self.groups):
             for source, there, onward, way in self.ways(step):
-                pl.when(both(there, onward))(self.copy(source, way).wait_send)
-                pl.when(there)(self.copy(source, 2).wait_send)
+                pl.when(both(there, onward))(lambda: self.copy(source, way).wait_send())
+                pl.when(there)(lambda: self.copy(source, 2).wait_send())
 
 
 def chain_semaphores(groups):
@@ -1322,11 +1322,16 @@
     lax.fori_loop(me + 1, n, tell, 0)
     host(hosted[1:])
 
-    def hear(place, state):
+    def hear(place, carry):
         heard(place).wait_recv()
-        return theirs[place, 0:1] * state + theirs[place, 1:2]
-
-    carry_in = lax.fori_loop(0, me, hear, zeros)
+        return carry
+
+    lax.fori_loop(0, me, hear, 0)
+    carry_in = zeros
+    for place in range(n):
+        gone = place < me
+        through = jnp.where(gone, theirs[place, 0:1], 1.0)
+        carry_in = through * carry_in + jnp.where(gone, theirs[place, 1:2], 0.0)
     edge_ref[8:] = jnp.broadcast_to(carry_in, (8, width))
     chain.step(1)
 
@@ -1387,8 +1392,8 @@
 
 
 def first_body(n, hidden_units, *refs):
-    given, refs = refs[:13], refs[13:]
-    weights, gates, ffn, (x_ref, norm_ref, par_ref, gain_ref, cot_ref) = (
+    given, refs = refs[:12], refs[12:]
+    weights, gates, ffn, (x_ref, gains_ref, par_ref, all_cot_ref) = (
         given[:3],
         given[3:5],
         given[5:8],
@@ -1398,6 +1403,10 @@
     scratch, sems = refs[:10], refs[10:]
     gather_sems, forward_sems, gate_sem = sems[:7], sems[7:-1], sems[-1]
     me = lax.axis_index("seq")
+    norm_ref, gain_ref = gains_ref.at[pl.ds(0, 1)], gains_ref.at[pl.ds(1, 1)]
+    half = x_ref.shape[0] // 2
+    start = pl.multiple_of(lax.axis_index("ch") * half, half)
+    cot_ref = all_cot_ref.at[pl.ds(start, half)]
     greet_all(n, me, True)
     steps = gather_begin(
         n, (*weights, *gates, *ffn, x_ref, norm_ref, *outs[:8], *gather_sems), True
@@ -1474,7 +1483,7 @@
     )(one, last, *weights, gates, par, x_half, gain, column, cotangent)
 
 
-def gather_forward(weights, gates, ffn, x, norm_gain, par, gain, cotangent):
+def gather_forward(weights, gates, ffn, x, gains, par, cotangent):
     n = lax.axis_size("seq")
     groups = n // INNER
     tokens, model = x.shape
@@ -1507,7 +1516,7 @@
             shape((2, 3, groups // 2, rows, most), BF16),
             shape((groups, 2, half, model), BF16),
         ),
-        in_specs=[HBM] * 8 + [VMEM] * 4 + [HBM],
+        in_specs=[HBM] * 8 + [VMEM] * 3 + [HBM],
         out_specs=(HBM,) * 5 + (VMEM,) * 11 + (HBM,) * 2,
         scratch_shapes=[
             pltpu.VMEM((2, heads, n, part, size), BF16),
@@ -1540,7 +1549,7 @@
         ],
         compiler_params=params(9, 60),
         name="gather_forward",
-    )(*weights, *gates, *ffn, x, norm_gain, par, gain, cotangent)
+    )(*weights, *gates, *ffn, x, gains, par, cotangent)
 
 
 def backward_body(
@@ -1683,12 +1692,16 @@
     lax.fori_loop(0, me, tell, 0)
     host(hosted[2:3])
 
-    def hear(turn, state):
-        place = n - 1 - turn
-        heard(place).wait_recv()
-        return theirs[place, 0:1] * state + theirs[place, 1:2]
-
-    carry_in = lax.fori_loop(0, n - 1 - me, hear, zeros)
+    def hear(turn, carry):
+        heard(n - 1 - turn).wait_recv()
+        return carry
+
+    lax.fori_loop(0, n - 1 - me, hear, 0)
+    carry_in = zeros
+    for place in reversed(range(n)):
+        gone = place > me
+        through = jnp.where(gone, theirs[place, 0:1], 1.0)
+        carry_in = through * carry_in + jnp.where(gone, theirs[place, 1:2], 0.0)
 
     def finish(turn, carry):
         r = pl.ds(pl.multiple_of((tiles - 1 - turn) * 8, 8), 8)
@@ -1750,6 +1763,36 @@
             dy_ref[...], w_branch[cols], FLIPPED, preferred_element_type=F32
         )
 
+    rows = own.shape[3]
+    chunk = 32 if rows % 32 == 0 else rows
+    outs = []
+
+    def collect(piece):
+        kind, at = divmod(piece, pieces)
+        for h in range(2):
+            hosted[piece][h].wait()
+
+            def add(turn, carry, h=h):
+                r = pl.ds(pl.multiple_of(turn * chunk, chunk), chunk)
+                own[h, kind, at, r] = (
+                    own[h, kind, at, r].astype(F32) + near_ref[h, kind, at, r].astype(F32)
+                ).astype(BF16)
+                return carry
+
+            lax.fori_loop(0, rows // chunk, add, 0)
+            outs.append(
+                pltpu.make_async_copy(
+                    own.at[h, kind, at],
+                    column_ref.at[kind, h * pieces + at],
+                    out_sem.at[kind, at, h],
+                )
+            )
+            outs[-1].start()
+
+    own_load.wait()
+    for piece in range(3):
+        collect(piece)
+
     @pl.when(me + 1 < n)
     def _():
         rows_copy.wait_recv()
@@ -1797,7 +1840,7 @@
 
     def norm(at, total):
         r = pl.ds(pl.multiple_of(at * 16, 16), 16)
-        x = x_ref[r].astype(F32)
+        x = x_ref[pl.ds(pl.multiple_of(core * half + at * 16, 16), 16)].astype(F32)
         scale = lax.rsqrt(jnp.mean(x * x, axis=-1, keepdims=True) + 1e-06)
         grad = d_one[core, r].astype(F32) + d_one_got[r].astype(F32)
         back = grad * gain_ref[...]
@@ -1816,31 +1859,8 @@
     )
     share.start()
     exchange.wait_send()
-    own_load.wait()
-    part, rows = own.shape[2:4]
-    chunk = 16 if rows % 16 == 0 else rows
-    outs = []
-    for kind in range(kinds):
-        for h in range(2):
-            for place in range(part):
-                hosted[kind * part + place][h].wait()
-
-                def add(at, carry, kind=kind, h=h, place=place):
-                    r = pl.ds(pl.multiple_of(at * chunk, chunk), chunk)
-                    own[h, kind, place, r] = (
-                        own[h, kind, place, r].astype(F32) + near_ref[h, kind, place, r].astype(F32)
-                    ).astype(BF16)
-                    return carry
-
-                lax.fori_loop(0, rows // chunk, add, 0)
-            outs.append(
-                pltpu.make_async_copy(
-                    own.at[h, kind],
-                    column_ref.at[kind, pl.ds(h * part, part)],
-                    out_sem.at[kind, h],
-                )
-            )
-            outs[-1].start()
+    for piece in range(3, len(hosted)):
+        collect(piece)
     for copy in outs:
         copy.wait()
     pltpu.make_async_remote_copy(
@@ -1911,7 +1931,7 @@
             dma(()),
             dma((3,)),
             dma(()),
-            dma((kinds, 2)),
+            dma((kinds, part, 2)),
         ],
         compiler_params=params(5, 60),
         name="mixer_backward",
@@ -2503,8 +2523,6 @@
     depth = ffn_gate.shape[0]
     groups = n // INNER
     hidden_units = ffn_gate.shape[1]
-    x_half = my_half(inputs)
-    cot_half = my_half(cotangent)
     par = jnp.concatenate(
         [
             channel_params,
@@ -2517,16 +2535,18 @@
     mixer_set = [input_weight, branch_weight, out_weight.T]
     gate_set = [gate_x_blocks, gate_a_blocks]
     ffn_set = [ffn_gate, ffn_up, ffn_down.T]
-    gain_one, gain_two = norm_gain.reshape(1, model), ffn_gain.reshape(1, model)
+    gains = jnp.stack([norm_gain, ffn_gain])
+    gain_one, gain_two = gains[:1], gains[1:]
     if depth % 16 == 0 and part % 16 == 0:
         made = gather_forward(
-            mixer_set, gate_set, ffn_set, inputs, gain_one, par, gain_two, cot_half
+            mixer_set, gate_set, ffn_set, inputs, gains, par, cotangent
         )
         *full_mixer, full_gates, column, n_one, n_one_turned, _ = made[:8]
         full_mixer = [w.reshape(model, width) for w in full_mixer]
         gates = full_gates.reshape(2, heads, size, size)
         made = made[8:]
     else:
+        cot_half = my_half(cotangent)
         *full_mixer, full_gates, column, n_one, n_one_turned, last_rows = gather_weights(
             mixer_set, gate_set, ffn_set, inputs, gain_one
         )
@@ -2538,7 +2558,7 @@
             full_mixer,
             gates,
             par,
-            x_half,
+            my_half(inputs),
             gain_two,
             column,
             cot_half,
@@ -2547,7 +2567,7 @@
     x_branch, y_pre, conv_out, states, branch_out, edge, resid, n_two, near, cots = made
     if groups <= 4 and depth % 16 == 0:
         block_out, d_resid, d_mixed, d_ffn_gain_term, d_mixed_turned, halves, mine, _ = feed_forward(
-            n_two, cots, column, near, resid, ffn_gain.reshape(1, model), hidden_units
+            n_two, cots, column, near, resid, gain_two, hidden_units
         )
         block_out = block_out.reshape(tok_rows, model)
         d_mixed = d_mixed.reshape(tok_rows, model)
@@ -2559,8 +2579,8 @@
     d_y, d_xb, d_gates, d_par, d_inputs, d_norm_gain_term, column_back = mixer_backward(
         d_mixed,
         full_mixer,
-        x_half,
-        norm_gain.reshape(1, model),
+        inputs,
+        gain_one,
         d_resid,
         y_pre,
         states,

time: 706 us -> 703 us (level)
  no operation moved by 1% of the time
where the time goes in v8:
time: 703 us; the launch traced here: 694 us
  Pallas kernels  670 us (95%)
  local copies, waits for them, and re-layouts  14.1 us (2%)
  other arithmetic  8.28 us (1%)
    pallas_call x1, Pallas kernels, gather_forward(): pl.pallas_call(functools.partial(first_body, n, hidden_units), out_shape=...  233 us
    pallas_call x1, Pallas kernels, feed_forward(): pl.pallas_call(functools.partial(ffn_body, n, hidden_units), out_shape=(j...  199 us
    pallas_call x1, Pallas kernels, scatter_mixer(): pl.pallas_call(functools.partial(scatter_body, n), out_shape=(jax.ShapeDt...  187 us
    pallas_call x1, Pallas kernels, mixer_backward(): pl.pallas_call(functools.partial(backward_body, n, hidden_units), out_sha...  50.9 us

profile of v8, /device:TPU:25, one launch (start us, length us, event | category | flops | bytes accessed | tf_op | source)
XLA Modules:
  0.0 693.7 jit_solution(8408999305218407874)
XLA Ops:
  0.7 0.1 pad.3.clone
  0.7 0.7 stack.9.gain_ref
  1.4 0.7 stack.10.refs_5_
  2.2 0.8 compare_select_fusion
  3.0 0.6 pad_maximum_fusion.refs_9_
  3.6 1.5 maximum_maximum_fusion.refs_10_.par_ref
  5.1 233.1 %gather_forward.1 = (bf16[16,160,1280]{2,1,0:T(8,128)(2,1)}, bf16[16,160,1280]{2,1,0:T(8,128)(2,1)}, bf16[16,160,1280]{2,1,0:T(8,128)(2,1)}, bf16[2,5,16,16,256]...) custom-call(bf16[160,1280]{1,0:T(8,128)(2,1)} %refs_0_.1, ...), custom_call_target="tpu_custom_call" | custom-call | tf_op jit(solution)/shard_map/gather_forward/pallas_call | solution.py:1499
  238.2 0.0 copy-done.2
  238.2 0.0 copy-done.3
  238.2 198.7 %feed_forward.1 = (bf16[2,128,2560]{2,1,0:T(8,128)(2,1)}, f32[128,2560]{1,0:T(8,128)}, bf16[2,128,2560]{2,1,0:T(8,128)(2,1)}, f32[1,2560]{1,0:T(1,128)}, bf16[25...) custom-call(bf16[128,2560]{1,0:T(8,128)(2,1)} %get-tuple-element.46., ...), custom_call_target="tpu_custom_call" | custom-call | tf_op jit(solution)/shard_map/feed_forward/pallas_call | solution.py:2371
  436.9 50.9 %mixer_backward.1 = (bf16[256,1280]{1,0:T(8,128)(2,1)}, bf16[256,1280]{1,0:T(8,128)(2,1)}, bf16[16,2,16,1280]{3,2,1,0:T(8,128)(2,1)}, f32[8,1280]{1,0:T(8,128)},...) custom-call(bf16[256,2560]{1,0:T(8,128)(2,1)} %bitcast.34, ...), custom_call_target="tpu_custom_call" | custom-call | tf_op jit(solution)/shard_map/mixer_backward/pallas_call | solution.py:1890
  487.8 187.4 %scatter_mixer.1 = (f32[512,1280]{1,0:T(8,128)}, f32[16,1280]{1,0:T(8,128)}, bf16[3,160,3840]{2,1,0:T(8,128)(2,1)}) custom-call(bf16[16,160,256]{2,1,0:T(8,128)(2,1)} %bitcast.36, bf16[16,160,256]{2,1,0:T(8,128)(2,1)} %bitcast.37, bf16[256,1280]{1,0:T(8,128)(2,1)} %get-tuple-element.68.dy_ref, bf16[256,1280]{1,0:T(8,128)(2,1)} %get-tuple-element.69.dxb_ref, ...), custom_call_target="tpu_custom_call" | custom-call | tf_op jit(solution)/shard_map/scatter_mixer/pallas_call | solution.py:1079
  675.2 0.9 fusion
  676.1 1.4 slice.44
  677.5 0.6 reshape.79
  678.1 0.6 reshape.77
  678.7 0.9 slice.45
  679.6 3.1 slice_bitcast_fusion
  682.8 0.7 copy.28
  683.5 0.7 copy.27
  684.2 5.3 convert_bitcast_fusion
  689.5 1.1 copy.31
  690.6 1.2 copy-done
  691.7 1.5 copy.32
  (8 shorter events, 0.1 us)
Async XLA Ops:
  1.4 236.7 %copy-start.2 = (f32[1,2560]{1,0:T(1,128)}, f32[1,2560]{1,0:T(1,128)S(1)}, u32[]{:S(2)}) copy-start(f32[1,2560]{1,0:T(1,128)S(1)} %stack.9.gain_ref) | copy-start | bytes 30724
  2.2 236.0 %copy-start.3 = (f32[1,2560]{1,0:T(1,128)}, f32[1,2560]{1,0:T(1,128)S(1)}, u32[]{:S(2)}) copy-start(f32[1,2560]{1,0:T(1,128)S(1)} %stack.10.refs_5_) | copy-start | bytes 30724
  684.2 5.4 copy-start.1
  689.5 2.2 copy-start

commit v9 on v8

--- a/solution.py
+++ b/solution.py
@@ -172,7 +172,7 @@
                 recv_m.at[kind, h, source],
                 target,
             )
-            for kind, (given, dst) in enumerate(pairs)
+            for kind, (given, dst) in ((at, pairs[at]) for at in (3, 0, 1, 2))
             if kind in kinds
         ]
 
@@ -1217,7 +1217,10 @@
         last, columns, rows_before, gather_finish, gates_load = gathered
         last(0)
         loads[0].start()
+        last(3)
+        gates_load.start()
         rows_before()
+        columns()
         x_start = core * half
     _, _, by_x, by_y, _ = whereabouts()
     part = column_ref.shape[1] // 2
@@ -1251,8 +1254,7 @@
     keep = chain.keep(kept)
     chain.start()
     keep.start()
-    if gathered is None:
-        host(hosted[:1])
+    host(hosted[:1])
     loads[0].wait()
     for start in range(0, width, size):
         cols = slice(start, start + size)
@@ -1261,22 +1263,19 @@
         wide[8:, cols] = low.astype(F32)
         low = jnp.dot(last_ref[...], by_columns(w_in, cols), preferred_element_type=F32).astype(BF16)
         wide[:8, cols] = low.astype(F32)[8:]
-    if gathered is not None:
-        last(1)
-        loads[1].start()
-        last(3)
-        gates_load.start()
-        columns()
-        host(hosted[:1])
+
+    def branch():
+        loads[1].wait()
+        for start in range(0, width, size):
+            cols = slice(start, start + size)
+            yp_ref[:, cols] = jnp.dot(
+                one_ref[...], by_columns(w_branch, cols), preferred_element_type=F32
+            )
+
+    if gathered is None:
+        branch()
+    else:
         gates_load.wait()
-    loads[1].wait()
-    for start in range(0, width, size):
-        cols = slice(start, start + size)
-        yp_ref[:, cols] = jnp.dot(one_ref[...], by_columns(w_branch, cols), preferred_element_type=F32)
-
-    if gathered is not None:
-        last(2)
-        loads[2].start()
     edge_ref[:8] = wide[:8]
     first = first_row(tokens)
     for head in range(width // size):
@@ -1321,6 +1320,12 @@
 
     lax.fori_loop(me + 1, n, tell, 0)
     host(hosted[1:])
+    if gathered is not None:
+        last(1)
+        loads[1].start()
+        last(2)
+        loads[2].start()
+        branch()
 
     def hear(place, carry):
         heard(place).wait_recv()

time: 703 us -> 703 us (level)
  no operation moved by 1% of the time
where the time goes in v9:
time: 703 us; the launch traced here: 694 us
  Pallas kernels  670 us (95%)
  local copies, waits for them, and re-layouts  14.1 us (2%)
  other arithmetic  8.28 us (1%)
    pallas_call x1, Pallas kernels, gather_forward(): pl.pallas_call(functools.partial(first_body, n, hidden_units), out_shape=...  233 us
    pallas_call x1, Pallas kernels, feed_forward(): pl.pallas_call(functools.partial(ffn_body, n, hidden_units), out_shape=(j...  199 us
    pallas_call x1, Pallas kernels, scatter_mixer(): pl.pallas_call(functools.partial(scatter_body, n), out_shape=(jax.ShapeDt...  187 us
    pallas_call x1, Pallas kernels, mixer_backward(): pl.pallas_call(functools.partial(backward_body, n, hidden_units), out_sha...  51.5 us

profile of v9, /device:TPU:25, one launch (start us, length us, event | category | flops | bytes accessed | tf_op | source)
XLA Modules:
  0.0 693.7 jit_solution(15302623362415466729)
XLA Ops:
  0.7 0.1 pad.3.clone
  0.7 0.7 stack.9.gain_ref
  1.4 0.7 stack.10.refs_5_
  2.2 0.8 compare_select_fusion
  3.0 0.6 pad_maximum_fusion.refs_9_
  3.6 1.5 maximum_maximum_fusion.refs_10_.par_ref
  5.1 232.6 %gather_forward.1 = (bf16[16,160,1280]{2,1,0:T(8,128)(2,1)}, bf16[16,160,1280]{2,1,0:T(8,128)(2,1)}, bf16[16,160,1280]{2,1,0:T(8,128)(2,1)}, bf16[2,5,16,16,256]...) custom-call(bf16[160,1280]{1,0:T(8,128)(2,1)} %refs_0_.1, ...), custom_call_target="tpu_custom_call" | custom-call | tf_op jit(solution)/shard_map/gather_forward/pallas_call | solution.py:1504
  237.7 0.0 copy-done.2
  237.7 0.0 copy-done.3
  237.7 199.1 %feed_forward.1 = (bf16[2,128,2560]{2,1,0:T(8,128)(2,1)}, f32[128,2560]{1,0:T(8,128)}, bf16[2,128,2560]{2,1,0:T(8,128)(2,1)}, f32[1,2560]{1,0:T(1,128)}, bf16[25...) custom-call(bf16[128,2560]{1,0:T(8,128)(2,1)} %get-tuple-element.46., ...), custom_call_target="tpu_custom_call" | custom-call | tf_op jit(solution)/shard_map/feed_forward/pallas_call | solution.py:2376
  436.8 51.5 %mixer_backward.1 = (bf16[256,1280]{1,0:T(8,128)(2,1)}, bf16[256,1280]{1,0:T(8,128)(2,1)}, bf16[16,2,16,1280]{3,2,1,0:T(8,128)(2,1)}, f32[8,1280]{1,0:T(8,128)},...) custom-call(bf16[256,2560]{1,0:T(8,128)(2,1)} %bitcast.34, ...), custom_call_target="tpu_custom_call" | custom-call | tf_op jit(solution)/shard_map/mixer_backward/pallas_call | solution.py:1895
  488.3 187.0 %scatter_mixer.1 = (f32[512,1280]{1,0:T(8,128)}, f32[16,1280]{1,0:T(8,128)}, bf16[3,160,3840]{2,1,0:T(8,128)(2,1)}) custom-call(bf16[16,160,256]{2,1,0:T(8,128)(2,1)} %bitcast.36, bf16[16,160,256]{2,1,0:T(8,128)(2,1)} %bitcast.37, bf16[256,1280]{1,0:T(8,128)(2,1)} %get-tuple-element.68.dy_ref, bf16[256,1280]{1,0:T(8,128)(2,1)} %get-tuple-element.69.dxb_ref, ...), custom_call_target="tpu_custom_call" | custom-call | tf_op jit(solution)/shard_map/scatter_mixer/pallas_call | solution.py:1079
  675.3 0.9 fusion
  676.1 1.4 slice.44
  677.5 0.6 reshape.79
  678.1 0.6 reshape.77
  678.7 0.9 slice.45
  679.7 3.1 slice_bitcast_fusion
  682.9 0.7 copy.28
  683.5 0.7 copy.27
  684.2 5.3 convert_bitcast_fusion
  689.6 1.1 copy.31
  690.6 1.2 copy-done
  691.8 1.5 copy.32
  (8 shorter events, 0.1 us)
Async XLA Ops:
  1.4 236.3 %copy-start.2 = (f32[1,2560]{1,0:T(1,128)}, f32[1,2560]{1,0:T(1,128)S(1)}, u32[]{:S(2)}) copy-start(f32[1,2560]{1,0:T(1,128)S(1)} %stack.9.gain_ref) | copy-start | bytes 30724
  2.2 235.6 %copy-start.3 = (f32[1,2560]{1,0:T(1,128)}, f32[1,2560]{1,0:T(1,128)S(1)}, u32[]{:S(2)}) copy-start(f32[1,2560]{1,0:T(1,128)S(1)} %stack.10.refs_5_) | copy-start | bytes 30724
  684.2 5.4 copy-start.1
  689.6 2.2 copy-start

commit v10 on v8

--- a/solution.py
+++ b/solution.py
@@ -2126,7 +2126,7 @@
             box.at[0, core], got.at[kind, slot], send_z.at[kind, 0], recv_r.at[kind, slot], by_x
         )
 
-    chunk = 16
+    chunk = 32
 
     def rows_of(at):
         return pl.ds(pl.multiple_of(at * chunk, chunk), chunk)

time: 703 us -> 702 us (level)
  no operation moved by 1% of the time
where the time goes in v10:
time: 702 us; the launch traced here: 693 us
  Pallas kernels  669 us (95%)
  local copies, waits for them, and re-layouts  14.1 us (2%)
  other arithmetic  8.28 us (1%)
    pallas_call x1, Pallas kernels, gather_forward(): pl.pallas_call(functools.partial(first_body, n, hidden_units), out_shape=...  233 us
    pallas_call x1, Pallas kernels, feed_forward(): pl.pallas_call(functools.partial(ffn_body, n, hidden_units), out_shape=(j...  198 us
    pallas_call x1, Pallas kernels, scatter_mixer(): pl.pallas_call(functools.partial(scatter_body, n), out_shape=(jax.ShapeDt...  187 us
    pallas_call x1, Pallas kernels, mixer_backward(): pl.pallas_call(functools.partial(backward_body, n, hidden_units), out_sha...  50.9 us

profile of v10, /device:TPU:25, one launch (start us, length us, event | category | flops | bytes accessed | tf_op | source)
XLA Modules:
  0.0 693.1 jit_solution(6338062881138628292)
XLA Ops:
  0.7 0.1 pad.3.clone
  0.7 0.7 stack.9.gain_ref
  1.4 0.7 stack.10.refs_5_
  2.2 0.8 compare_select_fusion
  3.0 0.6 pad_maximum_fusion.refs_9_
  3.6 1.5 maximum_maximum_fusion.refs_10_.par_ref
  5.1 233.1 %gather_forward.1 = (bf16[16,160,1280]{2,1,0:T(8,128)(2,1)}, bf16[16,160,1280]{2,1,0:T(8,128)(2,1)}, bf16[16,160,1280]{2,1,0:T(8,128)(2,1)}, bf16[2,5,16,16,256]...) custom-call(bf16[160,1280]{1,0:T(8,128)(2,1)} %refs_0_.1, ...), custom_call_target="tpu_custom_call" | custom-call | tf_op jit(solution)/shard_map/gather_forward/pallas_call | solution.py:1499
  238.2 0.0 copy-done.2
  238.2 0.0 copy-done.3
  238.2 198.1 %feed_forward.1 = (bf16[2,128,2560]{2,1,0:T(8,128)(2,1)}, f32[128,2560]{1,0:T(8,128)}, bf16[2,128,2560]{2,1,0:T(8,128)(2,1)}, f32[1,2560]{1,0:T(1,128)}, bf16[25...) custom-call(bf16[128,2560]{1,0:T(8,128)(2,1)} %get-tuple-element.46., ...), custom_call_target="tpu_custom_call" | custom-call | tf_op jit(solution)/shard_map/feed_forward/pallas_call | solution.py:2371
  436.3 50.9 %mixer_backward.1 = (bf16[256,1280]{1,0:T(8,128)(2,1)}, bf16[256,1280]{1,0:T(8,128)(2,1)}, bf16[16,2,16,1280]{3,2,1,0:T(8,128)(2,1)}, f32[8,1280]{1,0:T(8,128)},...) custom-call(bf16[256,2560]{1,0:T(8,128)(2,1)} %bitcast.34, ...), custom_call_target="tpu_custom_call" | custom-call | tf_op jit(solution)/shard_map/mixer_backward/pallas_call | solution.py:1890
  487.2 187.4 %scatter_mixer.1 = (f32[512,1280]{1,0:T(8,128)}, f32[16,1280]{1,0:T(8,128)}, bf16[3,160,3840]{2,1,0:T(8,128)(2,1)}) custom-call(bf16[16,160,256]{2,1,0:T(8,128)(2,1)} %bitcast.36, bf16[16,160,256]{2,1,0:T(8,128)(2,1)} %bitcast.37, bf16[256,1280]{1,0:T(8,128)(2,1)} %get-tuple-element.68.dy_ref, bf16[256,1280]{1,0:T(8,128)(2,1)} %get-tuple-element.69.dxb_ref, ...), custom_call_target="tpu_custom_call" | custom-call | tf_op jit(solution)/shard_map/scatter_mixer/pallas_call | solution.py:1079
  674.6 0.9 fusion
  675.5 1.4 slice.44
  676.9 0.6 reshape.79
  677.5 0.6 reshape.77
  678.1 0.9 slice.45
  679.0 3.1 slice_bitcast_fusion
  682.2 0.7 copy.28
  682.9 0.7 copy.27
  683.6 5.3 convert_bitcast_fusion
  688.9 1.1 copy.31
  690.0 1.2 copy-done
  691.1 1.5 copy.32
  (8 shorter events, 0.1 us)
Async XLA Ops:
  1.4 236.7 %copy-start.2 = (f32[1,2560]{1,0:T(1,128)}, f32[1,2560]{1,0:T(1,128)S(1)}, u32[]{:S(2)}) copy-start(f32[1,2560]{1,0:T(1,128)S(1)} %stack.9.gain_ref) | copy-start | bytes 30724
  2.2 236.0 %copy-start.3 = (f32[1,2560]{1,0:T(1,128)}, f32[1,2560]{1,0:T(1,128)S(1)}, u32[]{:S(2)}) copy-start(f32[1,2560]{1,0:T(1,128)S(1)} %stack.10.refs_5_) | copy-start | bytes 30724
  683.6 5.4 copy-start.1
  688.9 2.2 copy-start
